TPU v7x, 512 devices: a whole 4x4x16 slice. The times are simulated.
512 devices in a mesh: dp: 16 (over x, y_hi, core), expert: 32 (over y_lo, z).
Axes of the slice: x: 4, y: 4 (y_hi: 2, y_lo: 2; y = y_hi * 2 + y_lo), z: 16, core: 2. Of those that a mesh axis runs over, the one named last changes fastest.
Arguments:
- tokens: bfloat16 [65536, 2048], P(('dp', 'expert')), may hold values from -6 to 6
- expert_ids: int32 [65536, 1], P(('dp', 'expert')), may hold values from 0 to 31; in each aligned block of 128 rows (0 to 127, 128 to 255, ...) at most 8 rows name the same one
- gate_units: int32 [65536, 1], P(('dp', 'expert')), may hold values from 16 to 256
- cotangent: bfloat16 [65536, 2048], P(('dp', 'expert')), may hold values from -6 to 6
- w_gate: bfloat16 [32, 2048, 768], P('expert', 'dp'), may hold values from -0.125 to 0.125
- w_up: bfloat16 [32, 2048, 768], P('expert', 'dp'), may hold values from -0.125 to 0.125
- w_down: bfloat16 [32, 2048, 768], P('expert', 'dp'), may hold values from -0.21875 to 0.21875
Outputs:
- mixed: bfloat16 [65536, 2048], P(('dp', 'expert'))
- grad_tokens: bfloat16 [65536, 2048], P(('dp', 'expert'))
- grad_gate: float32 [32, 2048, 768], P('expert', 'dp')
- grad_up: float32 [32, 2048, 768], P('expert', 'dp')
- grad_down: float32 [32, 2048, 768], P('expert', 'dp')
Inputs may be any that keep to these rules, and one draw needn't show every extreme that they name: `expert_ids`: each row names one expert; the 128 rows of one device name no expert more than 8 times, a bound that some block reaches.
All inputs are finite; a program needn't handle non-finite values.
Results may differ from a plain program's by a relative error of at most 0.0057.
Values may be sent and summed in bfloat16 or wider, within the bound.
No kernel may reach another device: no remote copies, remote signals or barrier semaphores. Data moves between devices by JAX's collectives and lax.ppermute only.
A program may use at most 128 MiB of HBM per device.

v0:
```python
import jax
import jax.numpy as jnp
from jax import lax
from jax.sharding import PartitionSpec as P


def expert_rows(rows_x, rows_g, gate_w, up_w, down_w):
    contract_one = (((1,), (1,)), ((), ()))
    pre = jnp.dot(rows_x, gate_w, preferred_element_type=jnp.float32)
    lin = jnp.dot(rows_x, up_w, preferred_element_type=jnp.float32)
    sig = jax.nn.sigmoid(pre)
    active = pre * sig
    hidden = (active * lin).astype(jnp.bfloat16)
    out = lax.dot_general(hidden, down_w, contract_one, preferred_element_type=jnp.float32).astype(
        jnp.bfloat16
    )
    d_hid = jnp.dot(rows_g, down_w, preferred_element_type=jnp.float32)
    d_pre = (d_hid * lin * sig * (1.0 + pre * (1.0 - sig))).astype(jnp.bfloat16)
    d_lin = (d_hid * active).astype(jnp.bfloat16)
    back = lax.dot_general(d_pre, gate_w, contract_one, preferred_element_type=jnp.float32)
    back = (
        back + lax.dot_general(d_lin, up_w, contract_one, preferred_element_type=jnp.float32)
    ).astype(jnp.bfloat16)
    return (out, back, hidden, d_pre, d_lin)


def routing_slots(flags, capacity, limit):
    ranks = jnp.cumsum(flags, axis=0) - 1
    offsets = capacity * jnp.arange(flags.shape[1], dtype=jnp.int32)
    column = jnp.sum(flags * (ranks + offsets[None, :]), axis=1)
    used = jnp.sum(flags, axis=1) > 0
    return jnp.where(used, column, limit)


def place(rows, slots, count):
    buffer = jnp.zeros((count + 1, rows.shape[1]), rows.dtype).at[slots].set(rows)
    return buffer[:count]


def fetch(buffer, slots):
    extended = jnp.concatenate([buffer, jnp.zeros((1, buffer.shape[1]), buffer.dtype)], axis=0)
    return extended[slots]


def feature_blocks(owned_x, owned_g):
    groups = lax.axis_size("dp")
    block = owned_x.shape[1] // groups
    split_x = owned_x.reshape(owned_x.shape[0], groups, block)
    split_g = owned_g.reshape(owned_g.shape[0], groups, block)
    column_x, column_g = (
        lax.all_to_all(split_x, "dp", split_axis=1, concat_axis=0, tiled=True),
        lax.all_to_all(split_g, "dp", split_axis=1, concat_axis=0, tiled=True),
    )
    return (column_x.reshape(-1, block), column_g.reshape(-1, block))


def local(tokens, expert_ids, gate_units, cotangent, w_gate, w_up, w_down):
    tok, width = tokens.shape
    top = expert_ids.shape[1]
    experts = lax.axis_size("expert")
    capacity = min(tok, 2 * tok * top // experts)
    flat_ids = expert_ids.reshape(-1)
    scale = gate_units.reshape(-1).astype(jnp.float32) / 256.0
    row_token = jnp.arange(tok * top, dtype=jnp.int32) // top
    rows_x = tokens[row_token]
    rows_g = (scale[:, None] * cotangent[row_token].astype(jnp.float32)).astype(jnp.bfloat16)
    labels = jnp.arange(experts, dtype=jnp.int32)
    onehot = (flat_ids[:, None] == labels[None, :]).astype(jnp.int32)
    full_gate, full_up, full_down = (
        lax.all_gather(w_gate, "dp", axis=1, tiled=True),
        lax.all_gather(w_up, "dp", axis=1, tiled=True),
        lax.all_gather(w_down, "dp", axis=1, tiled=True),
    )
    full_gate, full_up, full_down = (full_gate[0], full_up[0], full_down[0])
    slots = routing_slots(onehot, capacity, experts * capacity)
    send_x = place(rows_x, slots, experts * capacity).reshape(experts, capacity, width)
    send_g = place(rows_g, slots, experts * capacity).reshape(experts, capacity, width)
    recv_x, recv_g = (
        lax.all_to_all(send_x, "expert", split_axis=0, concat_axis=0, tiled=True),
        lax.all_to_all(send_g, "expert", split_axis=0, concat_axis=0, tiled=True),
    )
    owned_x = recv_x.reshape(-1, width)
    owned_g = recv_g.reshape(-1, width)
    out, back, hidden, d_pre, d_lin = expert_rows(owned_x, owned_g, full_gate, full_up, full_down)
    got_out, got_back = (
        lax.all_to_all(
            out.reshape(experts, capacity, width), "expert", split_axis=0, concat_axis=0, tiled=True
        ),
        lax.all_to_all(
            back.reshape(experts, capacity, width),
            "expert",
            split_axis=0,
            concat_axis=0,
            tiled=True,
        ),
    )
    column_x, column_g = feature_blocks(owned_x, owned_g)
    row_out = fetch(got_out.reshape(-1, width), slots)
    row_back = fetch(got_back.reshape(-1, width), slots)
    mixed = jnp.sum(
        (scale[:, None] * row_out.astype(jnp.float32)).reshape(tok, top, width), axis=1
    ).astype(jnp.bfloat16)
    grad_tokens = jnp.sum(row_back.astype(jnp.float32).reshape(tok, top, width), axis=1).astype(
        jnp.bfloat16
    )
    contract_zero = (((0,), (0,)), ((), ()))
    piece_hidden = lax.all_gather(hidden, "dp", axis=0, tiled=True)
    piece_pre = lax.all_gather(d_pre, "dp", axis=0, tiled=True)
    piece_lin = lax.all_gather(d_lin, "dp", axis=0, tiled=True)
    first = lax.dot_general(column_x, piece_pre, contract_zero, preferred_element_type=jnp.float32)
    second = lax.dot_general(column_x, piece_lin, contract_zero, preferred_element_type=jnp.float32)
    third = lax.dot_general(
        column_g, piece_hidden, contract_zero, preferred_element_type=jnp.float32
    )
    return (mixed, grad_tokens, first[None], second[None], third[None])


def solution(mesh):
    placed = (
        P(("dp", "expert"), None),
        P(("dp", "expert"), None),
        P(("dp", "expert"), None),
        P(("dp", "expert"), None),
        P("expert", "dp", None),
        P("expert", "dp", None),
        P("expert", "dp", None),
    )
    return jax.shard_map(
        local,
        mesh=mesh,
        in_specs=placed,
        out_specs=(
            P(("dp", "expert"), None),
            P(("dp", "expert"), None),
            P("expert", "dp", None),
            P("expert", "dp", None),
            P("expert", "dp", None),
        ),
        check_vma=False,
    )
```

profile of v0, /device:TPU:1, one launch (start us, length us, event | category | flops | bytes accessed | tf_op | source)
XLA Modules:
  0.0 506.6 jit_solution(9242575686954864589)
XLA Ops:
  7.2 0.0 copy-start
  7.2 0.0 all-gather.11.cloned.1.call-start
  7.2 0.7 all-gather.11.cloned.1.call-update
  7.9 0.0 all-gather.9.cloned.1.call-start
  8.0 0.7 all-gather.9.cloned.1.call-update
  8.7 0.7 fusion.37
  9.4 0.2 reduce_window_sum.11
  9.6 0.8 fusion.38
  10.4 0.7 multiply_bitcast_fusion
  11.1 0.0 copy-done
  11.1 3.4 scatter_custom_fusion.1
  14.6 1.0 slice_bitcast_fusion
  15.6 17.0 %all-to-all-start.2 = ((bf16[32,8,2048]{2,1,0:T(8,128)(2,1)}), bf16[32,8,2048]{2,1,0:T(8,128)(2,1)S(1)}, u32[]{:S(2)}, u32[]{:S(2)}) async-start(bf16[32,8,2048]{2,1,0:T(8,128)(2,1)} %slice_bitcast_fusion), calls=%async_computation.2 | async-start | bytes 2097152 | tf_op jit(solution)/shard_map/all_to_all | solution.py:80
  32.6 0.0 all-gather.7.cloned.1.call-start
  32.7 0.7 all-gather.7.cloned.1.call-update
  33.4 3.9 scatter_custom_fusion
  37.2 1.1 slice_bitcast_fusion.1
  38.3 44.0 %all-to-all-done.2 = bf16[32,8,2048]{2,1,0:T(8,128)(2,1)S(1)} async-done(((bf16[32,8,2048]{2,1,0:T(8,128)(2,1)}), bf16[32,8,2048]{2,1,0:T(8,128)(2,1)S(1)}, u32[]{:S(2)}, u32[]{:S(2)}) %all-to-all-start.2) | async-done | bytes 1048608 | tf_op jit(solution)/shard_map/all_to_all | solution.py:80
  82.3 9.2 %all-to-all-start = ((bf16[32,8,2048]{2,1,0:T(8,128)(2,1)}), bf16[32,8,2048]{2,1,0:T(8,128)(2,1)S(1)}, u32[]{:S(2)}, u32[]{:S(2)}) async-start(bf16[32,8,2048]{2,1,0:T(8,128)(2,1)} %slice_bitcast_fusion.1), calls=%async_computation | async-start | bytes 2097152 | tf_op jit(solution)/shard_map/all_to_all | solution.py:79
  91.5 0.0 all-gather.13.cloned.1.call-start
  91.6 0.0 all-gather.11.cloned.1.call-done
  91.6 3.7 fusion
  95.3 0.0 copy-done.2
  95.3 45.9 %all-to-all-done = bf16[32,8,2048]{2,1,0:T(8,128)(2,1)S(1)} async-done(((bf16[32,8,2048]{2,1,0:T(8,128)(2,1)}), bf16[32,8,2048]{2,1,0:T(8,128)(2,1)S(1)}, u32[]{:S(2)}, u32[]{:S(2)}) %all-to-all-start) | async-done | bytes 1048608 | tf_op jit(solution)/shard_map/all_to_all | solution.py:79
  141.2 18.4 %all-gather.9.cloned.1.call-done = bf16[1,2048,768]{2,1,0:T(8,128)(2,1)} async-done(((bf16[1,128,768]{2,1,0:T(8,128)(2,1)}), bf16[1,2048,768]{2,1,0:T(8,128)(2,1)}) %all-gather.9.cloned.1.call-update) | async-done | bytes 3145744 | tf_op jit(solution)/shard_map/all_gather | solution.py:71
  159.6 3.7 fusion.6
  163.4 65.1 %all-gather.7.cloned.1.call-done = bf16[1,2048,768]{2,1,0:T(8,128)(2,1)} async-done(((bf16[1,128,768]{2,1,0:T(8,128)(2,1)}), bf16[1,2048,768]{2,1,0:T(8,128)(2,1)}) %all-gather.7.cloned.1.call-update) | async-done | bytes 3145744 | tf_op jit(solution)/shard_map/all_gather | solution.py:70
  228.4 0.0 copy-done.7
  228.5 4.3 multiply_convert_fusion.3
  232.7 0.0 all-gather.13.cloned.1.call-update
  232.8 0.0 all-gather.15.cloned.1.call-start
  232.8 0.5 all-gather.15.cloned.1.call-update
  233.4 0.0 all-gather.17.cloned.1.call-start
  233.4 0.5 all-gather.17.cloned.1.call-update
  233.9 0.0 copy-start.6
  233.9 0.2 copy.16
  234.2 1.2 copy.14
  235.4 3.9 all-to-all-start.4
  239.3 0.0 copy-done.6
  239.3 0.0 copy-start.5
  239.4 4.0 fusion.21
  243.3 13.6 %all-to-all-done.4 = bf16[256,16,128]{2,0,1:T(8,128)(2,1)S(1)} async-done(((bf16[256,16,128]{2,0,1:T(8,128)(2,1)}), bf16[256,16,128]{2,0,1:T(8,128)(2,1)S(1)}, u32[]{:S(2)}, u32[]{:S(2)}) %all-to-all-start.4) | async-done | bytes 1048608 | tf_op jit(solution)/shard_map/all_to_all | solution.py:51
  256.9 12.9 %all-to-all-start.1 = ((bf16[32,8,2048]{2,1,0:T(8,128)(2,1)}), bf16[32,8,2048]{2,1,0:T(8,128)(2,1)S(1)}, u32[]{:S(2)}, u32[]{:S(2)}) async-start(bf16[32,8,2048]{2,1,0:T(8,128)(2,1)} %fusion.21), calls=%async_computation.1 | async-start | bytes 2097152 | tf_op jit(solution)/shard_map/all_to_all | solution.py:86
  269.8 0.0 copy-done.5
  269.8 0.0 copy-start.4
  269.8 3.0 fusion.4
  272.9 2.0 fusion.24
  274.9 44.3 %all-to-all-done.1 = bf16[32,8,2048]{2,1,0:T(8,128)(2,1)S(1)} async-done(((bf16[32,8,2048]{2,1,0:T(8,128)(2,1)}), bf16[32,8,2048]{2,1,0:T(8,128)(2,1)S(1)}, u32[]{:S(2)}, u32[]{:S(2)}) %all-to-all-start.1) | async-done | bytes 1048608 | tf_op jit(solution)/shard_map/all_to_all | solution.py:86
  319.3 8.8 %all-to-all-start.3 = ((bf16[32,8,2048]{2,1,0:T(8,128)(2,1)}), bf16[32,8,2048]{2,1,0:T(8,128)(2,1)}, u32[]{:S(2)}, u32[]{:S(2)}) async-start(bf16[32,8,2048]{2,1,0:T(8,128)(2,1)} %fusion.24), calls=%async_computation.3 | async-start | bytes 2097152 | tf_op jit(solution)/shard_map/all_to_all | solution.py:89
  328.1 1.4 copy.17
  329.5 1.2 copy.15
  330.8 1.3 concatenate.6
  332.1 0.9 gather_fusion
  333.0 45.1 %all-to-all-done.3 = bf16[32,8,2048]{2,1,0:T(8,128)(2,1)} async-done(((bf16[32,8,2048]{2,1,0:T(8,128)(2,1)}), bf16[32,8,2048]{2,1,0:T(8,128)(2,1)}, u32[]{:S(2)}, u32[]{:S(2)}) %all-to-all-start.3) | async-done | bytes 1048608 | tf_op jit(solution)/shard_map/all_to_all | solution.py:89
  378.1 8.7 %all-to-all-start.5 = ((bf16[256,16,128]{2,0,1:T(8,128)(2,1)}), bf16[256,16,128]{2,0,1:T(8,128)(2,1)}, u32[]{:S(2)}, u32[]{:S(2)}) async-start(bf16[256,16,128]{2,0,1:T(8,128)(2,1)} %copy.15), calls=%async_computation.5 | async-start | bytes 2097152 | tf_op jit(solution)/shard_map/all_to_all | solution.py:52
  386.8 0.9 multiply_convert_fusion.1
  387.8 1.3 concatenate.7
  389.1 1.7 gather_fusion.1
  390.8 4.6 convolution_bitcast_fusion.2
  395.4 16.1 %all-gather.15.cloned.1.call-done = bf16[4096,768]{1,0:T(8,128)(2,1)} async-done(((bf16[256,768]{1,0:T(8,128)(2,1)}), bf16[4096,768]{1,0:T(8,128)(2,1)}) %all-gather.15.cloned.1.call-update) | async-done | bytes 6291472 | tf_op jit(solution)/shard_map/all_gather | solution.py:109
  411.5 4.6 convolution_bitcast_fusion.1
  416.0 0.0 all-to-all-done.5
  416.1 78.7 %all-gather.17.cloned.1.call-done = bf16[4096,768]{1,0:T(8,128)(2,1)} async-done(((bf16[256,768]{1,0:T(8,128)(2,1)}), bf16[4096,768]{1,0:T(8,128)(2,1)}) %all-gather.17.cloned.1.call-update) | async-done | bytes 6291472 | tf_op jit(solution)/shard_map/all_gather | solution.py:107
  494.8 4.9 convolution_bitcast_fusion
  (13 shorter events, 0.0 us)
Async XLA Ops:
  7.2 3.9 copy-start
  7.2 84.4 %all-gather.11.cloned.1.call-start = ((), (), s32[]{:S(2)}) async-start(), calls=%async_computation.8 | async-start | bytes 3342336 | tf_op jit(solution)/shard_map/all_gather | solution.py:72
  7.9 151.7 %all-gather.9.cloned.1.call-start = ((), (), s32[]{:S(2)}) async-start(), calls=%async_computation.7 | async-start | bytes 3342336 | tf_op jit(solution)/shard_map/all_gather | solution.py:71
  15.6 66.8 %all-to-all-start.2 = ((bf16[32,8,2048]{2,1,0:T(8,128)(2,1)}), bf16[32,8,2048]{2,1,0:T(8,128)(2,1)S(1)}, u32[]{:S(2)}, u32[]{:S(2)}) async-start(bf16[32,8,2048]{2,1,0:T(8,128)(2,1)} %slice_bitcast_fusion), calls=%async_computation.2 | async-start | bytes 2097152 | tf_op jit(solution)/shard_map/all_to_all | solution.py:80
  32.6 195.8 %all-gather.7.cloned.1.call-start = ((), (), s32[]{:S(2)}) async-start(), calls=%async_computation.6 | async-start | bytes 3342336 | tf_op jit(solution)/shard_map/all_gather | solution.py:70
  82.3 13.0 %copy-start.2 = (bf16[32,8,2048]{2,1,0:T(8,128)(2,1)}, bf16[32,8,2048]{2,1,0:T(8,128)(2,1)S(1)}, u32[]{:S(2)}) copy-start(bf16[32,8,2048]{2,1,0:T(8,128)(2,1)S(1)} %all-to-all-done.2) | copy-start | bytes 3145732
  82.3 58.9 %all-to-all-start = ((bf16[32,8,2048]{2,1,0:T(8,128)(2,1)}), bf16[32,8,2048]{2,1,0:T(8,128)(2,1)S(1)}, u32[]{:S(2)}, u32[]{:S(2)}) async-start(bf16[32,8,2048]{2,1,0:T(8,128)(2,1)} %slice_bitcast_fusion.1), calls=%async_computation | async-start | bytes 2097152 | tf_op jit(solution)/shard_map/all_to_all | solution.py:79
  91.5 299.3 %all-gather.13.cloned.1.call-start = ((), (), s32[]{:S(2)}) async-start(), calls=%async_computation.9 | async-start | bytes 6684672 | tf_op jit(solution)/shard_map/all_gather | solution.py:108
  141.2 87.2 %copy-start.7 = (f32[256,768]{1,0:T(8,128)S(1)}, f32[256,768]{1,0:T(8,128)}, u32[]{:S(2)}) copy-start(f32[256,768]{1,0:T(8,128)} %fusion) | copy-start | bytes 2359300
  232.8 178.7 %all-gather.15.cloned.1.call-start = ((), (), s32[]{:S(2)}) async-start(), calls=%async_computation.10 | async-start | bytes 6684672 | tf_op jit(solution)/shard_map/all_gather | solution.py:109
  233.4 261.4 %all-gather.17.cloned.1.call-start = ((), (), s32[]{:S(2)}) async-start(), calls=%async_computation.11 | async-start | bytes 6684672 | tf_op jit(solution)/shard_map/all_gather | solution.py:107
  233.9 5.4 %copy-start.6 = (bf16[256,768]{1,0:T(8,128)(2,1)S(1)}, bf16[256,768]{1,0:T(8,128)(2,1)}, u32[]{:S(2)}) copy-start(bf16[256,768]{1,0:T(8,128)(2,1)} %get-tuple-element.9) | copy-start | bytes 1179652
  235.4 21.5 %all-to-all-start.4 = ((bf16[256,16,128]{2,0,1:T(8,128)(2,1)}), bf16[256,16,128]{2,0,1:T(8,128)(2,1)S(1)}, u32[]{:S(2)}, u32[]{:S(2)}) async-start(bf16[256,16,128]{2,0,1:T(8,128)(2,1)} %copy.14), calls=%async_computation.4 | async-start | bytes 2097152 | tf_op jit(solution)/shard_map/all_to_all | solution.py:51
  239.3 30.5 %copy-start.5 = (bf16[256,768]{1,0:T(8,128)(2,1)S(1)}, bf16[256,768]{1,0:T(8,128)(2,1)}, u32[]{:S(2)}) copy-start(bf16[256,768]{1,0:T(8,128)(2,1)} %get-tuple-element.8) | copy-start | bytes 1179652
  256.9 62.4 %all-to-all-start.1 = ((bf16[32,8,2048]{2,1,0:T(8,128)(2,1)}), bf16[32,8,2048]{2,1,0:T(8,128)(2,1)S(1)}, u32[]{:S(2)}, u32[]{:S(2)}) async-start(bf16[32,8,2048]{2,1,0:T(8,128)(2,1)} %fusion.21), calls=%async_computation.1 | async-start | bytes 2097152 | tf_op jit(solution)/shard_map/all_to_all | solution.py:86
  269.8 3.1 copy-start.3
  269.8 3.1 copy-start.4
  319.3 11.5 %copy-start.1 = (bf16[32,8,2048]{2,1,0:T(8,128)(2,1)}, bf16[32,8,2048]{2,1,0:T(8,128)(2,1)S(1)}, u32[]{:S(2)}) copy-start(bf16[32,8,2048]{2,1,0:T(8,128)(2,1)S(1)} %all-to-all-done.1) | copy-start | bytes 3145732
  319.3 58.8 %all-to-all-start.3 = ((bf16[32,8,2048]{2,1,0:T(8,128)(2,1)}), bf16[32,8,2048]{2,1,0:T(8,128)(2,1)}, u32[]{:S(2)}, u32[]{:S(2)}) async-start(bf16[32,8,2048]{2,1,0:T(8,128)(2,1)} %fusion.24), calls=%async_computation.3 | async-start | bytes 2097152 | tf_op jit(solution)/shard_map/all_to_all | solution.py:89
  378.1 38.0 %all-to-all-start.5 = ((bf16[256,16,128]{2,0,1:T(8,128)(2,1)}), bf16[256,16,128]{2,0,1:T(8,128)(2,1)}, u32[]{:S(2)}, u32[]{:S(2)}) async-start(bf16[256,16,128]{2,0,1:T(8,128)(2,1)} %copy.15), calls=%async_computation.5 | async-start | bytes 2097152 | tf_op jit(solution)/shard_map/all_to_all | solution.py:52
Sparse Core Ops, SparseCore 0:
  11.3 75.5 all-gather.10
  90.2 69.4 all-gather.8
  162.9 65.4 all-gather.6
  232.9 85.2 all-gather.12
  321.9 89.5 all-gather.14
  414.6 80.1 all-gather.16
where the time goes:
time: 508 us; the launch traced here: 507 us
  waiting for transfers between devices  374 us (74%)
  starting transfers between devices  60.8 us (12%)
  matrix products  34.9 us (7%)
  local copies, waits for them, and re-layouts  15.4 us (3%)
  between operations  14.3 us (3%)
  other arithmetic  6.8 us (1%)
    all_gather x1, waiting for transfers between devices, local(): piece_hidden = lax.all_gather(hidden, 'dp', axis=0, tiled=True)  78.7 us
    all_gather x1, waiting for transfers between devices, local(): lax.all_gather(w_gate, 'dp', axis=1, tiled=True)  65.1 us
    all_to_all x1, waiting for transfers between devices, local(): lax.all_to_all(send_x, 'expert', split_axis=0, concat_axis=0, tiled=True)  45.9 us
    all_to_all x1, waiting for transfers between devices, local(): lax.all_to_all(back.reshape(experts, capacity, width), 'expert', split_ax...  45.1 us
    all_to_all x1, waiting for transfers between devices, local(): lax.all_to_all(out.reshape(experts, capacity, width), 'expert', split_axi...  44.3 us
    all_to_all x1, waiting for transfers between devices, local(): lax.all_to_all(send_g, 'expert', split_axis=0, concat_axis=0, tiled=True)  44 us
    all_gather x1, waiting for transfers between devices, local(): lax.all_gather(w_up, 'dp', axis=1, tiled=True)  18.4 us
    all_to_all x1, starting transfers between devices, local(): lax.all_to_all(send_g, 'expert', split_axis=0, concat_axis=0, tiled=True)  17 us
  transfers between devices with their start and end apart: 12, of which 9 were waited for; matrix products, arithmetic and copies ran while one was open for 9% of the time, Pallas kernels for 0%

commit v1 on v0

v1 whole, which is shorter than its diff:
```python
import jax
import jax.numpy as jnp
from jax import lax
from jax.experimental import pallas as pl
from jax.experimental.pallas import tpu as pltpu
from jax.sharding import PartitionSpec as P

BF, F32 = jnp.bfloat16, jnp.float32
NN = (((1,), (0,)), ((), ()))
NT = (((1,), (1,)), ((), ()))
TN = (((0,), (0,)), ((), ()))
VM = pltpu.VMEM


def mm(a, b, dims):
    return lax.dot_general(a, b, dims, preferred_element_type=F32)


def params(mib):
    return pltpu.CompilerParams(vmem_limit_bytes=mib << 20)


def place_kernel(experts, capacity, ids_ref, unit_ref, tok_ref, cot_ref, send_ref, pick_ref):
    tok, width = tok_ref.shape
    labels = lax.broadcasted_iota(jnp.int32, (tok, experts), 1)
    onehot = ids_ref[...] == labels
    row = lax.broadcasted_iota(jnp.int32, (tok, tok), 0)
    col = lax.broadcasted_iota(jnp.int32, (tok, tok), 1)
    before = jnp.where(col < row, 1.0, 0.0).astype(BF)
    hot = jnp.where(onehot, 1.0, 0.0)
    ranks = mm(before, hot.astype(BF), NN)
    rank = jnp.sum(ranks * hot, axis=1, keepdims=True).astype(jnp.int32)
    slot = ids_ref[...] * capacity + rank
    places = lax.broadcasted_iota(jnp.int32, (tok, experts * capacity), 1)
    pick = jnp.where(slot == places, 1.0, 0.0).astype(BF)
    pick_ref[...] = pick
    scale = unit_ref[...].astype(F32) / 256.0
    step = width // 4
    for c in range(4):
        part = pl.ds(c * step, step)
        send_ref[:, part] = mm(pick, tok_ref[:, part], TN).astype(BF)
        rows = (scale * cot_ref[:, part].astype(F32)).astype(BF)
        send_ref[:, pl.ds(width + c * step, step)] = mm(pick, rows, TN).astype(BF)


def expert_kernel(steps, x_ref, g_ref, w_ref, send_ref, hid_ref, dpre_ref, dlin_ref, pre, lin, dhid):
    i = pl.program_id(0)
    parts, _, block, hidden_units = w_ref.shape
    span = parts * block
    width = send_ref.shape[1] // 2
    w_gate = w_ref[:, 0].reshape(span, hidden_units)
    w_up = w_ref[:, 1].reshape(span, hidden_units)
    w_down = w_ref[:, 2].reshape(span, hidden_units)

    @pl.when(i == 0)
    def _():
        pre[...] = jnp.zeros_like(pre)
        lin[...] = jnp.zeros_like(lin)
        dhid[...] = jnp.zeros_like(dhid)

    @pl.when(i < steps)
    def _():
        pre[...] += mm(x_ref[...], w_gate, NN)
        lin[...] += mm(x_ref[...], w_up, NN)
        dhid[...] += mm(g_ref[...], w_down, NN)

    @pl.when(i == steps)
    def _():
        p, u, d = pre[...], lin[...], dhid[...]
        sig = jax.nn.sigmoid(p)
        active = p * sig
        hid_ref[...] = (active * u).astype(BF)
        dpre_ref[...] = (d * u * sig * (1.0 + p * (1.0 - sig))).astype(BF)
        dlin_ref[...] = (d * active).astype(BF)

    @pl.when(i >= steps)
    def _():
        at = pl.multiple_of((i - steps) * span, span)
        send_ref[:, pl.ds(at, span)] = mm(hid_ref[...], w_down, NT).astype(BF)
        back = mm(dpre_ref[...], w_gate, NT) + mm(dlin_ref[...], w_up, NT)
        send_ref[:, pl.ds(at + width, span)] = back.astype(BF)


def grad_kernel(groups, added, order_ref, rows_ref, dpre_ref, dlin_ref, hid_ref, *refs):
    extra, outs = (refs[:3], refs[3:]) if added else ((), refs)
    width = rows_ref.shape[1] // 2
    block = outs[0].shape[1]
    for m, (first, right) in enumerate(((0, dpre_ref), (0, dlin_ref), (width, hid_ref))):
        done = 0
        for n, size in enumerate(groups):
            out = outs[m * len(groups) + n]
            for j in range(size):
                at = pl.multiple_of(order_ref[done + j] * block, block)
                left = rows_ref[:, pl.ds(first + at, block)]
                value = mm(left, right[...], TN)
                if added:
                    value = value + extra[m][done + j].astype(F32)
                out[j] = value.astype(BF)
            done += size


def finish_kernel(pick_ref, unit_ref, got_ref, mixed_ref, back_ref):
    width = mixed_ref.shape[1]
    scale = unit_ref[...].astype(F32) / 256.0
    step = width // 4
    for c in range(4):
        part = pl.ds(c * step, step)
        mixed_ref[:, part] = (scale * mm(pick_ref[...], got_ref[:, part], NN)).astype(BF)
        other = pl.ds(width + c * step, step)
        back_ref[:, part] = mm(pick_ref[...], got_ref[:, other], NN).astype(BF)


def call(kernel, outs, mib, flops, args, smem=0):
    in_specs = [pl.BlockSpec(memory_space=pltpu.SMEM)] * smem
    in_specs += [pl.BlockSpec(memory_space=VM)] * (len(args) - smem)
    moved = sum(a.size * a.dtype.itemsize for a in args)
    moved += sum(o.size * o.dtype.itemsize for o in outs)
    return pl.pallas_call(
        kernel,
        out_shape=outs,
        in_specs=in_specs,
        out_specs=[pl.BlockSpec(memory_space=VM)] * len(outs),
        compiler_params=params(mib),
        cost_estimate=pl.CostEstimate(flops=flops, bytes_accessed=moved, transcendentals=0),
    )(*args)


def experts_call(rows, weights):
    parts = 2
    count, both = rows.shape
    groups, _, block, units = weights.shape
    steps = groups // parts
    span = parts * block
    shape = jax.ShapeDtypeStruct
    small = pl.BlockSpec((count, units), lambda i: (0, 0))
    return pl.pallas_call(
        lambda *refs: expert_kernel(steps, *refs),
        grid=(2 * steps,),
        in_specs=[
            pl.BlockSpec((count, span), lambda i: (0, jnp.minimum(i, steps - 1))),
            pl.BlockSpec((count, span), lambda i: (0, steps + jnp.minimum(i, steps - 1))),
            pl.BlockSpec((parts, 3, block, units), lambda i: (lax.rem(i, steps), 0, 0, 0)),
        ],
        out_specs=[pl.BlockSpec((count, both), lambda i: (0, 0)), small, small, small],
        out_shape=[shape((count, both), BF)] + [shape((count, units), BF)] * 3,
        scratch_shapes=[VM((count, units), F32)] * 3,
        compiler_params=params(32),
        cost_estimate=pl.CostEstimate(
            flops=6 * count * both * units,
            bytes_accessed=4 * weights.size + 4 * rows.size,
            transcendentals=count * units,
        ),
    )(rows, rows, weights)


def local(tokens, expert_ids, gate_units, cotangent, w_gate, w_up, w_down):
    tok, width = tokens.shape
    experts = lax.axis_size("expert")
    groups = lax.axis_size("dp")
    capacity = min(tok, 2 * tok // experts)
    slots = experts * capacity
    block, units = w_gate.shape[1:]
    shape = jax.ShapeDtypeStruct

    own_weights = jnp.concatenate([w_gate, w_up, w_down], axis=0).reshape(3 * block, units)
    weights = lax.all_gather(own_weights, "dp", axis=0, tiled=True)
    weights = weights.reshape(groups, 3, block, units)

    send, pick = call(
        lambda *refs: place_kernel(experts, capacity, *refs),
        [shape((slots, 2 * width), BF), shape((tok, slots), BF)],
        24,
        4 * tok * slots * width,
        (expert_ids, gate_units, tokens, cotangent),
    )

    def exchange(rows):
        cut = rows.reshape(experts, capacity, 2 * width)
        got = lax.all_to_all(cut, "expert", split_axis=0, concat_axis=0, tiled=True)
        return got.reshape(slots, 2 * width)

    rows = exchange(send)
    answer, hidden, d_pre, d_lin = experts_call(rows, weights)
    got = exchange(answer)

    me = lax.axis_index("dp")
    x, far, core = me // 4, (me // 2) % 2, me % 2
    k = jnp.arange(groups // 2, dtype=jnp.int32)
    place = ((x + k // 2) % 4) * 4 + ((far + k) % 2) * 2
    partial = shape((8, block, units), BF)
    flops = 3 * slots * width * units
    away = call(
        lambda *refs: grad_kernel((8,), False, *refs),
        [partial] * 3,
        24,
        flops,
        (place + (1 - core), rows, d_pre, d_lin, hidden),
        smem=1,
    )
    swap = [(i, i ^ 1) for i in range(groups)]
    extra = [lax.ppermute(a, "dp", swap) for a in away]
    pair = shape((2, block, units), BF)
    sums = call(
        lambda *refs: grad_kernel((2, 2, 2, 2), True, *refs),
        [pair] * 12,
        32,
        flops,
        (place + core, rows, d_pre, d_lin, hidden, *extra),
        smem=1,
    )
    grads = []
    for m in range(3):
        total, *others = sums[4 * m : 4 * m + 4]
        total = total.astype(F32)
        for n, part in enumerate(others):
            ring = [(i, (i + 4 * (n + 1)) % groups) for i in range(groups)]
            total = total + lax.ppermute(part, "dp", ring).astype(F32)
        cross = lax.ppermute(total[1].astype(BF), "dp", [(i, i ^ 2) for i in range(groups)])
        grads.append((total[0] + cross.astype(F32))[None])

    mixed, grad_tokens = call(
        finish_kernel,
        [shape((tok, width), BF)] * 2,
        24,
        4 * tok * slots * width,
        (pick, gate_units, got),
    )
    return (mixed, grad_tokens, *grads)


def solution(mesh):
    placed = (
        P(("dp", "expert"), None),
        P(("dp", "expert"), None),
        P(("dp", "expert"), None),
        P(("dp", "expert"), None),
        P("expert", "dp", None),
        P("expert", "dp", None),
        P("expert", "dp", None),
    )
    return jax.shard_map(
        local,
        mesh=mesh,
        in_specs=placed,
        out_specs=(
            P(("dp", "expert"), None),
            P(("dp", "expert"), None),
            P("expert", "dp", None),
            P("expert", "dp", None),
            P("expert", "dp", None),
        ),
        check_vma=False,
    )
```

time: 508 us -> 256 us (0.50)
  the two profiles are of different devices: /device:TPU:1 before, /device:TPU:39 now
where the time goes in v1:
time: 256 us; the launch traced here: 255 us
  blocking collectives  115 us (45%)
  waiting for transfers between devices  49.2 us (19%)
  starting transfers between devices  46.8 us (18%)
  Pallas kernels  17.1 us (7%)
  between operations  14.4 us (6%)
  local copies, waits for them, and re-layouts  7.69 us (3%)
  other arithmetic  5 us (2%)
    all_to_all x1, blocking collectives, exchange(): got = lax.all_to_all(cut, 'expert', split_axis=0, concat_axis=0, tiled=True)  115 us
    ppermute x9, waiting for transfers between devices, local(): total = total + lax.ppermute(part, 'dp', ring).astype(F32)  26.9 us
    ppermute x9, starting transfers between devices, local(): total = total + lax.ppermute(part, 'dp', ring).astype(F32)  23.7 us
    all_to_all x1, waiting for transfers between devices, exchange(): got = lax.all_to_all(cut, 'expert', split_axis=0, concat_axis=0, tiled=True)  16.6 us
    ppermute x3, starting transfers between devices, local(): lax.ppermute(total[1].astype(BF), 'dp', [(i, i ^ 2) for i in range(groups)])  11.3 us
    pallas_call x1, Pallas kernels, experts_call(): pl.pallas_call(lambda *refs: expert_kernel(steps, *refs), grid=(2 * steps...  10.6 us
    unnamed x20, local copies, waits for them, and re-layouts  7.62 us
    ppermute x3, starting transfers between devices, local(): extra = [lax.ppermute(a, 'dp', swap) for a in away]  7.47 us
  transfers between devices with their start and end apart: 17, of which 8 were waited for; matrix products, arithmetic and copies ran while one was open for 1% of the time, Pallas kernels for 2%

profile of v1, /device:TPU:39, one launch (start us, length us, event | category | flops | bytes accessed | tf_op | source)
XLA Modules:
  0.0 255.4 jit_solution(9622088886132004899)
XLA Ops:
  7.2 0.0 copy-start.7
  7.2 0.0 copy-start.8
  7.2 0.0 copy-start.4
  7.2 0.0 copy-start.5
  7.2 0.0 all-gather.2.cloned.1.call-start
  7.3 2.1 pad_maximum_fusion
  9.3 0.0 all-gather.2.cloned.1.call-update
  9.4 0.0 copy-done.7
  9.4 0.1 copy.12.refs_0_
  9.5 0.0 copy-done.8
  9.5 0.1 copy.13.refs_1_.unit_ref
  9.6 0.0 copy-done.4
  9.6 0.0 copy-done.5
  9.6 1.1 shard_map.110
  10.7 115.2 %all_to_all.10 = bf16[32,8,4096]{2,1,0:T(8,128)(2,1)S(1)} all-to-all(bf16[32,8,4096]{2,1,0:T(8,128)(2,1)S(1)} %bitcast.42), channel_id=1, replica_groups=mesh['dp'=16,'expert'=32] {'expert'}, dimensions={0} | all-to-all | bytes 4194304 | tf_op jit(solution)/shard_map/all_to_all | solution.py:179
  125.9 4.4 %copy-done.6 = bf16[6144,768]{1,0:T(8,128)(2,1)S(1)} copy-done((bf16[6144,768]{1,0:T(8,128)(2,1)S(1)}, bf16[6144,768]{1,0:T(8,128)(2,1)}, u32[]{:S(2)}) %copy-start.6) | copy-done | bytes 9437208
  130.4 10.6 %shard_map.111 = (bf16[256,4096]{1,0:T(8,128)(2,1)S(1)}, bf16[256,768]{1,0:T(8,128)(2,1)S(1)}, bf16[256,768]{1,0:T(8,128)(2,1)S(1)}, bf16[256,768]{1,0:T(8,128)(2,1)S(1)}) custom-call(bf16[256,4096]{1,0:T(8,128)(2,1)S(1)} %bitcast.37, bf16[256,4096]{1,0:T(8,128)(2,1)S(1)} %bitcast.38, bf16[16,3,128,768]{3,2,1,0:T(8,128)(2,1)S(1)} %bitcast.43), custom_call_target="tpu_custom_call" | custom-call | flops 4831838208 | bytes 23068672 | tf_op jit(solution)/shard_map/pallas_call | solution.py:136
  140.9 0.0 copy-done
  140.9 0.0 copy-start.3
  140.9 1.3 copy-done.3
  142.3 4.2 %all-to-all-start.1 = ((bf16[32,8,4096]{2,1,0:T(8,128)(2,1)}), bf16[32,8,4096]{2,1,0:T(8,128)(2,1)S(1)}, u32[]{:S(2)}, u32[]{:S(2)}) async-start(bf16[32,8,4096]{2,1,0:T(8,128)(2,1)} %bitcast.41), calls=%async_computation.1 | async-start | bytes 4194304 | tf_op jit(solution)/shard_map/all_to_all | solution.py:179
  146.6 0.0 copy-start.1
  146.6 1.6 copy-done.1
  148.2 2.0 shard_map.113
  150.2 3.1 %collective-permute-start = (bf16[8,128,768]{2,1,0:T(8,128)(2,1)S(1)}, bf16[8,128,768]{2,1,0:T(8,128)(2,1)S(1)}, u32[]{:S(2)}, u32[]{:S(2)}) collective-permute-start(bf16[8,128,768]{2,1,0:T(8,128)(2,1)S(1)} %get-tuple-element.36), channel_id=1, source_target_pairs={{0,32},{32,0},{64,96},{96,64},{128,160},{160,128},{192,224},{224,1... | collective-permute-start | bytes 4718600 | tf_op jit(solution)/shard_map/ppermute | solution.py:201
  153.3 1.9 collective-permute-start.1
  155.3 2.4 collective-permute-start.2
  157.7 0.0 collective-permute-done.refs_5_
  157.7 0.9 collective-permute-done.1.refs_6_
  158.6 2.2 collective-permute-done.2.refs_7_
  160.9 0.0 copy-done.2
  160.9 2.1 shard_map.114
  163.0 2.5 collective-permute-start.5
  165.5 2.7 %collective-permute-start.4 = (bf16[2,128,768]{2,1,0:T(8,128)(2,1)S(1)}, bf16[2,128,768]{2,1,0:T(8,128)(2,1)S(1)}, u32[]{:S(2)}, u32[]{:S(2)}) collective-permute-start(bf16[2,128,768]{2,1,0:T(8,128)(2,1)S(1)} %get-tuple-element.41), channel_id=1, source_target_pairs={{0,256},{32,288},{64,320},{96,352},{128,384},{160,416},{192,448},{... | collective-permute-start | bytes 1179656 | tf_op jit(solution)/shard_map/ppermute | solution.py:217
  168.2 3.7 %collective-permute-start.3 = (bf16[2,128,768]{2,1,0:T(8,128)(2,1)S(1)}, bf16[2,128,768]{2,1,0:T(8,128)(2,1)S(1)}, u32[]{:S(2)}, u32[]{:S(2)}) collective-permute-start(bf16[2,128,768]{2,1,0:T(8,128)(2,1)S(1)} %get-tuple-element.40), channel_id=1, source_target_pairs={{0,128},{32,160},{64,192},{96,224},{128,256},{160,288},{192,320},{... | collective-permute-start | bytes 1179656 | tf_op jit(solution)/shard_map/ppermute | solution.py:217
  172.0 2.0 collective-permute-start.9
  174.0 3.7 %collective-permute-start.8 = (bf16[2,128,768]{2,1,0:T(8,128)(2,1)S(1)}, bf16[2,128,768]{2,1,0:T(8,128)(2,1)S(1)}, u32[]{:S(2)}, u32[]{:S(2)}) collective-permute-start(bf16[2,128,768]{2,1,0:T(8,128)(2,1)S(1)} %get-tuple-element.45), channel_id=1, source_target_pairs={{0,256},{32,288},{64,320},{96,352},{128,384},{160,416},{192,448},{... | collective-permute-start | bytes 1179656 | tf_op jit(solution)/shard_map/ppermute | solution.py:217
  177.7 7.2 %collective-permute-done.5 = bf16[2,128,768]{2,1,0:T(8,128)(2,1)S(1)} collective-permute-done((bf16[2,128,768]{2,1,0:T(8,128)(2,1)S(1)}, bf16[2,128,768]{2,1,0:T(8,128)(2,1)S(1)}, u32[]{:S(2)}, u32[]{:S(2)}) %collective-permute-start.5) | collective-permute-done | bytes 393248 | tf_op jit(solution)/shard_map/ppermute | solution.py:217
  184.8 1.9 collective-permute-start.7
  186.8 0.0 collective-permute-done.4
  186.8 3.4 %collective-permute-start.13 = (bf16[2,128,768]{2,1,0:T(8,128)(2,1)S(1)}, bf16[2,128,768]{2,1,0:T(8,128)(2,1)S(1)}, u32[]{:S(2)}, u32[]{:S(2)}) collective-permute-start(bf16[2,128,768]{2,1,0:T(8,128)(2,1)S(1)} %get-tuple-element.50), channel_id=1, source_target_pairs={{0,384},{32,416},{64,448},{96,480},{128,0},{160,32},{192,64},{224,... | collective-permute-start | bytes 1179656 | tf_op jit(solution)/shard_map/ppermute | solution.py:217
  190.1 0.0 collective-permute-done.3
  190.1 1.9 collective-permute-start.12
  192.1 0.2 convert_add_fusion.2
  192.3 9.4 %collective-permute-done.9 = bf16[2,128,768]{2,1,0:T(8,128)(2,1)S(1)} collective-permute-done((bf16[2,128,768]{2,1,0:T(8,128)(2,1)S(1)}, bf16[2,128,768]{2,1,0:T(8,128)(2,1)S(1)}, u32[]{:S(2)}, u32[]{:S(2)}) %collective-permute-start.9) | collective-permute-done | bytes 393248 | tf_op jit(solution)/shard_map/ppermute | solution.py:217
  201.6 1.9 collective-permute-start.11
  203.6 0.0 collective-permute-done.8
  203.6 4.5 %collective-permute-start.6 = (bf16[128,768]{1,0:T(8,128)(2,1)S(1)}, bf16[128,768]{1,0:T(8,128)(2,1)S(1)}, u32[]{:S(2)}, u32[]{:S(2)}) collective-permute-start(bf16[128,768]{1,0:T(8,128)(2,1)S(1)} %fusion.6), channel_id=1, source_target_pairs={{0,64},{32,96},{64,0},{96,32},{128,192},{160,224},{192,128},{224,1... | collective-permute-start | bytes 589832 | tf_op jit(solution)/shard_map/ppermute | solution.py:218
  208.1 0.0 collective-permute-done.7
  208.1 0.2 convert_add_fusion.1
  208.3 2.3 collective-permute-start.10
  210.6 8.1 %collective-permute-done.13 = bf16[2,128,768]{2,1,0:T(8,128)(2,1)S(1)} collective-permute-done((bf16[2,128,768]{2,1,0:T(8,128)(2,1)S(1)}, bf16[2,128,768]{2,1,0:T(8,128)(2,1)S(1)}, u32[]{:S(2)}, u32[]{:S(2)}) %collective-permute-start.13) | collective-permute-done | bytes 393248 | tf_op jit(solution)/shard_map/ppermute | solution.py:217
  218.7 0.0 collective-permute-done.12
  218.7 2.3 collective-permute-done.11
  221.0 0.2 convert_add_fusion
  221.2 4.5 %collective-permute-start.14 = (bf16[128,768]{1,0:T(8,128)(2,1)S(1)}, bf16[128,768]{1,0:T(8,128)(2,1)S(1)}, u32[]{:S(2)}, u32[]{:S(2)}) collective-permute-start(bf16[128,768]{1,0:T(8,128)(2,1)S(1)} %fusion.8), channel_id=1, source_target_pairs={{0,64},{32,96},{64,0},{96,32},{128,192},{160,224},{192,128},{224,1... | collective-permute-start | bytes 589832 | tf_op jit(solution)/shard_map/ppermute | solution.py:218
  225.7 0.0 collective-permute-done.6
  225.7 0.8 fusion.5
  226.5 0.0 collective-permute-done.10
  226.5 0.8 fusion.3
  227.3 2.4 collective-permute-done.14
  229.7 0.8 fusion.1
  230.5 16.6 %all-to-all-done.1 = bf16[32,8,4096]{2,1,0:T(8,128)(2,1)S(1)} async-done(((bf16[32,8,4096]{2,1,0:T(8,128)(2,1)}), bf16[32,8,4096]{2,1,0:T(8,128)(2,1)S(1)}, u32[]{:S(2)}, u32[]{:S(2)}) %all-to-all-start.1) | async-done | bytes 2097184 | tf_op jit(solution)/shard_map/all_to_all | solution.py:179
  247.1 1.4 shard_map.112
  (9 shorter events, 0.1 us)
Async XLA Ops:
  7.2 2.2 copy-start.7
  7.2 2.3 copy-start.8
  7.2 2.4 copy-start.4
  7.2 2.4 copy-start.5
  7.2 118.7 %all-gather.2.cloned.1.call-start = ((), (), s32[]{:S(2)}) async-start(), calls=%async_computation.2 | async-start | bytes 10027008 | tf_op jit(solution)/shard_map/all_gather | solution.py:166
  125.9 15.0 %copy-start = (bf16[32,8,4096]{2,1,0:T(8,128)(2,1)}, bf16[32,8,4096]{2,1,0:T(8,128)(2,1)S(1)}, u32[]{:S(2)}) copy-start(bf16[32,8,4096]{2,1,0:T(8,128)(2,1)S(1)} %all_to_all.10) | copy-start | bytes 6291460
  125.9 4.4 %copy-start.6 = (bf16[6144,768]{1,0:T(8,128)(2,1)S(1)}, bf16[6144,768]{1,0:T(8,128)(2,1)}, u32[]{:S(2)}) copy-start(bf16[6144,768]{1,0:T(8,128)(2,1)} %all-gather.2.cloned.1.call-done) | copy-start | bytes 28311556
  140.9 1.4 copy-start.3
  142.3 104.8 %all-to-all-start.1 = ((bf16[32,8,4096]{2,1,0:T(8,128)(2,1)}), bf16[32,8,4096]{2,1,0:T(8,128)(2,1)S(1)}, u32[]{:S(2)}, u32[]{:S(2)}) async-start(bf16[32,8,4096]{2,1,0:T(8,128)(2,1)} %bitcast.41), calls=%async_computation.1 | async-start | bytes 4194304 | tf_op jit(solution)/shard_map/all_to_all | solution.py:179
  146.6 1.6 copy-start.1
  148.2 12.7 %copy-start.2 = (bf16[32,8,4096]{2,1,0:T(8,128)(2,1)S(1)}, bf16[32,8,4096]{2,1,0:T(8,128)(2,1)}, u32[]{:S(2)}) copy-start(bf16[32,8,4096]{2,1,0:T(8,128)(2,1)} %copy-done) | copy-start | bytes 6291460
  150.2 7.5 %collective-permute-start = (bf16[8,128,768]{2,1,0:T(8,128)(2,1)S(1)}, bf16[8,128,768]{2,1,0:T(8,128)(2,1)S(1)}, u32[]{:S(2)}, u32[]{:S(2)}) collective-permute-start(bf16[8,128,768]{2,1,0:T(8,128)(2,1)S(1)} %get-tuple-element.36), channel_id=1, source_target_pairs={{0,32},{32,0},{64,96},{96,64},{128,160},{160,128},{192,224},{224,1... | collective-permute-start | bytes 4718600 | tf_op jit(solution)/shard_map/ppermute | solution.py:201
  153.3 5.3 %collective-permute-start.1 = (bf16[8,128,768]{2,1,0:T(8,128)(2,1)S(1)}, bf16[8,128,768]{2,1,0:T(8,128)(2,1)S(1)}, u32[]{:S(2)}, u32[]{:S(2)}) collective-permute-start(bf16[8,128,768]{2,1,0:T(8,128)(2,1)S(1)} %get-tuple-element.37), channel_id=1, source_target_pairs={{0,32},{32,0},{64,96},{96,64},{128,160},{160,128},{192,224},{224,1... | collective-permute-start | bytes 4718600 | tf_op jit(solution)/shard_map/ppermute | solution.py:201
  155.3 5.6 %collective-permute-start.2 = (bf16[8,128,768]{2,1,0:T(8,128)(2,1)S(1)}, bf16[8,128,768]{2,1,0:T(8,128)(2,1)S(1)}, u32[]{:S(2)}, u32[]{:S(2)}) collective-permute-start(bf16[8,128,768]{2,1,0:T(8,128)(2,1)S(1)} %get-tuple-element.38), channel_id=1, source_target_pairs={{0,32},{32,0},{64,96},{96,64},{128,160},{160,128},{192,224},{224,1... | collective-permute-start | bytes 4718600 | tf_op jit(solution)/shard_map/ppermute | solution.py:201
  163.0 21.8 %collective-permute-start.5 = (bf16[2,128,768]{2,1,0:T(8,128)(2,1)S(1)}, bf16[2,128,768]{2,1,0:T(8,128)(2,1)S(1)}, u32[]{:S(2)}, u32[]{:S(2)}) collective-permute-start(bf16[2,128,768]{2,1,0:T(8,128)(2,1)S(1)} %get-tuple-element.42), channel_id=1, source_target_pairs={{0,384},{32,416},{64,448},{96,480},{128,0},{160,32},{192,64},{224,... | collective-permute-start | bytes 1179656 | tf_op jit(solution)/shard_map/ppermute | solution.py:217
  165.5 21.3 %collective-permute-start.4 = (bf16[2,128,768]{2,1,0:T(8,128)(2,1)S(1)}, bf16[2,128,768]{2,1,0:T(8,128)(2,1)S(1)}, u32[]{:S(2)}, u32[]{:S(2)}) collective-permute-start(bf16[2,128,768]{2,1,0:T(8,128)(2,1)S(1)} %get-tuple-element.41), channel_id=1, source_target_pairs={{0,256},{32,288},{64,320},{96,352},{128,384},{160,416},{192,448},{... | collective-permute-start | bytes 1179656 | tf_op jit(solution)/shard_map/ppermute | solution.py:217
  168.2 21.9 %collective-permute-start.3 = (bf16[2,128,768]{2,1,0:T(8,128)(2,1)S(1)}, bf16[2,128,768]{2,1,0:T(8,128)(2,1)S(1)}, u32[]{:S(2)}, u32[]{:S(2)}) collective-permute-start(bf16[2,128,768]{2,1,0:T(8,128)(2,1)S(1)} %get-tuple-element.40), channel_id=1, source_target_pairs={{0,128},{32,160},{64,192},{96,224},{128,256},{160,288},{192,320},{... | collective-permute-start | bytes 1179656 | tf_op jit(solution)/shard_map/ppermute | solution.py:217
  172.0 29.7 %collective-permute-start.9 = (bf16[2,128,768]{2,1,0:T(8,128)(2,1)S(1)}, bf16[2,128,768]{2,1,0:T(8,128)(2,1)S(1)}, u32[]{:S(2)}, u32[]{:S(2)}) collective-permute-start(bf16[2,128,768]{2,1,0:T(8,128)(2,1)S(1)} %get-tuple-element.46), channel_id=1, source_target_pairs={{0,384},{32,416},{64,448},{96,480},{128,0},{160,32},{192,64},{224,... | collective-permute-start | bytes 1179656 | tf_op jit(solution)/shard_map/ppermute | solution.py:217
  174.0 29.6 %collective-permute-start.8 = (bf16[2,128,768]{2,1,0:T(8,128)(2,1)S(1)}, bf16[2,128,768]{2,1,0:T(8,128)(2,1)S(1)}, u32[]{:S(2)}, u32[]{:S(2)}) collective-permute-start(bf16[2,128,768]{2,1,0:T(8,128)(2,1)S(1)} %get-tuple-element.45), channel_id=1, source_target_pairs={{0,256},{32,288},{64,320},{96,352},{128,384},{160,416},{192,448},{... | collective-permute-start | bytes 1179656 | tf_op jit(solution)/shard_map/ppermute | solution.py:217
  184.8 23.2 %collective-permute-start.7 = (bf16[2,128,768]{2,1,0:T(8,128)(2,1)S(1)}, bf16[2,128,768]{2,1,0:T(8,128)(2,1)S(1)}, u32[]{:S(2)}, u32[]{:S(2)}) collective-permute-start(bf16[2,128,768]{2,1,0:T(8,128)(2,1)S(1)} %get-tuple-element.44), channel_id=1, source_target_pairs={{0,128},{32,160},{64,192},{96,224},{128,256},{160,288},{192,320},{... | collective-permute-start | bytes 1179656 | tf_op jit(solution)/shard_map/ppermute | solution.py:217
  186.8 31.9 %collective-permute-start.13 = (bf16[2,128,768]{2,1,0:T(8,128)(2,1)S(1)}, bf16[2,128,768]{2,1,0:T(8,128)(2,1)S(1)}, u32[]{:S(2)}, u32[]{:S(2)}) collective-permute-start(bf16[2,128,768]{2,1,0:T(8,128)(2,1)S(1)} %get-tuple-element.50), channel_id=1, source_target_pairs={{0,384},{32,416},{64,448},{96,480},{128,0},{160,32},{192,64},{224,... | collective-permute-start | bytes 1179656 | tf_op jit(solution)/shard_map/ppermute | solution.py:217
  190.1 28.6 %collective-permute-start.12 = (bf16[2,128,768]{2,1,0:T(8,128)(2,1)S(1)}, bf16[2,128,768]{2,1,0:T(8,128)(2,1)S(1)}, u32[]{:S(2)}, u32[]{:S(2)}) collective-permute-start(bf16[2,128,768]{2,1,0:T(8,128)(2,1)S(1)} %get-tuple-element.49), channel_id=1, source_target_pairs={{0,256},{32,288},{64,320},{96,352},{128,384},{160,416},{192,448},{... | collective-permute-start | bytes 1179656 | tf_op jit(solution)/shard_map/ppermute | solution.py:217
  201.6 19.4 %collective-permute-start.11 = (bf16[2,128,768]{2,1,0:T(8,128)(2,1)S(1)}, bf16[2,128,768]{2,1,0:T(8,128)(2,1)S(1)}, u32[]{:S(2)}, u32[]{:S(2)}) collective-permute-start(bf16[2,128,768]{2,1,0:T(8,128)(2,1)S(1)} %get-tuple-element.48), channel_id=1, source_target_pairs={{0,128},{32,160},{64,192},{96,224},{128,256},{160,288},{192,320},{... | collective-permute-start | bytes 1179656 | tf_op jit(solution)/shard_map/ppermute | solution.py:217
  203.6 22.2 %collective-permute-start.6 = (bf16[128,768]{1,0:T(8,128)(2,1)S(1)}, bf16[128,768]{1,0:T(8,128)(2,1)S(1)}, u32[]{:S(2)}, u32[]{:S(2)}) collective-permute-start(bf16[128,768]{1,0:T(8,128)(2,1)S(1)} %fusion.6), channel_id=1, source_target_pairs={{0,64},{32,96},{64,0},{96,32},{128,192},{160,224},{192,128},{224,1... | collective-permute-start | bytes 589832 | tf_op jit(solution)/shard_map/ppermute | solution.py:218
  208.3 18.2 %collective-permute-start.10 = (bf16[128,768]{1,0:T(8,128)(2,1)S(1)}, bf16[128,768]{1,0:T(8,128)(2,1)S(1)}, u32[]{:S(2)}, u32[]{:S(2)}) collective-permute-start(bf16[128,768]{1,0:T(8,128)(2,1)S(1)} %fusion.7), channel_id=1, source_target_pairs={{0,64},{32,96},{64,0},{96,32},{128,192},{160,224},{192,128},{224,1... | collective-permute-start | bytes 589832 | tf_op jit(solution)/shard_map/ppermute | solution.py:218
  221.2 8.5 %collective-permute-start.14 = (bf16[128,768]{1,0:T(8,128)(2,1)S(1)}, bf16[128,768]{1,0:T(8,128)(2,1)S(1)}, u32[]{:S(2)}, u32[]{:S(2)}) collective-permute-start(bf16[128,768]{1,0:T(8,128)(2,1)S(1)} %fusion.8), channel_id=1, source_target_pairs={{0,64},{32,96},{64,0},{96,32},{128,192},{160,224},{192,128},{224,1... | collective-permute-start | bytes 589832 | tf_op jit(solution)/shard_map/ppermute | solution.py:218
Sparse Core Ops, SparseCore 0:
  11.3 105.6 all-gather.1

commit v2 on v1

v2 whole, which is shorter than its diff:
```python
import jax
import jax.numpy as jnp
from jax import lax
from jax.experimental import pallas as pl
from jax.experimental.pallas import tpu as pltpu
from jax.sharding import PartitionSpec as P

BF, F32 = jnp.bfloat16, jnp.float32
NN = (((1,), (0,)), ((), ()))
NT = (((1,), (1,)), ((), ()))
TN = (((0,), (0,)), ((), ()))
VM = pltpu.VMEM


def mm(a, b, dims):
    return lax.dot_general(a, b, dims, preferred_element_type=F32)


def params(mib):
    return pltpu.CompilerParams(vmem_limit_bytes=mib << 20)


def place_kernel(experts, capacity, ids_ref, unit_ref, tok_ref, cot_ref, send_ref, pick_ref):
    i = pl.program_id(0)
    half = pl.num_programs(0) // 2
    tok = tok_ref.shape[0]

    @pl.when(i == 0)
    def _():
        labels = lax.broadcasted_iota(jnp.int32, (tok, experts), 1)
        row = lax.broadcasted_iota(jnp.int32, (tok, tok), 0)
        col = lax.broadcasted_iota(jnp.int32, (tok, tok), 1)
        before = jnp.where(col < row, 1.0, 0.0).astype(BF)
        hot = jnp.where(ids_ref[...] == labels, 1.0, 0.0)
        ranks = mm(before, hot.astype(BF), NN)
        rank = jnp.sum(ranks * hot, axis=1, keepdims=True).astype(jnp.int32)
        slot = ids_ref[...] * capacity + rank
        places = lax.broadcasted_iota(jnp.int32, (tok, experts * capacity), 1)
        pick_ref[...] = jnp.where(slot == places, 1.0, 0.0).astype(BF)

    @pl.when(i < half)
    def _():
        send_ref[...] = mm(pick_ref[...], tok_ref[...], TN).astype(BF)

    @pl.when(i >= half)
    def _():
        scale = unit_ref[...].astype(F32) / 256.0
        rows = (scale * cot_ref[...].astype(F32)).astype(BF)
        send_ref[...] = mm(pick_ref[...], rows, TN).astype(BF)


def place_call(experts, capacity, ids, units, tokens, cotangent):
    tok, width = tokens.shape
    slots = experts * capacity
    half = 4
    step = width // half
    shape = jax.ShapeDtypeStruct
    column = pl.BlockSpec((tok, 1), lambda i: (0, 0))
    return pl.pallas_call(
        lambda *refs: place_kernel(experts, capacity, *refs),
        grid=(2 * half,),
        in_specs=[
            column,
            column,
            pl.BlockSpec((tok, step), lambda i: (0, jnp.minimum(i, half - 1))),
            pl.BlockSpec((tok, step), lambda i: (0, jnp.maximum(i - half, 0))),
        ],
        out_specs=[
            pl.BlockSpec((slots, step), lambda i: (0, i)),
            pl.BlockSpec((tok, slots), lambda i: (0, 0)),
        ],
        out_shape=[shape((slots, 2 * width), BF), shape((tok, slots), BF)],
        compiler_params=params(56),
        cost_estimate=pl.CostEstimate(
            flops=4 * tok * slots * width, bytes_accessed=12 * tok * width, transcendentals=0
        ),
    )(ids, units, tokens, cotangent)


def expert_kernel(order_ref, rows_ref, *refs):
    pairs = order_ref.shape[0] - 1
    shards = refs[: 2 * pairs]
    send_ref, hid_ref, dpre_ref, dlin_ref = refs[2 * pairs :]
    block, units = shards[0].shape[1:]
    width = rows_ref.shape[1] // 2
    core = order_ref[pairs]

    def spots(p, first):
        at = order_ref[p] * 2
        return [pl.ds(pl.multiple_of(first + (at + c) * block, block), block) for c in (core, 1 - core)]

    def left(p, first):
        return jnp.concatenate([rows_ref[:, s] for s in spots(p, first)], axis=1)

    def right(p, m, cols):
        return jnp.concatenate([w[m, :, cols] for w in shards[2 * p : 2 * p + 2]], axis=0)

    step = 256
    for n in range(units // step):
        cols = pl.ds(n * step, step)
        pre, lin, dhid = 0.0, 0.0, 0.0
        for p in range(pairs):
            x, g = left(p, 0), left(p, width)
            pre = pre + mm(x, right(p, 0, cols), NN)
            lin = lin + mm(x, right(p, 1, cols), NN)
            dhid = dhid + mm(g, right(p, 2, cols), NN)
        sig = jax.nn.sigmoid(pre)
        active = pre * sig
        hid_ref[:, cols] = (active * lin).astype(BF)
        dpre_ref[:, cols] = (dhid * lin * sig * (1.0 + pre * (1.0 - sig))).astype(BF)
        dlin_ref[:, cols] = (dhid * active).astype(BF)
    every = pl.ds(0, units)
    for p in range(pairs):
        out = mm(hid_ref[...], right(p, 2, every), NT)
        back = mm(dpre_ref[...], right(p, 0, every), NT) + mm(dlin_ref[...], right(p, 1, every), NT)
        for first, value in ((0, out.astype(BF)), (width, back.astype(BF))):
            for n, s in enumerate(spots(p, first)):
                send_ref[:, s] = value[:, n * block : (n + 1) * block]


def grad_kernel(groups, added, order_ref, rows_ref, dpre_ref, dlin_ref, hid_ref, *refs):
    extra, outs = (refs[:3], refs[3:]) if added else ((), refs)
    width = rows_ref.shape[1] // 2
    block = outs[0].shape[1]
    for m, (first, right) in enumerate(((0, dpre_ref), (0, dlin_ref), (width, hid_ref))):
        done = 0
        for n, size in enumerate(groups):
            out = outs[m * len(groups) + n]
            for j in range(size):
                at = pl.multiple_of(order_ref[done + j] * block, block)
                left = rows_ref[:, pl.ds(first + at, block)]
                value = mm(left, right[...], TN)
                if added:
                    value = value + extra[m][done + j].astype(F32)
                out[j] = value.astype(BF)
            done += size


def finish_kernel(pick_ref, unit_ref, got_ref, mixed_ref, back_ref):
    width = mixed_ref.shape[1]
    scale = unit_ref[...].astype(F32) / 256.0
    step = width // 4
    for c in range(4):
        part = pl.ds(c * step, step)
        mixed_ref[:, part] = (scale * mm(pick_ref[...], got_ref[:, part], NN)).astype(BF)
        other = pl.ds(width + c * step, step)
        back_ref[:, part] = mm(pick_ref[...], got_ref[:, other], NN).astype(BF)


def call(kernel, outs, mib, flops, args, smem=0):
    in_specs = [pl.BlockSpec(memory_space=pltpu.SMEM)] * smem
    in_specs += [pl.BlockSpec(memory_space=VM)] * (len(args) - smem)
    moved = sum(a.size * a.dtype.itemsize for a in args)
    moved += sum(o.size * o.dtype.itemsize for o in outs)
    return pl.pallas_call(
        kernel,
        out_shape=outs,
        in_specs=in_specs,
        out_specs=[pl.BlockSpec(memory_space=VM)] * len(outs),
        compiler_params=params(mib),
        cost_estimate=pl.CostEstimate(flops=flops, bytes_accessed=moved, transcendentals=0),
    )(*args)


def local(tokens, expert_ids, gate_units, cotangent, w_gate, w_up, w_down):
    tok, width = tokens.shape
    experts = lax.axis_size("expert")
    groups = lax.axis_size("dp")
    capacity = min(tok, 2 * tok // experts)
    slots = experts * capacity
    block, units = w_gate.shape[1:]
    shape = jax.ShapeDtypeStruct

    me = lax.axis_index("dp")
    x, far, core = me >> 2, (me >> 1) & 1, me & 1
    k = jnp.arange(8, dtype=jnp.int32)

    def permute(a, to):
        return lax.ppermute(a, "dp", [(i, to(i)) for i in range(groups)])

    send, pick = place_call(experts, capacity, expert_ids, gate_units, tokens, cotangent)

    own = jnp.concatenate([w_gate, w_up, w_down], axis=0)
    across = permute(own, lambda i: i ^ 2)
    shards = []
    for start in (own, across):
        for n in range(4):
            shard = permute(start, lambda i: (i + 4 * n) % groups) if n else start
            shards += [shard, permute(shard, lambda i: i ^ 1)]
    source = ((x - k) & 3) * 2 + (far ^ (k >> 2))
    source = jnp.concatenate([source, core[None]])

    def exchange(rows):
        cut = rows.reshape(experts, capacity, 2 * width)
        got = lax.all_to_all(cut, "expert", split_axis=0, concat_axis=0, tiled=True)
        return got.reshape(slots, 2 * width)

    rows = exchange(send)
    small = shape((slots, units), BF)
    answer, hidden, d_pre, d_lin = call(
        expert_kernel,
        [shape((slots, 2 * width), BF), small, small, small],
        32,
        12 * slots * width * units,
        (source, rows, *shards),
        smem=1,
    )
    got = exchange(answer)

    place = ((x + (k >> 1)) & 3) * 4 + (far ^ (k & 1)) * 2
    partial = shape((8, block, units), BF)
    flops = 3 * slots * width * units
    away = call(
        lambda *refs: grad_kernel((8,), False, *refs),
        [partial] * 3,
        24,
        flops,
        (place + (1 - core), rows, d_pre, d_lin, hidden),
        smem=1,
    )
    extra = [permute(a, lambda i: i ^ 1) for a in away]
    pair = shape((2, block, units), BF)
    sums = call(
        lambda *refs: grad_kernel((2, 2, 2, 2), True, *refs),
        [pair] * 12,
        32,
        flops,
        (place + core, rows, d_pre, d_lin, hidden, *extra),
        smem=1,
    )
    grads = []
    for m in range(3):
        total, *others = sums[4 * m : 4 * m + 4]
        total = total.astype(F32)
        for n, part in enumerate(others):
            total = total + permute(part, lambda i: (i + 4 * (n + 1)) % groups).astype(F32)
        cross = permute(total[1].astype(BF), lambda i: i ^ 2)
        grads.append((total[0] + cross.astype(F32))[None])

    mixed, grad_tokens = call(
        finish_kernel,
        [shape((tok, width), BF)] * 2,
        24,
        4 * tok * slots * width,
        (pick, gate_units, got),
    )
    return (mixed, grad_tokens, *grads)


def solution(mesh):
    placed = (
        P(("dp", "expert"), None),
        P(("dp", "expert"), None),
        P(("dp", "expert"), None),
        P(("dp", "expert"), None),
        P("expert", "dp", None),
        P("expert", "dp", None),
        P("expert", "dp", None),
    )
    return jax.shard_map(
        local,
        mesh=mesh,
        in_specs=placed,
        out_specs=(
            P(("dp", "expert"), None),
            P(("dp", "expert"), None),
            P("expert", "dp", None),
            P("expert", "dp", None),
            P("expert", "dp", None),
        ),
        check_vma=False,
    )
```

time: 256 us -> 252 us (0.984)
  the two profiles are of different devices: /device:TPU:39 before, /device:TPU:33 now
where the time goes in v2:
time: 252 us; the launch traced here: 251 us
  starting transfers between devices  126 us (50%)
  waiting for transfers between devices  77.9 us (31%)
  local copies, waits for them, and re-layouts  21.4 us (8%)
  Pallas kernels  20.9 us (8%)
  other arithmetic  2.99 us (1%)
    ppermute x30, starting transfers between devices, permute(): return lax.ppermute(a, 'dp', [(i, to(i)) for i in range(groups)])  106 us
    all_to_all x2, waiting for transfers between devices, exchange(): got = lax.all_to_all(cut, 'expert', split_axis=0, concat_axis=0, tiled=True)  40.3 us
    ppermute x30, waiting for transfers between devices, permute(): return lax.ppermute(a, 'dp', [(i, to(i)) for i in range(groups)])  37.6 us
    unnamed x54, local copies, waits for them, and re-layouts  21.3 us
    all_to_all x2, starting transfers between devices, exchange(): got = lax.all_to_all(cut, 'expert', split_axis=0, concat_axis=0, tiled=True)  19.8 us
    pallas_call x4, Pallas kernels, call(): pl.pallas_call(kernel, out_shape=outs, in_specs=in_specs, out_specs=[pl.B...  14.1 us
    pallas_call x1, Pallas kernels, place_call(): pl.pallas_call(lambda *refs: place_kernel(experts, capacity, *refs), grid...  6.87 us
  transfers between devices with their start and end apart: 32, of which 14 were waited for; matrix products, arithmetic and copies ran while one was open for 1% of the time, Pallas kernels for 2%

profile of v2, /device:TPU:33, one launch (start us, length us, event | category | flops | bytes accessed | tf_op | source)
XLA Modules:
  0.0 250.6 jit_solution(17935381161931963662)
XLA Ops:
  0.6 1.4 copy.13.refs_1_.unit_ref
  2.0 1.4 copy.12.refs_0_
  3.4 6.9 %shard_map.110 = (bf16[256,4096]{1,0:T(8,128)(2,1)}, bf16[128,256]{1,0:T(8,128)(2,1)}) custom-call(s32[128,1]{1,0:T(8,128)} %copy.12.refs_0_, s32[128,1]{1,0:T(8,128)} %copy.13.refs_1_.unit_ref, bf16[128,2048]{1,0:T(8,128)(2,1)} %refs_2_.1, bf16[128,2048]{1,0:T(8,128)(2,1)} %refs_3_.1), custom_call_target="tpu_custom_call" | custom-call | flops 268435456 | bytes 3145728 | tf_op jit(solution)/shard_map/pallas_call | solution.py:59
  10.3 16.0 %all-to-all-start = ((bf16[32,8,4096]{2,1,0:T(8,128)(2,1)}), bf16[32,8,4096]{2,1,0:T(8,128)(2,1)S(1)}, u32[]{:S(2)}, u32[]{:S(2)}) async-start(bf16[32,8,4096]{2,1,0:T(8,128)(2,1)} %bitcast.40), calls=%async_computation | async-start | bytes 4194304 | tf_op jit(solution)/shard_map/all_to_all | solution.py:195
  26.4 4.5 %collective-permute-start.7 = (bf16[3,128,768]{2,1,0:T(8,128)(2,1)S(1)}, bf16[3,128,768]{2,1,0:T(8,128)(2,1)S(1)}, u32[]{:S(2)}, u32[]{:S(2)}) collective-permute-start(bf16[3,128,768]{2,1,0:T(8,128)(2,1)S(1)} %constant_dynamic-update-slice_fusion.refs_0_), channel_id=1, source_target_pairs={{0,64},{32,96},{64,0},{96,32},{128,192},{160,224},{192,128},{224,1... | collective-permute-start | bytes 1769480 | tf_op jit(solution)/shard_map/ppermute | solution.py:179
  30.9 4.4 %collective-permute-start.5 = (bf16[3,128,768]{2,1,0:T(8,128)(2,1)S(1)}, bf16[3,128,768]{2,1,0:T(8,128)(2,1)S(1)}, u32[]{:S(2)}, u32[]{:S(2)}) collective-permute-start(bf16[3,128,768]{2,1,0:T(8,128)(2,1)S(1)} %constant_dynamic-update-slice_fusion.refs_0_), channel_id=1, source_target_pairs={{0,384},{32,416},{64,448},{96,480},{128,0},{160,32},{192,64},{224,... | collective-permute-start | bytes 1769480 | tf_op jit(solution)/shard_map/ppermute | solution.py:179
  35.3 2.4 collective-permute-start.3
  37.7 2.5 %collective-permute-start.1 = (bf16[3,128,768]{2,1,0:T(8,128)(2,1)S(1)}, bf16[3,128,768]{2,1,0:T(8,128)(2,1)S(1)}, u32[]{:S(2)}, u32[]{:S(2)}) collective-permute-start(bf16[3,128,768]{2,1,0:T(8,128)(2,1)S(1)} %constant_dynamic-update-slice_fusion.refs_0_), channel_id=1, source_target_pairs={{0,128},{32,160},{64,192},{96,224},{128,256},{160,288},{192,320},{... | collective-permute-start | bytes 1769480 | tf_op jit(solution)/shard_map/ppermute | solution.py:179
  40.2 4.3 %collective-permute-start = (bf16[3,128,768]{2,1,0:T(8,128)(2,1)S(1)}, bf16[3,128,768]{2,1,0:T(8,128)(2,1)S(1)}, u32[]{:S(2)}, u32[]{:S(2)}) collective-permute-start(bf16[3,128,768]{2,1,0:T(8,128)(2,1)S(1)} %constant_dynamic-update-slice_fusion.refs_0_), channel_id=1, source_target_pairs={{0,32},{32,0},{64,96},{96,64},{128,160},{160,128},{192,224},{224,1... | collective-permute-start | bytes 1769480 | tf_op jit(solution)/shard_map/ppermute | solution.py:179
  46.1 4.4 %collective-permute-start.13 = (bf16[3,128,768]{2,1,0:T(8,128)(2,1)S(1)}, bf16[3,128,768]{2,1,0:T(8,128)(2,1)}, u32[]{:S(2)}, u32[]{:S(2)}) collective-permute-start(bf16[3,128,768]{2,1,0:T(8,128)(2,1)S(1)} %collective-permute-done.7.refs_8_), channel_id=1, source_target_pairs={{0,384},{32,416},{64,448},{96,480},{128,0},{160,32},{192,64},{224,... | collective-permute-start | bytes 1769480 | tf_op jit(solution)/shard_map/ppermute | solution.py:179
  50.5 2.5 collective-permute-start.11
  52.9 9.9 %collective-permute-start.9 = (bf16[3,128,768]{2,1,0:T(8,128)(2,1)S(1)}, bf16[3,128,768]{2,1,0:T(8,128)(2,1)}, u32[]{:S(2)}, u32[]{:S(2)}) collective-permute-start(bf16[3,128,768]{2,1,0:T(8,128)(2,1)S(1)} %collective-permute-done.7.refs_8_), channel_id=1, source_target_pairs={{0,128},{32,160},{64,192},{96,224},{128,256},{160,288},{192,320},{... | collective-permute-start | bytes 1769480 | tf_op jit(solution)/shard_map/ppermute | solution.py:179
  62.8 5.9 %collective-permute-done.1.refs_2_ = bf16[3,128,768]{2,1,0:T(8,128)(2,1)S(1)} collective-permute-done((bf16[3,128,768]{2,1,0:T(8,128)(2,1)S(1)}, bf16[3,128,768]{2,1,0:T(8,128)(2,1)S(1)}, u32[]{:S(2)}, u32[]{:S(2)}) %collective-permute-start.1) | collective-permute-done | bytes 589856 | tf_op jit(solution)/shard_map/ppermute | solution.py:179
  68.8 4.1 %collective-permute-start.8 = (bf16[3,128,768]{2,1,0:T(8,128)(2,1)S(1)}, bf16[3,128,768]{2,1,0:T(8,128)(2,1)S(1)}, u32[]{:S(2)}, u32[]{:S(2)}) collective-permute-start(bf16[3,128,768]{2,1,0:T(8,128)(2,1)S(1)} %collective-permute-done.7.refs_8_), channel_id=1, source_target_pairs={{0,32},{32,0},{64,96},{96,64},{128,160},{160,128},{192,224},{224,1... | collective-permute-start | bytes 1769480 | tf_op jit(solution)/shard_map/ppermute | solution.py:179
  72.9 0.9 copy-done.8
  73.8 0.9 copy-done.16
  74.6 1.9 collective-permute-start.6
  77.4 11.3 %collective-permute-start.4 = (bf16[3,128,768]{2,1,0:T(8,128)(2,1)S(1)}, bf16[3,128,768]{2,1,0:T(8,128)(2,1)}, u32[]{:S(2)}, u32[]{:S(2)}) collective-permute-start(bf16[3,128,768]{2,1,0:T(8,128)(2,1)S(1)} %collective-permute-done.3.refs_4_), channel_id=1, source_target_pairs={{0,32},{32,0},{64,96},{96,64},{128,160},{160,128},{192,224},{224,1... | collective-permute-start | bytes 1769480 | tf_op jit(solution)/shard_map/ppermute | solution.py:179
  88.7 0.8 copy-done.12
  89.5 1.9 collective-permute-start.2
  92.3 2.4 collective-permute-start.14
  95.5 1.9 collective-permute-start.12
  98.2 2.4 collective-permute-start.10
  100.8 1.8 collective-permute-done.10.refs_11_
  102.6 24.2 %all-to-all-done = bf16[32,8,4096]{2,1,0:T(8,128)(2,1)S(1)} async-done(((bf16[32,8,4096]{2,1,0:T(8,128)(2,1)}), bf16[32,8,4096]{2,1,0:T(8,128)(2,1)S(1)}, u32[]{:S(2)}, u32[]{:S(2)}) %all-to-all-start) | async-done | bytes 2097184 | tf_op jit(solution)/shard_map/all_to_all | solution.py:195
  126.8 1.5 copy-done.7
  128.3 1.1 copy-done.9
  129.3 1.1 copy-done.11
  130.4 1.1 copy-done.13
  131.5 1.1 copy-done.15
  132.5 1.1 copy-done.17
  133.6 1.1 copy-done.19
  134.7 1.1 copy-done.21
  135.7 8.6 %shard_map.111 = (bf16[256,4096]{1,0:T(8,128)(2,1)S(1)}, bf16[256,768]{1,0:T(8,128)(2,1)S(1)}, bf16[256,768]{1,0:T(8,128)(2,1)S(1)}, bf16[256,768]{1,0:T(8,128)(2,1)S(1)}) custom-call(s32[9]{0:T(128)S(1)} %pad_add_fusion.order_ref, bf16[256,4096]{1,0:T(8,128)(2,1)S(1)} %bitcast.36, bf16[3,128,768]{2,1,0:T(8,128)(2,1)S(1)} %copy-done.7, ...), custom_call_target="tpu_custom_call" | custom-call | flops 4831838208 | bytes 14811172 | tf_op jit(solution)/shard_map/pallas_call | solution.py:155
  144.4 1.4 copy-done.3
  145.8 3.8 %all-to-all-start.1 = ((bf16[32,8,4096]{2,1,0:T(8,128)(2,1)}), bf16[32,8,4096]{2,1,0:T(8,128)(2,1)S(1)}, u32[]{:S(2)}, u32[]{:S(2)}) async-start(bf16[32,8,4096]{2,1,0:T(8,128)(2,1)} %bitcast.39), calls=%async_computation.1 | async-start | bytes 4194304 | tf_op jit(solution)/shard_map/all_to_all | solution.py:195
  149.6 1.6 copy-done.1
  151.2 2.0 shard_map.113
  153.1 2.7 %collective-permute-start.15 = (bf16[8,128,768]{2,1,0:T(8,128)(2,1)S(1)}, bf16[8,128,768]{2,1,0:T(8,128)(2,1)S(1)}, u32[]{:S(2)}, u32[]{:S(2)}) collective-permute-start(bf16[8,128,768]{2,1,0:T(8,128)(2,1)S(1)} %get-tuple-element.36), channel_id=1, source_target_pairs={{0,32},{32,0},{64,96},{96,64},{128,160},{160,128},{192,224},{224,1... | collective-permute-start | bytes 4718600 | tf_op jit(solution)/shard_map/ppermute | solution.py:179
  155.8 1.9 collective-permute-start.16
  157.7 2.6 %collective-permute-start.17 = (bf16[8,128,768]{2,1,0:T(8,128)(2,1)S(1)}, bf16[8,128,768]{2,1,0:T(8,128)(2,1)S(1)}, u32[]{:S(2)}, u32[]{:S(2)}) collective-permute-start(bf16[8,128,768]{2,1,0:T(8,128)(2,1)S(1)} %get-tuple-element.38), channel_id=1, source_target_pairs={{0,32},{32,0},{64,96},{96,64},{128,160},{160,128},{192,224},{224,1... | collective-permute-start | bytes 4718600 | tf_op jit(solution)/shard_map/ppermute | solution.py:179
  161.1 2.2 collective-permute-done.17.refs_7_
  163.4 2.1 shard_map.114
  165.4 3.1 %collective-permute-start.18 = (bf16[2,128,768]{2,1,0:T(8,128)(2,1)S(1)}, bf16[2,128,768]{2,1,0:T(8,128)(2,1)S(1)}, u32[]{:S(2)}, u32[]{:S(2)}) collective-permute-start(bf16[2,128,768]{2,1,0:T(8,128)(2,1)S(1)} %get-tuple-element.40), channel_id=1, source_target_pairs={{0,128},{32,160},{64,192},{96,224},{128,256},{160,288},{192,320},{... | collective-permute-start | bytes 1179656 | tf_op jit(solution)/shard_map/ppermute | solution.py:179
  168.6 4.3 %collective-permute-start.19 = (bf16[2,128,768]{2,1,0:T(8,128)(2,1)S(1)}, bf16[2,128,768]{2,1,0:T(8,128)(2,1)S(1)}, u32[]{:S(2)}, u32[]{:S(2)}) collective-permute-start(bf16[2,128,768]{2,1,0:T(8,128)(2,1)S(1)} %get-tuple-element.41), channel_id=1, source_target_pairs={{0,256},{32,288},{64,320},{96,352},{128,384},{160,416},{192,448},{... | collective-permute-start | bytes 1179656 | tf_op jit(solution)/shard_map/ppermute | solution.py:179
  172.9 3.1 %collective-permute-start.20 = (bf16[2,128,768]{2,1,0:T(8,128)(2,1)S(1)}, bf16[2,128,768]{2,1,0:T(8,128)(2,1)S(1)}, u32[]{:S(2)}, u32[]{:S(2)}) collective-permute-start(bf16[2,128,768]{2,1,0:T(8,128)(2,1)S(1)} %get-tuple-element.42), channel_id=1, source_target_pairs={{0,384},{32,416},{64,448},{96,480},{128,0},{160,32},{192,64},{224,... | collective-permute-start | bytes 1179656 | tf_op jit(solution)/shard_map/ppermute | solution.py:179
  176.0 2.2 collective-permute-start.22
  178.2 2.8 %collective-permute-start.23 = (bf16[2,128,768]{2,1,0:T(8,128)(2,1)S(1)}, bf16[2,128,768]{2,1,0:T(8,128)(2,1)S(1)}, u32[]{:S(2)}, u32[]{:S(2)}) collective-permute-start(bf16[2,128,768]{2,1,0:T(8,128)(2,1)S(1)} %get-tuple-element.45), channel_id=1, source_target_pairs={{0,256},{32,288},{64,320},{96,352},{128,384},{160,416},{192,448},{... | collective-permute-start | bytes 1179656 | tf_op jit(solution)/shard_map/ppermute | solution.py:179
  181.0 3.4 %collective-permute-start.24 = (bf16[2,128,768]{2,1,0:T(8,128)(2,1)S(1)}, bf16[2,128,768]{2,1,0:T(8,128)(2,1)S(1)}, u32[]{:S(2)}, u32[]{:S(2)}) collective-permute-start(bf16[2,128,768]{2,1,0:T(8,128)(2,1)S(1)} %get-tuple-element.46), channel_id=1, source_target_pairs={{0,384},{32,416},{64,448},{96,480},{128,0},{160,32},{192,64},{224,... | collective-permute-start | bytes 1179656 | tf_op jit(solution)/shard_map/ppermute | solution.py:179
  184.5 4.0 %collective-permute-done.19 = bf16[2,128,768]{2,1,0:T(8,128)(2,1)S(1)} collective-permute-done((bf16[2,128,768]{2,1,0:T(8,128)(2,1)S(1)}, bf16[2,128,768]{2,1,0:T(8,128)(2,1)S(1)}, u32[]{:S(2)}, u32[]{:S(2)}) %collective-permute-start.19) | collective-permute-done | bytes 393248 | tf_op jit(solution)/shard_map/ppermute | solution.py:179
  188.4 1.9 collective-permute-start.26
  190.4 4.1 %collective-permute-start.27 = (bf16[2,128,768]{2,1,0:T(8,128)(2,1)S(1)}, bf16[2,128,768]{2,1,0:T(8,128)(2,1)S(1)}, u32[]{:S(2)}, u32[]{:S(2)}) collective-permute-start(bf16[2,128,768]{2,1,0:T(8,128)(2,1)S(1)} %get-tuple-element.49), channel_id=1, source_target_pairs={{0,256},{32,288},{64,320},{96,352},{128,384},{160,416},{192,448},{... | collective-permute-start | bytes 1179656 | tf_op jit(solution)/shard_map/ppermute | solution.py:179
  194.7 3.2 %collective-permute-done.22 = bf16[2,128,768]{2,1,0:T(8,128)(2,1)S(1)} collective-permute-done((bf16[2,128,768]{2,1,0:T(8,128)(2,1)S(1)}, bf16[2,128,768]{2,1,0:T(8,128)(2,1)S(1)}, u32[]{:S(2)}, u32[]{:S(2)}) %collective-permute-start.22) | collective-permute-done | bytes 393248 | tf_op jit(solution)/shard_map/ppermute | solution.py:179
  198.0 2.0 collective-permute-start.28
  200.0 5.4 %collective-permute-done.23 = bf16[2,128,768]{2,1,0:T(8,128)(2,1)S(1)} collective-permute-done((bf16[2,128,768]{2,1,0:T(8,128)(2,1)S(1)}, bf16[2,128,768]{2,1,0:T(8,128)(2,1)S(1)}, u32[]{:S(2)}, u32[]{:S(2)}) %collective-permute-start.23) | collective-permute-done | bytes 393248 | tf_op jit(solution)/shard_map/ppermute | solution.py:179
  205.3 4.5 %collective-permute-start.21 = (bf16[128,768]{1,0:T(8,128)(2,1)S(1)}, bf16[128,768]{1,0:T(8,128)(2,1)S(1)}, u32[]{:S(2)}, u32[]{:S(2)}) collective-permute-start(bf16[128,768]{1,0:T(8,128)(2,1)S(1)} %fusion.6), channel_id=1, source_target_pairs={{0,64},{32,96},{64,0},{96,32},{128,192},{160,224},{192,128},{224,1... | collective-permute-start | bytes 589832 | tf_op jit(solution)/shard_map/ppermute | solution.py:179
  210.1 2.3 collective-permute-start.25
  212.4 2.4 collective-permute-done.26
  214.8 7.4 %collective-permute-done.27 = bf16[2,128,768]{2,1,0:T(8,128)(2,1)S(1)} collective-permute-done((bf16[2,128,768]{2,1,0:T(8,128)(2,1)S(1)}, bf16[2,128,768]{2,1,0:T(8,128)(2,1)S(1)}, u32[]{:S(2)}, u32[]{:S(2)}) %collective-permute-start.27) | collective-permute-done | bytes 393248 | tf_op jit(solution)/shard_map/ppermute | solution.py:179
  222.2 1.2 collective-permute-done.28
  223.6 4.7 %collective-permute-start.29 = (bf16[128,768]{1,0:T(8,128)(2,1)S(1)}, bf16[128,768]{1,0:T(8,128)(2,1)S(1)}, u32[]{:S(2)}, u32[]{:S(2)}) collective-permute-start(bf16[128,768]{1,0:T(8,128)(2,1)S(1)} %fusion.8), channel_id=1, source_target_pairs={{0,64},{32,96},{64,0},{96,32},{128,192},{160,224},{192,128},{224,1... | collective-permute-start | bytes 589832 | tf_op jit(solution)/shard_map/ppermute | solution.py:179
  229.9 2.4 collective-permute-done.29
  233.1 16.1 %all-to-all-done.1 = bf16[32,8,4096]{2,1,0:T(8,128)(2,1)S(1)} async-done(((bf16[32,8,4096]{2,1,0:T(8,128)(2,1)}), bf16[32,8,4096]{2,1,0:T(8,128)(2,1)S(1)}, u32[]{:S(2)}, u32[]{:S(2)}) %all-to-all-start.1) | async-done | bytes 2097184 | tf_op jit(solution)/shard_map/all_to_all | solution.py:195
  249.2 1.4 shard_map.112
  (72 shorter events, 8.8 us)
Async XLA Ops:
  10.3 16.0 %copy-start.22 = (bf16[1,128,768]{2,1,0:T(8,128)(2,1)S(1)}, bf16[1,128,768]{2,1,0:T(8,128)(2,1)}, u32[]{:S(2)}) copy-start(bf16[1,128,768]{2,1,0:T(8,128)(2,1)} %param.11) | copy-start | bytes 589828
  10.3 16.0 %copy-start.23 = (bf16[1,128,768]{2,1,0:T(8,128)(2,1)S(1)}, bf16[1,128,768]{2,1,0:T(8,128)(2,1)}, u32[]{:S(2)}) copy-start(bf16[1,128,768]{2,1,0:T(8,128)(2,1)} %param.12) | copy-start | bytes 589828
  10.3 16.0 %copy-start.24 = (bf16[1,128,768]{2,1,0:T(8,128)(2,1)S(1)}, bf16[1,128,768]{2,1,0:T(8,128)(2,1)}, u32[]{:S(2)}) copy-start(bf16[1,128,768]{2,1,0:T(8,128)(2,1)} %param.13) | copy-start | bytes 589828
  10.3 116.5 %all-to-all-start = ((bf16[32,8,4096]{2,1,0:T(8,128)(2,1)}), bf16[32,8,4096]{2,1,0:T(8,128)(2,1)S(1)}, u32[]{:S(2)}, u32[]{:S(2)}) async-start(bf16[32,8,4096]{2,1,0:T(8,128)(2,1)} %bitcast.40), calls=%async_computation | async-start | bytes 4194304 | tf_op jit(solution)/shard_map/all_to_all | solution.py:195
  26.4 19.7 %collective-permute-start.7 = (bf16[3,128,768]{2,1,0:T(8,128)(2,1)S(1)}, bf16[3,128,768]{2,1,0:T(8,128)(2,1)S(1)}, u32[]{:S(2)}, u32[]{:S(2)}) collective-permute-start(bf16[3,128,768]{2,1,0:T(8,128)(2,1)S(1)} %constant_dynamic-update-slice_fusion.refs_0_), channel_id=1, source_target_pairs={{0,64},{32,96},{64,0},{96,32},{128,192},{160,224},{192,128},{224,1... | collective-permute-start | bytes 1769480 | tf_op jit(solution)/shard_map/ppermute | solution.py:179
  30.9 19.6 %collective-permute-start.5 = (bf16[3,128,768]{2,1,0:T(8,128)(2,1)S(1)}, bf16[3,128,768]{2,1,0:T(8,128)(2,1)S(1)}, u32[]{:S(2)}, u32[]{:S(2)}) collective-permute-start(bf16[3,128,768]{2,1,0:T(8,128)(2,1)S(1)} %constant_dynamic-update-slice_fusion.refs_0_), channel_id=1, source_target_pairs={{0,384},{32,416},{64,448},{96,480},{128,0},{160,32},{192,64},{224,... | collective-permute-start | bytes 1769480 | tf_op jit(solution)/shard_map/ppermute | solution.py:179
  35.3 17.7 %collective-permute-start.3 = (bf16[3,128,768]{2,1,0:T(8,128)(2,1)S(1)}, bf16[3,128,768]{2,1,0:T(8,128)(2,1)S(1)}, u32[]{:S(2)}, u32[]{:S(2)}) collective-permute-start(bf16[3,128,768]{2,1,0:T(8,128)(2,1)S(1)} %constant_dynamic-update-slice_fusion.refs_0_), channel_id=1, source_target_pairs={{0,256},{32,288},{64,320},{96,352},{128,384},{160,416},{192,448},{... | collective-permute-start | bytes 1769480 | tf_op jit(solution)/shard_map/ppermute | solution.py:179
  37.7 31.0 %collective-permute-start.1 = (bf16[3,128,768]{2,1,0:T(8,128)(2,1)S(1)}, bf16[3,128,768]{2,1,0:T(8,128)(2,1)S(1)}, u32[]{:S(2)}, u32[]{:S(2)}) collective-permute-start(bf16[3,128,768]{2,1,0:T(8,128)(2,1)S(1)} %constant_dynamic-update-slice_fusion.refs_0_), channel_id=1, source_target_pairs={{0,128},{32,160},{64,192},{96,224},{128,256},{160,288},{192,320},{... | collective-permute-start | bytes 1769480 | tf_op jit(solution)/shard_map/ppermute | solution.py:179
  40.2 33.5 %collective-permute-start = (bf16[3,128,768]{2,1,0:T(8,128)(2,1)S(1)}, bf16[3,128,768]{2,1,0:T(8,128)(2,1)S(1)}, u32[]{:S(2)}, u32[]{:S(2)}) collective-permute-start(bf16[3,128,768]{2,1,0:T(8,128)(2,1)S(1)} %constant_dynamic-update-slice_fusion.refs_0_), channel_id=1, source_target_pairs={{0,32},{32,0},{64,96},{96,64},{128,160},{160,128},{192,224},{224,1... | collective-permute-start | bytes 1769480 | tf_op jit(solution)/shard_map/ppermute | solution.py:179
  44.5 0.8 copy-start.6
  46.1 31.3 %collective-permute-start.13 = (bf16[3,128,768]{2,1,0:T(8,128)(2,1)S(1)}, bf16[3,128,768]{2,1,0:T(8,128)(2,1)}, u32[]{:S(2)}, u32[]{:S(2)}) collective-permute-start(bf16[3,128,768]{2,1,0:T(8,128)(2,1)S(1)} %collective-permute-done.7.refs_8_), channel_id=1, source_target_pairs={{0,384},{32,416},{64,448},{96,480},{128,0},{160,32},{192,64},{224,... | collective-permute-start | bytes 1769480 | tf_op jit(solution)/shard_map/ppermute | solution.py:179
  50.5 39.0 %collective-permute-start.11 = (bf16[3,128,768]{2,1,0:T(8,128)(2,1)S(1)}, bf16[3,128,768]{2,1,0:T(8,128)(2,1)}, u32[]{:S(2)}, u32[]{:S(2)}) collective-permute-start(bf16[3,128,768]{2,1,0:T(8,128)(2,1)S(1)} %collective-permute-done.7.refs_8_), channel_id=1, source_target_pairs={{0,256},{32,288},{64,320},{96,352},{128,384},{160,416},{192,448},{... | collective-permute-start | bytes 1769480 | tf_op jit(solution)/shard_map/ppermute | solution.py:179
  52.9 39.3 %collective-permute-start.9 = (bf16[3,128,768]{2,1,0:T(8,128)(2,1)S(1)}, bf16[3,128,768]{2,1,0:T(8,128)(2,1)}, u32[]{:S(2)}, u32[]{:S(2)}) collective-permute-start(bf16[3,128,768]{2,1,0:T(8,128)(2,1)S(1)} %collective-permute-done.7.refs_8_), channel_id=1, source_target_pairs={{0,128},{32,160},{64,192},{96,224},{128,256},{160,288},{192,320},{... | collective-permute-start | bytes 1769480 | tf_op jit(solution)/shard_map/ppermute | solution.py:179
  68.8 25.9 %collective-permute-start.8 = (bf16[3,128,768]{2,1,0:T(8,128)(2,1)S(1)}, bf16[3,128,768]{2,1,0:T(8,128)(2,1)S(1)}, u32[]{:S(2)}, u32[]{:S(2)}) collective-permute-start(bf16[3,128,768]{2,1,0:T(8,128)(2,1)S(1)} %collective-permute-done.7.refs_8_), channel_id=1, source_target_pairs={{0,32},{32,0},{64,96},{96,64},{128,160},{160,128},{192,224},{224,1... | collective-permute-start | bytes 1769480 | tf_op jit(solution)/shard_map/ppermute | solution.py:179
  72.9 0.9 copy-start.8
  73.8 0.9 copy-start.16
  74.6 22.8 %collective-permute-start.6 = (bf16[3,128,768]{2,1,0:T(8,128)(2,1)S(1)}, bf16[3,128,768]{2,1,0:T(8,128)(2,1)S(1)}, u32[]{:S(2)}, u32[]{:S(2)}) collective-permute-start(bf16[3,128,768]{2,1,0:T(8,128)(2,1)S(1)} %collective-permute-done.5.refs_6_), channel_id=1, source_target_pairs={{0,32},{32,0},{64,96},{96,64},{128,160},{160,128},{192,224},{224,1... | collective-permute-start | bytes 1769480 | tf_op jit(solution)/shard_map/ppermute | solution.py:179
  76.5 0.8 copy-start.10
  77.4 23.4 %collective-permute-start.4 = (bf16[3,128,768]{2,1,0:T(8,128)(2,1)S(1)}, bf16[3,128,768]{2,1,0:T(8,128)(2,1)}, u32[]{:S(2)}, u32[]{:S(2)}) collective-permute-start(bf16[3,128,768]{2,1,0:T(8,128)(2,1)S(1)} %collective-permute-done.3.refs_4_), channel_id=1, source_target_pairs={{0,32},{32,0},{64,96},{96,64},{128,160},{160,128},{192,224},{224,1... | collective-permute-start | bytes 1769480 | tf_op jit(solution)/shard_map/ppermute | solution.py:179
  88.7 0.8 copy-start.12
  89.5 11.2 %collective-permute-start.2 = (bf16[3,128,768]{2,1,0:T(8,128)(2,1)S(1)}, bf16[3,128,768]{2,1,0:T(8,128)(2,1)}, u32[]{:S(2)}, u32[]{:S(2)}) collective-permute-start(bf16[3,128,768]{2,1,0:T(8,128)(2,1)S(1)} %collective-permute-done.1.refs_2_), channel_id=1, source_target_pairs={{0,32},{32,0},{64,96},{96,64},{128,160},{160,128},{192,224},{224,1... | collective-permute-start | bytes 1769480 | tf_op jit(solution)/shard_map/ppermute | solution.py:179
  91.4 0.8 copy-start.14
  92.3 8.5 %collective-permute-start.14 = (bf16[3,128,768]{2,1,0:T(8,128)(2,1)}, bf16[3,128,768]{2,1,0:T(8,128)(2,1)}, u32[]{:S(2)}, u32[]{:S(2)}) collective-permute-start(bf16[3,128,768]{2,1,0:T(8,128)(2,1)} %collective-permute-done.13.refs_14_), channel_id=1, source_target_pairs={{0,32},{32,0},{64,96},{96,64},{128,160},{160,128},{192,224},{224,1... | collective-permute-start | bytes 1769480 | tf_op jit(solution)/shard_map/ppermute | solution.py:179
  94.7 0.8 copy-start.18
  95.5 5.3 %collective-permute-start.12 = (bf16[3,128,768]{2,1,0:T(8,128)(2,1)}, bf16[3,128,768]{2,1,0:T(8,128)(2,1)}, u32[]{:S(2)}, u32[]{:S(2)}) collective-permute-start(bf16[3,128,768]{2,1,0:T(8,128)(2,1)} %collective-permute-done.11.refs_12_), channel_id=1, source_target_pairs={{0,32},{32,0},{64,96},{96,64},{128,160},{160,128},{192,224},{224,1... | collective-permute-start | bytes 1769480 | tf_op jit(solution)/shard_map/ppermute | solution.py:179
  97.4 0.8 copy-start.20
  98.2 4.4 %collective-permute-start.10 = (bf16[3,128,768]{2,1,0:T(8,128)(2,1)}, bf16[3,128,768]{2,1,0:T(8,128)(2,1)}, u32[]{:S(2)}, u32[]{:S(2)}) collective-permute-start(bf16[3,128,768]{2,1,0:T(8,128)(2,1)} %collective-permute-done.9.refs_10_), channel_id=1, source_target_pairs={{0,32},{32,0},{64,96},{96,64},{128,160},{160,128},{192,224},{224,1... | collective-permute-start | bytes 1769480 | tf_op jit(solution)/shard_map/ppermute | solution.py:179
  126.8 17.6 %copy-start = (bf16[32,8,4096]{2,1,0:T(8,128)(2,1)}, bf16[32,8,4096]{2,1,0:T(8,128)(2,1)S(1)}, u32[]{:S(2)}) copy-start(bf16[32,8,4096]{2,1,0:T(8,128)(2,1)S(1)} %all-to-all-done) | copy-start | bytes 6291460
  126.8 1.5 copy-start.7
  128.3 1.1 copy-start.9
  129.3 1.1 copy-start.11
  130.4 1.1 copy-start.13
  131.5 1.1 copy-start.15
  132.5 1.1 copy-start.17
  133.6 1.1 copy-start.19
  134.7 1.1 copy-start.21
  144.4 1.4 copy-start.3
  145.8 103.4 %all-to-all-start.1 = ((bf16[32,8,4096]{2,1,0:T(8,128)(2,1)}), bf16[32,8,4096]{2,1,0:T(8,128)(2,1)S(1)}, u32[]{:S(2)}, u32[]{:S(2)}) async-start(bf16[32,8,4096]{2,1,0:T(8,128)(2,1)} %bitcast.39), calls=%async_computation.1 | async-start | bytes 4194304 | tf_op jit(solution)/shard_map/all_to_all | solution.py:195
  149.6 1.6 copy-start.1
  151.2 12.2 %copy-start.2 = (bf16[32,8,4096]{2,1,0:T(8,128)(2,1)S(1)}, bf16[32,8,4096]{2,1,0:T(8,128)(2,1)}, u32[]{:S(2)}) copy-start(bf16[32,8,4096]{2,1,0:T(8,128)(2,1)} %copy-done) | copy-start | bytes 6291460
  153.1 7.2 %collective-permute-start.15 = (bf16[8,128,768]{2,1,0:T(8,128)(2,1)S(1)}, bf16[8,128,768]{2,1,0:T(8,128)(2,1)S(1)}, u32[]{:S(2)}, u32[]{:S(2)}) collective-permute-start(bf16[8,128,768]{2,1,0:T(8,128)(2,1)S(1)} %get-tuple-element.36), channel_id=1, source_target_pairs={{0,32},{32,0},{64,96},{96,64},{128,160},{160,128},{192,224},{224,1... | collective-permute-start | bytes 4718600 | tf_op jit(solution)/shard_map/ppermute | solution.py:179
  155.8 5.3 %collective-permute-start.16 = (bf16[8,128,768]{2,1,0:T(8,128)(2,1)S(1)}, bf16[8,128,768]{2,1,0:T(8,128)(2,1)S(1)}, u32[]{:S(2)}, u32[]{:S(2)}) collective-permute-start(bf16[8,128,768]{2,1,0:T(8,128)(2,1)S(1)} %get-tuple-element.37), channel_id=1, source_target_pairs={{0,32},{32,0},{64,96},{96,64},{128,160},{160,128},{192,224},{224,1... | collective-permute-start | bytes 4718600 | tf_op jit(solution)/shard_map/ppermute | solution.py:179
  157.7 5.6 %collective-permute-start.17 = (bf16[8,128,768]{2,1,0:T(8,128)(2,1)S(1)}, bf16[8,128,768]{2,1,0:T(8,128)(2,1)S(1)}, u32[]{:S(2)}, u32[]{:S(2)}) collective-permute-start(bf16[8,128,768]{2,1,0:T(8,128)(2,1)S(1)} %get-tuple-element.38), channel_id=1, source_target_pairs={{0,32},{32,0},{64,96},{96,64},{128,160},{160,128},{192,224},{224,1... | collective-permute-start | bytes 4718600 | tf_op jit(solution)/shard_map/ppermute | solution.py:179
  165.4 15.6 %collective-permute-start.18 = (bf16[2,128,768]{2,1,0:T(8,128)(2,1)S(1)}, bf16[2,128,768]{2,1,0:T(8,128)(2,1)S(1)}, u32[]{:S(2)}, u32[]{:S(2)}) collective-permute-start(bf16[2,128,768]{2,1,0:T(8,128)(2,1)S(1)} %get-tuple-element.40), channel_id=1, source_target_pairs={{0,128},{32,160},{64,192},{96,224},{128,256},{160,288},{192,320},{... | collective-permute-start | bytes 1179656 | tf_op jit(solution)/shard_map/ppermute | solution.py:179
  168.6 19.9 %collective-permute-start.19 = (bf16[2,128,768]{2,1,0:T(8,128)(2,1)S(1)}, bf16[2,128,768]{2,1,0:T(8,128)(2,1)S(1)}, u32[]{:S(2)}, u32[]{:S(2)}) collective-permute-start(bf16[2,128,768]{2,1,0:T(8,128)(2,1)S(1)} %get-tuple-element.41), channel_id=1, source_target_pairs={{0,256},{32,288},{64,320},{96,352},{128,384},{160,416},{192,448},{... | collective-permute-start | bytes 1179656 | tf_op jit(solution)/shard_map/ppermute | solution.py:179
  172.9 17.4 %collective-permute-start.20 = (bf16[2,128,768]{2,1,0:T(8,128)(2,1)S(1)}, bf16[2,128,768]{2,1,0:T(8,128)(2,1)S(1)}, u32[]{:S(2)}, u32[]{:S(2)}) collective-permute-start(bf16[2,128,768]{2,1,0:T(8,128)(2,1)S(1)} %get-tuple-element.42), channel_id=1, source_target_pairs={{0,384},{32,416},{64,448},{96,480},{128,0},{160,32},{192,64},{224,... | collective-permute-start | bytes 1179656 | tf_op jit(solution)/shard_map/ppermute | solution.py:179
  176.0 22.0 %collective-permute-start.22 = (bf16[2,128,768]{2,1,0:T(8,128)(2,1)S(1)}, bf16[2,128,768]{2,1,0:T(8,128)(2,1)S(1)}, u32[]{:S(2)}, u32[]{:S(2)}) collective-permute-start(bf16[2,128,768]{2,1,0:T(8,128)(2,1)S(1)} %get-tuple-element.44), channel_id=1, source_target_pairs={{0,128},{32,160},{64,192},{96,224},{128,256},{160,288},{192,320},{... | collective-permute-start | bytes 1179656 | tf_op jit(solution)/shard_map/ppermute | solution.py:179
  178.2 27.1 %collective-permute-start.23 = (bf16[2,128,768]{2,1,0:T(8,128)(2,1)S(1)}, bf16[2,128,768]{2,1,0:T(8,128)(2,1)S(1)}, u32[]{:S(2)}, u32[]{:S(2)}) collective-permute-start(bf16[2,128,768]{2,1,0:T(8,128)(2,1)S(1)} %get-tuple-element.45), channel_id=1, source_target_pairs={{0,256},{32,288},{64,320},{96,352},{128,384},{160,416},{192,448},{... | collective-permute-start | bytes 1179656 | tf_op jit(solution)/shard_map/ppermute | solution.py:179
  181.0 28.8 %collective-permute-start.24 = (bf16[2,128,768]{2,1,0:T(8,128)(2,1)S(1)}, bf16[2,128,768]{2,1,0:T(8,128)(2,1)S(1)}, u32[]{:S(2)}, u32[]{:S(2)}) collective-permute-start(bf16[2,128,768]{2,1,0:T(8,128)(2,1)S(1)} %get-tuple-element.46), channel_id=1, source_target_pairs={{0,384},{32,416},{64,448},{96,480},{128,0},{160,32},{192,64},{224,... | collective-permute-start | bytes 1179656 | tf_op jit(solution)/shard_map/ppermute | solution.py:179
  188.4 26.3 %collective-permute-start.26 = (bf16[2,128,768]{2,1,0:T(8,128)(2,1)S(1)}, bf16[2,128,768]{2,1,0:T(8,128)(2,1)S(1)}, u32[]{:S(2)}, u32[]{:S(2)}) collective-permute-start(bf16[2,128,768]{2,1,0:T(8,128)(2,1)S(1)} %get-tuple-element.48), channel_id=1, source_target_pairs={{0,128},{32,160},{64,192},{96,224},{128,256},{160,288},{192,320},{... | collective-permute-start | bytes 1179656 | tf_op jit(solution)/shard_map/ppermute | solution.py:179
  190.4 31.8 %collective-permute-start.27 = (bf16[2,128,768]{2,1,0:T(8,128)(2,1)S(1)}, bf16[2,128,768]{2,1,0:T(8,128)(2,1)S(1)}, u32[]{:S(2)}, u32[]{:S(2)}) collective-permute-start(bf16[2,128,768]{2,1,0:T(8,128)(2,1)S(1)} %get-tuple-element.49), channel_id=1, source_target_pairs={{0,256},{32,288},{64,320},{96,352},{128,384},{160,416},{192,448},{... | collective-permute-start | bytes 1179656 | tf_op jit(solution)/shard_map/ppermute | solution.py:179
  198.0 25.4 %collective-permute-start.28 = (bf16[2,128,768]{2,1,0:T(8,128)(2,1)S(1)}, bf16[2,128,768]{2,1,0:T(8,128)(2,1)S(1)}, u32[]{:S(2)}, u32[]{:S(2)}) collective-permute-start(bf16[2,128,768]{2,1,0:T(8,128)(2,1)S(1)} %get-tuple-element.50), channel_id=1, source_target_pairs={{0,384},{32,416},{64,448},{96,480},{128,0},{160,32},{192,64},{224,... | collective-permute-start | bytes 1179656 | tf_op jit(solution)/shard_map/ppermute | solution.py:179
  205.3 23.0 %collective-permute-start.21 = (bf16[128,768]{1,0:T(8,128)(2,1)S(1)}, bf16[128,768]{1,0:T(8,128)(2,1)S(1)}, u32[]{:S(2)}, u32[]{:S(2)}) collective-permute-start(bf16[128,768]{1,0:T(8,128)(2,1)S(1)} %fusion.6), channel_id=1, source_target_pairs={{0,64},{32,96},{64,0},{96,32},{128,192},{160,224},{192,128},{224,1... | collective-permute-start | bytes 589832 | tf_op jit(solution)/shard_map/ppermute | solution.py:179
  210.1 19.1 %collective-permute-start.25 = (bf16[128,768]{1,0:T(8,128)(2,1)S(1)}, bf16[128,768]{1,0:T(8,128)(2,1)S(1)}, u32[]{:S(2)}, u32[]{:S(2)}) collective-permute-start(bf16[128,768]{1,0:T(8,128)(2,1)S(1)} %fusion.7), channel_id=1, source_target_pairs={{0,64},{32,96},{64,0},{96,32},{128,192},{160,224},{192,128},{224,1... | collective-permute-start | bytes 589832 | tf_op jit(solution)/shard_map/ppermute | solution.py:179
  223.6 25.6 %copy-start.4 = (s32[128,1]{1,0:T(8,128)S(1)}, s32[128,1]{1,0:T(8,128)}, u32[]{:S(2)}) copy-start(s32[128,1]{1,0:T(8,128)} %copy.13.refs_1_.unit_ref) | copy-start | bytes 1540
  223.6 25.6 %copy-start.5 = (bf16[128,256]{1,0:T(8,128)(2,1)S(1)}, bf16[128,256]{1,0:T(8,128)(2,1)}, u32[]{:S(2)}) copy-start(bf16[128,256]{1,0:T(8,128)(2,1)} %get-tuple-element.28.pick_ref) | copy-start | bytes 196612
  223.6 8.7 %collective-permute-start.29 = (bf16[128,768]{1,0:T(8,128)(2,1)S(1)}, bf16[128,768]{1,0:T(8,128)(2,1)S(1)}, u32[]{:S(2)}, u32[]{:S(2)}) collective-permute-start(bf16[128,768]{1,0:T(8,128)(2,1)S(1)} %fusion.8), channel_id=1, source_target_pairs={{0,64},{32,96},{64,0},{96,32},{128,192},{160,224},{192,128},{224,1... | collective-permute-start | bytes 589832 | tf_op jit(solution)/shard_map/ppermute | solution.py:179

commit v3 on v2

--- a/solution.py
+++ b/solution.py
@@ -20,69 +20,44 @@
     return pltpu.CompilerParams(vmem_limit_bytes=mib << 20)
 
 
+def column(row):
+    n = row.shape[1]
+    down = lax.broadcasted_iota(jnp.int32, (n, n), 0)
+    along = lax.broadcasted_iota(jnp.int32, (n, n), 1)
+    return jnp.sum(jnp.where(down == along, row, 0.0), axis=1, keepdims=True)
+
+
 def place_kernel(experts, capacity, ids_ref, unit_ref, tok_ref, cot_ref, send_ref, pick_ref):
-    i = pl.program_id(0)
-    half = pl.num_programs(0) // 2
-    tok = tok_ref.shape[0]
-
-    @pl.when(i == 0)
-    def _():
-        labels = lax.broadcasted_iota(jnp.int32, (tok, experts), 1)
-        row = lax.broadcasted_iota(jnp.int32, (tok, tok), 0)
-        col = lax.broadcasted_iota(jnp.int32, (tok, tok), 1)
-        before = jnp.where(col < row, 1.0, 0.0).astype(BF)
-        hot = jnp.where(ids_ref[...] == labels, 1.0, 0.0)
-        ranks = mm(before, hot.astype(BF), NN)
-        rank = jnp.sum(ranks * hot, axis=1, keepdims=True).astype(jnp.int32)
-        slot = ids_ref[...] * capacity + rank
-        places = lax.broadcasted_iota(jnp.int32, (tok, experts * capacity), 1)
-        pick_ref[...] = jnp.where(slot == places, 1.0, 0.0).astype(BF)
-
-    @pl.when(i < half)
-    def _():
-        send_ref[...] = mm(pick_ref[...], tok_ref[...], TN).astype(BF)
-
-    @pl.when(i >= half)
-    def _():
-        scale = unit_ref[...].astype(F32) / 256.0
-        rows = (scale * cot_ref[...].astype(F32)).astype(BF)
-        send_ref[...] = mm(pick_ref[...], rows, TN).astype(BF)
-
-
-def place_call(experts, capacity, ids, units, tokens, cotangent):
-    tok, width = tokens.shape
-    slots = experts * capacity
-    half = 4
-    step = width // half
-    shape = jax.ShapeDtypeStruct
-    column = pl.BlockSpec((tok, 1), lambda i: (0, 0))
-    return pl.pallas_call(
-        lambda *refs: place_kernel(experts, capacity, *refs),
-        grid=(2 * half,),
-        in_specs=[
-            column,
-            column,
-            pl.BlockSpec((tok, step), lambda i: (0, jnp.minimum(i, half - 1))),
-            pl.BlockSpec((tok, step), lambda i: (0, jnp.maximum(i - half, 0))),
-        ],
-        out_specs=[
-            pl.BlockSpec((slots, step), lambda i: (0, i)),
-            pl.BlockSpec((tok, slots), lambda i: (0, 0)),
-        ],
-        out_shape=[shape((slots, 2 * width), BF), shape((tok, slots), BF)],
-        compiler_params=params(56),
-        cost_estimate=pl.CostEstimate(
-            flops=4 * tok * slots * width, bytes_accessed=12 * tok * width, transcendentals=0
-        ),
-    )(ids, units, tokens, cotangent)
+    tok, width = tok_ref.shape
+    ids = ids_ref[...]
+    labels = lax.broadcasted_iota(jnp.int32, (experts, tok), 0)
+    down = lax.broadcasted_iota(jnp.int32, (tok, tok), 0)
+    along = lax.broadcasted_iota(jnp.int32, (tok, tok), 1)
+    before = jnp.where(down < along, 1.0, 0.0).astype(BF)
+    hot = jnp.where(ids == labels, 1.0, 0.0)
+    ranks = mm(hot.astype(BF), before, NN)
+    rank = jnp.sum(ranks * hot, axis=0, keepdims=True).astype(jnp.int32)
+    slot = ids * capacity + rank
+    places = lax.broadcasted_iota(jnp.int32, (experts * capacity, tok), 0)
+    pick = jnp.where(slot == places, 1.0, 0.0).astype(BF)
+    pick_ref[...] = pick
+    scale = column(unit_ref[...].astype(F32) / 256.0)
+    step = width // 4
+    for c in range(4):
+        part = pl.ds(c * step, step)
+        send_ref[:, part] = mm(pick, tok_ref[:, part], NN).astype(BF)
+        rows = (scale * cot_ref[:, part].astype(F32)).astype(BF)
+        send_ref[:, pl.ds(width + c * step, step)] = mm(pick, rows, NN).astype(BF)
 
 
 def expert_kernel(order_ref, rows_ref, *refs):
     pairs = order_ref.shape[0] - 1
-    shards = refs[: 2 * pairs]
-    send_ref, hid_ref, dpre_ref, dlin_ref = refs[2 * pairs :]
-    block, units = shards[0].shape[1:]
+    send_ref, hid_ref, dpre_ref, dlin_ref, shards, sems = refs[2 * pairs :]
+    block, units = shards.shape[2:]
     width = rows_ref.shape[1] // 2
+    copies = [pltpu.make_async_copy(refs[n], shards.at[n], sems.at[n]) for n in range(2 * pairs)]
+    for copy in copies:
+        copy.start()
     core = order_ref[pairs]
 
     def spots(p, first):
@@ -93,13 +68,16 @@
         return jnp.concatenate([rows_ref[:, s] for s in spots(p, first)], axis=1)
 
     def right(p, m, cols):
-        return jnp.concatenate([w[m, :, cols] for w in shards[2 * p : 2 * p + 2]], axis=0)
+        return jnp.concatenate([shards[n, m, :, cols] for n in (2 * p, 2 * p + 1)], axis=0)
 
     step = 256
     for n in range(units // step):
         cols = pl.ds(n * step, step)
         pre, lin, dhid = 0.0, 0.0, 0.0
         for p in range(pairs):
+            if n == 0:
+                copies[2 * p].wait()
+                copies[2 * p + 1].wait()
             x, g = left(p, 0), left(p, width)
             pre = pre + mm(x, right(p, 0, cols), NN)
             lin = lin + mm(x, right(p, 1, cols), NN)
@@ -138,18 +116,19 @@
 
 def finish_kernel(pick_ref, unit_ref, got_ref, mixed_ref, back_ref):
     width = mixed_ref.shape[1]
-    scale = unit_ref[...].astype(F32) / 256.0
+    scale = column(unit_ref[...].astype(F32) / 256.0)
     step = width // 4
     for c in range(4):
         part = pl.ds(c * step, step)
-        mixed_ref[:, part] = (scale * mm(pick_ref[...], got_ref[:, part], NN)).astype(BF)
+        mixed_ref[:, part] = (scale * mm(pick_ref[...], got_ref[:, part], TN)).astype(BF)
         other = pl.ds(width + c * step, step)
-        back_ref[:, part] = mm(pick_ref[...], got_ref[:, other], NN).astype(BF)
-
-
-def call(kernel, outs, mib, flops, args, smem=0):
+        back_ref[:, part] = mm(pick_ref[...], got_ref[:, other], TN).astype(BF)
+
+
+def call(kernel, outs, mib, flops, args, smem=0, left=0, scratch=()):
     in_specs = [pl.BlockSpec(memory_space=pltpu.SMEM)] * smem
-    in_specs += [pl.BlockSpec(memory_space=VM)] * (len(args) - smem)
+    in_specs += [pl.BlockSpec(memory_space=VM)] * (len(args) - smem - left)
+    in_specs += [pl.BlockSpec(memory_space=pl.ANY)] * left
     moved = sum(a.size * a.dtype.itemsize for a in args)
     moved += sum(o.size * o.dtype.itemsize for o in outs)
     return pl.pallas_call(
@@ -157,6 +136,7 @@
         out_shape=outs,
         in_specs=in_specs,
         out_specs=[pl.BlockSpec(memory_space=VM)] * len(outs),
+        scratch_shapes=scratch,
         compiler_params=params(mib),
         cost_estimate=pl.CostEstimate(flops=flops, bytes_accessed=moved, transcendentals=0),
     )(*args)
@@ -178,7 +158,14 @@
     def permute(a, to):
         return lax.ppermute(a, "dp", [(i, to(i)) for i in range(groups)])
 
-    send, pick = place_call(experts, capacity, expert_ids, gate_units, tokens, cotangent)
+    ids, scales = expert_ids.reshape(1, tok), gate_units.reshape(1, tok)
+    send, pick = call(
+        lambda *refs: place_kernel(experts, capacity, *refs),
+        [shape((slots, 2 * width), BF), shape((slots, tok), BF)],
+        56,
+        4 * tok * slots * width,
+        (ids, scales, tokens, cotangent),
+    )
 
     own = jnp.concatenate([w_gate, w_up, w_down], axis=0)
     across = permute(own, lambda i: i ^ 2)
@@ -200,10 +187,12 @@
     answer, hidden, d_pre, d_lin = call(
         expert_kernel,
         [shape((slots, 2 * width), BF), small, small, small],
-        32,
+        56,
         12 * slots * width * units,
         (source, rows, *shards),
         smem=1,
+        left=len(shards),
+        scratch=[VM((len(shards), 3, block, units), BF), pltpu.SemaphoreType.DMA((len(shards),))],
     )
     got = exchange(answer)
 
@@ -242,7 +231,7 @@
         [shape((tok, width), BF)] * 2,
         24,
         4 * tok * slots * width,
-        (pick, gate_units, got),
+        (pick, scales, got),
     )
     return (mixed, grad_tokens, *grads)
 

time: 252 us -> 240 us (0.952)
  local copies, waits for them, and re-layouts: 21.4 us -> 3.12 us
  waiting for transfers between devices: 77.9 us -> 81 us
  starting transfers between devices: 126 us -> 129 us
    unnamed x54 -> x36, local copies, waits for them, and re-layouts: 21.3 us -> 3.03 us
    pallas_call x4 -> x5, Pallas kernels: 14.1 us -> 21.1 us  [call(): pl.pallas_call(kernel, out_shape=outs, in_specs=in_specs, out_specs=[pl.B...]
    pallas_call x1 -> x0, Pallas kernels: 6.87 us -> none  [place_call(): pl.pallas_call(lambda *refs: place_kernel(experts, capacity, *refs), grid...]
    ppermute x30, starting transfers between devices: 106 us -> 109 us  [permute(): return lax.ppermute(a, 'dp', [(i, to(i)) for i in range(groups)])]
  transfers between devices with their start and end apart: 32 -> 32, of which waited for: 14 -> 15; matrix products, arithmetic and copies ran while one was open for 1% -> 2% of each run, Pallas kernels for 2% -> 2%
where the time goes in v3:
time: 240 us; the launch traced here: 239 us
  starting transfers between devices  129 us (54%)
  waiting for transfers between devices  81 us (34%)
  Pallas kernels  21.1 us (9%)
  other arithmetic  3.57 us (1%)
  local copies, waits for them, and re-layouts  3.12 us (1%)
    ppermute x30, starting transfers between devices, permute(): return lax.ppermute(a, 'dp', [(i, to(i)) for i in range(groups)])  109 us
    all_to_all x2, waiting for transfers between devices, exchange(): got = lax.all_to_all(cut, 'expert', split_axis=0, concat_axis=0, tiled=True)  41.8 us
    ppermute x30, waiting for transfers between devices, permute(): return lax.ppermute(a, 'dp', [(i, to(i)) for i in range(groups)])  39.2 us
    pallas_call x5, Pallas kernels, call(): pl.pallas_call(kernel, out_shape=outs, in_specs=in_specs, out_specs=[pl.B...  21.1 us
    all_to_all x2, starting transfers between devices, exchange(): got = lax.all_to_all(cut, 'expert', split_axis=0, concat_axis=0, tiled=True)  19.9 us
  transfers between devices with their start and end apart: 32, of which 15 were waited for; matrix products, arithmetic and copies ran while one was open for 2% of the time, Pallas kernels for 2%

profile of v3, /device:TPU:33, one launch (start us, length us, event | category | flops | bytes accessed | tf_op | source)
XLA Modules:
  0.0 239.0 jit_solution(9673746174706033473)
XLA Ops:
  0.6 3.4 %shard_map.110 = (bf16[256,4096]{1,0:T(8,128)(2,1)}, bf16[256,128]{1,0:T(8,128)(2,1)}) custom-call(s32[1,128]{1,0:T(1,128)} %bitcast.45, s32[1,128]{1,0:T(1,128)} %bitcast.41, bf16[128,2048]{1,0:T(8,128)(2,1)} %refs_2_.1, bf16[128,2048]{1,0:T(8,128)(2,1)} %refs_3_.1), custom_call_target="tpu_custom_call" | custom-call | flops 268435456 | bytes 3212288 | tf_op jit(solution)/shard_map/pallas_call | solution.py:134
  4.1 15.9 %all-to-all-start = ((bf16[32,8,4096]{2,1,0:T(8,128)(2,1)}), bf16[32,8,4096]{2,1,0:T(8,128)(2,1)S(1)}, u32[]{:S(2)}, u32[]{:S(2)}) async-start(bf16[32,8,4096]{2,1,0:T(8,128)(2,1)} %bitcast.44), calls=%async_computation | async-start | bytes 4194304 | tf_op jit(solution)/shard_map/all_to_all | solution.py:182
  20.1 4.5 %collective-permute-start.7 = (bf16[3,128,768]{2,1,0:T(8,128)(2,1)S(1)}, bf16[3,128,768]{2,1,0:T(8,128)(2,1)S(1)}, u32[]{:S(2)}, u32[]{:S(2)}) collective-permute-start(bf16[3,128,768]{2,1,0:T(8,128)(2,1)S(1)} %constant_dynamic-update-slice_fusion.refs_0_), channel_id=1, source_target_pairs={{0,64},{32,96},{64,0},{96,32},{128,192},{160,224},{192,128},{224,1... | collective-permute-start | bytes 1769480 | tf_op jit(solution)/shard_map/ppermute | solution.py:159
  24.7 4.4 %collective-permute-start.5 = (bf16[3,128,768]{2,1,0:T(8,128)(2,1)S(1)}, bf16[3,128,768]{2,1,0:T(8,128)(2,1)S(1)}, u32[]{:S(2)}, u32[]{:S(2)}) collective-permute-start(bf16[3,128,768]{2,1,0:T(8,128)(2,1)S(1)} %constant_dynamic-update-slice_fusion.refs_0_), channel_id=1, source_target_pairs={{0,384},{32,416},{64,448},{96,480},{128,0},{160,32},{192,64},{224,... | collective-permute-start | bytes 1769480 | tf_op jit(solution)/shard_map/ppermute | solution.py:159
  29.1 2.4 %collective-permute-start.3 = (bf16[3,128,768]{2,1,0:T(8,128)(2,1)S(1)}, bf16[3,128,768]{2,1,0:T(8,128)(2,1)}, u32[]{:S(2)}, u32[]{:S(2)}) collective-permute-start(bf16[3,128,768]{2,1,0:T(8,128)(2,1)S(1)} %constant_dynamic-update-slice_fusion.refs_0_), channel_id=1, source_target_pairs={{0,256},{32,288},{64,320},{96,352},{128,384},{160,416},{192,448},{... | collective-permute-start | bytes 1769480 | tf_op jit(solution)/shard_map/ppermute | solution.py:159
  31.5 2.5 %collective-permute-start.1 = (bf16[3,128,768]{2,1,0:T(8,128)(2,1)S(1)}, bf16[3,128,768]{2,1,0:T(8,128)(2,1)}, u32[]{:S(2)}, u32[]{:S(2)}) collective-permute-start(bf16[3,128,768]{2,1,0:T(8,128)(2,1)S(1)} %constant_dynamic-update-slice_fusion.refs_0_), channel_id=1, source_target_pairs={{0,128},{32,160},{64,192},{96,224},{128,256},{160,288},{192,320},{... | collective-permute-start | bytes 1769480 | tf_op jit(solution)/shard_map/ppermute | solution.py:159
  34.0 4.3 %collective-permute-start = (bf16[3,128,768]{2,1,0:T(8,128)(2,1)S(1)}, bf16[3,128,768]{2,1,0:T(8,128)(2,1)S(1)}, u32[]{:S(2)}, u32[]{:S(2)}) collective-permute-start(bf16[3,128,768]{2,1,0:T(8,128)(2,1)S(1)} %constant_dynamic-update-slice_fusion.refs_0_), channel_id=1, source_target_pairs={{0,32},{32,0},{64,96},{96,64},{128,160},{160,128},{192,224},{224,1... | collective-permute-start | bytes 1769480 | tf_op jit(solution)/shard_map/ppermute | solution.py:159
  38.3 1.7 collective-permute-done.7.refs_8_
  40.0 4.3 %collective-permute-start.13 = (bf16[3,128,768]{2,1,0:T(8,128)(2,1)S(1)}, bf16[3,128,768]{2,1,0:T(8,128)(2,1)}, u32[]{:S(2)}, u32[]{:S(2)}) collective-permute-start(bf16[3,128,768]{2,1,0:T(8,128)(2,1)S(1)} %collective-permute-done.7.refs_8_), channel_id=1, source_target_pairs={{0,384},{32,416},{64,448},{96,480},{128,0},{160,32},{192,64},{224,... | collective-permute-start | bytes 1769480 | tf_op jit(solution)/shard_map/ppermute | solution.py:159
  44.3 2.4 %collective-permute-start.11 = (bf16[3,128,768]{2,1,0:T(8,128)(2,1)S(1)}, bf16[3,128,768]{2,1,0:T(8,128)(2,1)}, u32[]{:S(2)}, u32[]{:S(2)}) collective-permute-start(bf16[3,128,768]{2,1,0:T(8,128)(2,1)S(1)} %collective-permute-done.7.refs_8_), channel_id=1, source_target_pairs={{0,256},{32,288},{64,320},{96,352},{128,384},{160,416},{192,448},{... | collective-permute-start | bytes 1769480 | tf_op jit(solution)/shard_map/ppermute | solution.py:159
  46.7 10.0 %collective-permute-start.9 = (bf16[3,128,768]{2,1,0:T(8,128)(2,1)S(1)}, bf16[3,128,768]{2,1,0:T(8,128)(2,1)}, u32[]{:S(2)}, u32[]{:S(2)}) collective-permute-start(bf16[3,128,768]{2,1,0:T(8,128)(2,1)S(1)} %collective-permute-done.7.refs_8_), channel_id=1, source_target_pairs={{0,128},{32,160},{64,192},{96,224},{128,256},{160,288},{192,320},{... | collective-permute-start | bytes 1769480 | tf_op jit(solution)/shard_map/ppermute | solution.py:159
  56.7 5.9 %collective-permute-done.1.refs_2_ = bf16[3,128,768]{2,1,0:T(8,128)(2,1)} collective-permute-done((bf16[3,128,768]{2,1,0:T(8,128)(2,1)S(1)}, bf16[3,128,768]{2,1,0:T(8,128)(2,1)}, u32[]{:S(2)}, u32[]{:S(2)}) %collective-permute-start.1) | collective-permute-done | bytes 589856 | tf_op jit(solution)/shard_map/ppermute | solution.py:159
  62.6 4.0 %collective-permute-start.8 = (bf16[3,128,768]{2,1,0:T(8,128)(2,1)S(1)}, bf16[3,128,768]{2,1,0:T(8,128)(2,1)S(1)}, u32[]{:S(2)}, u32[]{:S(2)}) collective-permute-start(bf16[3,128,768]{2,1,0:T(8,128)(2,1)S(1)} %collective-permute-done.7.refs_8_), channel_id=1, source_target_pairs={{0,32},{32,0},{64,96},{96,64},{128,160},{160,128},{192,224},{224,1... | collective-permute-start | bytes 1769480 | tf_op jit(solution)/shard_map/ppermute | solution.py:159
  66.7 1.9 collective-permute-start.6
  68.6 13.8 %collective-permute-start.4 = (bf16[3,128,768]{2,1,0:T(8,128)(2,1)}, bf16[3,128,768]{2,1,0:T(8,128)(2,1)}, u32[]{:S(2)}, u32[]{:S(2)}) collective-permute-start(bf16[3,128,768]{2,1,0:T(8,128)(2,1)} %collective-permute-done.3.refs_4_), channel_id=1, source_target_pairs={{0,32},{32,0},{64,96},{96,64},{128,160},{160,128},{192,224},{224,1... | collective-permute-start | bytes 1769480 | tf_op jit(solution)/shard_map/ppermute | solution.py:159
  82.5 1.9 collective-permute-start.2
  84.4 1.2 collective-permute-done.9.refs_10_
  85.6 2.5 %collective-permute-start.14 = (bf16[3,128,768]{2,1,0:T(8,128)(2,1)}, bf16[3,128,768]{2,1,0:T(8,128)(2,1)}, u32[]{:S(2)}, u32[]{:S(2)}) collective-permute-start(bf16[3,128,768]{2,1,0:T(8,128)(2,1)} %collective-permute-done.13.refs_14_), channel_id=1, source_target_pairs={{0,32},{32,0},{64,96},{96,64},{128,160},{160,128},{192,224},{224,1... | collective-permute-start | bytes 1769480 | tf_op jit(solution)/shard_map/ppermute | solution.py:159
  88.2 1.9 collective-permute-start.12
  90.1 2.4 %collective-permute-start.10 = (bf16[3,128,768]{2,1,0:T(8,128)(2,1)}, bf16[3,128,768]{2,1,0:T(8,128)(2,1)}, u32[]{:S(2)}, u32[]{:S(2)}) collective-permute-start(bf16[3,128,768]{2,1,0:T(8,128)(2,1)} %collective-permute-done.9.refs_10_), channel_id=1, source_target_pairs={{0,32},{32,0},{64,96},{96,64},{128,160},{160,128},{192,224},{224,1... | collective-permute-start | bytes 1769480 | tf_op jit(solution)/shard_map/ppermute | solution.py:159
  92.6 0.7 pad_add_fusion.order_ref
  93.3 1.2 collective-permute-done.10.refs_11_
  94.5 26.0 %all-to-all-done = bf16[32,8,4096]{2,1,0:T(8,128)(2,1)S(1)} async-done(((bf16[32,8,4096]{2,1,0:T(8,128)(2,1)}), bf16[32,8,4096]{2,1,0:T(8,128)(2,1)S(1)}, u32[]{:S(2)}, u32[]{:S(2)}) %all-to-all-start) | async-done | bytes 2097184 | tf_op jit(solution)/shard_map/all_to_all | solution.py:182
  120.5 1.3 copy-done
  121.9 12.1 %shard_map.111 = (bf16[256,4096]{1,0:T(8,128)(2,1)}, bf16[256,768]{1,0:T(8,128)(2,1)}, bf16[256,768]{1,0:T(8,128)(2,1)}, bf16[256,768]{1,0:T(8,128)(2,1)}) custom-call(s32[9]{0:T(128)} %pad_add_fusion.order_ref, bf16[256,4096]{1,0:T(8,128)(2,1)} %bitcast.38, bf16[3,128,768]{2,1,0:T(8,128)(2,1)} %copy-done.11, bf16[3,128,768]{2,1,0:T(8,128)(2,1)} %copy-done.14, ...), custom_call_target="tpu_custom_call" | custom-call | flops 4831838208 | bytes 14811172 | tf_op jit(solution)/shard_map/pallas_call | solution.py:134
  134.0 0.0 copy-start.3
  134.0 0.0 copy-start.4
  134.0 0.0 copy-start.5
  134.0 3.9 %all-to-all-start.1 = ((bf16[32,8,4096]{2,1,0:T(8,128)(2,1)}), bf16[32,8,4096]{2,1,0:T(8,128)(2,1)S(1)}, u32[]{:S(2)}, u32[]{:S(2)}) async-start(bf16[32,8,4096]{2,1,0:T(8,128)(2,1)} %bitcast.43), calls=%async_computation.1 | async-start | bytes 4194304 | tf_op jit(solution)/shard_map/all_to_all | solution.py:182
  138.0 1.6 copy-done.1
  139.6 2.0 shard_map.113
  141.6 2.7 %collective-permute-start.15 = (bf16[8,128,768]{2,1,0:T(8,128)(2,1)S(1)}, bf16[8,128,768]{2,1,0:T(8,128)(2,1)S(1)}, u32[]{:S(2)}, u32[]{:S(2)}) collective-permute-start(bf16[8,128,768]{2,1,0:T(8,128)(2,1)S(1)} %get-tuple-element.36), channel_id=1, source_target_pairs={{0,32},{32,0},{64,96},{96,64},{128,160},{160,128},{192,224},{224,1... | collective-permute-start | bytes 4718600 | tf_op jit(solution)/shard_map/ppermute | solution.py:159
  144.3 1.9 collective-permute-start.16
  146.2 2.6 %collective-permute-start.17 = (bf16[8,128,768]{2,1,0:T(8,128)(2,1)S(1)}, bf16[8,128,768]{2,1,0:T(8,128)(2,1)S(1)}, u32[]{:S(2)}, u32[]{:S(2)}) collective-permute-start(bf16[8,128,768]{2,1,0:T(8,128)(2,1)S(1)} %get-tuple-element.38), channel_id=1, source_target_pairs={{0,32},{32,0},{64,96},{96,64},{128,160},{160,128},{192,224},{224,1... | collective-permute-start | bytes 4718600 | tf_op jit(solution)/shard_map/ppermute | solution.py:159
  148.8 0.8 collective-permute-done.16.refs_6_
  149.6 2.2 collective-permute-done.17.refs_7_
  151.8 2.2 shard_map.114
  154.1 3.1 %collective-permute-start.18 = (bf16[2,128,768]{2,1,0:T(8,128)(2,1)S(1)}, bf16[2,128,768]{2,1,0:T(8,128)(2,1)S(1)}, u32[]{:S(2)}, u32[]{:S(2)}) collective-permute-start(bf16[2,128,768]{2,1,0:T(8,128)(2,1)S(1)} %get-tuple-element.40), channel_id=1, source_target_pairs={{0,128},{32,160},{64,192},{96,224},{128,256},{160,288},{192,320},{... | collective-permute-start | bytes 1179656 | tf_op jit(solution)/shard_map/ppermute | solution.py:159
  157.2 4.4 %collective-permute-start.19 = (bf16[2,128,768]{2,1,0:T(8,128)(2,1)S(1)}, bf16[2,128,768]{2,1,0:T(8,128)(2,1)S(1)}, u32[]{:S(2)}, u32[]{:S(2)}) collective-permute-start(bf16[2,128,768]{2,1,0:T(8,128)(2,1)S(1)} %get-tuple-element.41), channel_id=1, source_target_pairs={{0,256},{32,288},{64,320},{96,352},{128,384},{160,416},{192,448},{... | collective-permute-start | bytes 1179656 | tf_op jit(solution)/shard_map/ppermute | solution.py:159
  161.6 3.0 %collective-permute-start.20 = (bf16[2,128,768]{2,1,0:T(8,128)(2,1)S(1)}, bf16[2,128,768]{2,1,0:T(8,128)(2,1)S(1)}, u32[]{:S(2)}, u32[]{:S(2)}) collective-permute-start(bf16[2,128,768]{2,1,0:T(8,128)(2,1)S(1)} %get-tuple-element.42), channel_id=1, source_target_pairs={{0,384},{32,416},{64,448},{96,480},{128,0},{160,32},{192,64},{224,... | collective-permute-start | bytes 1179656 | tf_op jit(solution)/shard_map/ppermute | solution.py:159
  164.6 2.2 collective-permute-start.22
  166.9 2.8 %collective-permute-start.23 = (bf16[2,128,768]{2,1,0:T(8,128)(2,1)S(1)}, bf16[2,128,768]{2,1,0:T(8,128)(2,1)S(1)}, u32[]{:S(2)}, u32[]{:S(2)}) collective-permute-start(bf16[2,128,768]{2,1,0:T(8,128)(2,1)S(1)} %get-tuple-element.45), channel_id=1, source_target_pairs={{0,256},{32,288},{64,320},{96,352},{128,384},{160,416},{192,448},{... | collective-permute-start | bytes 1179656 | tf_op jit(solution)/shard_map/ppermute | solution.py:159
  169.7 3.4 %collective-permute-start.24 = (bf16[2,128,768]{2,1,0:T(8,128)(2,1)S(1)}, bf16[2,128,768]{2,1,0:T(8,128)(2,1)S(1)}, u32[]{:S(2)}, u32[]{:S(2)}) collective-permute-start(bf16[2,128,768]{2,1,0:T(8,128)(2,1)S(1)} %get-tuple-element.46), channel_id=1, source_target_pairs={{0,384},{32,416},{64,448},{96,480},{128,0},{160,32},{192,64},{224,... | collective-permute-start | bytes 1179656 | tf_op jit(solution)/shard_map/ppermute | solution.py:159
  173.1 3.9 %collective-permute-done.19 = bf16[2,128,768]{2,1,0:T(8,128)(2,1)S(1)} collective-permute-done((bf16[2,128,768]{2,1,0:T(8,128)(2,1)S(1)}, bf16[2,128,768]{2,1,0:T(8,128)(2,1)S(1)}, u32[]{:S(2)}, u32[]{:S(2)}) %collective-permute-start.19) | collective-permute-done | bytes 393248 | tf_op jit(solution)/shard_map/ppermute | solution.py:159
  177.1 1.9 collective-permute-start.26
  179.0 4.1 %collective-permute-start.27 = (bf16[2,128,768]{2,1,0:T(8,128)(2,1)S(1)}, bf16[2,128,768]{2,1,0:T(8,128)(2,1)S(1)}, u32[]{:S(2)}, u32[]{:S(2)}) collective-permute-start(bf16[2,128,768]{2,1,0:T(8,128)(2,1)S(1)} %get-tuple-element.49), channel_id=1, source_target_pairs={{0,256},{32,288},{64,320},{96,352},{128,384},{160,416},{192,448},{... | collective-permute-start | bytes 1179656 | tf_op jit(solution)/shard_map/ppermute | solution.py:159
  183.1 0.2 convert_add_fusion.2
  183.4 3.3 %collective-permute-done.22 = bf16[2,128,768]{2,1,0:T(8,128)(2,1)S(1)} collective-permute-done((bf16[2,128,768]{2,1,0:T(8,128)(2,1)S(1)}, bf16[2,128,768]{2,1,0:T(8,128)(2,1)S(1)}, u32[]{:S(2)}, u32[]{:S(2)}) %collective-permute-start.22) | collective-permute-done | bytes 393248 | tf_op jit(solution)/shard_map/ppermute | solution.py:159
  186.6 1.9 collective-permute-start.28
  188.6 5.4 %collective-permute-done.23 = bf16[2,128,768]{2,1,0:T(8,128)(2,1)S(1)} collective-permute-done((bf16[2,128,768]{2,1,0:T(8,128)(2,1)S(1)}, bf16[2,128,768]{2,1,0:T(8,128)(2,1)S(1)}, u32[]{:S(2)}, u32[]{:S(2)}) %collective-permute-start.23) | collective-permute-done | bytes 393248 | tf_op jit(solution)/shard_map/ppermute | solution.py:159
  194.0 4.5 %collective-permute-start.21 = (bf16[128,768]{1,0:T(8,128)(2,1)S(1)}, bf16[128,768]{1,0:T(8,128)(2,1)S(1)}, u32[]{:S(2)}, u32[]{:S(2)}) collective-permute-start(bf16[128,768]{1,0:T(8,128)(2,1)S(1)} %fusion.6), channel_id=1, source_target_pairs={{0,64},{32,96},{64,0},{96,32},{128,192},{160,224},{192,128},{224,1... | collective-permute-start | bytes 589832 | tf_op jit(solution)/shard_map/ppermute | solution.py:159
  198.5 0.2 convert_add_fusion.1
  198.8 2.2 collective-permute-start.25
  201.0 2.5 %collective-permute-done.26 = bf16[2,128,768]{2,1,0:T(8,128)(2,1)S(1)} collective-permute-done((bf16[2,128,768]{2,1,0:T(8,128)(2,1)S(1)}, bf16[2,128,768]{2,1,0:T(8,128)(2,1)S(1)}, u32[]{:S(2)}, u32[]{:S(2)}) %collective-permute-start.26) | collective-permute-done | bytes 393248 | tf_op jit(solution)/shard_map/ppermute | solution.py:159
  203.4 7.4 %collective-permute-done.27 = bf16[2,128,768]{2,1,0:T(8,128)(2,1)S(1)} collective-permute-done((bf16[2,128,768]{2,1,0:T(8,128)(2,1)S(1)}, bf16[2,128,768]{2,1,0:T(8,128)(2,1)S(1)}, u32[]{:S(2)}, u32[]{:S(2)}) %collective-permute-start.27) | collective-permute-done | bytes 393248 | tf_op jit(solution)/shard_map/ppermute | solution.py:159
  210.8 1.2 collective-permute-done.28
  212.0 0.2 convert_add_fusion
  212.3 4.7 %collective-permute-start.29 = (bf16[128,768]{1,0:T(8,128)(2,1)S(1)}, bf16[128,768]{1,0:T(8,128)(2,1)S(1)}, u32[]{:S(2)}, u32[]{:S(2)}) collective-permute-start(bf16[128,768]{1,0:T(8,128)(2,1)S(1)} %fusion.8), channel_id=1, source_target_pairs={{0,64},{32,96},{64,0},{96,32},{128,192},{160,224},{192,128},{224,1... | collective-permute-start | bytes 589832 | tf_op jit(solution)/shard_map/ppermute | solution.py:159
  217.0 0.8 fusion.5
  217.8 0.8 fusion.3
  218.5 2.5 %collective-permute-done.29 = bf16[128,768]{1,0:T(8,128)(2,1)S(1)} collective-permute-done((bf16[128,768]{1,0:T(8,128)(2,1)S(1)}, bf16[128,768]{1,0:T(8,128)(2,1)S(1)}, u32[]{:S(2)}, u32[]{:S(2)}) %collective-permute-start.29) | collective-permute-done | bytes 196640 | tf_op jit(solution)/shard_map/ppermute | solution.py:159
  221.0 0.8 fusion.1
  221.8 15.8 %all-to-all-done.1 = bf16[32,8,4096]{2,1,0:T(8,128)(2,1)S(1)} async-done(((bf16[32,8,4096]{2,1,0:T(8,128)(2,1)}), bf16[32,8,4096]{2,1,0:T(8,128)(2,1)S(1)}, u32[]{:S(2)}, u32[]{:S(2)}) %all-to-all-start.1) | async-done | bytes 2097184 | tf_op jit(solution)/shard_map/all_to_all | solution.py:182
  237.6 1.4 shard_map.112
  (54 shorter events, 0.2 us)
Async XLA Ops:
  4.1 16.0 %copy-start.8 = (bf16[1,128,768]{2,1,0:T(8,128)(2,1)S(1)}, bf16[1,128,768]{2,1,0:T(8,128)(2,1)}, u32[]{:S(2)}) copy-start(bf16[1,128,768]{2,1,0:T(8,128)(2,1)} %param.11) | copy-start | bytes 589828
  4.1 16.0 %copy-start.9 = (bf16[1,128,768]{2,1,0:T(8,128)(2,1)S(1)}, bf16[1,128,768]{2,1,0:T(8,128)(2,1)}, u32[]{:S(2)}) copy-start(bf16[1,128,768]{2,1,0:T(8,128)(2,1)} %param.12) | copy-start | bytes 589828
  4.1 16.0 %copy-start.10 = (bf16[1,128,768]{2,1,0:T(8,128)(2,1)S(1)}, bf16[1,128,768]{2,1,0:T(8,128)(2,1)}, u32[]{:S(2)}) copy-start(bf16[1,128,768]{2,1,0:T(8,128)(2,1)} %param.13) | copy-start | bytes 589828
  4.1 116.5 %all-to-all-start = ((bf16[32,8,4096]{2,1,0:T(8,128)(2,1)}), bf16[32,8,4096]{2,1,0:T(8,128)(2,1)S(1)}, u32[]{:S(2)}, u32[]{:S(2)}) async-start(bf16[32,8,4096]{2,1,0:T(8,128)(2,1)} %bitcast.44), calls=%async_computation | async-start | bytes 4194304 | tf_op jit(solution)/shard_map/all_to_all | solution.py:182
  20.1 100.4 %copy-start.11 = (bf16[3,128,768]{2,1,0:T(8,128)(2,1)}, bf16[3,128,768]{2,1,0:T(8,128)(2,1)S(1)}, u32[]{:S(2)}) copy-start(bf16[3,128,768]{2,1,0:T(8,128)(2,1)S(1)} %constant_dynamic-update-slice_fusion.refs_0_) | copy-start | bytes 1769476
  20.1 19.8 %collective-permute-start.7 = (bf16[3,128,768]{2,1,0:T(8,128)(2,1)S(1)}, bf16[3,128,768]{2,1,0:T(8,128)(2,1)S(1)}, u32[]{:S(2)}, u32[]{:S(2)}) collective-permute-start(bf16[3,128,768]{2,1,0:T(8,128)(2,1)S(1)} %constant_dynamic-update-slice_fusion.refs_0_), channel_id=1, source_target_pairs={{0,64},{32,96},{64,0},{96,32},{128,192},{160,224},{192,128},{224,1... | collective-permute-start | bytes 1769480 | tf_op jit(solution)/shard_map/ppermute | solution.py:159
  24.7 19.6 %collective-permute-start.5 = (bf16[3,128,768]{2,1,0:T(8,128)(2,1)S(1)}, bf16[3,128,768]{2,1,0:T(8,128)(2,1)S(1)}, u32[]{:S(2)}, u32[]{:S(2)}) collective-permute-start(bf16[3,128,768]{2,1,0:T(8,128)(2,1)S(1)} %constant_dynamic-update-slice_fusion.refs_0_), channel_id=1, source_target_pairs={{0,384},{32,416},{64,448},{96,480},{128,0},{160,32},{192,64},{224,... | collective-permute-start | bytes 1769480 | tf_op jit(solution)/shard_map/ppermute | solution.py:159
  29.1 17.7 %collective-permute-start.3 = (bf16[3,128,768]{2,1,0:T(8,128)(2,1)S(1)}, bf16[3,128,768]{2,1,0:T(8,128)(2,1)}, u32[]{:S(2)}, u32[]{:S(2)}) collective-permute-start(bf16[3,128,768]{2,1,0:T(8,128)(2,1)S(1)} %constant_dynamic-update-slice_fusion.refs_0_), channel_id=1, source_target_pairs={{0,256},{32,288},{64,320},{96,352},{128,384},{160,416},{192,448},{... | collective-permute-start | bytes 1769480 | tf_op jit(solution)/shard_map/ppermute | solution.py:159
  31.5 31.1 %collective-permute-start.1 = (bf16[3,128,768]{2,1,0:T(8,128)(2,1)S(1)}, bf16[3,128,768]{2,1,0:T(8,128)(2,1)}, u32[]{:S(2)}, u32[]{:S(2)}) collective-permute-start(bf16[3,128,768]{2,1,0:T(8,128)(2,1)S(1)} %constant_dynamic-update-slice_fusion.refs_0_), channel_id=1, source_target_pairs={{0,128},{32,160},{64,192},{96,224},{128,256},{160,288},{192,320},{... | collective-permute-start | bytes 1769480 | tf_op jit(solution)/shard_map/ppermute | solution.py:159
  34.0 32.6 %collective-permute-start = (bf16[3,128,768]{2,1,0:T(8,128)(2,1)S(1)}, bf16[3,128,768]{2,1,0:T(8,128)(2,1)S(1)}, u32[]{:S(2)}, u32[]{:S(2)}) collective-permute-start(bf16[3,128,768]{2,1,0:T(8,128)(2,1)S(1)} %constant_dynamic-update-slice_fusion.refs_0_), channel_id=1, source_target_pairs={{0,32},{32,0},{64,96},{96,64},{128,160},{160,128},{192,224},{224,1... | collective-permute-start | bytes 1769480 | tf_op jit(solution)/shard_map/ppermute | solution.py:159
  40.0 52.6 %copy-start.12 = (bf16[3,128,768]{2,1,0:T(8,128)(2,1)}, bf16[3,128,768]{2,1,0:T(8,128)(2,1)S(1)}, u32[]{:S(2)}) copy-start(bf16[3,128,768]{2,1,0:T(8,128)(2,1)S(1)} %collective-permute-done.7.refs_8_) | copy-start | bytes 1769476
  40.0 28.6 %collective-permute-start.13 = (bf16[3,128,768]{2,1,0:T(8,128)(2,1)S(1)}, bf16[3,128,768]{2,1,0:T(8,128)(2,1)}, u32[]{:S(2)}, u32[]{:S(2)}) collective-permute-start(bf16[3,128,768]{2,1,0:T(8,128)(2,1)S(1)} %collective-permute-done.7.refs_8_), channel_id=1, source_target_pairs={{0,384},{32,416},{64,448},{96,480},{128,0},{160,32},{192,64},{224,... | collective-permute-start | bytes 1769480 | tf_op jit(solution)/shard_map/ppermute | solution.py:159
  44.3 43.9 %copy-start.13 = (bf16[3,128,768]{2,1,0:T(8,128)(2,1)}, bf16[3,128,768]{2,1,0:T(8,128)(2,1)S(1)}, u32[]{:S(2)}) copy-start(bf16[3,128,768]{2,1,0:T(8,128)(2,1)S(1)} %collective-permute-done.5.refs_6_) | copy-start | bytes 1769476
  44.3 38.2 %collective-permute-start.11 = (bf16[3,128,768]{2,1,0:T(8,128)(2,1)S(1)}, bf16[3,128,768]{2,1,0:T(8,128)(2,1)}, u32[]{:S(2)}, u32[]{:S(2)}) collective-permute-start(bf16[3,128,768]{2,1,0:T(8,128)(2,1)S(1)} %collective-permute-done.7.refs_8_), channel_id=1, source_target_pairs={{0,256},{32,288},{64,320},{96,352},{128,384},{160,416},{192,448},{... | collective-permute-start | bytes 1769480 | tf_op jit(solution)/shard_map/ppermute | solution.py:159
  46.7 38.9 %collective-permute-start.9 = (bf16[3,128,768]{2,1,0:T(8,128)(2,1)S(1)}, bf16[3,128,768]{2,1,0:T(8,128)(2,1)}, u32[]{:S(2)}, u32[]{:S(2)}) collective-permute-start(bf16[3,128,768]{2,1,0:T(8,128)(2,1)S(1)} %collective-permute-done.7.refs_8_), channel_id=1, source_target_pairs={{0,128},{32,160},{64,192},{96,224},{128,256},{160,288},{192,320},{... | collective-permute-start | bytes 1769480 | tf_op jit(solution)/shard_map/ppermute | solution.py:159
  62.6 25.5 %collective-permute-start.8 = (bf16[3,128,768]{2,1,0:T(8,128)(2,1)S(1)}, bf16[3,128,768]{2,1,0:T(8,128)(2,1)S(1)}, u32[]{:S(2)}, u32[]{:S(2)}) collective-permute-start(bf16[3,128,768]{2,1,0:T(8,128)(2,1)S(1)} %collective-permute-done.7.refs_8_), channel_id=1, source_target_pairs={{0,32},{32,0},{64,96},{96,64},{128,160},{160,128},{192,224},{224,1... | collective-permute-start | bytes 1769480 | tf_op jit(solution)/shard_map/ppermute | solution.py:159
  66.7 23.4 %copy-start.14 = (bf16[3,128,768]{2,1,0:T(8,128)(2,1)}, bf16[3,128,768]{2,1,0:T(8,128)(2,1)S(1)}, u32[]{:S(2)}) copy-start(bf16[3,128,768]{2,1,0:T(8,128)(2,1)S(1)} %collective-permute-done.refs_1_) | copy-start | bytes 1769476
  66.7 23.4 %collective-permute-start.6 = (bf16[3,128,768]{2,1,0:T(8,128)(2,1)S(1)}, bf16[3,128,768]{2,1,0:T(8,128)(2,1)S(1)}, u32[]{:S(2)}, u32[]{:S(2)}) collective-permute-start(bf16[3,128,768]{2,1,0:T(8,128)(2,1)S(1)} %collective-permute-done.5.refs_6_), channel_id=1, source_target_pairs={{0,32},{32,0},{64,96},{96,64},{128,160},{160,128},{192,224},{224,1... | collective-permute-start | bytes 1769480 | tf_op jit(solution)/shard_map/ppermute | solution.py:159
  68.6 24.6 %collective-permute-start.4 = (bf16[3,128,768]{2,1,0:T(8,128)(2,1)}, bf16[3,128,768]{2,1,0:T(8,128)(2,1)}, u32[]{:S(2)}, u32[]{:S(2)}) collective-permute-start(bf16[3,128,768]{2,1,0:T(8,128)(2,1)} %collective-permute-done.3.refs_4_), channel_id=1, source_target_pairs={{0,32},{32,0},{64,96},{96,64},{128,160},{160,128},{192,224},{224,1... | collective-permute-start | bytes 1769480 | tf_op jit(solution)/shard_map/ppermute | solution.py:159
  82.5 10.8 %collective-permute-start.2 = (bf16[3,128,768]{2,1,0:T(8,128)(2,1)}, bf16[3,128,768]{2,1,0:T(8,128)(2,1)}, u32[]{:S(2)}, u32[]{:S(2)}) collective-permute-start(bf16[3,128,768]{2,1,0:T(8,128)(2,1)} %collective-permute-done.1.refs_2_), channel_id=1, source_target_pairs={{0,32},{32,0},{64,96},{96,64},{128,160},{160,128},{192,224},{224,1... | collective-permute-start | bytes 1769480 | tf_op jit(solution)/shard_map/ppermute | solution.py:159
  85.6 7.6 %collective-permute-start.14 = (bf16[3,128,768]{2,1,0:T(8,128)(2,1)}, bf16[3,128,768]{2,1,0:T(8,128)(2,1)}, u32[]{:S(2)}, u32[]{:S(2)}) collective-permute-start(bf16[3,128,768]{2,1,0:T(8,128)(2,1)} %collective-permute-done.13.refs_14_), channel_id=1, source_target_pairs={{0,32},{32,0},{64,96},{96,64},{128,160},{160,128},{192,224},{224,1... | collective-permute-start | bytes 1769480 | tf_op jit(solution)/shard_map/ppermute | solution.py:159
  88.2 4.4 %copy-start.15 = (bf16[3,128,768]{2,1,0:T(8,128)(2,1)}, bf16[3,128,768]{2,1,0:T(8,128)(2,1)S(1)}, u32[]{:S(2)}) copy-start(bf16[3,128,768]{2,1,0:T(8,128)(2,1)S(1)} %collective-permute-done.8.refs_9_) | copy-start | bytes 1769476
  88.2 5.1 %collective-permute-start.12 = (bf16[3,128,768]{2,1,0:T(8,128)(2,1)}, bf16[3,128,768]{2,1,0:T(8,128)(2,1)}, u32[]{:S(2)}, u32[]{:S(2)}) collective-permute-start(bf16[3,128,768]{2,1,0:T(8,128)(2,1)} %collective-permute-done.11.refs_12_), channel_id=1, source_target_pairs={{0,32},{32,0},{64,96},{96,64},{128,160},{160,128},{192,224},{224,1... | collective-permute-start | bytes 1769480 | tf_op jit(solution)/shard_map/ppermute | solution.py:159
  90.1 2.4 %copy-start.16 = (bf16[3,128,768]{2,1,0:T(8,128)(2,1)}, bf16[3,128,768]{2,1,0:T(8,128)(2,1)S(1)}, u32[]{:S(2)}) copy-start(bf16[3,128,768]{2,1,0:T(8,128)(2,1)S(1)} %collective-permute-done.6.refs_7_) | copy-start | bytes 1769476
  90.1 4.4 %collective-permute-start.10 = (bf16[3,128,768]{2,1,0:T(8,128)(2,1)}, bf16[3,128,768]{2,1,0:T(8,128)(2,1)}, u32[]{:S(2)}, u32[]{:S(2)}) collective-permute-start(bf16[3,128,768]{2,1,0:T(8,128)(2,1)} %collective-permute-done.9.refs_10_), channel_id=1, source_target_pairs={{0,32},{32,0},{64,96},{96,64},{128,160},{160,128},{192,224},{224,1... | collective-permute-start | bytes 1769480 | tf_op jit(solution)/shard_map/ppermute | solution.py:159
  120.5 1.4 copy-start
  134.0 4.0 %copy-start.3 = (bf16[256,768]{1,0:T(8,128)(2,1)S(1)}, bf16[256,768]{1,0:T(8,128)(2,1)}, u32[]{:S(2)}) copy-start(bf16[256,768]{1,0:T(8,128)(2,1)} %get-tuple-element.35.refs_4_) | copy-start | bytes 1179652
  134.0 4.0 %copy-start.4 = (bf16[256,768]{1,0:T(8,128)(2,1)S(1)}, bf16[256,768]{1,0:T(8,128)(2,1)}, u32[]{:S(2)}) copy-start(bf16[256,768]{1,0:T(8,128)(2,1)} %get-tuple-element.33.refs_2_) | copy-start | bytes 1179652
  134.0 4.0 %copy-start.5 = (bf16[256,768]{1,0:T(8,128)(2,1)S(1)}, bf16[256,768]{1,0:T(8,128)(2,1)}, u32[]{:S(2)}) copy-start(bf16[256,768]{1,0:T(8,128)(2,1)} %get-tuple-element.34.refs_3_) | copy-start | bytes 1179652
  134.0 103.6 %all-to-all-start.1 = ((bf16[32,8,4096]{2,1,0:T(8,128)(2,1)}), bf16[32,8,4096]{2,1,0:T(8,128)(2,1)S(1)}, u32[]{:S(2)}, u32[]{:S(2)}) async-start(bf16[32,8,4096]{2,1,0:T(8,128)(2,1)} %bitcast.43), calls=%async_computation.1 | async-start | bytes 4194304 | tf_op jit(solution)/shard_map/all_to_all | solution.py:182
  138.0 1.6 copy-start.1
  139.6 12.3 %copy-start.2 = (bf16[32,8,4096]{2,1,0:T(8,128)(2,1)S(1)}, bf16[32,8,4096]{2,1,0:T(8,128)(2,1)}, u32[]{:S(2)}) copy-start(bf16[32,8,4096]{2,1,0:T(8,128)(2,1)} %copy-done) | copy-start | bytes 6291460
  141.6 7.3 %collective-permute-start.15 = (bf16[8,128,768]{2,1,0:T(8,128)(2,1)S(1)}, bf16[8,128,768]{2,1,0:T(8,128)(2,1)S(1)}, u32[]{:S(2)}, u32[]{:S(2)}) collective-permute-start(bf16[8,128,768]{2,1,0:T(8,128)(2,1)S(1)} %get-tuple-element.36), channel_id=1, source_target_pairs={{0,32},{32,0},{64,96},{96,64},{128,160},{160,128},{192,224},{224,1... | collective-permute-start | bytes 4718600 | tf_op jit(solution)/shard_map/ppermute | solution.py:159
  144.3 5.3 %collective-permute-start.16 = (bf16[8,128,768]{2,1,0:T(8,128)(2,1)S(1)}, bf16[8,128,768]{2,1,0:T(8,128)(2,1)S(1)}, u32[]{:S(2)}, u32[]{:S(2)}) collective-permute-start(bf16[8,128,768]{2,1,0:T(8,128)(2,1)S(1)} %get-tuple-element.37), channel_id=1, source_target_pairs={{0,32},{32,0},{64,96},{96,64},{128,160},{160,128},{192,224},{224,1... | collective-permute-start | bytes 4718600 | tf_op jit(solution)/shard_map/ppermute | solution.py:159
  146.2 5.6 %collective-permute-start.17 = (bf16[8,128,768]{2,1,0:T(8,128)(2,1)S(1)}, bf16[8,128,768]{2,1,0:T(8,128)(2,1)S(1)}, u32[]{:S(2)}, u32[]{:S(2)}) collective-permute-start(bf16[8,128,768]{2,1,0:T(8,128)(2,1)S(1)} %get-tuple-element.38), channel_id=1, source_target_pairs={{0,32},{32,0},{64,96},{96,64},{128,160},{160,128},{192,224},{224,1... | collective-permute-start | bytes 4718600 | tf_op jit(solution)/shard_map/ppermute | solution.py:159
  154.1 15.6 %collective-permute-start.18 = (bf16[2,128,768]{2,1,0:T(8,128)(2,1)S(1)}, bf16[2,128,768]{2,1,0:T(8,128)(2,1)S(1)}, u32[]{:S(2)}, u32[]{:S(2)}) collective-permute-start(bf16[2,128,768]{2,1,0:T(8,128)(2,1)S(1)} %get-tuple-element.40), channel_id=1, source_target_pairs={{0,128},{32,160},{64,192},{96,224},{128,256},{160,288},{192,320},{... | collective-permute-start | bytes 1179656 | tf_op jit(solution)/shard_map/ppermute | solution.py:159
  157.2 19.9 %collective-permute-start.19 = (bf16[2,128,768]{2,1,0:T(8,128)(2,1)S(1)}, bf16[2,128,768]{2,1,0:T(8,128)(2,1)S(1)}, u32[]{:S(2)}, u32[]{:S(2)}) collective-permute-start(bf16[2,128,768]{2,1,0:T(8,128)(2,1)S(1)} %get-tuple-element.41), channel_id=1, source_target_pairs={{0,256},{32,288},{64,320},{96,352},{128,384},{160,416},{192,448},{... | collective-permute-start | bytes 1179656 | tf_op jit(solution)/shard_map/ppermute | solution.py:159
  161.6 17.4 %collective-permute-start.20 = (bf16[2,128,768]{2,1,0:T(8,128)(2,1)S(1)}, bf16[2,128,768]{2,1,0:T(8,128)(2,1)S(1)}, u32[]{:S(2)}, u32[]{:S(2)}) collective-permute-start(bf16[2,128,768]{2,1,0:T(8,128)(2,1)S(1)} %get-tuple-element.42), channel_id=1, source_target_pairs={{0,384},{32,416},{64,448},{96,480},{128,0},{160,32},{192,64},{224,... | collective-permute-start | bytes 1179656 | tf_op jit(solution)/shard_map/ppermute | solution.py:159
  164.6 22.0 %collective-permute-start.22 = (bf16[2,128,768]{2,1,0:T(8,128)(2,1)S(1)}, bf16[2,128,768]{2,1,0:T(8,128)(2,1)S(1)}, u32[]{:S(2)}, u32[]{:S(2)}) collective-permute-start(bf16[2,128,768]{2,1,0:T(8,128)(2,1)S(1)} %get-tuple-element.44), channel_id=1, source_target_pairs={{0,128},{32,160},{64,192},{96,224},{128,256},{160,288},{192,320},{... | collective-permute-start | bytes 1179656 | tf_op jit(solution)/shard_map/ppermute | solution.py:159
  166.9 27.1 %collective-permute-start.23 = (bf16[2,128,768]{2,1,0:T(8,128)(2,1)S(1)}, bf16[2,128,768]{2,1,0:T(8,128)(2,1)S(1)}, u32[]{:S(2)}, u32[]{:S(2)}) collective-permute-start(bf16[2,128,768]{2,1,0:T(8,128)(2,1)S(1)} %get-tuple-element.45), channel_id=1, source_target_pairs={{0,256},{32,288},{64,320},{96,352},{128,384},{160,416},{192,448},{... | collective-permute-start | bytes 1179656 | tf_op jit(solution)/shard_map/ppermute | solution.py:159
  169.7 28.9 %collective-permute-start.24 = (bf16[2,128,768]{2,1,0:T(8,128)(2,1)S(1)}, bf16[2,128,768]{2,1,0:T(8,128)(2,1)S(1)}, u32[]{:S(2)}, u32[]{:S(2)}) collective-permute-start(bf16[2,128,768]{2,1,0:T(8,128)(2,1)S(1)} %get-tuple-element.46), channel_id=1, source_target_pairs={{0,384},{32,416},{64,448},{96,480},{128,0},{160,32},{192,64},{224,... | collective-permute-start | bytes 1179656 | tf_op jit(solution)/shard_map/ppermute | solution.py:159
  177.1 26.4 %collective-permute-start.26 = (bf16[2,128,768]{2,1,0:T(8,128)(2,1)S(1)}, bf16[2,128,768]{2,1,0:T(8,128)(2,1)S(1)}, u32[]{:S(2)}, u32[]{:S(2)}) collective-permute-start(bf16[2,128,768]{2,1,0:T(8,128)(2,1)S(1)} %get-tuple-element.48), channel_id=1, source_target_pairs={{0,128},{32,160},{64,192},{96,224},{128,256},{160,288},{192,320},{... | collective-permute-start | bytes 1179656 | tf_op jit(solution)/shard_map/ppermute | solution.py:159
  179.0 31.8 %collective-permute-start.27 = (bf16[2,128,768]{2,1,0:T(8,128)(2,1)S(1)}, bf16[2,128,768]{2,1,0:T(8,128)(2,1)S(1)}, u32[]{:S(2)}, u32[]{:S(2)}) collective-permute-start(bf16[2,128,768]{2,1,0:T(8,128)(2,1)S(1)} %get-tuple-element.49), channel_id=1, source_target_pairs={{0,256},{32,288},{64,320},{96,352},{128,384},{160,416},{192,448},{... | collective-permute-start | bytes 1179656 | tf_op jit(solution)/shard_map/ppermute | solution.py:159
  186.6 25.4 %collective-permute-start.28 = (bf16[2,128,768]{2,1,0:T(8,128)(2,1)S(1)}, bf16[2,128,768]{2,1,0:T(8,128)(2,1)S(1)}, u32[]{:S(2)}, u32[]{:S(2)}) collective-permute-start(bf16[2,128,768]{2,1,0:T(8,128)(2,1)S(1)} %get-tuple-element.50), channel_id=1, source_target_pairs={{0,384},{32,416},{64,448},{96,480},{128,0},{160,32},{192,64},{224,... | collective-permute-start | bytes 1179656 | tf_op jit(solution)/shard_map/ppermute | solution.py:159
  194.0 23.0 %collective-permute-start.21 = (bf16[128,768]{1,0:T(8,128)(2,1)S(1)}, bf16[128,768]{1,0:T(8,128)(2,1)S(1)}, u32[]{:S(2)}, u32[]{:S(2)}) collective-permute-start(bf16[128,768]{1,0:T(8,128)(2,1)S(1)} %fusion.6), channel_id=1, source_target_pairs={{0,64},{32,96},{64,0},{96,32},{128,192},{160,224},{192,128},{224,1... | collective-permute-start | bytes 589832 | tf_op jit(solution)/shard_map/ppermute | solution.py:159
  198.8 19.0 %collective-permute-start.25 = (bf16[128,768]{1,0:T(8,128)(2,1)S(1)}, bf16[128,768]{1,0:T(8,128)(2,1)S(1)}, u32[]{:S(2)}, u32[]{:S(2)}) collective-permute-start(bf16[128,768]{1,0:T(8,128)(2,1)S(1)} %fusion.7), channel_id=1, source_target_pairs={{0,64},{32,96},{64,0},{96,32},{128,192},{160,224},{192,128},{224,1... | collective-permute-start | bytes 589832 | tf_op jit(solution)/shard_map/ppermute | solution.py:159
  212.3 25.3 %copy-start.6 = (bf16[256,128]{1,0:T(8,128)(2,1)S(1)}, bf16[256,128]{1,0:T(8,128)(2,1)}, u32[]{:S(2)}) copy-start(bf16[256,128]{1,0:T(8,128)(2,1)} %get-tuple-element.28.pick_ref) | copy-start | bytes 196612
  212.3 25.3 %copy-start.7 = (s32[128,1]{0,1:T(1,128)S(1)}, s32[128,1]{0,1:T(1,128)}, u32[]{:S(2)}) copy-start(s32[128,1]{0,1:T(1,128)} %param.9) | copy-start | bytes 1540
  212.3 8.7 %collective-permute-start.29 = (bf16[128,768]{1,0:T(8,128)(2,1)S(1)}, bf16[128,768]{1,0:T(8,128)(2,1)S(1)}, u32[]{:S(2)}, u32[]{:S(2)}) collective-permute-start(bf16[128,768]{1,0:T(8,128)(2,1)S(1)} %fusion.8), channel_id=1, source_target_pairs={{0,64},{32,96},{64,0},{96,32},{128,192},{160,224},{192,128},{224,1... | collective-permute-start | bytes 589832 | tf_op jit(solution)/shard_map/ppermute | solution.py:159

commit v4 on v3

--- a/solution.py
+++ b/solution.py
@@ -50,50 +50,102 @@
         send_ref[:, pl.ds(width + c * step, step)] = mm(pick, rows, NN).astype(BF)
 
 
-def expert_kernel(order_ref, rows_ref, *refs):
+def expert_kernel(order_ref, *refs):
     pairs = order_ref.shape[0] - 1
-    send_ref, hid_ref, dpre_ref, dlin_ref, shards, sems = refs[2 * pairs :]
+    rows_in, shards_in = refs[0], refs[1 : 1 + 2 * pairs]
+    send_out, *mids_out = refs[1 + 2 * pairs : 5 + 2 * pairs]
+    rows, shards, send, hid, dpre, dlin, in_sems, out_sems = refs[5 + 2 * pairs :]
     block, units = shards.shape[2:]
-    width = rows_ref.shape[1] // 2
-    copies = [pltpu.make_async_copy(refs[n], shards.at[n], sems.at[n]) for n in range(2 * pairs)]
-    for copy in copies:
-        copy.start()
+    width = rows.shape[1] // 2
     core = order_ref[pairs]
+    halves = [pl.ds(0, width), pl.ds(width, width)]
+
+    loads = [
+        pltpu.make_async_copy(rows_in.at[:, h], rows.at[:, h], in_sems.at[n])
+        for n, h in enumerate(halves)
+    ]
+    loads += [
+        pltpu.make_async_copy(shards_in[n], shards.at[n], in_sems.at[2 + n])
+        for n in range(2 * pairs)
+    ]
+    for n in (0, 2, 3, 1, *range(4, 2 + 2 * pairs)):
+        loads[n].start()
+    stores = []
+
+    def store(source, target):
+        stores.append(pltpu.make_async_copy(source, target, out_sems.at[len(stores)]))
+        stores[-1].start()
 
     def spots(p, first):
         at = order_ref[p] * 2
         return [pl.ds(pl.multiple_of(first + (at + c) * block, block), block) for c in (core, 1 - core)]
 
     def left(p, first):
-        return jnp.concatenate([rows_ref[:, s] for s in spots(p, first)], axis=1)
+        return jnp.concatenate([rows[:, s] for s in spots(p, first)], axis=1)
 
     def right(p, m, cols):
         return jnp.concatenate([shards[n, m, :, cols] for n in (2 * p, 2 * p + 1)], axis=0)
 
-    step = 256
-    for n in range(units // step):
-        cols = pl.ds(n * step, step)
-        pre, lin, dhid = 0.0, 0.0, 0.0
+    every = pl.ds(0, units)
+    pre, lin, dhid = 0.0, 0.0, 0.0
+    loads[0].wait()
+    for p in range(pairs):
+        loads[2 + 2 * p].wait()
+        loads[3 + 2 * p].wait()
+        x = left(p, 0)
+        pre = pre + mm(x, right(p, 0, every), NN)
+        lin = lin + mm(x, right(p, 1, every), NN)
+        if p == 0:
+            loads[1].wait()
+        dhid = dhid + mm(left(p, width), right(p, 2, every), NN)
+    sig = jax.nn.sigmoid(pre)
+    active = pre * sig
+    hid[...] = (active * lin).astype(BF)
+    dpre[...] = (dhid * lin * sig * (1.0 + pre * (1.0 - sig))).astype(BF)
+    dlin[...] = (dhid * active).astype(BF)
+    for source, target in zip((hid, dpre, dlin), mids_out):
+        store(source, target)
+    for h, half in enumerate(halves):
         for p in range(pairs):
-            if n == 0:
-                copies[2 * p].wait()
-                copies[2 * p + 1].wait()
-            x, g = left(p, 0), left(p, width)
-            pre = pre + mm(x, right(p, 0, cols), NN)
-            lin = lin + mm(x, right(p, 1, cols), NN)
-            dhid = dhid + mm(g, right(p, 2, cols), NN)
-        sig = jax.nn.sigmoid(pre)
-        active = pre * sig
-        hid_ref[:, cols] = (active * lin).astype(BF)
-        dpre_ref[:, cols] = (dhid * lin * sig * (1.0 + pre * (1.0 - sig))).astype(BF)
-        dlin_ref[:, cols] = (dhid * active).astype(BF)
-    every = pl.ds(0, units)
-    for p in range(pairs):
-        out = mm(hid_ref[...], right(p, 2, every), NT)
-        back = mm(dpre_ref[...], right(p, 0, every), NT) + mm(dlin_ref[...], right(p, 1, every), NT)
-        for first, value in ((0, out.astype(BF)), (width, back.astype(BF))):
-            for n, s in enumerate(spots(p, first)):
-                send_ref[:, s] = value[:, n * block : (n + 1) * block]
+            if h == 0:
+                value = mm(hid[...], right(p, 2, every), NT)
+            else:
+                value = mm(dpre[...], right(p, 0, every), NT) + mm(dlin[...], right(p, 1, every), NT)
+            value = value.astype(BF)
+            for n, s in enumerate(spots(p, h * width)):
+                send[:, s] = value[:, n * block : (n + 1) * block]
+        store(send.at[:, half], send_out.at[:, half])
+    for copy in stores:
+        copy.wait()
+
+
+def experts_call(order, rows, shards):
+    slots, both = rows.shape
+    block, units = shards[0].shape[1:]
+    count = len(shards)
+    shape = jax.ShapeDtypeStruct
+    outs = [shape((slots, both), BF)] + [shape((slots, units), BF)] * 3
+    anywhere = pl.BlockSpec(memory_space=pl.ANY)
+    return pl.pallas_call(
+        expert_kernel,
+        in_specs=[pl.BlockSpec(memory_space=pltpu.SMEM)] + [anywhere] * (1 + count),
+        out_specs=[anywhere] * 4,
+        out_shape=outs,
+        scratch_shapes=[
+            VM((slots, both), BF),
+            VM((count, 3, block, units), BF),
+            VM((slots, both), BF),
+            *[VM((slots, units), BF)] * 3,
+            pltpu.SemaphoreType.DMA((2 + count,)),
+            pltpu.SemaphoreType.DMA((5,)),
+        ],
+        compiler_params=params(56),
+        cost_estimate=pl.CostEstimate(
+            flops=6 * slots * both * units,
+            bytes_accessed=4 * slots * both + 6 * count * block * units,
+            transcendentals=slots * units,
+        ),
+    )(order, rows, *shards)
 
 
 def grad_kernel(groups, added, order_ref, rows_ref, dpre_ref, dlin_ref, hid_ref, *refs):
@@ -125,10 +177,9 @@
         back_ref[:, part] = mm(pick_ref[...], got_ref[:, other], TN).astype(BF)
 
 
-def call(kernel, outs, mib, flops, args, smem=0, left=0, scratch=()):
+def call(kernel, outs, mib, flops, args, smem=0):
     in_specs = [pl.BlockSpec(memory_space=pltpu.SMEM)] * smem
-    in_specs += [pl.BlockSpec(memory_space=VM)] * (len(args) - smem - left)
-    in_specs += [pl.BlockSpec(memory_space=pl.ANY)] * left
+    in_specs += [pl.BlockSpec(memory_space=VM)] * (len(args) - smem)
     moved = sum(a.size * a.dtype.itemsize for a in args)
     moved += sum(o.size * o.dtype.itemsize for o in outs)
     return pl.pallas_call(
@@ -136,7 +187,6 @@
         out_shape=outs,
         in_specs=in_specs,
         out_specs=[pl.BlockSpec(memory_space=VM)] * len(outs),
-        scratch_shapes=scratch,
         compiler_params=params(mib),
         cost_estimate=pl.CostEstimate(flops=flops, bytes_accessed=moved, transcendentals=0),
     )(*args)
@@ -183,17 +233,7 @@
         return got.reshape(slots, 2 * width)
 
     rows = exchange(send)
-    small = shape((slots, units), BF)
-    answer, hidden, d_pre, d_lin = call(
-        expert_kernel,
-        [shape((slots, 2 * width), BF), small, small, small],
-        56,
-        12 * slots * width * units,
-        (source, rows, *shards),
-        smem=1,
-        left=len(shards),
-        scratch=[VM((len(shards), 3, block, units), BF), pltpu.SemaphoreType.DMA((len(shards),))],
-    )
+    answer, hidden, d_pre, d_lin = experts_call(source, rows, shards)
     got = exchange(answer)
 
     place = ((x + (k >> 1)) & 3) * 4 + (far ^ (k & 1)) * 2
@@ -202,7 +242,7 @@
     away = call(
         lambda *refs: grad_kernel((8,), False, *refs),
         [partial] * 3,
-        24,
+        56,
         flops,
         (place + (1 - core), rows, d_pre, d_lin, hidden),
         smem=1,
@@ -212,7 +252,7 @@
     sums = call(
         lambda *refs: grad_kernel((2, 2, 2, 2), True, *refs),
         [pair] * 12,
-        32,
+        56,
         flops,
         (place + core, rows, d_pre, d_lin, hidden, *extra),
         smem=1,

time: 240 us -> 239 us (level)
  waiting for transfers between devices: 81 us -> 70.9 us
  Pallas kernels: 21.1 us -> 26.8 us
    pallas_call x0 -> x1, Pallas kernels: none -> 10.6 us  [experts_call(): pl.pallas_call(expert_kernel, in_specs=[pl.BlockSpec(memory_space=pltpu.S...]
    all_to_all x2, waiting for transfers between devices: 41.8 us -> 34.6 us  [exchange(): got = lax.all_to_all(cut, 'expert', split_axis=0, concat_axis=0, tiled=True)]
    pallas_call x5 -> x4, Pallas kernels: 21.1 us -> 16.2 us  [call(): pl.pallas_call(kernel, out_shape=outs, in_specs=in_specs, out_specs=[pl.B...]
    ppermute x30, waiting for transfers between devices: 39.2 us -> 36.2 us  [permute(): return lax.ppermute(a, 'dp', [(i, to(i)) for i in range(groups)])]
  transfers between devices with their start and end apart: 32 -> 32, of which waited for: 15 -> 15; matrix products, arithmetic and copies ran while one was open for 2% -> 2% of each run, Pallas kernels for 2% -> 5%
where the time goes in v4:
time: 239 us; the launch traced here: 237 us
  starting transfers between devices  130 us (54%)
  waiting for transfers between devices  70.9 us (30%)
  Pallas kernels  26.8 us (11%)
  other arithmetic  5.58 us (2%)
  local copies, waits for them, and re-layouts  2.81 us (1%)
    ppermute x30, starting transfers between devices, permute(): return lax.ppermute(a, 'dp', [(i, to(i)) for i in range(groups)])  110 us
    ppermute x30, waiting for transfers between devices, permute(): return lax.ppermute(a, 'dp', [(i, to(i)) for i in range(groups)])  36.2 us
    all_to_all x2, waiting for transfers between devices, exchange(): got = lax.all_to_all(cut, 'expert', split_axis=0, concat_axis=0, tiled=True)  34.6 us
    all_to_all x2, starting transfers between devices, exchange(): got = lax.all_to_all(cut, 'expert', split_axis=0, concat_axis=0, tiled=True)  19.8 us
    pallas_call x4, Pallas kernels, call(): pl.pallas_call(kernel, out_shape=outs, in_specs=in_specs, out_specs=[pl.B...  16.2 us
    pallas_call x1, Pallas kernels, experts_call(): pl.pallas_call(expert_kernel, in_specs=[pl.BlockSpec(memory_space=pltpu.S...  10.6 us
  transfers between devices with their start and end apart: 32, of which 15 were waited for; matrix products, arithmetic and copies ran while one was open for 2% of the time, Pallas kernels for 5%

profile of v4, /device:TPU:33, one launch (start us, length us, event | category | flops | bytes accessed | tf_op | source)
XLA Modules:
  0.0 237.4 jit_solution(3565950103559612183)
XLA Ops:
  0.6 3.4 %shard_map.110 = (bf16[256,4096]{1,0:T(8,128)(2,1)}, bf16[256,128]{1,0:T(8,128)(2,1)}) custom-call(s32[1,128]{1,0:T(1,128)} %bitcast.45, s32[1,128]{1,0:T(1,128)} %bitcast.38, bf16[128,2048]{1,0:T(8,128)(2,1)} %refs_2_.1, bf16[128,2048]{1,0:T(8,128)(2,1)} %refs_3_.1), custom_call_target="tpu_custom_call" | custom-call | flops 268435456 | bytes 3212288 | tf_op jit(solution)/shard_map/pallas_call | solution.py:185
  4.1 15.9 %all-to-all-start = ((bf16[32,8,4096]{2,1,0:T(8,128)(2,1)}), bf16[32,8,4096]{2,1,0:T(8,128)(2,1)S(1)}, u32[]{:S(2)}, u32[]{:S(2)}) async-start(bf16[32,8,4096]{2,1,0:T(8,128)(2,1)} %bitcast.44), calls=%async_computation | async-start | bytes 4194304 | tf_op jit(solution)/shard_map/all_to_all | solution.py:232
  20.1 4.5 %collective-permute-start.7 = (bf16[3,128,768]{2,1,0:T(8,128)(2,1)S(1)}, bf16[3,128,768]{2,1,0:T(8,128)(2,1)S(1)}, u32[]{:S(2)}, u32[]{:S(2)}) collective-permute-start(bf16[3,128,768]{2,1,0:T(8,128)(2,1)S(1)} %constant_dynamic-update-slice_fusion.refs_1_), channel_id=1, source_target_pairs={{0,64},{32,96},{64,0},{96,32},{128,192},{160,224},{192,128},{224,1... | collective-permute-start | bytes 1769480 | tf_op jit(solution)/shard_map/ppermute | solution.py:209
  24.7 4.4 %collective-permute-start.5 = (bf16[3,128,768]{2,1,0:T(8,128)(2,1)S(1)}, bf16[3,128,768]{2,1,0:T(8,128)(2,1)S(1)}, u32[]{:S(2)}, u32[]{:S(2)}) collective-permute-start(bf16[3,128,768]{2,1,0:T(8,128)(2,1)S(1)} %constant_dynamic-update-slice_fusion.refs_1_), channel_id=1, source_target_pairs={{0,384},{32,416},{64,448},{96,480},{128,0},{160,32},{192,64},{224,... | collective-permute-start | bytes 1769480 | tf_op jit(solution)/shard_map/ppermute | solution.py:209
  29.1 2.4 %collective-permute-start.3 = (bf16[3,128,768]{2,1,0:T(8,128)(2,1)S(1)}, bf16[3,128,768]{2,1,0:T(8,128)(2,1)}, u32[]{:S(2)}, u32[]{:S(2)}) collective-permute-start(bf16[3,128,768]{2,1,0:T(8,128)(2,1)S(1)} %constant_dynamic-update-slice_fusion.refs_1_), channel_id=1, source_target_pairs={{0,256},{32,288},{64,320},{96,352},{128,384},{160,416},{192,448},{... | collective-permute-start | bytes 1769480 | tf_op jit(solution)/shard_map/ppermute | solution.py:209
  31.5 2.5 %collective-permute-start.1 = (bf16[3,128,768]{2,1,0:T(8,128)(2,1)S(1)}, bf16[3,128,768]{2,1,0:T(8,128)(2,1)}, u32[]{:S(2)}, u32[]{:S(2)}) collective-permute-start(bf16[3,128,768]{2,1,0:T(8,128)(2,1)S(1)} %constant_dynamic-update-slice_fusion.refs_1_), channel_id=1, source_target_pairs={{0,128},{32,160},{64,192},{96,224},{128,256},{160,288},{192,320},{... | collective-permute-start | bytes 1769480 | tf_op jit(solution)/shard_map/ppermute | solution.py:209
  34.0 4.3 %collective-permute-start = (bf16[3,128,768]{2,1,0:T(8,128)(2,1)S(1)}, bf16[3,128,768]{2,1,0:T(8,128)(2,1)S(1)}, u32[]{:S(2)}, u32[]{:S(2)}) collective-permute-start(bf16[3,128,768]{2,1,0:T(8,128)(2,1)S(1)} %constant_dynamic-update-slice_fusion.refs_1_), channel_id=1, source_target_pairs={{0,32},{32,0},{64,96},{96,64},{128,160},{160,128},{192,224},{224,1... | collective-permute-start | bytes 1769480 | tf_op jit(solution)/shard_map/ppermute | solution.py:209
  38.3 1.7 collective-permute-done.7.refs_9_
  40.0 4.3 %collective-permute-start.13 = (bf16[3,128,768]{2,1,0:T(8,128)(2,1)S(1)}, bf16[3,128,768]{2,1,0:T(8,128)(2,1)}, u32[]{:S(2)}, u32[]{:S(2)}) collective-permute-start(bf16[3,128,768]{2,1,0:T(8,128)(2,1)S(1)} %collective-permute-done.7.refs_9_), channel_id=1, source_target_pairs={{0,384},{32,416},{64,448},{96,480},{128,0},{160,32},{192,64},{224,... | collective-permute-start | bytes 1769480 | tf_op jit(solution)/shard_map/ppermute | solution.py:209
  44.3 2.5 %collective-permute-start.11 = (bf16[3,128,768]{2,1,0:T(8,128)(2,1)S(1)}, bf16[3,128,768]{2,1,0:T(8,128)(2,1)}, u32[]{:S(2)}, u32[]{:S(2)}) collective-permute-start(bf16[3,128,768]{2,1,0:T(8,128)(2,1)S(1)} %collective-permute-done.7.refs_9_), channel_id=1, source_target_pairs={{0,256},{32,288},{64,320},{96,352},{128,384},{160,416},{192,448},{... | collective-permute-start | bytes 1769480 | tf_op jit(solution)/shard_map/ppermute | solution.py:209
  46.7 10.0 %collective-permute-start.9 = (bf16[3,128,768]{2,1,0:T(8,128)(2,1)S(1)}, bf16[3,128,768]{2,1,0:T(8,128)(2,1)}, u32[]{:S(2)}, u32[]{:S(2)}) collective-permute-start(bf16[3,128,768]{2,1,0:T(8,128)(2,1)S(1)} %collective-permute-done.7.refs_9_), channel_id=1, source_target_pairs={{0,128},{32,160},{64,192},{96,224},{128,256},{160,288},{192,320},{... | collective-permute-start | bytes 1769480 | tf_op jit(solution)/shard_map/ppermute | solution.py:209
  56.7 5.9 %collective-permute-done.1.refs_3_ = bf16[3,128,768]{2,1,0:T(8,128)(2,1)} collective-permute-done((bf16[3,128,768]{2,1,0:T(8,128)(2,1)S(1)}, bf16[3,128,768]{2,1,0:T(8,128)(2,1)}, u32[]{:S(2)}, u32[]{:S(2)}) %collective-permute-start.1) | collective-permute-done | bytes 589856 | tf_op jit(solution)/shard_map/ppermute | solution.py:209
  62.6 4.0 %collective-permute-start.8 = (bf16[3,128,768]{2,1,0:T(8,128)(2,1)S(1)}, bf16[3,128,768]{2,1,0:T(8,128)(2,1)S(1)}, u32[]{:S(2)}, u32[]{:S(2)}) collective-permute-start(bf16[3,128,768]{2,1,0:T(8,128)(2,1)S(1)} %collective-permute-done.7.refs_9_), channel_id=1, source_target_pairs={{0,32},{32,0},{64,96},{96,64},{128,160},{160,128},{192,224},{224,1... | collective-permute-start | bytes 1769480 | tf_op jit(solution)/shard_map/ppermute | solution.py:209
  66.7 1.9 collective-permute-start.6
  68.6 13.8 %collective-permute-start.4 = (bf16[3,128,768]{2,1,0:T(8,128)(2,1)}, bf16[3,128,768]{2,1,0:T(8,128)(2,1)}, u32[]{:S(2)}, u32[]{:S(2)}) collective-permute-start(bf16[3,128,768]{2,1,0:T(8,128)(2,1)} %collective-permute-done.3.refs_5_), channel_id=1, source_target_pairs={{0,32},{32,0},{64,96},{96,64},{128,160},{160,128},{192,224},{224,1... | collective-permute-start | bytes 1769480 | tf_op jit(solution)/shard_map/ppermute | solution.py:209
  82.5 1.9 collective-permute-start.2
  84.4 1.2 collective-permute-done.9.refs_11_
  85.6 2.5 %collective-permute-start.14 = (bf16[3,128,768]{2,1,0:T(8,128)(2,1)}, bf16[3,128,768]{2,1,0:T(8,128)(2,1)}, u32[]{:S(2)}, u32[]{:S(2)}) collective-permute-start(bf16[3,128,768]{2,1,0:T(8,128)(2,1)} %collective-permute-done.13.refs_15_), channel_id=1, source_target_pairs={{0,32},{32,0},{64,96},{96,64},{128,160},{160,128},{192,224},{224,1... | collective-permute-start | bytes 1769480 | tf_op jit(solution)/shard_map/ppermute | solution.py:209
  88.2 1.9 collective-permute-start.12
  90.1 2.4 %collective-permute-start.10 = (bf16[3,128,768]{2,1,0:T(8,128)(2,1)}, bf16[3,128,768]{2,1,0:T(8,128)(2,1)}, u32[]{:S(2)}, u32[]{:S(2)}) collective-permute-start(bf16[3,128,768]{2,1,0:T(8,128)(2,1)} %collective-permute-done.9.refs_11_), channel_id=1, source_target_pairs={{0,32},{32,0},{64,96},{96,64},{128,160},{160,128},{192,224},{224,1... | collective-permute-start | bytes 1769480 | tf_op jit(solution)/shard_map/ppermute | solution.py:209
  92.6 0.5 xor_add_fusion
  93.1 0.6 pad_add_fusion.order_ref
  93.7 0.8 collective-permute-done.10.refs_12_
  94.5 26.0 %all-to-all-done = bf16[32,8,4096]{2,1,0:T(8,128)(2,1)S(1)} async-done(((bf16[32,8,4096]{2,1,0:T(8,128)(2,1)}), bf16[32,8,4096]{2,1,0:T(8,128)(2,1)S(1)}, u32[]{:S(2)}, u32[]{:S(2)}) %all-to-all-start) | async-done | bytes 2097184 | tf_op jit(solution)/shard_map/all_to_all | solution.py:232
  120.6 1.4 copy-done.2
  121.9 10.6 %shard_map.111 = (bf16[256,4096]{1,0:T(8,128)(2,1)}, bf16[256,768]{1,0:T(8,128)(2,1)}, bf16[256,768]{1,0:T(8,128)(2,1)}, bf16[256,768]{1,0:T(8,128)(2,1)}) custom-call(s32[9]{0:T(128)} %pad_add_fusion.order_ref, bf16[256,4096]{1,0:T(8,128)(2,1)} %bitcast.40, bf16[3,128,768]{2,1,0:T(8,128)(2,1)} %copy-done.11, bf16[3,128,768]{2,1,0:T(8,128)(2,1)} %copy-done.14, ...), custom_call_target="tpu_custom_call" | custom-call | flops 4831838208 | bytes 13631488 | tf_op jit(solution)/shard_map/pallas_call | solution.py:129
  132.5 3.8 %all-to-all-start.1 = ((bf16[32,8,4096]{2,1,0:T(8,128)(2,1)}), bf16[32,8,4096]{2,1,0:T(8,128)(2,1)S(1)}, u32[]{:S(2)}, u32[]{:S(2)}) async-start(bf16[32,8,4096]{2,1,0:T(8,128)(2,1)} %bitcast.43), calls=%async_computation.1 | async-start | bytes 4194304 | tf_op jit(solution)/shard_map/all_to_all | solution.py:232
  136.3 4.8 %shard_map.113 = (bf16[8,128,768]{2,1,0:T(8,128)(2,1)}, bf16[8,128,768]{2,1,0:T(8,128)(2,1)}, bf16[8,128,768]{2,1,0:T(8,128)(2,1)}) custom-call(s32[8]{0:T(128)} %get-tuple-element.52.refs_0_, bf16[256,4096]{1,0:T(8,128)(2,1)} %bitcast.41, bf16[256,768]{1,0:T(8,128)(2,1)} %get-tuple-element.33.refs_2_, bf16[256,768]{1,0:T(8,128)(2,1)} %get-tuple-element.34.refs_3_, ...), custom_call_target="tpu_custom_call" | custom-call | flops 1207959552 | bytes 7995424 | tf_op jit(solution)/shard_map/pallas_call | solution.py:185
  141.1 2.7 %collective-permute-start.15 = (bf16[8,128,768]{2,1,0:T(8,128)(2,1)}, bf16[8,128,768]{2,1,0:T(8,128)(2,1)S(1)}, u32[]{:S(2)}, u32[]{:S(2)}) collective-permute-start(bf16[8,128,768]{2,1,0:T(8,128)(2,1)} %get-tuple-element.36), channel_id=1, source_target_pairs={{0,32},{32,0},{64,96},{96,64},{128,160},{160,128},{192,224},{224,1... | collective-permute-start | bytes 4718600 | tf_op jit(solution)/shard_map/ppermute | solution.py:209
  143.8 1.9 collective-permute-start.16
  145.7 2.6 %collective-permute-start.17 = (bf16[8,128,768]{2,1,0:T(8,128)(2,1)}, bf16[8,128,768]{2,1,0:T(8,128)(2,1)S(1)}, u32[]{:S(2)}, u32[]{:S(2)}) collective-permute-start(bf16[8,128,768]{2,1,0:T(8,128)(2,1)} %get-tuple-element.38), channel_id=1, source_target_pairs={{0,32},{32,0},{64,96},{96,64},{128,160},{160,128},{192,224},{224,1... | collective-permute-start | bytes 4718600 | tf_op jit(solution)/shard_map/ppermute | solution.py:209
  148.3 0.6 broadcast_add_fusion.1.refs_0_
  148.9 0.4 collective-permute-done.16.refs_6_
  149.3 2.2 collective-permute-done.17.refs_7_
  151.6 1.3 copy-done.5
  152.9 6.5 %shard_map.114 = (bf16[2,128,768]{2,1,0:T(8,128)(2,1)}, bf16[2,128,768]{2,1,0:T(8,128)(2,1)}, bf16[2,128,768]{2,1,0:T(8,128)(2,1)}, bf16[2,128,768]{2,1,0:T(8,12...) custom-call(s32[8]{0:T(128)} %broadcast_add_fusion.1.refs_0_, ...), custom_call_target="tpu_custom_call" | custom-call | flops 1207959552 | bytes 12714016 | tf_op jit(solution)/shard_map/pallas_call | solution.py:185
  159.4 3.3 %collective-permute-start.18 = (bf16[2,128,768]{2,1,0:T(8,128)(2,1)}, bf16[2,128,768]{2,1,0:T(8,128)(2,1)S(1)}, u32[]{:S(2)}, u32[]{:S(2)}) collective-permute-start(bf16[2,128,768]{2,1,0:T(8,128)(2,1)} %get-tuple-element.40), channel_id=1, source_target_pairs={{0,128},{32,160},{64,192},{96,224},{128,256},{160,288},{192,320},{... | collective-permute-start | bytes 1179656 | tf_op jit(solution)/shard_map/ppermute | solution.py:209
  162.7 4.3 %collective-permute-start.19 = (bf16[2,128,768]{2,1,0:T(8,128)(2,1)}, bf16[2,128,768]{2,1,0:T(8,128)(2,1)S(1)}, u32[]{:S(2)}, u32[]{:S(2)}) collective-permute-start(bf16[2,128,768]{2,1,0:T(8,128)(2,1)} %get-tuple-element.41), channel_id=1, source_target_pairs={{0,256},{32,288},{64,320},{96,352},{128,384},{160,416},{192,448},{... | collective-permute-start | bytes 1179656 | tf_op jit(solution)/shard_map/ppermute | solution.py:209
  167.0 3.1 %collective-permute-start.20 = (bf16[2,128,768]{2,1,0:T(8,128)(2,1)}, bf16[2,128,768]{2,1,0:T(8,128)(2,1)S(1)}, u32[]{:S(2)}, u32[]{:S(2)}) collective-permute-start(bf16[2,128,768]{2,1,0:T(8,128)(2,1)} %get-tuple-element.42), channel_id=1, source_target_pairs={{0,384},{32,416},{64,448},{96,480},{128,0},{160,32},{192,64},{224,... | collective-permute-start | bytes 1179656 | tf_op jit(solution)/shard_map/ppermute | solution.py:209
  170.1 2.2 collective-permute-start.22
  172.3 2.8 %collective-permute-start.23 = (bf16[2,128,768]{2,1,0:T(8,128)(2,1)}, bf16[2,128,768]{2,1,0:T(8,128)(2,1)S(1)}, u32[]{:S(2)}, u32[]{:S(2)}) collective-permute-start(bf16[2,128,768]{2,1,0:T(8,128)(2,1)} %get-tuple-element.45), channel_id=1, source_target_pairs={{0,256},{32,288},{64,320},{96,352},{128,384},{160,416},{192,448},{... | collective-permute-start | bytes 1179656 | tf_op jit(solution)/shard_map/ppermute | solution.py:209
  175.1 3.4 %collective-permute-start.24 = (bf16[2,128,768]{2,1,0:T(8,128)(2,1)}, bf16[2,128,768]{2,1,0:T(8,128)(2,1)S(1)}, u32[]{:S(2)}, u32[]{:S(2)}) collective-permute-start(bf16[2,128,768]{2,1,0:T(8,128)(2,1)} %get-tuple-element.46), channel_id=1, source_target_pairs={{0,384},{32,416},{64,448},{96,480},{128,0},{160,32},{192,64},{224,... | collective-permute-start | bytes 1179656 | tf_op jit(solution)/shard_map/ppermute | solution.py:209
  178.5 4.1 %collective-permute-done.19 = bf16[2,128,768]{2,1,0:T(8,128)(2,1)S(1)} collective-permute-done((bf16[2,128,768]{2,1,0:T(8,128)(2,1)}, bf16[2,128,768]{2,1,0:T(8,128)(2,1)S(1)}, u32[]{:S(2)}, u32[]{:S(2)}) %collective-permute-start.19) | collective-permute-done | bytes 393248 | tf_op jit(solution)/shard_map/ppermute | solution.py:209
  182.7 1.9 collective-permute-start.26
  184.6 4.3 %collective-permute-start.27 = (bf16[2,128,768]{2,1,0:T(8,128)(2,1)}, bf16[2,128,768]{2,1,0:T(8,128)(2,1)S(1)}, u32[]{:S(2)}, u32[]{:S(2)}) collective-permute-start(bf16[2,128,768]{2,1,0:T(8,128)(2,1)} %get-tuple-element.49), channel_id=1, source_target_pairs={{0,256},{32,288},{64,320},{96,352},{128,384},{160,416},{192,448},{... | collective-permute-start | bytes 1179656 | tf_op jit(solution)/shard_map/ppermute | solution.py:209
  188.9 1.2 convert_add_fusion.2
  190.2 2.1 collective-permute-done.22
  192.3 3.1 %collective-permute-start.28 = (bf16[2,128,768]{2,1,0:T(8,128)(2,1)S(1)}, bf16[2,128,768]{2,1,0:T(8,128)(2,1)S(1)}, u32[]{:S(2)}, u32[]{:S(2)}) collective-permute-start(bf16[2,128,768]{2,1,0:T(8,128)(2,1)S(1)} %copy-done.17), channel_id=1, source_target_pairs={{0,384},{32,416},{64,448},{96,480},{128,0},{160,32},{192,64},{224,... | collective-permute-start | bytes 1179656 | tf_op jit(solution)/shard_map/ppermute | solution.py:209
  195.4 4.1 %collective-permute-done.23 = bf16[2,128,768]{2,1,0:T(8,128)(2,1)S(1)} collective-permute-done((bf16[2,128,768]{2,1,0:T(8,128)(2,1)}, bf16[2,128,768]{2,1,0:T(8,128)(2,1)S(1)}, u32[]{:S(2)}, u32[]{:S(2)}) %collective-permute-start.23) | collective-permute-done | bytes 393248 | tf_op jit(solution)/shard_map/ppermute | solution.py:209
  199.6 4.5 %collective-permute-start.21 = (bf16[128,768]{1,0:T(8,128)(2,1)S(1)}, bf16[128,768]{1,0:T(8,128)(2,1)S(1)}, u32[]{:S(2)}, u32[]{:S(2)}) collective-permute-start(bf16[128,768]{1,0:T(8,128)(2,1)S(1)} %fusion.6), channel_id=1, source_target_pairs={{0,64},{32,96},{64,0},{96,32},{128,192},{160,224},{192,128},{224,1... | collective-permute-start | bytes 589832 | tf_op jit(solution)/shard_map/ppermute | solution.py:209
  204.1 0.2 convert_add_fusion.1
  204.3 2.3 collective-permute-start.25
  206.6 2.5 %collective-permute-done.26 = bf16[2,128,768]{2,1,0:T(8,128)(2,1)S(1)} collective-permute-done((bf16[2,128,768]{2,1,0:T(8,128)(2,1)}, bf16[2,128,768]{2,1,0:T(8,128)(2,1)S(1)}, u32[]{:S(2)}, u32[]{:S(2)}) %collective-permute-start.26) | collective-permute-done | bytes 393248 | tf_op jit(solution)/shard_map/ppermute | solution.py:209
  209.1 7.3 %collective-permute-done.27 = bf16[2,128,768]{2,1,0:T(8,128)(2,1)S(1)} collective-permute-done((bf16[2,128,768]{2,1,0:T(8,128)(2,1)}, bf16[2,128,768]{2,1,0:T(8,128)(2,1)S(1)}, u32[]{:S(2)}, u32[]{:S(2)}) %collective-permute-start.27) | collective-permute-done | bytes 393248 | tf_op jit(solution)/shard_map/ppermute | solution.py:209
  216.4 1.2 collective-permute-done.28
  217.7 0.2 convert_add_fusion
  217.9 0.0 copy-start.1
  217.9 4.7 %collective-permute-start.29 = (bf16[128,768]{1,0:T(8,128)(2,1)S(1)}, bf16[128,768]{1,0:T(8,128)(2,1)S(1)}, u32[]{:S(2)}, u32[]{:S(2)}) collective-permute-start(bf16[128,768]{1,0:T(8,128)(2,1)S(1)} %fusion.8), channel_id=1, source_target_pairs={{0,64},{32,96},{64,0},{96,32},{128,192},{160,224},{192,128},{224,1... | collective-permute-start | bytes 589832 | tf_op jit(solution)/shard_map/ppermute | solution.py:209
  222.6 0.8 fusion.5
  223.4 0.8 fusion.3
  224.1 2.4 %collective-permute-done.29 = bf16[128,768]{1,0:T(8,128)(2,1)S(1)} collective-permute-done((bf16[128,768]{1,0:T(8,128)(2,1)S(1)}, bf16[128,768]{1,0:T(8,128)(2,1)S(1)}, u32[]{:S(2)}, u32[]{:S(2)}) %collective-permute-start.29) | collective-permute-done | bytes 196640 | tf_op jit(solution)/shard_map/ppermute | solution.py:209
  226.5 0.8 fusion.1
  227.3 8.6 %all-to-all-done.1 = bf16[32,8,4096]{2,1,0:T(8,128)(2,1)S(1)} async-done(((bf16[32,8,4096]{2,1,0:T(8,128)(2,1)}), bf16[32,8,4096]{2,1,0:T(8,128)(2,1)S(1)}, u32[]{:S(2)}, u32[]{:S(2)}) %all-to-all-start.1) | async-done | bytes 2097184 | tf_op jit(solution)/shard_map/all_to_all | solution.py:232
  235.9 1.4 shard_map.112
  (56 shorter events, 0.2 us)
Async XLA Ops:
  4.1 16.0 %copy-start.8 = (bf16[1,128,768]{2,1,0:T(8,128)(2,1)S(1)}, bf16[1,128,768]{2,1,0:T(8,128)(2,1)}, u32[]{:S(2)}) copy-start(bf16[1,128,768]{2,1,0:T(8,128)(2,1)} %param.11) | copy-start | bytes 589828
  4.1 16.0 %copy-start.9 = (bf16[1,128,768]{2,1,0:T(8,128)(2,1)S(1)}, bf16[1,128,768]{2,1,0:T(8,128)(2,1)}, u32[]{:S(2)}) copy-start(bf16[1,128,768]{2,1,0:T(8,128)(2,1)} %param.12) | copy-start | bytes 589828
  4.1 16.0 %copy-start.10 = (bf16[1,128,768]{2,1,0:T(8,128)(2,1)S(1)}, bf16[1,128,768]{2,1,0:T(8,128)(2,1)}, u32[]{:S(2)}) copy-start(bf16[1,128,768]{2,1,0:T(8,128)(2,1)} %param.13) | copy-start | bytes 589828
  4.1 116.5 %all-to-all-start = ((bf16[32,8,4096]{2,1,0:T(8,128)(2,1)}), bf16[32,8,4096]{2,1,0:T(8,128)(2,1)S(1)}, u32[]{:S(2)}, u32[]{:S(2)}) async-start(bf16[32,8,4096]{2,1,0:T(8,128)(2,1)} %bitcast.44), calls=%async_computation | async-start | bytes 4194304 | tf_op jit(solution)/shard_map/all_to_all | solution.py:232
  20.1 100.4 %copy-start.11 = (bf16[3,128,768]{2,1,0:T(8,128)(2,1)}, bf16[3,128,768]{2,1,0:T(8,128)(2,1)S(1)}, u32[]{:S(2)}) copy-start(bf16[3,128,768]{2,1,0:T(8,128)(2,1)S(1)} %constant_dynamic-update-slice_fusion.refs_1_) | copy-start | bytes 1769476
  20.1 19.8 %collective-permute-start.7 = (bf16[3,128,768]{2,1,0:T(8,128)(2,1)S(1)}, bf16[3,128,768]{2,1,0:T(8,128)(2,1)S(1)}, u32[]{:S(2)}, u32[]{:S(2)}) collective-permute-start(bf16[3,128,768]{2,1,0:T(8,128)(2,1)S(1)} %constant_dynamic-update-slice_fusion.refs_1_), channel_id=1, source_target_pairs={{0,64},{32,96},{64,0},{96,32},{128,192},{160,224},{192,128},{224,1... | collective-permute-start | bytes 1769480 | tf_op jit(solution)/shard_map/ppermute | solution.py:209
  24.7 19.6 %collective-permute-start.5 = (bf16[3,128,768]{2,1,0:T(8,128)(2,1)S(1)}, bf16[3,128,768]{2,1,0:T(8,128)(2,1)S(1)}, u32[]{:S(2)}, u32[]{:S(2)}) collective-permute-start(bf16[3,128,768]{2,1,0:T(8,128)(2,1)S(1)} %constant_dynamic-update-slice_fusion.refs_1_), channel_id=1, source_target_pairs={{0,384},{32,416},{64,448},{96,480},{128,0},{160,32},{192,64},{224,... | collective-permute-start | bytes 1769480 | tf_op jit(solution)/shard_map/ppermute | solution.py:209
  29.1 17.7 %collective-permute-start.3 = (bf16[3,128,768]{2,1,0:T(8,128)(2,1)S(1)}, bf16[3,128,768]{2,1,0:T(8,128)(2,1)}, u32[]{:S(2)}, u32[]{:S(2)}) collective-permute-start(bf16[3,128,768]{2,1,0:T(8,128)(2,1)S(1)} %constant_dynamic-update-slice_fusion.refs_1_), channel_id=1, source_target_pairs={{0,256},{32,288},{64,320},{96,352},{128,384},{160,416},{192,448},{... | collective-permute-start | bytes 1769480 | tf_op jit(solution)/shard_map/ppermute | solution.py:209
  31.5 31.1 %collective-permute-start.1 = (bf16[3,128,768]{2,1,0:T(8,128)(2,1)S(1)}, bf16[3,128,768]{2,1,0:T(8,128)(2,1)}, u32[]{:S(2)}, u32[]{:S(2)}) collective-permute-start(bf16[3,128,768]{2,1,0:T(8,128)(2,1)S(1)} %constant_dynamic-update-slice_fusion.refs_1_), channel_id=1, source_target_pairs={{0,128},{32,160},{64,192},{96,224},{128,256},{160,288},{192,320},{... | collective-permute-start | bytes 1769480 | tf_op jit(solution)/shard_map/ppermute | solution.py:209
  34.0 32.6 %collective-permute-start = (bf16[3,128,768]{2,1,0:T(8,128)(2,1)S(1)}, bf16[3,128,768]{2,1,0:T(8,128)(2,1)S(1)}, u32[]{:S(2)}, u32[]{:S(2)}) collective-permute-start(bf16[3,128,768]{2,1,0:T(8,128)(2,1)S(1)} %constant_dynamic-update-slice_fusion.refs_1_), channel_id=1, source_target_pairs={{0,32},{32,0},{64,96},{96,64},{128,160},{160,128},{192,224},{224,1... | collective-permute-start | bytes 1769480 | tf_op jit(solution)/shard_map/ppermute | solution.py:209
  40.0 80.6 %copy-start.12 = (bf16[3,128,768]{2,1,0:T(8,128)(2,1)}, bf16[3,128,768]{2,1,0:T(8,128)(2,1)S(1)}, u32[]{:S(2)}) copy-start(bf16[3,128,768]{2,1,0:T(8,128)(2,1)S(1)} %collective-permute-done.7.refs_9_) | copy-start | bytes 1769476
  40.0 28.6 %collective-permute-start.13 = (bf16[3,128,768]{2,1,0:T(8,128)(2,1)S(1)}, bf16[3,128,768]{2,1,0:T(8,128)(2,1)}, u32[]{:S(2)}, u32[]{:S(2)}) collective-permute-start(bf16[3,128,768]{2,1,0:T(8,128)(2,1)S(1)} %collective-permute-done.7.refs_9_), channel_id=1, source_target_pairs={{0,384},{32,416},{64,448},{96,480},{128,0},{160,32},{192,64},{224,... | collective-permute-start | bytes 1769480 | tf_op jit(solution)/shard_map/ppermute | solution.py:209
  44.3 43.9 %copy-start.13 = (bf16[3,128,768]{2,1,0:T(8,128)(2,1)}, bf16[3,128,768]{2,1,0:T(8,128)(2,1)S(1)}, u32[]{:S(2)}) copy-start(bf16[3,128,768]{2,1,0:T(8,128)(2,1)S(1)} %collective-permute-done.5.refs_7_) | copy-start | bytes 1769476
  44.3 38.2 %collective-permute-start.11 = (bf16[3,128,768]{2,1,0:T(8,128)(2,1)S(1)}, bf16[3,128,768]{2,1,0:T(8,128)(2,1)}, u32[]{:S(2)}, u32[]{:S(2)}) collective-permute-start(bf16[3,128,768]{2,1,0:T(8,128)(2,1)S(1)} %collective-permute-done.7.refs_9_), channel_id=1, source_target_pairs={{0,256},{32,288},{64,320},{96,352},{128,384},{160,416},{192,448},{... | collective-permute-start | bytes 1769480 | tf_op jit(solution)/shard_map/ppermute | solution.py:209
  46.7 38.9 %collective-permute-start.9 = (bf16[3,128,768]{2,1,0:T(8,128)(2,1)S(1)}, bf16[3,128,768]{2,1,0:T(8,128)(2,1)}, u32[]{:S(2)}, u32[]{:S(2)}) collective-permute-start(bf16[3,128,768]{2,1,0:T(8,128)(2,1)S(1)} %collective-permute-done.7.refs_9_), channel_id=1, source_target_pairs={{0,128},{32,160},{64,192},{96,224},{128,256},{160,288},{192,320},{... | collective-permute-start | bytes 1769480 | tf_op jit(solution)/shard_map/ppermute | solution.py:209
  62.6 25.5 %collective-permute-start.8 = (bf16[3,128,768]{2,1,0:T(8,128)(2,1)S(1)}, bf16[3,128,768]{2,1,0:T(8,128)(2,1)S(1)}, u32[]{:S(2)}, u32[]{:S(2)}) collective-permute-start(bf16[3,128,768]{2,1,0:T(8,128)(2,1)S(1)} %collective-permute-done.7.refs_9_), channel_id=1, source_target_pairs={{0,32},{32,0},{64,96},{96,64},{128,160},{160,128},{192,224},{224,1... | collective-permute-start | bytes 1769480 | tf_op jit(solution)/shard_map/ppermute | solution.py:209
  66.7 23.4 %copy-start.14 = (bf16[3,128,768]{2,1,0:T(8,128)(2,1)}, bf16[3,128,768]{2,1,0:T(8,128)(2,1)S(1)}, u32[]{:S(2)}) copy-start(bf16[3,128,768]{2,1,0:T(8,128)(2,1)S(1)} %collective-permute-done.refs_2_) | copy-start | bytes 1769476
  66.7 23.4 %collective-permute-start.6 = (bf16[3,128,768]{2,1,0:T(8,128)(2,1)S(1)}, bf16[3,128,768]{2,1,0:T(8,128)(2,1)S(1)}, u32[]{:S(2)}, u32[]{:S(2)}) collective-permute-start(bf16[3,128,768]{2,1,0:T(8,128)(2,1)S(1)} %collective-permute-done.5.refs_7_), channel_id=1, source_target_pairs={{0,32},{32,0},{64,96},{96,64},{128,160},{160,128},{192,224},{224,1... | collective-permute-start | bytes 1769480 | tf_op jit(solution)/shard_map/ppermute | solution.py:209
  68.6 25.0 %collective-permute-start.4 = (bf16[3,128,768]{2,1,0:T(8,128)(2,1)}, bf16[3,128,768]{2,1,0:T(8,128)(2,1)}, u32[]{:S(2)}, u32[]{:S(2)}) collective-permute-start(bf16[3,128,768]{2,1,0:T(8,128)(2,1)} %collective-permute-done.3.refs_5_), channel_id=1, source_target_pairs={{0,32},{32,0},{64,96},{96,64},{128,160},{160,128},{192,224},{224,1... | collective-permute-start | bytes 1769480 | tf_op jit(solution)/shard_map/ppermute | solution.py:209
  82.5 11.2 %collective-permute-start.2 = (bf16[3,128,768]{2,1,0:T(8,128)(2,1)}, bf16[3,128,768]{2,1,0:T(8,128)(2,1)}, u32[]{:S(2)}, u32[]{:S(2)}) collective-permute-start(bf16[3,128,768]{2,1,0:T(8,128)(2,1)} %collective-permute-done.1.refs_3_), channel_id=1, source_target_pairs={{0,32},{32,0},{64,96},{96,64},{128,160},{160,128},{192,224},{224,1... | collective-permute-start | bytes 1769480 | tf_op jit(solution)/shard_map/ppermute | solution.py:209
  85.6 8.0 %collective-permute-start.14 = (bf16[3,128,768]{2,1,0:T(8,128)(2,1)}, bf16[3,128,768]{2,1,0:T(8,128)(2,1)}, u32[]{:S(2)}, u32[]{:S(2)}) collective-permute-start(bf16[3,128,768]{2,1,0:T(8,128)(2,1)} %collective-permute-done.13.refs_15_), channel_id=1, source_target_pairs={{0,32},{32,0},{64,96},{96,64},{128,160},{160,128},{192,224},{224,1... | collective-permute-start | bytes 1769480 | tf_op jit(solution)/shard_map/ppermute | solution.py:209
  88.2 4.4 %copy-start.15 = (bf16[3,128,768]{2,1,0:T(8,128)(2,1)}, bf16[3,128,768]{2,1,0:T(8,128)(2,1)S(1)}, u32[]{:S(2)}) copy-start(bf16[3,128,768]{2,1,0:T(8,128)(2,1)S(1)} %collective-permute-done.8.refs_10_) | copy-start | bytes 1769476
  88.2 5.5 %collective-permute-start.12 = (bf16[3,128,768]{2,1,0:T(8,128)(2,1)}, bf16[3,128,768]{2,1,0:T(8,128)(2,1)}, u32[]{:S(2)}, u32[]{:S(2)}) collective-permute-start(bf16[3,128,768]{2,1,0:T(8,128)(2,1)} %collective-permute-done.11.refs_13_), channel_id=1, source_target_pairs={{0,32},{32,0},{64,96},{96,64},{128,160},{160,128},{192,224},{224,1... | collective-permute-start | bytes 1769480 | tf_op jit(solution)/shard_map/ppermute | solution.py:209
  90.1 2.4 %copy-start.16 = (bf16[3,128,768]{2,1,0:T(8,128)(2,1)}, bf16[3,128,768]{2,1,0:T(8,128)(2,1)S(1)}, u32[]{:S(2)}) copy-start(bf16[3,128,768]{2,1,0:T(8,128)(2,1)S(1)} %collective-permute-done.6.refs_8_) | copy-start | bytes 1769476
  90.1 4.4 %collective-permute-start.10 = (bf16[3,128,768]{2,1,0:T(8,128)(2,1)}, bf16[3,128,768]{2,1,0:T(8,128)(2,1)}, u32[]{:S(2)}, u32[]{:S(2)}) collective-permute-start(bf16[3,128,768]{2,1,0:T(8,128)(2,1)} %collective-permute-done.9.refs_11_), channel_id=1, source_target_pairs={{0,32},{32,0},{64,96},{96,64},{128,160},{160,128},{192,224},{224,1... | collective-permute-start | bytes 1769480 | tf_op jit(solution)/shard_map/ppermute | solution.py:209
  120.5 1.4 copy-start.2
  132.5 103.4 %all-to-all-start.1 = ((bf16[32,8,4096]{2,1,0:T(8,128)(2,1)}), bf16[32,8,4096]{2,1,0:T(8,128)(2,1)S(1)}, u32[]{:S(2)}, u32[]{:S(2)}) async-start(bf16[32,8,4096]{2,1,0:T(8,128)(2,1)} %bitcast.43), calls=%async_computation.1 | async-start | bytes 4194304 | tf_op jit(solution)/shard_map/all_to_all | solution.py:232
  141.1 7.8 %collective-permute-start.15 = (bf16[8,128,768]{2,1,0:T(8,128)(2,1)}, bf16[8,128,768]{2,1,0:T(8,128)(2,1)S(1)}, u32[]{:S(2)}, u32[]{:S(2)}) collective-permute-start(bf16[8,128,768]{2,1,0:T(8,128)(2,1)} %get-tuple-element.36), channel_id=1, source_target_pairs={{0,32},{32,0},{64,96},{96,64},{128,160},{160,128},{192,224},{224,1... | collective-permute-start | bytes 4718600 | tf_op jit(solution)/shard_map/ppermute | solution.py:209
  143.8 5.5 %collective-permute-start.16 = (bf16[8,128,768]{2,1,0:T(8,128)(2,1)}, bf16[8,128,768]{2,1,0:T(8,128)(2,1)S(1)}, u32[]{:S(2)}, u32[]{:S(2)}) collective-permute-start(bf16[8,128,768]{2,1,0:T(8,128)(2,1)} %get-tuple-element.37), channel_id=1, source_target_pairs={{0,32},{32,0},{64,96},{96,64},{128,160},{160,128},{192,224},{224,1... | collective-permute-start | bytes 4718600 | tf_op jit(solution)/shard_map/ppermute | solution.py:209
  145.7 5.8 %collective-permute-start.17 = (bf16[8,128,768]{2,1,0:T(8,128)(2,1)}, bf16[8,128,768]{2,1,0:T(8,128)(2,1)S(1)}, u32[]{:S(2)}, u32[]{:S(2)}) collective-permute-start(bf16[8,128,768]{2,1,0:T(8,128)(2,1)} %get-tuple-element.38), channel_id=1, source_target_pairs={{0,32},{32,0},{64,96},{96,64},{128,160},{160,128},{192,224},{224,1... | collective-permute-start | bytes 4718600 | tf_op jit(solution)/shard_map/ppermute | solution.py:209
  148.9 2.6 %copy-start.3 = (bf16[8,128,768]{2,1,0:T(8,128)(2,1)}, bf16[8,128,768]{2,1,0:T(8,128)(2,1)S(1)}, u32[]{:S(2)}) copy-start(bf16[8,128,768]{2,1,0:T(8,128)(2,1)S(1)} %collective-permute-done.15.refs_5_) | copy-start | bytes 4718596
  149.3 2.3 copy-start.4
  151.6 1.3 copy-start.5
  159.4 32.9 %copy-start.17 = (bf16[2,128,768]{2,1,0:T(8,128)(2,1)S(1)}, bf16[2,128,768]{2,1,0:T(8,128)(2,1)}, u32[]{:S(2)}) copy-start(bf16[2,128,768]{2,1,0:T(8,128)(2,1)} %get-tuple-element.50) | copy-start | bytes 1179652
  159.4 44.7 %copy-start.7 = (bf16[2,128,768]{2,1,0:T(8,128)(2,1)S(1)}, bf16[2,128,768]{2,1,0:T(8,128)(2,1)}, u32[]{:S(2)}) copy-start(bf16[2,128,768]{2,1,0:T(8,128)(2,1)} %get-tuple-element.43) | copy-start | bytes 1179652
  159.4 15.7 %collective-permute-start.18 = (bf16[2,128,768]{2,1,0:T(8,128)(2,1)}, bf16[2,128,768]{2,1,0:T(8,128)(2,1)S(1)}, u32[]{:S(2)}, u32[]{:S(2)}) collective-permute-start(bf16[2,128,768]{2,1,0:T(8,128)(2,1)} %get-tuple-element.40), channel_id=1, source_target_pairs={{0,128},{32,160},{64,192},{96,224},{128,256},{160,288},{192,320},{... | collective-permute-start | bytes 1179656 | tf_op jit(solution)/shard_map/ppermute | solution.py:209
  162.7 20.0 %collective-permute-start.19 = (bf16[2,128,768]{2,1,0:T(8,128)(2,1)}, bf16[2,128,768]{2,1,0:T(8,128)(2,1)S(1)}, u32[]{:S(2)}, u32[]{:S(2)}) collective-permute-start(bf16[2,128,768]{2,1,0:T(8,128)(2,1)} %get-tuple-element.41), channel_id=1, source_target_pairs={{0,256},{32,288},{64,320},{96,352},{128,384},{160,416},{192,448},{... | collective-permute-start | bytes 1179656 | tf_op jit(solution)/shard_map/ppermute | solution.py:209
  167.0 17.6 %collective-permute-start.20 = (bf16[2,128,768]{2,1,0:T(8,128)(2,1)}, bf16[2,128,768]{2,1,0:T(8,128)(2,1)S(1)}, u32[]{:S(2)}, u32[]{:S(2)}) collective-permute-start(bf16[2,128,768]{2,1,0:T(8,128)(2,1)} %get-tuple-element.42), channel_id=1, source_target_pairs={{0,384},{32,416},{64,448},{96,480},{128,0},{160,32},{192,64},{224,... | collective-permute-start | bytes 1179656 | tf_op jit(solution)/shard_map/ppermute | solution.py:209
  170.1 22.2 %collective-permute-start.22 = (bf16[2,128,768]{2,1,0:T(8,128)(2,1)}, bf16[2,128,768]{2,1,0:T(8,128)(2,1)S(1)}, u32[]{:S(2)}, u32[]{:S(2)}) collective-permute-start(bf16[2,128,768]{2,1,0:T(8,128)(2,1)} %get-tuple-element.44), channel_id=1, source_target_pairs={{0,128},{32,160},{64,192},{96,224},{128,256},{160,288},{192,320},{... | collective-permute-start | bytes 1179656 | tf_op jit(solution)/shard_map/ppermute | solution.py:209
  172.3 27.3 %collective-permute-start.23 = (bf16[2,128,768]{2,1,0:T(8,128)(2,1)}, bf16[2,128,768]{2,1,0:T(8,128)(2,1)S(1)}, u32[]{:S(2)}, u32[]{:S(2)}) collective-permute-start(bf16[2,128,768]{2,1,0:T(8,128)(2,1)} %get-tuple-element.45), channel_id=1, source_target_pairs={{0,256},{32,288},{64,320},{96,352},{128,384},{160,416},{192,448},{... | collective-permute-start | bytes 1179656 | tf_op jit(solution)/shard_map/ppermute | solution.py:209
  175.1 29.0 %collective-permute-start.24 = (bf16[2,128,768]{2,1,0:T(8,128)(2,1)}, bf16[2,128,768]{2,1,0:T(8,128)(2,1)S(1)}, u32[]{:S(2)}, u32[]{:S(2)}) collective-permute-start(bf16[2,128,768]{2,1,0:T(8,128)(2,1)} %get-tuple-element.46), channel_id=1, source_target_pairs={{0,384},{32,416},{64,448},{96,480},{128,0},{160,32},{192,64},{224,... | collective-permute-start | bytes 1179656 | tf_op jit(solution)/shard_map/ppermute | solution.py:209
  182.7 26.4 %collective-permute-start.26 = (bf16[2,128,768]{2,1,0:T(8,128)(2,1)}, bf16[2,128,768]{2,1,0:T(8,128)(2,1)S(1)}, u32[]{:S(2)}, u32[]{:S(2)}) collective-permute-start(bf16[2,128,768]{2,1,0:T(8,128)(2,1)} %get-tuple-element.48), channel_id=1, source_target_pairs={{0,128},{32,160},{64,192},{96,224},{128,256},{160,288},{192,320},{... | collective-permute-start | bytes 1179656 | tf_op jit(solution)/shard_map/ppermute | solution.py:209
  184.6 31.8 %collective-permute-start.27 = (bf16[2,128,768]{2,1,0:T(8,128)(2,1)}, bf16[2,128,768]{2,1,0:T(8,128)(2,1)S(1)}, u32[]{:S(2)}, u32[]{:S(2)}) collective-permute-start(bf16[2,128,768]{2,1,0:T(8,128)(2,1)} %get-tuple-element.49), channel_id=1, source_target_pairs={{0,256},{32,288},{64,320},{96,352},{128,384},{160,416},{192,448},{... | collective-permute-start | bytes 1179656 | tf_op jit(solution)/shard_map/ppermute | solution.py:209
  190.1 27.5 %copy-start.6 = (bf16[2,128,768]{2,1,0:T(8,128)(2,1)S(1)}, bf16[2,128,768]{2,1,0:T(8,128)(2,1)}, u32[]{:S(2)}) copy-start(bf16[2,128,768]{2,1,0:T(8,128)(2,1)} %get-tuple-element.47) | copy-start | bytes 1179652
  192.3 25.4 %collective-permute-start.28 = (bf16[2,128,768]{2,1,0:T(8,128)(2,1)S(1)}, bf16[2,128,768]{2,1,0:T(8,128)(2,1)S(1)}, u32[]{:S(2)}, u32[]{:S(2)}) collective-permute-start(bf16[2,128,768]{2,1,0:T(8,128)(2,1)S(1)} %copy-done.17), channel_id=1, source_target_pairs={{0,384},{32,416},{64,448},{96,480},{128,0},{160,32},{192,64},{224,... | collective-permute-start | bytes 1179656 | tf_op jit(solution)/shard_map/ppermute | solution.py:209
  199.6 23.0 %collective-permute-start.21 = (bf16[128,768]{1,0:T(8,128)(2,1)S(1)}, bf16[128,768]{1,0:T(8,128)(2,1)S(1)}, u32[]{:S(2)}, u32[]{:S(2)}) collective-permute-start(bf16[128,768]{1,0:T(8,128)(2,1)S(1)} %fusion.6), channel_id=1, source_target_pairs={{0,64},{32,96},{64,0},{96,32},{128,192},{160,224},{192,128},{224,1... | collective-permute-start | bytes 589832 | tf_op jit(solution)/shard_map/ppermute | solution.py:209
  204.3 19.0 %collective-permute-start.25 = (bf16[128,768]{1,0:T(8,128)(2,1)S(1)}, bf16[128,768]{1,0:T(8,128)(2,1)S(1)}, u32[]{:S(2)}, u32[]{:S(2)}) collective-permute-start(bf16[128,768]{1,0:T(8,128)(2,1)S(1)} %fusion.7), channel_id=1, source_target_pairs={{0,64},{32,96},{64,0},{96,32},{128,192},{160,224},{192,128},{224,1... | collective-permute-start | bytes 589832 | tf_op jit(solution)/shard_map/ppermute | solution.py:209
  217.9 18.1 %copy-start = (bf16[256,128]{1,0:T(8,128)(2,1)S(1)}, bf16[256,128]{1,0:T(8,128)(2,1)}, u32[]{:S(2)}) copy-start(bf16[256,128]{1,0:T(8,128)(2,1)} %get-tuple-element.28.pick_ref) | copy-start | bytes 196612
  217.9 18.1 %copy-start.1 = (s32[128,1]{0,1:T(1,128)S(1)}, s32[128,1]{0,1:T(1,128)}, u32[]{:S(2)}) copy-start(s32[128,1]{0,1:T(1,128)} %param.9) | copy-start | bytes 1540
  217.9 8.7 %collective-permute-start.29 = (bf16[128,768]{1,0:T(8,128)(2,1)S(1)}, bf16[128,768]{1,0:T(8,128)(2,1)S(1)}, u32[]{:S(2)}, u32[]{:S(2)}) collective-permute-start(bf16[128,768]{1,0:T(8,128)(2,1)S(1)} %fusion.8), channel_id=1, source_target_pairs={{0,64},{32,96},{64,0},{96,32},{128,192},{160,224},{192,128},{224,1... | collective-permute-start | bytes 589832 | tf_op jit(solution)/shard_map/ppermute | solution.py:209

commit v5 on v4

--- a/solution.py
+++ b/solution.py
@@ -12,6 +12,9 @@
 VM = pltpu.VMEM
 
 
+pin = pltpu.with_memory_space_constraint
+
+
 def mm(a, b, dims):
     return lax.dot_general(a, b, dims, preferred_element_type=F32)
 
@@ -27,8 +30,9 @@
     return jnp.sum(jnp.where(down == along, row, 0.0), axis=1, keepdims=True)
 
 
-def place_kernel(experts, capacity, ids_ref, unit_ref, tok_ref, cot_ref, send_ref, pick_ref):
+def place_kernel(experts, capacity, ids_ref, unit_ref, tok_ref, cot_ref, send_out, pick_ref, send, sems):
     tok, width = tok_ref.shape
+    slots, parts = send.shape[0], sems.shape[0]
     ids = ids_ref[...]
     labels = lax.broadcasted_iota(jnp.int32, (experts, tok), 0)
     down = lax.broadcasted_iota(jnp.int32, (tok, tok), 0)
@@ -38,43 +42,61 @@
     ranks = mm(hot.astype(BF), before, NN)
     rank = jnp.sum(ranks * hot, axis=0, keepdims=True).astype(jnp.int32)
     slot = ids * capacity + rank
-    places = lax.broadcasted_iota(jnp.int32, (experts * capacity, tok), 0)
+    places = lax.broadcasted_iota(jnp.int32, (slots, tok), 0)
     pick = jnp.where(slot == places, 1.0, 0.0).astype(BF)
     pick_ref[...] = pick
     scale = column(unit_ref[...].astype(F32) / 256.0)
-    step = width // 4
-    for c in range(4):
-        part = pl.ds(c * step, step)
-        send_ref[:, part] = mm(pick, tok_ref[:, part], NN).astype(BF)
-        rows = (scale * cot_ref[:, part].astype(F32)).astype(BF)
-        send_ref[:, pl.ds(width + c * step, step)] = mm(pick, rows, NN).astype(BF)
+    grads = (scale * cot_ref[...].astype(F32)).astype(BF)
+    step = slots // parts
+    stores = []
+    for n in range(parts):
+        cut = pl.ds(n * step, step)
+        some = pick[n * step : (n + 1) * step]
+        send[cut, :width] = mm(some, tok_ref[...], NN).astype(BF)
+        send[cut, width:] = mm(some, grads, NN).astype(BF)
+        stores.append(pltpu.make_async_copy(send.at[cut], send_out.at[cut], sems.at[n]))
+        stores[n].start()
+    for copy in stores:
+        copy.wait()
+
+
+def place_call(experts, capacity, ids, units, tokens, cotangent):
+    tok, width = tokens.shape
+    slots = experts * capacity
+    parts = 2
+    shape = jax.ShapeDtypeStruct
+    far, near = pl.BlockSpec(memory_space=pltpu.HBM), pl.BlockSpec(memory_space=VM)
+    return pl.pallas_call(
+        lambda *refs: place_kernel(experts, capacity, *refs),
+        in_specs=[near] * 4,
+        out_specs=[far, near],
+        out_shape=[pltpu.HBM((slots, 2 * width), BF), shape((slots, tok), BF)],
+        scratch_shapes=[VM((slots, 2 * width), BF), pltpu.SemaphoreType.DMA((parts,))],
+        compiler_params=params(24),
+        cost_estimate=pl.CostEstimate(
+            flops=4 * tok * slots * width, bytes_accessed=12 * tok * width, transcendentals=0
+        ),
+    )(ids, units, tokens, cotangent)
 
 
 def expert_kernel(order_ref, *refs):
     pairs = order_ref.shape[0] - 1
-    rows_in, shards_in = refs[0], refs[1 : 1 + 2 * pairs]
-    send_out, *mids_out = refs[1 + 2 * pairs : 5 + 2 * pairs]
-    rows, shards, send, hid, dpre, dlin, in_sems, out_sems = refs[5 + 2 * pairs :]
+    rows, shards_in = refs[0], refs[1 : 1 + 2 * pairs]
+    send_out, hid, dpre, dlin, shards, send, in_sems, out_sems = refs[1 + 2 * pairs :]
     block, units = shards.shape[2:]
     width = rows.shape[1] // 2
     core = order_ref[pairs]
     halves = [pl.ds(0, width), pl.ds(width, width)]
 
     loads = [
-        pltpu.make_async_copy(rows_in.at[:, h], rows.at[:, h], in_sems.at[n])
-        for n, h in enumerate(halves)
+        pltpu.make_async_copy(shards_in[n], shards.at[n], in_sems.at[n]) for n in range(2 * pairs)
     ]
-    loads += [
-        pltpu.make_async_copy(shards_in[n], shards.at[n], in_sems.at[2 + n])
-        for n in range(2 * pairs)
+    for load in loads:
+        load.start()
+    stores = [
+        pltpu.make_async_copy(send.at[:, half], send_out.at[:, half], out_sems.at[n])
+        for n, half in enumerate(halves)
     ]
-    for n in (0, 2, 3, 1, *range(4, 2 + 2 * pairs)):
-        loads[n].start()
-    stores = []
-
-    def store(source, target):
-        stores.append(pltpu.make_async_copy(source, target, out_sems.at[len(stores)]))
-        stores[-1].start()
 
     def spots(p, first):
         at = order_ref[p] * 2
@@ -88,24 +110,19 @@
 
     every = pl.ds(0, units)
     pre, lin, dhid = 0.0, 0.0, 0.0
-    loads[0].wait()
     for p in range(pairs):
-        loads[2 + 2 * p].wait()
-        loads[3 + 2 * p].wait()
+        loads[2 * p].wait()
+        loads[2 * p + 1].wait()
         x = left(p, 0)
         pre = pre + mm(x, right(p, 0, every), NN)
         lin = lin + mm(x, right(p, 1, every), NN)
-        if p == 0:
-            loads[1].wait()
         dhid = dhid + mm(left(p, width), right(p, 2, every), NN)
     sig = jax.nn.sigmoid(pre)
     active = pre * sig
     hid[...] = (active * lin).astype(BF)
     dpre[...] = (dhid * lin * sig * (1.0 + pre * (1.0 - sig))).astype(BF)
     dlin[...] = (dhid * active).astype(BF)
-    for source, target in zip((hid, dpre, dlin), mids_out):
-        store(source, target)
-    for h, half in enumerate(halves):
+    for h in range(2):
         for p in range(pairs):
             if h == 0:
                 value = mm(hid[...], right(p, 2, every), NT)
@@ -114,7 +131,7 @@
             value = value.astype(BF)
             for n, s in enumerate(spots(p, h * width)):
                 send[:, s] = value[:, n * block : (n + 1) * block]
-        store(send.at[:, half], send_out.at[:, half])
+        stores[h].start()
     for copy in stores:
         copy.wait()
 
@@ -124,28 +141,26 @@
     block, units = shards[0].shape[1:]
     count = len(shards)
     shape = jax.ShapeDtypeStruct
-    outs = [shape((slots, both), BF)] + [shape((slots, units), BF)] * 3
-    anywhere = pl.BlockSpec(memory_space=pl.ANY)
+    outs = [pltpu.HBM((slots, both), BF)] + [shape((slots, units), BF)] * 3
+    far, near = pl.BlockSpec(memory_space=pltpu.HBM), pl.BlockSpec(memory_space=VM)
     return pl.pallas_call(
         expert_kernel,
-        in_specs=[pl.BlockSpec(memory_space=pltpu.SMEM)] + [anywhere] * (1 + count),
-        out_specs=[anywhere] * 4,
+        in_specs=[pl.BlockSpec(memory_space=pltpu.SMEM), near] + [far] * count,
+        out_specs=[far, near, near, near],
         out_shape=outs,
         scratch_shapes=[
-            VM((slots, both), BF),
             VM((count, 3, block, units), BF),
             VM((slots, both), BF),
-            *[VM((slots, units), BF)] * 3,
-            pltpu.SemaphoreType.DMA((2 + count,)),
-            pltpu.SemaphoreType.DMA((5,)),
+            pltpu.SemaphoreType.DMA((count,)),
+            pltpu.SemaphoreType.DMA((2,)),
         ],
-        compiler_params=params(56),
+        compiler_params=params(32),
         cost_estimate=pl.CostEstimate(
             flops=6 * slots * both * units,
             bytes_accessed=4 * slots * both + 6 * count * block * units,
             transcendentals=slots * units,
         ),
-    )(order, rows, *shards)
+    )(order, pin(rows, pltpu.VMEM), *[pin(s, pltpu.HBM) for s in shards])
 
 
 def grad_kernel(groups, added, order_ref, rows_ref, dpre_ref, dlin_ref, hid_ref, *refs):
@@ -209,13 +224,7 @@
         return lax.ppermute(a, "dp", [(i, to(i)) for i in range(groups)])
 
     ids, scales = expert_ids.reshape(1, tok), gate_units.reshape(1, tok)
-    send, pick = call(
-        lambda *refs: place_kernel(experts, capacity, *refs),
-        [shape((slots, 2 * width), BF), shape((slots, tok), BF)],
-        56,
-        4 * tok * slots * width,
-        (ids, scales, tokens, cotangent),
-    )
+    send, pick = place_call(experts, capacity, ids, scales, tokens, cotangent)
 
     own = jnp.concatenate([w_gate, w_up, w_down], axis=0)
     across = permute(own, lambda i: i ^ 2)
@@ -242,7 +251,7 @@
     away = call(
         lambda *refs: grad_kernel((8,), False, *refs),
         [partial] * 3,
-        56,
+        24,
         flops,
         (place + (1 - core), rows, d_pre, d_lin, hidden),
         smem=1,
@@ -252,7 +261,7 @@
     sums = call(
         lambda *refs: grad_kernel((2, 2, 2, 2), True, *refs),
         [pair] * 12,
-        56,
+        32,
         flops,
         (place + core, rows, d_pre, d_lin, hidden, *extra),
         smem=1,

time: 239 us -> 239 us (level)
  waiting for transfers between devices: 70.9 us -> 82.1 us
  Pallas kernels: 26.8 us -> 17.3 us
  other arithmetic: 5.58 us -> 2.99 us
    pallas_call x4 -> x3, Pallas kernels: 16.2 us -> 5.46 us  [call(): pl.pallas_call(kernel, out_shape=outs, in_specs=in_specs, out_specs=[pl.B...]
    all_to_all x2, waiting for transfers between devices: 34.6 us -> 42.3 us  [exchange(): got = lax.all_to_all(cut, 'expert', split_axis=0, concat_axis=0, tiled=True)]
    ppermute x30, waiting for transfers between devices: 36.2 us -> 39.7 us  [permute(): return lax.ppermute(a, 'dp', [(i, to(i)) for i in range(groups)])]
  transfers between devices with their start and end apart: 32 -> 32, of which waited for: 15 -> 15; matrix products, arithmetic and copies ran while one was open for 2% -> 1% of each run, Pallas kernels for 5% -> 2%
where the time goes in v5:
time: 239 us; the launch traced here: 237 us
  starting transfers between devices  128 us (54%)
  waiting for transfers between devices  82.1 us (34%)
  Pallas kernels  17.3 us (7%)
  local copies, waits for them, and re-layouts  5.14 us (2%)
  other arithmetic  2.99 us (1%)
    ppermute x30, starting transfers between devices, permute(): return lax.ppermute(a, 'dp', [(i, to(i)) for i in range(groups)])  109 us
    all_to_all x2, waiting for transfers between devices, exchange(): got = lax.all_to_all(cut, 'expert', split_axis=0, concat_axis=0, tiled=True)  42.3 us
    ppermute x30, waiting for transfers between devices, permute(): return lax.ppermute(a, 'dp', [(i, to(i)) for i in range(groups)])  39.7 us
    all_to_all x2, starting transfers between devices, exchange(): got = lax.all_to_all(cut, 'expert', split_axis=0, concat_axis=0, tiled=True)  19.8 us
    pallas_call x1, Pallas kernels, experts_call(): pl.pallas_call(expert_kernel, in_specs=[pl.BlockSpec(memory_space=pltpu.S...  9.95 us
    pallas_call x3, Pallas kernels, call(): pl.pallas_call(kernel, out_shape=outs, in_specs=in_specs, out_specs=[pl.B...  5.46 us
    unnamed x38, local copies, waits for them, and re-layouts  5.06 us
  transfers between devices with their start and end apart: 32, of which 15 were waited for; matrix products, arithmetic and copies ran while one was open for 1% of the time, Pallas kernels for 2%

profile of v5, /device:TPU:33, one launch (start us, length us, event | category | flops | bytes accessed | tf_op | source)
XLA Modules:
  0.0 237.3 jit_solution(11532428847525135206)
XLA Ops:
  0.6 1.0 copy-done.3
  1.7 1.0 copy-done.4
  2.7 0.7 copy-done.5
  3.4 0.7 copy-done.7
  4.0 1.9 shard_map.110
  6.0 16.0 %all-to-all-start = ((bf16[32,8,4096]{2,1,0:T(8,128)(2,1)}), bf16[32,8,4096]{2,1,0:T(8,128)(2,1)S(1)}, u32[]{:S(2)}, u32[]{:S(2)}) async-start(bf16[32,8,4096]{2,1,0:T(8,128)(2,1)} %bitcast.45), calls=%async_computation | async-start | bytes 4194304 | tf_op jit(solution)/shard_map/all_to_all | solution.py:241
  22.1 4.5 %collective-permute-start.7 = (bf16[3,128,768]{2,1,0:T(8,128)(2,1)S(1)}, bf16[3,128,768]{2,1,0:T(8,128)(2,1)S(1)}, u32[]{:S(2)}, u32[]{:S(2)}) collective-permute-start(bf16[3,128,768]{2,1,0:T(8,128)(2,1)S(1)} %constant_dynamic-update-slice_fusion.refs_1_), channel_id=1, source_target_pairs={{0,64},{32,96},{64,0},{96,32},{128,192},{160,224},{192,128},{224,1... | collective-permute-start | bytes 1769480 | tf_op jit(solution)/shard_map/ppermute | solution.py:224
  26.6 4.4 %collective-permute-start.5 = (bf16[3,128,768]{2,1,0:T(8,128)(2,1)S(1)}, bf16[3,128,768]{2,1,0:T(8,128)(2,1)S(1)}, u32[]{:S(2)}, u32[]{:S(2)}) collective-permute-start(bf16[3,128,768]{2,1,0:T(8,128)(2,1)S(1)} %constant_dynamic-update-slice_fusion.refs_1_), channel_id=1, source_target_pairs={{0,384},{32,416},{64,448},{96,480},{128,0},{160,32},{192,64},{224,... | collective-permute-start | bytes 1769480 | tf_op jit(solution)/shard_map/ppermute | solution.py:224
  31.0 2.4 %collective-permute-start.3 = (bf16[3,128,768]{2,1,0:T(8,128)(2,1)S(1)}, bf16[3,128,768]{2,1,0:T(8,128)(2,1)S(1)}, u32[]{:S(2)}, u32[]{:S(2)}) collective-permute-start(bf16[3,128,768]{2,1,0:T(8,128)(2,1)S(1)} %constant_dynamic-update-slice_fusion.refs_1_), channel_id=1, source_target_pairs={{0,256},{32,288},{64,320},{96,352},{128,384},{160,416},{192,448},{... | collective-permute-start | bytes 1769480 | tf_op jit(solution)/shard_map/ppermute | solution.py:224
  33.4 2.5 %collective-permute-start.1 = (bf16[3,128,768]{2,1,0:T(8,128)(2,1)S(1)}, bf16[3,128,768]{2,1,0:T(8,128)(2,1)}, u32[]{:S(2)}, u32[]{:S(2)}) collective-permute-start(bf16[3,128,768]{2,1,0:T(8,128)(2,1)S(1)} %constant_dynamic-update-slice_fusion.refs_1_), channel_id=1, source_target_pairs={{0,128},{32,160},{64,192},{96,224},{128,256},{160,288},{192,320},{... | collective-permute-start | bytes 1769480 | tf_op jit(solution)/shard_map/ppermute | solution.py:224
  36.0 4.3 %collective-permute-start = (bf16[3,128,768]{2,1,0:T(8,128)(2,1)S(1)}, bf16[3,128,768]{2,1,0:T(8,128)(2,1)S(1)}, u32[]{:S(2)}, u32[]{:S(2)}) collective-permute-start(bf16[3,128,768]{2,1,0:T(8,128)(2,1)S(1)} %constant_dynamic-update-slice_fusion.refs_1_), channel_id=1, source_target_pairs={{0,32},{32,0},{64,96},{96,64},{128,160},{160,128},{192,224},{224,1... | collective-permute-start | bytes 1769480 | tf_op jit(solution)/shard_map/ppermute | solution.py:224
  40.2 1.6 collective-permute-done.7.refs_9_
  41.8 4.4 %collective-permute-start.13 = (bf16[3,128,768]{2,1,0:T(8,128)(2,1)S(1)}, bf16[3,128,768]{2,1,0:T(8,128)(2,1)}, u32[]{:S(2)}, u32[]{:S(2)}) collective-permute-start(bf16[3,128,768]{2,1,0:T(8,128)(2,1)S(1)} %collective-permute-done.7.refs_9_), channel_id=1, source_target_pairs={{0,384},{32,416},{64,448},{96,480},{128,0},{160,32},{192,64},{224,... | collective-permute-start | bytes 1769480 | tf_op jit(solution)/shard_map/ppermute | solution.py:224
  46.2 2.4 %collective-permute-start.11 = (bf16[3,128,768]{2,1,0:T(8,128)(2,1)S(1)}, bf16[3,128,768]{2,1,0:T(8,128)(2,1)}, u32[]{:S(2)}, u32[]{:S(2)}) collective-permute-start(bf16[3,128,768]{2,1,0:T(8,128)(2,1)S(1)} %collective-permute-done.7.refs_9_), channel_id=1, source_target_pairs={{0,256},{32,288},{64,320},{96,352},{128,384},{160,416},{192,448},{... | collective-permute-start | bytes 1769480 | tf_op jit(solution)/shard_map/ppermute | solution.py:224
  48.7 9.8 %collective-permute-start.9 = (bf16[3,128,768]{2,1,0:T(8,128)(2,1)S(1)}, bf16[3,128,768]{2,1,0:T(8,128)(2,1)}, u32[]{:S(2)}, u32[]{:S(2)}) collective-permute-start(bf16[3,128,768]{2,1,0:T(8,128)(2,1)S(1)} %collective-permute-done.7.refs_9_), channel_id=1, source_target_pairs={{0,128},{32,160},{64,192},{96,224},{128,256},{160,288},{192,320},{... | collective-permute-start | bytes 1769480 | tf_op jit(solution)/shard_map/ppermute | solution.py:224
  58.5 6.0 %collective-permute-done.1.refs_3_ = bf16[3,128,768]{2,1,0:T(8,128)(2,1)} collective-permute-done((bf16[3,128,768]{2,1,0:T(8,128)(2,1)S(1)}, bf16[3,128,768]{2,1,0:T(8,128)(2,1)}, u32[]{:S(2)}, u32[]{:S(2)}) %collective-permute-start.1) | collective-permute-done | bytes 589856 | tf_op jit(solution)/shard_map/ppermute | solution.py:224
  64.6 4.0 %collective-permute-start.8 = (bf16[3,128,768]{2,1,0:T(8,128)(2,1)S(1)}, bf16[3,128,768]{2,1,0:T(8,128)(2,1)S(1)}, u32[]{:S(2)}, u32[]{:S(2)}) collective-permute-start(bf16[3,128,768]{2,1,0:T(8,128)(2,1)S(1)} %collective-permute-done.7.refs_9_), channel_id=1, source_target_pairs={{0,32},{32,0},{64,96},{96,64},{128,160},{160,128},{192,224},{224,1... | collective-permute-start | bytes 1769480 | tf_op jit(solution)/shard_map/ppermute | solution.py:224
  68.6 1.9 collective-permute-start.6
  70.6 13.8 %collective-permute-start.4 = (bf16[3,128,768]{2,1,0:T(8,128)(2,1)S(1)}, bf16[3,128,768]{2,1,0:T(8,128)(2,1)}, u32[]{:S(2)}, u32[]{:S(2)}) collective-permute-start(bf16[3,128,768]{2,1,0:T(8,128)(2,1)S(1)} %collective-permute-done.3.refs_5_), channel_id=1, source_target_pairs={{0,32},{32,0},{64,96},{96,64},{128,160},{160,128},{192,224},{224,1... | collective-permute-start | bytes 1769480 | tf_op jit(solution)/shard_map/ppermute | solution.py:224
  84.4 1.9 collective-permute-start.2
  86.3 1.2 collective-permute-done.9.refs_11_
  87.6 2.5 %collective-permute-start.14 = (bf16[3,128,768]{2,1,0:T(8,128)(2,1)}, bf16[3,128,768]{2,1,0:T(8,128)(2,1)}, u32[]{:S(2)}, u32[]{:S(2)}) collective-permute-start(bf16[3,128,768]{2,1,0:T(8,128)(2,1)} %collective-permute-done.13.refs_15_), channel_id=1, source_target_pairs={{0,32},{32,0},{64,96},{96,64},{128,160},{160,128},{192,224},{224,1... | collective-permute-start | bytes 1769480 | tf_op jit(solution)/shard_map/ppermute | solution.py:224
  90.1 1.9 collective-permute-start.12
  92.1 2.4 %collective-permute-start.10 = (bf16[3,128,768]{2,1,0:T(8,128)(2,1)}, bf16[3,128,768]{2,1,0:T(8,128)(2,1)}, u32[]{:S(2)}, u32[]{:S(2)}) collective-permute-start(bf16[3,128,768]{2,1,0:T(8,128)(2,1)} %collective-permute-done.9.refs_11_), channel_id=1, source_target_pairs={{0,32},{32,0},{64,96},{96,64},{128,160},{160,128},{192,224},{224,1... | collective-permute-start | bytes 1769480 | tf_op jit(solution)/shard_map/ppermute | solution.py:224
  94.5 0.1 pad_add_fusion.order_ref
  94.6 1.8 collective-permute-done.10.refs_12_
  96.4 26.1 %all-to-all-done = bf16[32,8,4096]{2,1,0:T(8,128)(2,1)S(1)} async-done(((bf16[32,8,4096]{2,1,0:T(8,128)(2,1)}), bf16[32,8,4096]{2,1,0:T(8,128)(2,1)S(1)}, u32[]{:S(2)}, u32[]{:S(2)}) %all-to-all-start) | async-done | bytes 2097184 | tf_op jit(solution)/shard_map/all_to_all | solution.py:241
  122.5 9.9 %shard_map.111 = (bf16[256,4096]{1,0:T(8,128)(2,1)}, bf16[256,768]{1,0:T(8,128)(2,1)S(1)}, bf16[256,768]{1,0:T(8,128)(2,1)S(1)}, bf16[256,768]{1,0:T(8,128)(2,1)S(1)}) custom-call(s32[9]{0:T(128)S(1)} %pad_add_fusion.order_ref, bf16[256,4096]{1,0:T(8,128)(2,1)S(1)} %bitcast.38, bf16[3,128,768]{2,1,0:T(8,128)(2,1)} %copy-done.11, ...), custom_call_target="tpu_custom_call" | custom-call | flops 4831838208 | bytes 13631488 | tf_op jit(solution)/shard_map/pallas_call | solution.py:146
  132.5 3.8 %all-to-all-start.1 = ((bf16[32,8,4096]{2,1,0:T(8,128)(2,1)}), bf16[32,8,4096]{2,1,0:T(8,128)(2,1)S(1)}, u32[]{:S(2)}, u32[]{:S(2)}) async-start(bf16[32,8,4096]{2,1,0:T(8,128)(2,1)} %bitcast.44), calls=%async_computation.1 | async-start | bytes 4194304 | tf_op jit(solution)/shard_map/all_to_all | solution.py:241
  136.3 1.6 copy-done.1
  137.9 2.0 shard_map.113
  139.9 2.6 %collective-permute-start.15 = (bf16[8,128,768]{2,1,0:T(8,128)(2,1)S(1)}, bf16[8,128,768]{2,1,0:T(8,128)(2,1)S(1)}, u32[]{:S(2)}, u32[]{:S(2)}) collective-permute-start(bf16[8,128,768]{2,1,0:T(8,128)(2,1)S(1)} %get-tuple-element.36), channel_id=1, source_target_pairs={{0,32},{32,0},{64,96},{96,64},{128,160},{160,128},{192,224},{224,1... | collective-permute-start | bytes 4718600 | tf_op jit(solution)/shard_map/ppermute | solution.py:224
  142.5 1.9 collective-permute-start.16
  144.4 2.6 %collective-permute-start.17 = (bf16[8,128,768]{2,1,0:T(8,128)(2,1)S(1)}, bf16[8,128,768]{2,1,0:T(8,128)(2,1)S(1)}, u32[]{:S(2)}, u32[]{:S(2)}) collective-permute-start(bf16[8,128,768]{2,1,0:T(8,128)(2,1)S(1)} %get-tuple-element.38), channel_id=1, source_target_pairs={{0,32},{32,0},{64,96},{96,64},{128,160},{160,128},{192,224},{224,1... | collective-permute-start | bytes 4718600 | tf_op jit(solution)/shard_map/ppermute | solution.py:224
  147.1 0.8 collective-permute-done.16.refs_6_
  147.8 2.2 collective-permute-done.17.refs_7_
  150.1 2.1 shard_map.114
  152.2 3.2 %collective-permute-start.18 = (bf16[2,128,768]{2,1,0:T(8,128)(2,1)S(1)}, bf16[2,128,768]{2,1,0:T(8,128)(2,1)S(1)}, u32[]{:S(2)}, u32[]{:S(2)}) collective-permute-start(bf16[2,128,768]{2,1,0:T(8,128)(2,1)S(1)} %get-tuple-element.40), channel_id=1, source_target_pairs={{0,128},{32,160},{64,192},{96,224},{128,256},{160,288},{192,320},{... | collective-permute-start | bytes 1179656 | tf_op jit(solution)/shard_map/ppermute | solution.py:224
  155.3 4.3 %collective-permute-start.19 = (bf16[2,128,768]{2,1,0:T(8,128)(2,1)S(1)}, bf16[2,128,768]{2,1,0:T(8,128)(2,1)S(1)}, u32[]{:S(2)}, u32[]{:S(2)}) collective-permute-start(bf16[2,128,768]{2,1,0:T(8,128)(2,1)S(1)} %get-tuple-element.41), channel_id=1, source_target_pairs={{0,256},{32,288},{64,320},{96,352},{128,384},{160,416},{192,448},{... | collective-permute-start | bytes 1179656 | tf_op jit(solution)/shard_map/ppermute | solution.py:224
  159.7 3.0 %collective-permute-start.20 = (bf16[2,128,768]{2,1,0:T(8,128)(2,1)S(1)}, bf16[2,128,768]{2,1,0:T(8,128)(2,1)S(1)}, u32[]{:S(2)}, u32[]{:S(2)}) collective-permute-start(bf16[2,128,768]{2,1,0:T(8,128)(2,1)S(1)} %get-tuple-element.42), channel_id=1, source_target_pairs={{0,384},{32,416},{64,448},{96,480},{128,0},{160,32},{192,64},{224,... | collective-permute-start | bytes 1179656 | tf_op jit(solution)/shard_map/ppermute | solution.py:224
  162.7 2.2 collective-permute-start.22
  165.0 2.8 %collective-permute-start.23 = (bf16[2,128,768]{2,1,0:T(8,128)(2,1)S(1)}, bf16[2,128,768]{2,1,0:T(8,128)(2,1)S(1)}, u32[]{:S(2)}, u32[]{:S(2)}) collective-permute-start(bf16[2,128,768]{2,1,0:T(8,128)(2,1)S(1)} %get-tuple-element.45), channel_id=1, source_target_pairs={{0,256},{32,288},{64,320},{96,352},{128,384},{160,416},{192,448},{... | collective-permute-start | bytes 1179656 | tf_op jit(solution)/shard_map/ppermute | solution.py:224
  167.7 3.5 %collective-permute-start.24 = (bf16[2,128,768]{2,1,0:T(8,128)(2,1)S(1)}, bf16[2,128,768]{2,1,0:T(8,128)(2,1)S(1)}, u32[]{:S(2)}, u32[]{:S(2)}) collective-permute-start(bf16[2,128,768]{2,1,0:T(8,128)(2,1)S(1)} %get-tuple-element.46), channel_id=1, source_target_pairs={{0,384},{32,416},{64,448},{96,480},{128,0},{160,32},{192,64},{224,... | collective-permute-start | bytes 1179656 | tf_op jit(solution)/shard_map/ppermute | solution.py:224
  171.2 4.0 %collective-permute-done.19 = bf16[2,128,768]{2,1,0:T(8,128)(2,1)S(1)} collective-permute-done((bf16[2,128,768]{2,1,0:T(8,128)(2,1)S(1)}, bf16[2,128,768]{2,1,0:T(8,128)(2,1)S(1)}, u32[]{:S(2)}, u32[]{:S(2)}) %collective-permute-start.19) | collective-permute-done | bytes 393248 | tf_op jit(solution)/shard_map/ppermute | solution.py:224
  175.2 1.9 collective-permute-start.26
  177.1 4.1 %collective-permute-start.27 = (bf16[2,128,768]{2,1,0:T(8,128)(2,1)S(1)}, bf16[2,128,768]{2,1,0:T(8,128)(2,1)S(1)}, u32[]{:S(2)}, u32[]{:S(2)}) collective-permute-start(bf16[2,128,768]{2,1,0:T(8,128)(2,1)S(1)} %get-tuple-element.49), channel_id=1, source_target_pairs={{0,256},{32,288},{64,320},{96,352},{128,384},{160,416},{192,448},{... | collective-permute-start | bytes 1179656 | tf_op jit(solution)/shard_map/ppermute | solution.py:224
  181.2 0.2 convert_add_fusion.2
  181.4 3.3 %collective-permute-done.22 = bf16[2,128,768]{2,1,0:T(8,128)(2,1)S(1)} collective-permute-done((bf16[2,128,768]{2,1,0:T(8,128)(2,1)S(1)}, bf16[2,128,768]{2,1,0:T(8,128)(2,1)S(1)}, u32[]{:S(2)}, u32[]{:S(2)}) %collective-permute-start.22) | collective-permute-done | bytes 393248 | tf_op jit(solution)/shard_map/ppermute | solution.py:224
  184.7 2.0 collective-permute-start.28
  186.7 5.4 %collective-permute-done.23 = bf16[2,128,768]{2,1,0:T(8,128)(2,1)S(1)} collective-permute-done((bf16[2,128,768]{2,1,0:T(8,128)(2,1)S(1)}, bf16[2,128,768]{2,1,0:T(8,128)(2,1)S(1)}, u32[]{:S(2)}, u32[]{:S(2)}) %collective-permute-start.23) | collective-permute-done | bytes 393248 | tf_op jit(solution)/shard_map/ppermute | solution.py:224
  192.1 4.5 %collective-permute-start.21 = (bf16[128,768]{1,0:T(8,128)(2,1)S(1)}, bf16[128,768]{1,0:T(8,128)(2,1)S(1)}, u32[]{:S(2)}, u32[]{:S(2)}) collective-permute-start(bf16[128,768]{1,0:T(8,128)(2,1)S(1)} %fusion.6), channel_id=1, source_target_pairs={{0,64},{32,96},{64,0},{96,32},{128,192},{160,224},{192,128},{224,1... | collective-permute-start | bytes 589832 | tf_op jit(solution)/shard_map/ppermute | solution.py:224
  196.6 0.2 convert_add_fusion.1
  196.8 2.3 collective-permute-start.25
  199.1 2.4 %collective-permute-done.26 = bf16[2,128,768]{2,1,0:T(8,128)(2,1)S(1)} collective-permute-done((bf16[2,128,768]{2,1,0:T(8,128)(2,1)S(1)}, bf16[2,128,768]{2,1,0:T(8,128)(2,1)S(1)}, u32[]{:S(2)}, u32[]{:S(2)}) %collective-permute-start.26) | collective-permute-done | bytes 393248 | tf_op jit(solution)/shard_map/ppermute | solution.py:224
  201.5 7.4 %collective-permute-done.27 = bf16[2,128,768]{2,1,0:T(8,128)(2,1)S(1)} collective-permute-done((bf16[2,128,768]{2,1,0:T(8,128)(2,1)S(1)}, bf16[2,128,768]{2,1,0:T(8,128)(2,1)S(1)}, u32[]{:S(2)}, u32[]{:S(2)}) %collective-permute-start.27) | collective-permute-done | bytes 393248 | tf_op jit(solution)/shard_map/ppermute | solution.py:224
  208.9 1.2 collective-permute-done.28
  210.1 0.2 convert_add_fusion
  210.3 4.5 %collective-permute-start.29 = (bf16[128,768]{1,0:T(8,128)(2,1)S(1)}, bf16[128,768]{1,0:T(8,128)(2,1)S(1)}, u32[]{:S(2)}, u32[]{:S(2)}) collective-permute-start(bf16[128,768]{1,0:T(8,128)(2,1)S(1)} %fusion.8), channel_id=1, source_target_pairs={{0,64},{32,96},{64,0},{96,32},{128,192},{160,224},{192,128},{224,1... | collective-permute-start | bytes 589832 | tf_op jit(solution)/shard_map/ppermute | solution.py:224
  214.9 0.8 fusion.5
  215.7 0.8 fusion.3
  216.5 2.4 %collective-permute-done.29 = bf16[128,768]{1,0:T(8,128)(2,1)S(1)} collective-permute-done((bf16[128,768]{1,0:T(8,128)(2,1)S(1)}, bf16[128,768]{1,0:T(8,128)(2,1)S(1)}, u32[]{:S(2)}, u32[]{:S(2)}) %collective-permute-start.29) | collective-permute-done | bytes 196640 | tf_op jit(solution)/shard_map/ppermute | solution.py:224
  218.9 0.8 fusion.1
  219.6 16.3 %all-to-all-done.1 = bf16[32,8,4096]{2,1,0:T(8,128)(2,1)S(1)} async-done(((bf16[32,8,4096]{2,1,0:T(8,128)(2,1)}), bf16[32,8,4096]{2,1,0:T(8,128)(2,1)S(1)}, u32[]{:S(2)}, u32[]{:S(2)}) %all-to-all-start.1) | async-done | bytes 2097184 | tf_op jit(solution)/shard_map/all_to_all | solution.py:241
  235.9 1.4 shard_map.112
  (56 shorter events, 0.3 us)
Async XLA Ops:
  0.6 1.0 copy-start.3
  1.7 1.0 copy-start.4
  2.7 0.7 copy-start.5
  3.4 0.7 copy-start.7
  6.0 16.0 %copy-start.8 = (bf16[1,128,768]{2,1,0:T(8,128)(2,1)S(1)}, bf16[1,128,768]{2,1,0:T(8,128)(2,1)}, u32[]{:S(2)}) copy-start(bf16[1,128,768]{2,1,0:T(8,128)(2,1)} %param.11) | copy-start | bytes 589828
  6.0 16.0 %copy-start.9 = (bf16[1,128,768]{2,1,0:T(8,128)(2,1)S(1)}, bf16[1,128,768]{2,1,0:T(8,128)(2,1)}, u32[]{:S(2)}) copy-start(bf16[1,128,768]{2,1,0:T(8,128)(2,1)} %param.12) | copy-start | bytes 589828
  6.0 16.0 %copy-start.10 = (bf16[1,128,768]{2,1,0:T(8,128)(2,1)S(1)}, bf16[1,128,768]{2,1,0:T(8,128)(2,1)}, u32[]{:S(2)}) copy-start(bf16[1,128,768]{2,1,0:T(8,128)(2,1)} %param.13) | copy-start | bytes 589828
  6.0 116.5 %all-to-all-start = ((bf16[32,8,4096]{2,1,0:T(8,128)(2,1)}), bf16[32,8,4096]{2,1,0:T(8,128)(2,1)S(1)}, u32[]{:S(2)}, u32[]{:S(2)}) async-start(bf16[32,8,4096]{2,1,0:T(8,128)(2,1)} %bitcast.45), calls=%async_computation | async-start | bytes 4194304 | tf_op jit(solution)/shard_map/all_to_all | solution.py:241
  22.1 13.9 %copy-start.11 = (bf16[3,128,768]{2,1,0:T(8,128)(2,1)}, bf16[3,128,768]{2,1,0:T(8,128)(2,1)S(1)}, u32[]{:S(2)}) copy-start(bf16[3,128,768]{2,1,0:T(8,128)(2,1)S(1)} %constant_dynamic-update-slice_fusion.refs_1_) | copy-start | bytes 1769476
  22.1 19.8 %collective-permute-start.7 = (bf16[3,128,768]{2,1,0:T(8,128)(2,1)S(1)}, bf16[3,128,768]{2,1,0:T(8,128)(2,1)S(1)}, u32[]{:S(2)}, u32[]{:S(2)}) collective-permute-start(bf16[3,128,768]{2,1,0:T(8,128)(2,1)S(1)} %constant_dynamic-update-slice_fusion.refs_1_), channel_id=1, source_target_pairs={{0,64},{32,96},{64,0},{96,32},{128,192},{160,224},{192,128},{224,1... | collective-permute-start | bytes 1769480 | tf_op jit(solution)/shard_map/ppermute | solution.py:224
  26.6 19.6 %collective-permute-start.5 = (bf16[3,128,768]{2,1,0:T(8,128)(2,1)S(1)}, bf16[3,128,768]{2,1,0:T(8,128)(2,1)S(1)}, u32[]{:S(2)}, u32[]{:S(2)}) collective-permute-start(bf16[3,128,768]{2,1,0:T(8,128)(2,1)S(1)} %constant_dynamic-update-slice_fusion.refs_1_), channel_id=1, source_target_pairs={{0,384},{32,416},{64,448},{96,480},{128,0},{160,32},{192,64},{224,... | collective-permute-start | bytes 1769480 | tf_op jit(solution)/shard_map/ppermute | solution.py:224
  31.0 17.7 %collective-permute-start.3 = (bf16[3,128,768]{2,1,0:T(8,128)(2,1)S(1)}, bf16[3,128,768]{2,1,0:T(8,128)(2,1)S(1)}, u32[]{:S(2)}, u32[]{:S(2)}) collective-permute-start(bf16[3,128,768]{2,1,0:T(8,128)(2,1)S(1)} %constant_dynamic-update-slice_fusion.refs_1_), channel_id=1, source_target_pairs={{0,256},{32,288},{64,320},{96,352},{128,384},{160,416},{192,448},{... | collective-permute-start | bytes 1769480 | tf_op jit(solution)/shard_map/ppermute | solution.py:224
  33.4 31.1 %collective-permute-start.1 = (bf16[3,128,768]{2,1,0:T(8,128)(2,1)S(1)}, bf16[3,128,768]{2,1,0:T(8,128)(2,1)}, u32[]{:S(2)}, u32[]{:S(2)}) collective-permute-start(bf16[3,128,768]{2,1,0:T(8,128)(2,1)S(1)} %constant_dynamic-update-slice_fusion.refs_1_), channel_id=1, source_target_pairs={{0,128},{32,160},{64,192},{96,224},{128,256},{160,288},{192,320},{... | collective-permute-start | bytes 1769480 | tf_op jit(solution)/shard_map/ppermute | solution.py:224
  36.0 32.6 %collective-permute-start = (bf16[3,128,768]{2,1,0:T(8,128)(2,1)S(1)}, bf16[3,128,768]{2,1,0:T(8,128)(2,1)S(1)}, u32[]{:S(2)}, u32[]{:S(2)}) collective-permute-start(bf16[3,128,768]{2,1,0:T(8,128)(2,1)S(1)} %constant_dynamic-update-slice_fusion.refs_1_), channel_id=1, source_target_pairs={{0,32},{32,0},{64,96},{96,64},{128,160},{160,128},{192,224},{224,1... | collective-permute-start | bytes 1769480 | tf_op jit(solution)/shard_map/ppermute | solution.py:224
  41.8 26.8 %copy-start.12 = (bf16[3,128,768]{2,1,0:T(8,128)(2,1)}, bf16[3,128,768]{2,1,0:T(8,128)(2,1)S(1)}, u32[]{:S(2)}) copy-start(bf16[3,128,768]{2,1,0:T(8,128)(2,1)S(1)} %collective-permute-done.7.refs_9_) | copy-start | bytes 1769476
  41.8 28.7 %collective-permute-start.13 = (bf16[3,128,768]{2,1,0:T(8,128)(2,1)S(1)}, bf16[3,128,768]{2,1,0:T(8,128)(2,1)}, u32[]{:S(2)}, u32[]{:S(2)}) collective-permute-start(bf16[3,128,768]{2,1,0:T(8,128)(2,1)S(1)} %collective-permute-done.7.refs_9_), channel_id=1, source_target_pairs={{0,384},{32,416},{64,448},{96,480},{128,0},{160,32},{192,64},{224,... | collective-permute-start | bytes 1769480 | tf_op jit(solution)/shard_map/ppermute | solution.py:224
  46.2 43.9 %copy-start.13 = (bf16[3,128,768]{2,1,0:T(8,128)(2,1)}, bf16[3,128,768]{2,1,0:T(8,128)(2,1)S(1)}, u32[]{:S(2)}) copy-start(bf16[3,128,768]{2,1,0:T(8,128)(2,1)S(1)} %collective-permute-done.5.refs_7_) | copy-start | bytes 1769476
  46.2 38.2 %collective-permute-start.11 = (bf16[3,128,768]{2,1,0:T(8,128)(2,1)S(1)}, bf16[3,128,768]{2,1,0:T(8,128)(2,1)}, u32[]{:S(2)}, u32[]{:S(2)}) collective-permute-start(bf16[3,128,768]{2,1,0:T(8,128)(2,1)S(1)} %collective-permute-done.7.refs_9_), channel_id=1, source_target_pairs={{0,256},{32,288},{64,320},{96,352},{128,384},{160,416},{192,448},{... | collective-permute-start | bytes 1769480 | tf_op jit(solution)/shard_map/ppermute | solution.py:224
  48.7 73.8 %copy-start.14 = (bf16[3,128,768]{2,1,0:T(8,128)(2,1)}, bf16[3,128,768]{2,1,0:T(8,128)(2,1)S(1)}, u32[]{:S(2)}) copy-start(bf16[3,128,768]{2,1,0:T(8,128)(2,1)S(1)} %collective-permute-done.3.refs_5_) | copy-start | bytes 1769476
  48.7 38.9 %collective-permute-start.9 = (bf16[3,128,768]{2,1,0:T(8,128)(2,1)S(1)}, bf16[3,128,768]{2,1,0:T(8,128)(2,1)}, u32[]{:S(2)}, u32[]{:S(2)}) collective-permute-start(bf16[3,128,768]{2,1,0:T(8,128)(2,1)S(1)} %collective-permute-done.7.refs_9_), channel_id=1, source_target_pairs={{0,128},{32,160},{64,192},{96,224},{128,256},{160,288},{192,320},{... | collective-permute-start | bytes 1769480 | tf_op jit(solution)/shard_map/ppermute | solution.py:224
  64.6 25.5 %collective-permute-start.8 = (bf16[3,128,768]{2,1,0:T(8,128)(2,1)S(1)}, bf16[3,128,768]{2,1,0:T(8,128)(2,1)S(1)}, u32[]{:S(2)}, u32[]{:S(2)}) collective-permute-start(bf16[3,128,768]{2,1,0:T(8,128)(2,1)S(1)} %collective-permute-done.7.refs_9_), channel_id=1, source_target_pairs={{0,32},{32,0},{64,96},{96,64},{128,160},{160,128},{192,224},{224,1... | collective-permute-start | bytes 1769480 | tf_op jit(solution)/shard_map/ppermute | solution.py:224
  68.6 23.4 %copy-start.15 = (bf16[3,128,768]{2,1,0:T(8,128)(2,1)}, bf16[3,128,768]{2,1,0:T(8,128)(2,1)S(1)}, u32[]{:S(2)}) copy-start(bf16[3,128,768]{2,1,0:T(8,128)(2,1)S(1)} %collective-permute-done.refs_2_) | copy-start | bytes 1769476
  68.6 23.4 %collective-permute-start.6 = (bf16[3,128,768]{2,1,0:T(8,128)(2,1)S(1)}, bf16[3,128,768]{2,1,0:T(8,128)(2,1)S(1)}, u32[]{:S(2)}, u32[]{:S(2)}) collective-permute-start(bf16[3,128,768]{2,1,0:T(8,128)(2,1)S(1)} %collective-permute-done.5.refs_7_), channel_id=1, source_target_pairs={{0,32},{32,0},{64,96},{96,64},{128,160},{160,128},{192,224},{224,1... | collective-permute-start | bytes 1769480 | tf_op jit(solution)/shard_map/ppermute | solution.py:224
  70.6 24.0 %collective-permute-start.4 = (bf16[3,128,768]{2,1,0:T(8,128)(2,1)S(1)}, bf16[3,128,768]{2,1,0:T(8,128)(2,1)}, u32[]{:S(2)}, u32[]{:S(2)}) collective-permute-start(bf16[3,128,768]{2,1,0:T(8,128)(2,1)S(1)} %collective-permute-done.3.refs_5_), channel_id=1, source_target_pairs={{0,32},{32,0},{64,96},{96,64},{128,160},{160,128},{192,224},{224,1... | collective-permute-start | bytes 1769480 | tf_op jit(solution)/shard_map/ppermute | solution.py:224
  84.4 10.2 %collective-permute-start.2 = (bf16[3,128,768]{2,1,0:T(8,128)(2,1)}, bf16[3,128,768]{2,1,0:T(8,128)(2,1)}, u32[]{:S(2)}, u32[]{:S(2)}) collective-permute-start(bf16[3,128,768]{2,1,0:T(8,128)(2,1)} %collective-permute-done.1.refs_3_), channel_id=1, source_target_pairs={{0,32},{32,0},{64,96},{96,64},{128,160},{160,128},{192,224},{224,1... | collective-permute-start | bytes 1769480 | tf_op jit(solution)/shard_map/ppermute | solution.py:224
  87.6 7.0 %collective-permute-start.14 = (bf16[3,128,768]{2,1,0:T(8,128)(2,1)}, bf16[3,128,768]{2,1,0:T(8,128)(2,1)}, u32[]{:S(2)}, u32[]{:S(2)}) collective-permute-start(bf16[3,128,768]{2,1,0:T(8,128)(2,1)} %collective-permute-done.13.refs_15_), channel_id=1, source_target_pairs={{0,32},{32,0},{64,96},{96,64},{128,160},{160,128},{192,224},{224,1... | collective-permute-start | bytes 1769480 | tf_op jit(solution)/shard_map/ppermute | solution.py:224
  90.1 4.4 %copy-start.16 = (bf16[3,128,768]{2,1,0:T(8,128)(2,1)}, bf16[3,128,768]{2,1,0:T(8,128)(2,1)S(1)}, u32[]{:S(2)}) copy-start(bf16[3,128,768]{2,1,0:T(8,128)(2,1)S(1)} %collective-permute-done.8.refs_10_) | copy-start | bytes 1769476
  90.1 4.5 %collective-permute-start.12 = (bf16[3,128,768]{2,1,0:T(8,128)(2,1)}, bf16[3,128,768]{2,1,0:T(8,128)(2,1)}, u32[]{:S(2)}, u32[]{:S(2)}) collective-permute-start(bf16[3,128,768]{2,1,0:T(8,128)(2,1)} %collective-permute-done.11.refs_13_), channel_id=1, source_target_pairs={{0,32},{32,0},{64,96},{96,64},{128,160},{160,128},{192,224},{224,1... | collective-permute-start | bytes 1769480 | tf_op jit(solution)/shard_map/ppermute | solution.py:224
  92.0 2.4 %copy-start.17 = (bf16[3,128,768]{2,1,0:T(8,128)(2,1)}, bf16[3,128,768]{2,1,0:T(8,128)(2,1)S(1)}, u32[]{:S(2)}) copy-start(bf16[3,128,768]{2,1,0:T(8,128)(2,1)S(1)} %collective-permute-done.6.refs_8_) | copy-start | bytes 1769476
  92.1 4.4 %collective-permute-start.10 = (bf16[3,128,768]{2,1,0:T(8,128)(2,1)}, bf16[3,128,768]{2,1,0:T(8,128)(2,1)}, u32[]{:S(2)}, u32[]{:S(2)}) collective-permute-start(bf16[3,128,768]{2,1,0:T(8,128)(2,1)} %collective-permute-done.9.refs_11_), channel_id=1, source_target_pairs={{0,32},{32,0},{64,96},{96,64},{128,160},{160,128},{192,224},{224,1... | collective-permute-start | bytes 1769480 | tf_op jit(solution)/shard_map/ppermute | solution.py:224
  122.5 10.0 %copy-start = (bf16[32,8,4096]{2,1,0:T(8,128)(2,1)}, bf16[32,8,4096]{2,1,0:T(8,128)(2,1)S(1)}, u32[]{:S(2)}) copy-start(bf16[32,8,4096]{2,1,0:T(8,128)(2,1)S(1)} %all-to-all-done) | copy-start | bytes 6291460
  132.5 103.4 %all-to-all-start.1 = ((bf16[32,8,4096]{2,1,0:T(8,128)(2,1)}), bf16[32,8,4096]{2,1,0:T(8,128)(2,1)S(1)}, u32[]{:S(2)}, u32[]{:S(2)}) async-start(bf16[32,8,4096]{2,1,0:T(8,128)(2,1)} %bitcast.44), calls=%async_computation.1 | async-start | bytes 4194304 | tf_op jit(solution)/shard_map/all_to_all | solution.py:241
  136.3 1.6 copy-start.1
  137.9 12.2 %copy-start.2 = (bf16[32,8,4096]{2,1,0:T(8,128)(2,1)S(1)}, bf16[32,8,4096]{2,1,0:T(8,128)(2,1)}, u32[]{:S(2)}) copy-start(bf16[32,8,4096]{2,1,0:T(8,128)(2,1)} %copy-done) | copy-start | bytes 6291460
  139.9 7.2 %collective-permute-start.15 = (bf16[8,128,768]{2,1,0:T(8,128)(2,1)S(1)}, bf16[8,128,768]{2,1,0:T(8,128)(2,1)S(1)}, u32[]{:S(2)}, u32[]{:S(2)}) collective-permute-start(bf16[8,128,768]{2,1,0:T(8,128)(2,1)S(1)} %get-tuple-element.36), channel_id=1, source_target_pairs={{0,32},{32,0},{64,96},{96,64},{128,160},{160,128},{192,224},{224,1... | collective-permute-start | bytes 4718600 | tf_op jit(solution)/shard_map/ppermute | solution.py:224
  142.5 5.3 %collective-permute-start.16 = (bf16[8,128,768]{2,1,0:T(8,128)(2,1)S(1)}, bf16[8,128,768]{2,1,0:T(8,128)(2,1)S(1)}, u32[]{:S(2)}, u32[]{:S(2)}) collective-permute-start(bf16[8,128,768]{2,1,0:T(8,128)(2,1)S(1)} %get-tuple-element.37), channel_id=1, source_target_pairs={{0,32},{32,0},{64,96},{96,64},{128,160},{160,128},{192,224},{224,1... | collective-permute-start | bytes 4718600 | tf_op jit(solution)/shard_map/ppermute | solution.py:224
  144.4 5.6 %collective-permute-start.17 = (bf16[8,128,768]{2,1,0:T(8,128)(2,1)S(1)}, bf16[8,128,768]{2,1,0:T(8,128)(2,1)S(1)}, u32[]{:S(2)}, u32[]{:S(2)}) collective-permute-start(bf16[8,128,768]{2,1,0:T(8,128)(2,1)S(1)} %get-tuple-element.38), channel_id=1, source_target_pairs={{0,32},{32,0},{64,96},{96,64},{128,160},{160,128},{192,224},{224,1... | collective-permute-start | bytes 4718600 | tf_op jit(solution)/shard_map/ppermute | solution.py:224
  152.2 15.6 %collective-permute-start.18 = (bf16[2,128,768]{2,1,0:T(8,128)(2,1)S(1)}, bf16[2,128,768]{2,1,0:T(8,128)(2,1)S(1)}, u32[]{:S(2)}, u32[]{:S(2)}) collective-permute-start(bf16[2,128,768]{2,1,0:T(8,128)(2,1)S(1)} %get-tuple-element.40), channel_id=1, source_target_pairs={{0,128},{32,160},{64,192},{96,224},{128,256},{160,288},{192,320},{... | collective-permute-start | bytes 1179656 | tf_op jit(solution)/shard_map/ppermute | solution.py:224
  155.3 19.9 %collective-permute-start.19 = (bf16[2,128,768]{2,1,0:T(8,128)(2,1)S(1)}, bf16[2,128,768]{2,1,0:T(8,128)(2,1)S(1)}, u32[]{:S(2)}, u32[]{:S(2)}) collective-permute-start(bf16[2,128,768]{2,1,0:T(8,128)(2,1)S(1)} %get-tuple-element.41), channel_id=1, source_target_pairs={{0,256},{32,288},{64,320},{96,352},{128,384},{160,416},{192,448},{... | collective-permute-start | bytes 1179656 | tf_op jit(solution)/shard_map/ppermute | solution.py:224
  159.7 17.4 %collective-permute-start.20 = (bf16[2,128,768]{2,1,0:T(8,128)(2,1)S(1)}, bf16[2,128,768]{2,1,0:T(8,128)(2,1)S(1)}, u32[]{:S(2)}, u32[]{:S(2)}) collective-permute-start(bf16[2,128,768]{2,1,0:T(8,128)(2,1)S(1)} %get-tuple-element.42), channel_id=1, source_target_pairs={{0,384},{32,416},{64,448},{96,480},{128,0},{160,32},{192,64},{224,... | collective-permute-start | bytes 1179656 | tf_op jit(solution)/shard_map/ppermute | solution.py:224
  162.7 22.0 %collective-permute-start.22 = (bf16[2,128,768]{2,1,0:T(8,128)(2,1)S(1)}, bf16[2,128,768]{2,1,0:T(8,128)(2,1)S(1)}, u32[]{:S(2)}, u32[]{:S(2)}) collective-permute-start(bf16[2,128,768]{2,1,0:T(8,128)(2,1)S(1)} %get-tuple-element.44), channel_id=1, source_target_pairs={{0,128},{32,160},{64,192},{96,224},{128,256},{160,288},{192,320},{... | collective-permute-start | bytes 1179656 | tf_op jit(solution)/shard_map/ppermute | solution.py:224
  165.0 27.1 %collective-permute-start.23 = (bf16[2,128,768]{2,1,0:T(8,128)(2,1)S(1)}, bf16[2,128,768]{2,1,0:T(8,128)(2,1)S(1)}, u32[]{:S(2)}, u32[]{:S(2)}) collective-permute-start(bf16[2,128,768]{2,1,0:T(8,128)(2,1)S(1)} %get-tuple-element.45), channel_id=1, source_target_pairs={{0,256},{32,288},{64,320},{96,352},{128,384},{160,416},{192,448},{... | collective-permute-start | bytes 1179656 | tf_op jit(solution)/shard_map/ppermute | solution.py:224
  167.7 28.8 %collective-permute-start.24 = (bf16[2,128,768]{2,1,0:T(8,128)(2,1)S(1)}, bf16[2,128,768]{2,1,0:T(8,128)(2,1)S(1)}, u32[]{:S(2)}, u32[]{:S(2)}) collective-permute-start(bf16[2,128,768]{2,1,0:T(8,128)(2,1)S(1)} %get-tuple-element.46), channel_id=1, source_target_pairs={{0,384},{32,416},{64,448},{96,480},{128,0},{160,32},{192,64},{224,... | collective-permute-start | bytes 1179656 | tf_op jit(solution)/shard_map/ppermute | solution.py:224
  175.2 26.3 %collective-permute-start.26 = (bf16[2,128,768]{2,1,0:T(8,128)(2,1)S(1)}, bf16[2,128,768]{2,1,0:T(8,128)(2,1)S(1)}, u32[]{:S(2)}, u32[]{:S(2)}) collective-permute-start(bf16[2,128,768]{2,1,0:T(8,128)(2,1)S(1)} %get-tuple-element.48), channel_id=1, source_target_pairs={{0,128},{32,160},{64,192},{96,224},{128,256},{160,288},{192,320},{... | collective-permute-start | bytes 1179656 | tf_op jit(solution)/shard_map/ppermute | solution.py:224
  177.1 31.8 %collective-permute-start.27 = (bf16[2,128,768]{2,1,0:T(8,128)(2,1)S(1)}, bf16[2,128,768]{2,1,0:T(8,128)(2,1)S(1)}, u32[]{:S(2)}, u32[]{:S(2)}) collective-permute-start(bf16[2,128,768]{2,1,0:T(8,128)(2,1)S(1)} %get-tuple-element.49), channel_id=1, source_target_pairs={{0,256},{32,288},{64,320},{96,352},{128,384},{160,416},{192,448},{... | collective-permute-start | bytes 1179656 | tf_op jit(solution)/shard_map/ppermute | solution.py:224
  184.7 25.4 %collective-permute-start.28 = (bf16[2,128,768]{2,1,0:T(8,128)(2,1)S(1)}, bf16[2,128,768]{2,1,0:T(8,128)(2,1)S(1)}, u32[]{:S(2)}, u32[]{:S(2)}) collective-permute-start(bf16[2,128,768]{2,1,0:T(8,128)(2,1)S(1)} %get-tuple-element.50), channel_id=1, source_target_pairs={{0,384},{32,416},{64,448},{96,480},{128,0},{160,32},{192,64},{224,... | collective-permute-start | bytes 1179656 | tf_op jit(solution)/shard_map/ppermute | solution.py:224
  192.1 22.8 %collective-permute-start.21 = (bf16[128,768]{1,0:T(8,128)(2,1)S(1)}, bf16[128,768]{1,0:T(8,128)(2,1)S(1)}, u32[]{:S(2)}, u32[]{:S(2)}) collective-permute-start(bf16[128,768]{1,0:T(8,128)(2,1)S(1)} %fusion.6), channel_id=1, source_target_pairs={{0,64},{32,96},{64,0},{96,32},{128,192},{160,224},{192,128},{224,1... | collective-permute-start | bytes 589832 | tf_op jit(solution)/shard_map/ppermute | solution.py:224
  196.8 18.9 %collective-permute-start.25 = (bf16[128,768]{1,0:T(8,128)(2,1)S(1)}, bf16[128,768]{1,0:T(8,128)(2,1)S(1)}, u32[]{:S(2)}, u32[]{:S(2)}) collective-permute-start(bf16[128,768]{1,0:T(8,128)(2,1)S(1)} %fusion.7), channel_id=1, source_target_pairs={{0,64},{32,96},{64,0},{96,32},{128,192},{160,224},{192,128},{224,1... | collective-permute-start | bytes 589832 | tf_op jit(solution)/shard_map/ppermute | solution.py:224
  210.3 25.6 %copy-start.6 = (s32[128,1]{0,1:T(1,128)S(1)}, s32[128,1]{0,1:T(1,128)}, u32[]{:S(2)}) copy-start(s32[128,1]{0,1:T(1,128)} %param.9) | copy-start | bytes 1540
  210.3 8.5 %collective-permute-start.29 = (bf16[128,768]{1,0:T(8,128)(2,1)S(1)}, bf16[128,768]{1,0:T(8,128)(2,1)S(1)}, u32[]{:S(2)}, u32[]{:S(2)}) collective-permute-start(bf16[128,768]{1,0:T(8,128)(2,1)S(1)} %fusion.8), channel_id=1, source_target_pairs={{0,64},{32,96},{64,0},{96,32},{128,192},{160,224},{192,128},{224,1... | collective-permute-start | bytes 589832 | tf_op jit(solution)/shard_map/ppermute | solution.py:224

commit v6 on v5

--- a/solution.py
+++ b/solution.py
@@ -30,14 +30,20 @@
     return jnp.sum(jnp.where(down == along, row, 0.0), axis=1, keepdims=True)
 
 
-def place_kernel(experts, capacity, ids_ref, unit_ref, tok_ref, cot_ref, send_out, pick_ref, send, sems):
+def place_kernel(experts, capacity, ids_in, unit_in, tok_in, cot_in, send_out, pick_ref, *scratch):
+    ids_ref, unit_ref, tok_ref, cot_ref, send, in_sems, out_sems = scratch
     tok, width = tok_ref.shape
-    slots, parts = send.shape[0], sems.shape[0]
-    ids = ids_ref[...]
+    slots, parts = send.shape[0], out_sems.shape[0]
+    pairs = ((ids_in, ids_ref), (unit_in, unit_ref), (tok_in, tok_ref), (cot_in, cot_ref))
+    loads = [pltpu.make_async_copy(a, b, in_sems.at[n]) for n, (a, b) in enumerate(pairs)]
+    for load in loads:
+        load.start()
     labels = lax.broadcasted_iota(jnp.int32, (experts, tok), 0)
     down = lax.broadcasted_iota(jnp.int32, (tok, tok), 0)
     along = lax.broadcasted_iota(jnp.int32, (tok, tok), 1)
     before = jnp.where(down < along, 1.0, 0.0).astype(BF)
+    loads[0].wait()
+    ids = ids_ref[...]
     hot = jnp.where(ids == labels, 1.0, 0.0)
     ranks = mm(hot.astype(BF), before, NN)
     rank = jnp.sum(ranks * hot, axis=0, keepdims=True).astype(jnp.int32)
@@ -45,7 +51,10 @@
     places = lax.broadcasted_iota(jnp.int32, (slots, tok), 0)
     pick = jnp.where(slot == places, 1.0, 0.0).astype(BF)
     pick_ref[...] = pick
+    loads[1].wait()
     scale = column(unit_ref[...].astype(F32) / 256.0)
+    loads[2].wait()
+    loads[3].wait()
     grads = (scale * cot_ref[...].astype(F32)).astype(BF)
     step = slots // parts
     stores = []
@@ -54,29 +63,36 @@
         some = pick[n * step : (n + 1) * step]
         send[cut, :width] = mm(some, tok_ref[...], NN).astype(BF)
         send[cut, width:] = mm(some, grads, NN).astype(BF)
-        stores.append(pltpu.make_async_copy(send.at[cut], send_out.at[cut], sems.at[n]))
+        stores.append(pltpu.make_async_copy(send.at[cut], send_out.at[cut], out_sems.at[n]))
         stores[n].start()
     for copy in stores:
         copy.wait()
 
 
-def place_call(experts, capacity, ids, units, tokens, cotangent):
+def place_call(experts, capacity, *args):
+    ids, _, tokens, _ = args
     tok, width = tokens.shape
     slots = experts * capacity
-    parts = 2
+    parts = 4
     shape = jax.ShapeDtypeStruct
     far, near = pl.BlockSpec(memory_space=pltpu.HBM), pl.BlockSpec(memory_space=VM)
     return pl.pallas_call(
         lambda *refs: place_kernel(experts, capacity, *refs),
-        in_specs=[near] * 4,
+        in_specs=[far] * 4,
         out_specs=[far, near],
         out_shape=[pltpu.HBM((slots, 2 * width), BF), shape((slots, tok), BF)],
-        scratch_shapes=[VM((slots, 2 * width), BF), pltpu.SemaphoreType.DMA((parts,))],
+        scratch_shapes=[
+            *[VM(ids.shape, jnp.int32)] * 2,
+            *[VM((tok, width), BF)] * 2,
+            VM((slots, 2 * width), BF),
+            pltpu.SemaphoreType.DMA((4,)),
+            pltpu.SemaphoreType.DMA((parts,)),
+        ],
         compiler_params=params(24),
         cost_estimate=pl.CostEstimate(
             flops=4 * tok * slots * width, bytes_accessed=12 * tok * width, transcendentals=0
         ),
-    )(ids, units, tokens, cotangent)
+    )(*[pin(a, pltpu.HBM) for a in args])
 
 
 def expert_kernel(order_ref, *refs):
@@ -181,15 +197,34 @@
             done += size
 
 
-def finish_kernel(pick_ref, unit_ref, got_ref, mixed_ref, back_ref):
-    width = mixed_ref.shape[1]
+def finish_kernel(pick_ref, unit_ref, got_ref, mixed_out, back_out, mixed, back, sems):
+    width = mixed.shape[1]
     scale = column(unit_ref[...].astype(F32) / 256.0)
-    step = width // 4
-    for c in range(4):
-        part = pl.ds(c * step, step)
-        mixed_ref[:, part] = (scale * mm(pick_ref[...], got_ref[:, part], TN)).astype(BF)
-        other = pl.ds(width + c * step, step)
-        back_ref[:, part] = mm(pick_ref[...], got_ref[:, other], TN).astype(BF)
+    mixed[...] = (scale * mm(pick_ref[...], got_ref[:, :width], TN)).astype(BF)
+    first = pltpu.make_async_copy(mixed, mixed_out, sems.at[0])
+    first.start()
+    back[...] = mm(pick_ref[...], got_ref[:, width:], TN).astype(BF)
+    second = pltpu.make_async_copy(back, back_out, sems.at[1])
+    second.start()
+    first.wait()
+    second.wait()
+
+
+def finish_call(pick, units, got):
+    slots, tok = pick.shape
+    width = got.shape[1] // 2
+    far, near = pl.BlockSpec(memory_space=pltpu.HBM), pl.BlockSpec(memory_space=VM)
+    return pl.pallas_call(
+        finish_kernel,
+        in_specs=[near] * 3,
+        out_specs=[far] * 2,
+        out_shape=[pltpu.HBM((tok, width), BF)] * 2,
+        scratch_shapes=[*[VM((tok, width), BF)] * 2, pltpu.SemaphoreType.DMA((2,))],
+        compiler_params=params(24),
+        cost_estimate=pl.CostEstimate(
+            flops=4 * tok * slots * width, bytes_accessed=12 * tok * width, transcendentals=0
+        ),
+    )(pick, units, got)
 
 
 def call(kernel, outs, mib, flops, args, smem=0):
@@ -275,13 +310,7 @@
         cross = permute(total[1].astype(BF), lambda i: i ^ 2)
         grads.append((total[0] + cross.astype(F32))[None])
 
-    mixed, grad_tokens = call(
-        finish_kernel,
-        [shape((tok, width), BF)] * 2,
-        24,
-        4 * tok * slots * width,
-        (pick, scales, got),
-    )
+    mixed, grad_tokens = finish_call(pick, scales, got)
     return (mixed, grad_tokens, *grads)
 
 

time: 239 us -> 236 us (0.987)
  local copies, waits for them, and re-layouts: 5.14 us -> 1.76 us
    unnamed x38 -> x30, local copies, waits for them, and re-layouts: 5.06 us -> 1.68 us
    pallas_call x3 -> x2, Pallas kernels: 5.46 us -> 4.05 us  [call(): pl.pallas_call(kernel, out_shape=outs, in_specs=in_specs, out_specs=[pl.B...]
where the time goes in v6:
time: 236 us; the launch traced here: 235 us
  starting transfers between devices  128 us (54%)
  waiting for transfers between devices  82.1 us (35%)
  Pallas kernels  18.2 us (8%)
  other arithmetic  2.99 us (1%)
    ppermute x30, starting transfers between devices, permute(): return lax.ppermute(a, 'dp', [(i, to(i)) for i in range(groups)])  109 us
    all_to_all x2, waiting for transfers between devices, exchange(): got = lax.all_to_all(cut, 'expert', split_axis=0, concat_axis=0, tiled=True)  42.3 us
    ppermute x30, waiting for transfers between devices, permute(): return lax.ppermute(a, 'dp', [(i, to(i)) for i in range(groups)])  39.8 us
    all_to_all x2, starting transfers between devices, exchange(): got = lax.all_to_all(cut, 'expert', split_axis=0, concat_axis=0, tiled=True)  19.8 us
    pallas_call x1, Pallas kernels, experts_call(): pl.pallas_call(expert_kernel, in_specs=[pl.BlockSpec(memory_space=pltpu.S...  9.93 us
  transfers between devices with their start and end apart: 32, of which 15 were waited for; matrix products, arithmetic and copies ran while one was open for 1% of the time, Pallas kernels for 2%

profile of v6, /device:TPU:33, one launch (start us, length us, event | category | flops | bytes accessed | tf_op | source)
XLA Modules:
  0.0 235.0 jit_solution(18342043675190327472)
XLA Ops:
  0.6 2.9 %shard_map.110 = (bf16[256,4096]{1,0:T(8,128)(2,1)}, bf16[256,128]{1,0:T(8,128)(2,1)S(1)}) custom-call(s32[1,128]{1,0:T(1,128)} %bitcast.45, s32[1,128]{1,0:T(1,128)} %bitcast.41, bf16[128,2048]{1,0:T(8,128)(2,1)} %refs_2_.1, bf16[128,2048]{1,0:T(8,128)(2,1)} %refs_3_.1), custom_call_target="tpu_custom_call" | custom-call | flops 268435456 | bytes 3145728 | tf_op jit(solution)/shard_map/pallas_call | solution.py:79
  3.6 0.0 copy-start.4
  3.6 0.0 copy-start.5
  3.6 0.0 copy-start.6
  3.6 16.0 %all-to-all-start = ((bf16[32,8,4096]{2,1,0:T(8,128)(2,1)}), bf16[32,8,4096]{2,1,0:T(8,128)(2,1)S(1)}, u32[]{:S(2)}, u32[]{:S(2)}) async-start(bf16[32,8,4096]{2,1,0:T(8,128)(2,1)} %bitcast.44), calls=%async_computation | async-start | bytes 4194304 | tf_op jit(solution)/shard_map/all_to_all | solution.py:276
  19.7 4.5 %collective-permute-start.7 = (bf16[3,128,768]{2,1,0:T(8,128)(2,1)S(1)}, bf16[3,128,768]{2,1,0:T(8,128)(2,1)S(1)}, u32[]{:S(2)}, u32[]{:S(2)}) collective-permute-start(bf16[3,128,768]{2,1,0:T(8,128)(2,1)S(1)} %constant_dynamic-update-slice_fusion.refs_1_), channel_id=1, source_target_pairs={{0,64},{32,96},{64,0},{96,32},{128,192},{160,224},{192,128},{224,1... | collective-permute-start | bytes 1769480 | tf_op jit(solution)/shard_map/ppermute | solution.py:259
  24.2 4.4 %collective-permute-start.5 = (bf16[3,128,768]{2,1,0:T(8,128)(2,1)S(1)}, bf16[3,128,768]{2,1,0:T(8,128)(2,1)S(1)}, u32[]{:S(2)}, u32[]{:S(2)}) collective-permute-start(bf16[3,128,768]{2,1,0:T(8,128)(2,1)S(1)} %constant_dynamic-update-slice_fusion.refs_1_), channel_id=1, source_target_pairs={{0,384},{32,416},{64,448},{96,480},{128,0},{160,32},{192,64},{224,... | collective-permute-start | bytes 1769480 | tf_op jit(solution)/shard_map/ppermute | solution.py:259
  28.6 2.4 %collective-permute-start.3 = (bf16[3,128,768]{2,1,0:T(8,128)(2,1)S(1)}, bf16[3,128,768]{2,1,0:T(8,128)(2,1)S(1)}, u32[]{:S(2)}, u32[]{:S(2)}) collective-permute-start(bf16[3,128,768]{2,1,0:T(8,128)(2,1)S(1)} %constant_dynamic-update-slice_fusion.refs_1_), channel_id=1, source_target_pairs={{0,256},{32,288},{64,320},{96,352},{128,384},{160,416},{192,448},{... | collective-permute-start | bytes 1769480 | tf_op jit(solution)/shard_map/ppermute | solution.py:259
  31.0 2.5 %collective-permute-start.1 = (bf16[3,128,768]{2,1,0:T(8,128)(2,1)S(1)}, bf16[3,128,768]{2,1,0:T(8,128)(2,1)}, u32[]{:S(2)}, u32[]{:S(2)}) collective-permute-start(bf16[3,128,768]{2,1,0:T(8,128)(2,1)S(1)} %constant_dynamic-update-slice_fusion.refs_1_), channel_id=1, source_target_pairs={{0,128},{32,160},{64,192},{96,224},{128,256},{160,288},{192,320},{... | collective-permute-start | bytes 1769480 | tf_op jit(solution)/shard_map/ppermute | solution.py:259
  33.6 4.3 %collective-permute-start = (bf16[3,128,768]{2,1,0:T(8,128)(2,1)S(1)}, bf16[3,128,768]{2,1,0:T(8,128)(2,1)S(1)}, u32[]{:S(2)}, u32[]{:S(2)}) collective-permute-start(bf16[3,128,768]{2,1,0:T(8,128)(2,1)S(1)} %constant_dynamic-update-slice_fusion.refs_1_), channel_id=1, source_target_pairs={{0,32},{32,0},{64,96},{96,64},{128,160},{160,128},{192,224},{224,1... | collective-permute-start | bytes 1769480 | tf_op jit(solution)/shard_map/ppermute | solution.py:259
  37.8 1.6 collective-permute-done.7.refs_9_
  39.4 4.4 %collective-permute-start.13 = (bf16[3,128,768]{2,1,0:T(8,128)(2,1)S(1)}, bf16[3,128,768]{2,1,0:T(8,128)(2,1)}, u32[]{:S(2)}, u32[]{:S(2)}) collective-permute-start(bf16[3,128,768]{2,1,0:T(8,128)(2,1)S(1)} %collective-permute-done.7.refs_9_), channel_id=1, source_target_pairs={{0,384},{32,416},{64,448},{96,480},{128,0},{160,32},{192,64},{224,... | collective-permute-start | bytes 1769480 | tf_op jit(solution)/shard_map/ppermute | solution.py:259
  43.8 2.4 %collective-permute-start.11 = (bf16[3,128,768]{2,1,0:T(8,128)(2,1)S(1)}, bf16[3,128,768]{2,1,0:T(8,128)(2,1)}, u32[]{:S(2)}, u32[]{:S(2)}) collective-permute-start(bf16[3,128,768]{2,1,0:T(8,128)(2,1)S(1)} %collective-permute-done.7.refs_9_), channel_id=1, source_target_pairs={{0,256},{32,288},{64,320},{96,352},{128,384},{160,416},{192,448},{... | collective-permute-start | bytes 1769480 | tf_op jit(solution)/shard_map/ppermute | solution.py:259
  46.3 9.8 %collective-permute-start.9 = (bf16[3,128,768]{2,1,0:T(8,128)(2,1)S(1)}, bf16[3,128,768]{2,1,0:T(8,128)(2,1)}, u32[]{:S(2)}, u32[]{:S(2)}) collective-permute-start(bf16[3,128,768]{2,1,0:T(8,128)(2,1)S(1)} %collective-permute-done.7.refs_9_), channel_id=1, source_target_pairs={{0,128},{32,160},{64,192},{96,224},{128,256},{160,288},{192,320},{... | collective-permute-start | bytes 1769480 | tf_op jit(solution)/shard_map/ppermute | solution.py:259
  56.1 6.0 %collective-permute-done.1.refs_3_ = bf16[3,128,768]{2,1,0:T(8,128)(2,1)} collective-permute-done((bf16[3,128,768]{2,1,0:T(8,128)(2,1)S(1)}, bf16[3,128,768]{2,1,0:T(8,128)(2,1)}, u32[]{:S(2)}, u32[]{:S(2)}) %collective-permute-start.1) | collective-permute-done | bytes 589856 | tf_op jit(solution)/shard_map/ppermute | solution.py:259
  62.2 4.0 %collective-permute-start.8 = (bf16[3,128,768]{2,1,0:T(8,128)(2,1)S(1)}, bf16[3,128,768]{2,1,0:T(8,128)(2,1)S(1)}, u32[]{:S(2)}, u32[]{:S(2)}) collective-permute-start(bf16[3,128,768]{2,1,0:T(8,128)(2,1)S(1)} %collective-permute-done.7.refs_9_), channel_id=1, source_target_pairs={{0,32},{32,0},{64,96},{96,64},{128,160},{160,128},{192,224},{224,1... | collective-permute-start | bytes 1769480 | tf_op jit(solution)/shard_map/ppermute | solution.py:259
  66.3 1.9 collective-permute-start.6
  68.2 13.8 %collective-permute-start.4 = (bf16[3,128,768]{2,1,0:T(8,128)(2,1)S(1)}, bf16[3,128,768]{2,1,0:T(8,128)(2,1)}, u32[]{:S(2)}, u32[]{:S(2)}) collective-permute-start(bf16[3,128,768]{2,1,0:T(8,128)(2,1)S(1)} %collective-permute-done.3.refs_5_), channel_id=1, source_target_pairs={{0,32},{32,0},{64,96},{96,64},{128,160},{160,128},{192,224},{224,1... | collective-permute-start | bytes 1769480 | tf_op jit(solution)/shard_map/ppermute | solution.py:259
  82.0 1.9 collective-permute-start.2
  83.9 1.2 collective-permute-done.9.refs_11_
  85.2 2.5 %collective-permute-start.14 = (bf16[3,128,768]{2,1,0:T(8,128)(2,1)}, bf16[3,128,768]{2,1,0:T(8,128)(2,1)}, u32[]{:S(2)}, u32[]{:S(2)}) collective-permute-start(bf16[3,128,768]{2,1,0:T(8,128)(2,1)} %collective-permute-done.13.refs_15_), channel_id=1, source_target_pairs={{0,32},{32,0},{64,96},{96,64},{128,160},{160,128},{192,224},{224,1... | collective-permute-start | bytes 1769480 | tf_op jit(solution)/shard_map/ppermute | solution.py:259
  87.7 1.9 collective-permute-start.12
  89.7 2.4 %collective-permute-start.10 = (bf16[3,128,768]{2,1,0:T(8,128)(2,1)}, bf16[3,128,768]{2,1,0:T(8,128)(2,1)}, u32[]{:S(2)}, u32[]{:S(2)}) collective-permute-start(bf16[3,128,768]{2,1,0:T(8,128)(2,1)} %collective-permute-done.9.refs_11_), channel_id=1, source_target_pairs={{0,32},{32,0},{64,96},{96,64},{128,160},{160,128},{192,224},{224,1... | collective-permute-start | bytes 1769480 | tf_op jit(solution)/shard_map/ppermute | solution.py:259
  92.1 0.1 pad_add_fusion.order_ref
  92.2 1.8 collective-permute-done.10.refs_12_
  94.0 26.1 %all-to-all-done = bf16[32,8,4096]{2,1,0:T(8,128)(2,1)S(1)} async-done(((bf16[32,8,4096]{2,1,0:T(8,128)(2,1)}), bf16[32,8,4096]{2,1,0:T(8,128)(2,1)S(1)}, u32[]{:S(2)}, u32[]{:S(2)}) %all-to-all-start) | async-done | bytes 2097184 | tf_op jit(solution)/shard_map/all_to_all | solution.py:276
  120.1 9.9 %shard_map.111 = (bf16[256,4096]{1,0:T(8,128)(2,1)}, bf16[256,768]{1,0:T(8,128)(2,1)S(1)}, bf16[256,768]{1,0:T(8,128)(2,1)S(1)}, bf16[256,768]{1,0:T(8,128)(2,1)S(1)}) custom-call(s32[9]{0:T(128)S(1)} %pad_add_fusion.order_ref, bf16[256,4096]{1,0:T(8,128)(2,1)S(1)} %bitcast.38, bf16[3,128,768]{2,1,0:T(8,128)(2,1)} %copy-done.7, ...), custom_call_target="tpu_custom_call" | custom-call | flops 4831838208 | bytes 13631488 | tf_op jit(solution)/shard_map/pallas_call | solution.py:162
  130.1 3.8 %all-to-all-start.1 = ((bf16[32,8,4096]{2,1,0:T(8,128)(2,1)}), bf16[32,8,4096]{2,1,0:T(8,128)(2,1)S(1)}, u32[]{:S(2)}, u32[]{:S(2)}) async-start(bf16[32,8,4096]{2,1,0:T(8,128)(2,1)} %bitcast.43), calls=%async_computation.1 | async-start | bytes 4194304 | tf_op jit(solution)/shard_map/all_to_all | solution.py:276
  133.9 1.6 copy-done.1
  135.5 2.0 shard_map.113
  137.5 2.7 %collective-permute-start.15 = (bf16[8,128,768]{2,1,0:T(8,128)(2,1)S(1)}, bf16[8,128,768]{2,1,0:T(8,128)(2,1)S(1)}, u32[]{:S(2)}, u32[]{:S(2)}) collective-permute-start(bf16[8,128,768]{2,1,0:T(8,128)(2,1)S(1)} %get-tuple-element.36), channel_id=1, source_target_pairs={{0,32},{32,0},{64,96},{96,64},{128,160},{160,128},{192,224},{224,1... | collective-permute-start | bytes 4718600 | tf_op jit(solution)/shard_map/ppermute | solution.py:259
  140.1 1.9 collective-permute-start.16
  142.1 2.6 %collective-permute-start.17 = (bf16[8,128,768]{2,1,0:T(8,128)(2,1)S(1)}, bf16[8,128,768]{2,1,0:T(8,128)(2,1)S(1)}, u32[]{:S(2)}, u32[]{:S(2)}) collective-permute-start(bf16[8,128,768]{2,1,0:T(8,128)(2,1)S(1)} %get-tuple-element.38), channel_id=1, source_target_pairs={{0,32},{32,0},{64,96},{96,64},{128,160},{160,128},{192,224},{224,1... | collective-permute-start | bytes 4718600 | tf_op jit(solution)/shard_map/ppermute | solution.py:259
  144.7 0.8 collective-permute-done.16.refs_6_
  145.4 2.2 collective-permute-done.17.refs_7_
  147.7 2.1 shard_map.114
  149.8 3.1 %collective-permute-start.18 = (bf16[2,128,768]{2,1,0:T(8,128)(2,1)S(1)}, bf16[2,128,768]{2,1,0:T(8,128)(2,1)S(1)}, u32[]{:S(2)}, u32[]{:S(2)}) collective-permute-start(bf16[2,128,768]{2,1,0:T(8,128)(2,1)S(1)} %get-tuple-element.40), channel_id=1, source_target_pairs={{0,128},{32,160},{64,192},{96,224},{128,256},{160,288},{192,320},{... | collective-permute-start | bytes 1179656 | tf_op jit(solution)/shard_map/ppermute | solution.py:259
  152.9 4.4 %collective-permute-start.19 = (bf16[2,128,768]{2,1,0:T(8,128)(2,1)S(1)}, bf16[2,128,768]{2,1,0:T(8,128)(2,1)S(1)}, u32[]{:S(2)}, u32[]{:S(2)}) collective-permute-start(bf16[2,128,768]{2,1,0:T(8,128)(2,1)S(1)} %get-tuple-element.41), channel_id=1, source_target_pairs={{0,256},{32,288},{64,320},{96,352},{128,384},{160,416},{192,448},{... | collective-permute-start | bytes 1179656 | tf_op jit(solution)/shard_map/ppermute | solution.py:259
  157.3 3.0 %collective-permute-start.20 = (bf16[2,128,768]{2,1,0:T(8,128)(2,1)S(1)}, bf16[2,128,768]{2,1,0:T(8,128)(2,1)S(1)}, u32[]{:S(2)}, u32[]{:S(2)}) collective-permute-start(bf16[2,128,768]{2,1,0:T(8,128)(2,1)S(1)} %get-tuple-element.42), channel_id=1, source_target_pairs={{0,384},{32,416},{64,448},{96,480},{128,0},{160,32},{192,64},{224,... | collective-permute-start | bytes 1179656 | tf_op jit(solution)/shard_map/ppermute | solution.py:259
  160.3 2.3 collective-permute-start.22
  162.6 2.8 %collective-permute-start.23 = (bf16[2,128,768]{2,1,0:T(8,128)(2,1)S(1)}, bf16[2,128,768]{2,1,0:T(8,128)(2,1)S(1)}, u32[]{:S(2)}, u32[]{:S(2)}) collective-permute-start(bf16[2,128,768]{2,1,0:T(8,128)(2,1)S(1)} %get-tuple-element.45), channel_id=1, source_target_pairs={{0,256},{32,288},{64,320},{96,352},{128,384},{160,416},{192,448},{... | collective-permute-start | bytes 1179656 | tf_op jit(solution)/shard_map/ppermute | solution.py:259
  165.3 3.5 %collective-permute-start.24 = (bf16[2,128,768]{2,1,0:T(8,128)(2,1)S(1)}, bf16[2,128,768]{2,1,0:T(8,128)(2,1)S(1)}, u32[]{:S(2)}, u32[]{:S(2)}) collective-permute-start(bf16[2,128,768]{2,1,0:T(8,128)(2,1)S(1)} %get-tuple-element.46), channel_id=1, source_target_pairs={{0,384},{32,416},{64,448},{96,480},{128,0},{160,32},{192,64},{224,... | collective-permute-start | bytes 1179656 | tf_op jit(solution)/shard_map/ppermute | solution.py:259
  168.8 3.9 %collective-permute-done.19 = bf16[2,128,768]{2,1,0:T(8,128)(2,1)S(1)} collective-permute-done((bf16[2,128,768]{2,1,0:T(8,128)(2,1)S(1)}, bf16[2,128,768]{2,1,0:T(8,128)(2,1)S(1)}, u32[]{:S(2)}, u32[]{:S(2)}) %collective-permute-start.19) | collective-permute-done | bytes 393248 | tf_op jit(solution)/shard_map/ppermute | solution.py:259
  172.8 1.9 collective-permute-start.26
  174.7 4.1 %collective-permute-start.27 = (bf16[2,128,768]{2,1,0:T(8,128)(2,1)S(1)}, bf16[2,128,768]{2,1,0:T(8,128)(2,1)S(1)}, u32[]{:S(2)}, u32[]{:S(2)}) collective-permute-start(bf16[2,128,768]{2,1,0:T(8,128)(2,1)S(1)} %get-tuple-element.49), channel_id=1, source_target_pairs={{0,256},{32,288},{64,320},{96,352},{128,384},{160,416},{192,448},{... | collective-permute-start | bytes 1179656 | tf_op jit(solution)/shard_map/ppermute | solution.py:259
  178.8 0.2 convert_add_fusion.2
  179.0 3.3 %collective-permute-done.22 = bf16[2,128,768]{2,1,0:T(8,128)(2,1)S(1)} collective-permute-done((bf16[2,128,768]{2,1,0:T(8,128)(2,1)S(1)}, bf16[2,128,768]{2,1,0:T(8,128)(2,1)S(1)}, u32[]{:S(2)}, u32[]{:S(2)}) %collective-permute-start.22) | collective-permute-done | bytes 393248 | tf_op jit(solution)/shard_map/ppermute | solution.py:259
  182.3 1.9 collective-permute-start.28
  184.3 5.4 %collective-permute-done.23 = bf16[2,128,768]{2,1,0:T(8,128)(2,1)S(1)} collective-permute-done((bf16[2,128,768]{2,1,0:T(8,128)(2,1)S(1)}, bf16[2,128,768]{2,1,0:T(8,128)(2,1)S(1)}, u32[]{:S(2)}, u32[]{:S(2)}) %collective-permute-start.23) | collective-permute-done | bytes 393248 | tf_op jit(solution)/shard_map/ppermute | solution.py:259
  189.7 4.5 %collective-permute-start.21 = (bf16[128,768]{1,0:T(8,128)(2,1)S(1)}, bf16[128,768]{1,0:T(8,128)(2,1)S(1)}, u32[]{:S(2)}, u32[]{:S(2)}) collective-permute-start(bf16[128,768]{1,0:T(8,128)(2,1)S(1)} %fusion.6), channel_id=1, source_target_pairs={{0,64},{32,96},{64,0},{96,32},{128,192},{160,224},{192,128},{224,1... | collective-permute-start | bytes 589832 | tf_op jit(solution)/shard_map/ppermute | solution.py:259
  194.2 0.2 convert_add_fusion.1
  194.4 2.3 collective-permute-start.25
  196.7 2.4 %collective-permute-done.26 = bf16[2,128,768]{2,1,0:T(8,128)(2,1)S(1)} collective-permute-done((bf16[2,128,768]{2,1,0:T(8,128)(2,1)S(1)}, bf16[2,128,768]{2,1,0:T(8,128)(2,1)S(1)}, u32[]{:S(2)}, u32[]{:S(2)}) %collective-permute-start.26) | collective-permute-done | bytes 393248 | tf_op jit(solution)/shard_map/ppermute | solution.py:259
  199.1 7.4 %collective-permute-done.27 = bf16[2,128,768]{2,1,0:T(8,128)(2,1)S(1)} collective-permute-done((bf16[2,128,768]{2,1,0:T(8,128)(2,1)S(1)}, bf16[2,128,768]{2,1,0:T(8,128)(2,1)S(1)}, u32[]{:S(2)}, u32[]{:S(2)}) %collective-permute-start.27) | collective-permute-done | bytes 393248 | tf_op jit(solution)/shard_map/ppermute | solution.py:259
  206.5 1.2 collective-permute-done.28
  207.7 0.2 convert_add_fusion
  207.9 0.0 copy-start.3
  208.0 4.5 %collective-permute-start.29 = (bf16[128,768]{1,0:T(8,128)(2,1)S(1)}, bf16[128,768]{1,0:T(8,128)(2,1)S(1)}, u32[]{:S(2)}, u32[]{:S(2)}) collective-permute-start(bf16[128,768]{1,0:T(8,128)(2,1)S(1)} %fusion.8), channel_id=1, source_target_pairs={{0,64},{32,96},{64,0},{96,32},{128,192},{160,224},{192,128},{224,1... | collective-permute-start | bytes 589832 | tf_op jit(solution)/shard_map/ppermute | solution.py:259
  212.5 0.8 fusion.5
  213.3 0.8 fusion.3
  214.1 2.4 %collective-permute-done.29 = bf16[128,768]{1,0:T(8,128)(2,1)S(1)} collective-permute-done((bf16[128,768]{1,0:T(8,128)(2,1)S(1)}, bf16[128,768]{1,0:T(8,128)(2,1)S(1)}, u32[]{:S(2)}, u32[]{:S(2)}) %collective-permute-start.29) | collective-permute-done | bytes 196640 | tf_op jit(solution)/shard_map/ppermute | solution.py:259
  216.5 0.8 fusion.1
  217.2 16.3 %all-to-all-done.1 = bf16[32,8,4096]{2,1,0:T(8,128)(2,1)S(1)} async-done(((bf16[32,8,4096]{2,1,0:T(8,128)(2,1)}), bf16[32,8,4096]{2,1,0:T(8,128)(2,1)S(1)}, u32[]{:S(2)}, u32[]{:S(2)}) %all-to-all-start.1) | async-done | bytes 2097184 | tf_op jit(solution)/shard_map/all_to_all | solution.py:276
  233.5 1.3 shard_map.112
  (48 shorter events, 0.2 us)
Async XLA Ops:
  3.6 16.0 %copy-start.4 = (bf16[1,128,768]{2,1,0:T(8,128)(2,1)S(1)}, bf16[1,128,768]{2,1,0:T(8,128)(2,1)}, u32[]{:S(2)}) copy-start(bf16[1,128,768]{2,1,0:T(8,128)(2,1)} %param.11) | copy-start | bytes 589828
  3.6 16.0 %copy-start.5 = (bf16[1,128,768]{2,1,0:T(8,128)(2,1)S(1)}, bf16[1,128,768]{2,1,0:T(8,128)(2,1)}, u32[]{:S(2)}) copy-start(bf16[1,128,768]{2,1,0:T(8,128)(2,1)} %param.12) | copy-start | bytes 589828
  3.6 16.0 %copy-start.6 = (bf16[1,128,768]{2,1,0:T(8,128)(2,1)S(1)}, bf16[1,128,768]{2,1,0:T(8,128)(2,1)}, u32[]{:S(2)}) copy-start(bf16[1,128,768]{2,1,0:T(8,128)(2,1)} %param.13) | copy-start | bytes 589828
  3.6 116.5 %all-to-all-start = ((bf16[32,8,4096]{2,1,0:T(8,128)(2,1)}), bf16[32,8,4096]{2,1,0:T(8,128)(2,1)S(1)}, u32[]{:S(2)}, u32[]{:S(2)}) async-start(bf16[32,8,4096]{2,1,0:T(8,128)(2,1)} %bitcast.44), calls=%async_computation | async-start | bytes 4194304 | tf_op jit(solution)/shard_map/all_to_all | solution.py:276
  19.7 13.9 %copy-start.7 = (bf16[3,128,768]{2,1,0:T(8,128)(2,1)}, bf16[3,128,768]{2,1,0:T(8,128)(2,1)S(1)}, u32[]{:S(2)}) copy-start(bf16[3,128,768]{2,1,0:T(8,128)(2,1)S(1)} %constant_dynamic-update-slice_fusion.refs_1_) | copy-start | bytes 1769476
  19.7 19.7 %collective-permute-start.7 = (bf16[3,128,768]{2,1,0:T(8,128)(2,1)S(1)}, bf16[3,128,768]{2,1,0:T(8,128)(2,1)S(1)}, u32[]{:S(2)}, u32[]{:S(2)}) collective-permute-start(bf16[3,128,768]{2,1,0:T(8,128)(2,1)S(1)} %constant_dynamic-update-slice_fusion.refs_1_), channel_id=1, source_target_pairs={{0,64},{32,96},{64,0},{96,32},{128,192},{160,224},{192,128},{224,1... | collective-permute-start | bytes 1769480 | tf_op jit(solution)/shard_map/ppermute | solution.py:259
  24.2 19.6 %collective-permute-start.5 = (bf16[3,128,768]{2,1,0:T(8,128)(2,1)S(1)}, bf16[3,128,768]{2,1,0:T(8,128)(2,1)S(1)}, u32[]{:S(2)}, u32[]{:S(2)}) collective-permute-start(bf16[3,128,768]{2,1,0:T(8,128)(2,1)S(1)} %constant_dynamic-update-slice_fusion.refs_1_), channel_id=1, source_target_pairs={{0,384},{32,416},{64,448},{96,480},{128,0},{160,32},{192,64},{224,... | collective-permute-start | bytes 1769480 | tf_op jit(solution)/shard_map/ppermute | solution.py:259
  28.6 17.7 %collective-permute-start.3 = (bf16[3,128,768]{2,1,0:T(8,128)(2,1)S(1)}, bf16[3,128,768]{2,1,0:T(8,128)(2,1)S(1)}, u32[]{:S(2)}, u32[]{:S(2)}) collective-permute-start(bf16[3,128,768]{2,1,0:T(8,128)(2,1)S(1)} %constant_dynamic-update-slice_fusion.refs_1_), channel_id=1, source_target_pairs={{0,256},{32,288},{64,320},{96,352},{128,384},{160,416},{192,448},{... | collective-permute-start | bytes 1769480 | tf_op jit(solution)/shard_map/ppermute | solution.py:259
  31.0 31.1 %collective-permute-start.1 = (bf16[3,128,768]{2,1,0:T(8,128)(2,1)S(1)}, bf16[3,128,768]{2,1,0:T(8,128)(2,1)}, u32[]{:S(2)}, u32[]{:S(2)}) collective-permute-start(bf16[3,128,768]{2,1,0:T(8,128)(2,1)S(1)} %constant_dynamic-update-slice_fusion.refs_1_), channel_id=1, source_target_pairs={{0,128},{32,160},{64,192},{96,224},{128,256},{160,288},{192,320},{... | collective-permute-start | bytes 1769480 | tf_op jit(solution)/shard_map/ppermute | solution.py:259
  33.6 32.6 %collective-permute-start = (bf16[3,128,768]{2,1,0:T(8,128)(2,1)S(1)}, bf16[3,128,768]{2,1,0:T(8,128)(2,1)S(1)}, u32[]{:S(2)}, u32[]{:S(2)}) collective-permute-start(bf16[3,128,768]{2,1,0:T(8,128)(2,1)S(1)} %constant_dynamic-update-slice_fusion.refs_1_), channel_id=1, source_target_pairs={{0,32},{32,0},{64,96},{96,64},{128,160},{160,128},{192,224},{224,1... | collective-permute-start | bytes 1769480 | tf_op jit(solution)/shard_map/ppermute | solution.py:259
  39.4 26.8 %copy-start.8 = (bf16[3,128,768]{2,1,0:T(8,128)(2,1)}, bf16[3,128,768]{2,1,0:T(8,128)(2,1)S(1)}, u32[]{:S(2)}) copy-start(bf16[3,128,768]{2,1,0:T(8,128)(2,1)S(1)} %collective-permute-done.7.refs_9_) | copy-start | bytes 1769476
  39.4 28.8 %collective-permute-start.13 = (bf16[3,128,768]{2,1,0:T(8,128)(2,1)S(1)}, bf16[3,128,768]{2,1,0:T(8,128)(2,1)}, u32[]{:S(2)}, u32[]{:S(2)}) collective-permute-start(bf16[3,128,768]{2,1,0:T(8,128)(2,1)S(1)} %collective-permute-done.7.refs_9_), channel_id=1, source_target_pairs={{0,384},{32,416},{64,448},{96,480},{128,0},{160,32},{192,64},{224,... | collective-permute-start | bytes 1769480 | tf_op jit(solution)/shard_map/ppermute | solution.py:259
  43.8 43.9 %copy-start.9 = (bf16[3,128,768]{2,1,0:T(8,128)(2,1)}, bf16[3,128,768]{2,1,0:T(8,128)(2,1)S(1)}, u32[]{:S(2)}) copy-start(bf16[3,128,768]{2,1,0:T(8,128)(2,1)S(1)} %collective-permute-done.5.refs_7_) | copy-start | bytes 1769476
  43.8 38.2 %collective-permute-start.11 = (bf16[3,128,768]{2,1,0:T(8,128)(2,1)S(1)}, bf16[3,128,768]{2,1,0:T(8,128)(2,1)}, u32[]{:S(2)}, u32[]{:S(2)}) collective-permute-start(bf16[3,128,768]{2,1,0:T(8,128)(2,1)S(1)} %collective-permute-done.7.refs_9_), channel_id=1, source_target_pairs={{0,256},{32,288},{64,320},{96,352},{128,384},{160,416},{192,448},{... | collective-permute-start | bytes 1769480 | tf_op jit(solution)/shard_map/ppermute | solution.py:259
  46.3 73.8 %copy-start.10 = (bf16[3,128,768]{2,1,0:T(8,128)(2,1)}, bf16[3,128,768]{2,1,0:T(8,128)(2,1)S(1)}, u32[]{:S(2)}) copy-start(bf16[3,128,768]{2,1,0:T(8,128)(2,1)S(1)} %collective-permute-done.3.refs_5_) | copy-start | bytes 1769476
  46.3 38.9 %collective-permute-start.9 = (bf16[3,128,768]{2,1,0:T(8,128)(2,1)S(1)}, bf16[3,128,768]{2,1,0:T(8,128)(2,1)}, u32[]{:S(2)}, u32[]{:S(2)}) collective-permute-start(bf16[3,128,768]{2,1,0:T(8,128)(2,1)S(1)} %collective-permute-done.7.refs_9_), channel_id=1, source_target_pairs={{0,128},{32,160},{64,192},{96,224},{128,256},{160,288},{192,320},{... | collective-permute-start | bytes 1769480 | tf_op jit(solution)/shard_map/ppermute | solution.py:259
  62.2 25.5 %collective-permute-start.8 = (bf16[3,128,768]{2,1,0:T(8,128)(2,1)S(1)}, bf16[3,128,768]{2,1,0:T(8,128)(2,1)S(1)}, u32[]{:S(2)}, u32[]{:S(2)}) collective-permute-start(bf16[3,128,768]{2,1,0:T(8,128)(2,1)S(1)} %collective-permute-done.7.refs_9_), channel_id=1, source_target_pairs={{0,32},{32,0},{64,96},{96,64},{128,160},{160,128},{192,224},{224,1... | collective-permute-start | bytes 1769480 | tf_op jit(solution)/shard_map/ppermute | solution.py:259
  66.2 23.4 %copy-start.11 = (bf16[3,128,768]{2,1,0:T(8,128)(2,1)}, bf16[3,128,768]{2,1,0:T(8,128)(2,1)S(1)}, u32[]{:S(2)}) copy-start(bf16[3,128,768]{2,1,0:T(8,128)(2,1)S(1)} %collective-permute-done.refs_2_) | copy-start | bytes 1769476
  66.3 23.4 %collective-permute-start.6 = (bf16[3,128,768]{2,1,0:T(8,128)(2,1)S(1)}, bf16[3,128,768]{2,1,0:T(8,128)(2,1)S(1)}, u32[]{:S(2)}, u32[]{:S(2)}) collective-permute-start(bf16[3,128,768]{2,1,0:T(8,128)(2,1)S(1)} %collective-permute-done.5.refs_7_), channel_id=1, source_target_pairs={{0,32},{32,0},{64,96},{96,64},{128,160},{160,128},{192,224},{224,1... | collective-permute-start | bytes 1769480 | tf_op jit(solution)/shard_map/ppermute | solution.py:259
  68.2 24.0 %collective-permute-start.4 = (bf16[3,128,768]{2,1,0:T(8,128)(2,1)S(1)}, bf16[3,128,768]{2,1,0:T(8,128)(2,1)}, u32[]{:S(2)}, u32[]{:S(2)}) collective-permute-start(bf16[3,128,768]{2,1,0:T(8,128)(2,1)S(1)} %collective-permute-done.3.refs_5_), channel_id=1, source_target_pairs={{0,32},{32,0},{64,96},{96,64},{128,160},{160,128},{192,224},{224,1... | collective-permute-start | bytes 1769480 | tf_op jit(solution)/shard_map/ppermute | solution.py:259
  82.0 10.2 %collective-permute-start.2 = (bf16[3,128,768]{2,1,0:T(8,128)(2,1)}, bf16[3,128,768]{2,1,0:T(8,128)(2,1)}, u32[]{:S(2)}, u32[]{:S(2)}) collective-permute-start(bf16[3,128,768]{2,1,0:T(8,128)(2,1)} %collective-permute-done.1.refs_3_), channel_id=1, source_target_pairs={{0,32},{32,0},{64,96},{96,64},{128,160},{160,128},{192,224},{224,1... | collective-permute-start | bytes 1769480 | tf_op jit(solution)/shard_map/ppermute | solution.py:259
  85.2 7.0 %collective-permute-start.14 = (bf16[3,128,768]{2,1,0:T(8,128)(2,1)}, bf16[3,128,768]{2,1,0:T(8,128)(2,1)}, u32[]{:S(2)}, u32[]{:S(2)}) collective-permute-start(bf16[3,128,768]{2,1,0:T(8,128)(2,1)} %collective-permute-done.13.refs_15_), channel_id=1, source_target_pairs={{0,32},{32,0},{64,96},{96,64},{128,160},{160,128},{192,224},{224,1... | collective-permute-start | bytes 1769480 | tf_op jit(solution)/shard_map/ppermute | solution.py:259
  87.7 4.4 %copy-start.12 = (bf16[3,128,768]{2,1,0:T(8,128)(2,1)}, bf16[3,128,768]{2,1,0:T(8,128)(2,1)S(1)}, u32[]{:S(2)}) copy-start(bf16[3,128,768]{2,1,0:T(8,128)(2,1)S(1)} %collective-permute-done.8.refs_10_) | copy-start | bytes 1769476
  87.7 4.5 %collective-permute-start.12 = (bf16[3,128,768]{2,1,0:T(8,128)(2,1)}, bf16[3,128,768]{2,1,0:T(8,128)(2,1)}, u32[]{:S(2)}, u32[]{:S(2)}) collective-permute-start(bf16[3,128,768]{2,1,0:T(8,128)(2,1)} %collective-permute-done.11.refs_13_), channel_id=1, source_target_pairs={{0,32},{32,0},{64,96},{96,64},{128,160},{160,128},{192,224},{224,1... | collective-permute-start | bytes 1769480 | tf_op jit(solution)/shard_map/ppermute | solution.py:259
  89.7 2.4 %copy-start.13 = (bf16[3,128,768]{2,1,0:T(8,128)(2,1)}, bf16[3,128,768]{2,1,0:T(8,128)(2,1)S(1)}, u32[]{:S(2)}) copy-start(bf16[3,128,768]{2,1,0:T(8,128)(2,1)S(1)} %collective-permute-done.6.refs_8_) | copy-start | bytes 1769476
  89.7 4.4 %collective-permute-start.10 = (bf16[3,128,768]{2,1,0:T(8,128)(2,1)}, bf16[3,128,768]{2,1,0:T(8,128)(2,1)}, u32[]{:S(2)}, u32[]{:S(2)}) collective-permute-start(bf16[3,128,768]{2,1,0:T(8,128)(2,1)} %collective-permute-done.9.refs_11_), channel_id=1, source_target_pairs={{0,32},{32,0},{64,96},{96,64},{128,160},{160,128},{192,224},{224,1... | collective-permute-start | bytes 1769480 | tf_op jit(solution)/shard_map/ppermute | solution.py:259
  120.1 9.9 %copy-start = (bf16[32,8,4096]{2,1,0:T(8,128)(2,1)}, bf16[32,8,4096]{2,1,0:T(8,128)(2,1)S(1)}, u32[]{:S(2)}) copy-start(bf16[32,8,4096]{2,1,0:T(8,128)(2,1)S(1)} %all-to-all-done) | copy-start | bytes 6291460
  130.1 103.5 %all-to-all-start.1 = ((bf16[32,8,4096]{2,1,0:T(8,128)(2,1)}), bf16[32,8,4096]{2,1,0:T(8,128)(2,1)S(1)}, u32[]{:S(2)}, u32[]{:S(2)}) async-start(bf16[32,8,4096]{2,1,0:T(8,128)(2,1)} %bitcast.43), calls=%async_computation.1 | async-start | bytes 4194304 | tf_op jit(solution)/shard_map/all_to_all | solution.py:276
  133.9 1.6 copy-start.1
  135.5 12.2 %copy-start.2 = (bf16[32,8,4096]{2,1,0:T(8,128)(2,1)S(1)}, bf16[32,8,4096]{2,1,0:T(8,128)(2,1)}, u32[]{:S(2)}) copy-start(bf16[32,8,4096]{2,1,0:T(8,128)(2,1)} %copy-done) | copy-start | bytes 6291460
  137.5 7.2 %collective-permute-start.15 = (bf16[8,128,768]{2,1,0:T(8,128)(2,1)S(1)}, bf16[8,128,768]{2,1,0:T(8,128)(2,1)S(1)}, u32[]{:S(2)}, u32[]{:S(2)}) collective-permute-start(bf16[8,128,768]{2,1,0:T(8,128)(2,1)S(1)} %get-tuple-element.36), channel_id=1, source_target_pairs={{0,32},{32,0},{64,96},{96,64},{128,160},{160,128},{192,224},{224,1... | collective-permute-start | bytes 4718600 | tf_op jit(solution)/shard_map/ppermute | solution.py:259
  140.1 5.3 %collective-permute-start.16 = (bf16[8,128,768]{2,1,0:T(8,128)(2,1)S(1)}, bf16[8,128,768]{2,1,0:T(8,128)(2,1)S(1)}, u32[]{:S(2)}, u32[]{:S(2)}) collective-permute-start(bf16[8,128,768]{2,1,0:T(8,128)(2,1)S(1)} %get-tuple-element.37), channel_id=1, source_target_pairs={{0,32},{32,0},{64,96},{96,64},{128,160},{160,128},{192,224},{224,1... | collective-permute-start | bytes 4718600 | tf_op jit(solution)/shard_map/ppermute | solution.py:259
  142.1 5.6 %collective-permute-start.17 = (bf16[8,128,768]{2,1,0:T(8,128)(2,1)S(1)}, bf16[8,128,768]{2,1,0:T(8,128)(2,1)S(1)}, u32[]{:S(2)}, u32[]{:S(2)}) collective-permute-start(bf16[8,128,768]{2,1,0:T(8,128)(2,1)S(1)} %get-tuple-element.38), channel_id=1, source_target_pairs={{0,32},{32,0},{64,96},{96,64},{128,160},{160,128},{192,224},{224,1... | collective-permute-start | bytes 4718600 | tf_op jit(solution)/shard_map/ppermute | solution.py:259
  149.8 15.6 %collective-permute-start.18 = (bf16[2,128,768]{2,1,0:T(8,128)(2,1)S(1)}, bf16[2,128,768]{2,1,0:T(8,128)(2,1)S(1)}, u32[]{:S(2)}, u32[]{:S(2)}) collective-permute-start(bf16[2,128,768]{2,1,0:T(8,128)(2,1)S(1)} %get-tuple-element.40), channel_id=1, source_target_pairs={{0,128},{32,160},{64,192},{96,224},{128,256},{160,288},{192,320},{... | collective-permute-start | bytes 1179656 | tf_op jit(solution)/shard_map/ppermute | solution.py:259
  152.9 19.9 %collective-permute-start.19 = (bf16[2,128,768]{2,1,0:T(8,128)(2,1)S(1)}, bf16[2,128,768]{2,1,0:T(8,128)(2,1)S(1)}, u32[]{:S(2)}, u32[]{:S(2)}) collective-permute-start(bf16[2,128,768]{2,1,0:T(8,128)(2,1)S(1)} %get-tuple-element.41), channel_id=1, source_target_pairs={{0,256},{32,288},{64,320},{96,352},{128,384},{160,416},{192,448},{... | collective-permute-start | bytes 1179656 | tf_op jit(solution)/shard_map/ppermute | solution.py:259
  157.3 17.4 %collective-permute-start.20 = (bf16[2,128,768]{2,1,0:T(8,128)(2,1)S(1)}, bf16[2,128,768]{2,1,0:T(8,128)(2,1)S(1)}, u32[]{:S(2)}, u32[]{:S(2)}) collective-permute-start(bf16[2,128,768]{2,1,0:T(8,128)(2,1)S(1)} %get-tuple-element.42), channel_id=1, source_target_pairs={{0,384},{32,416},{64,448},{96,480},{128,0},{160,32},{192,64},{224,... | collective-permute-start | bytes 1179656 | tf_op jit(solution)/shard_map/ppermute | solution.py:259
  160.3 22.0 %collective-permute-start.22 = (bf16[2,128,768]{2,1,0:T(8,128)(2,1)S(1)}, bf16[2,128,768]{2,1,0:T(8,128)(2,1)S(1)}, u32[]{:S(2)}, u32[]{:S(2)}) collective-permute-start(bf16[2,128,768]{2,1,0:T(8,128)(2,1)S(1)} %get-tuple-element.44), channel_id=1, source_target_pairs={{0,128},{32,160},{64,192},{96,224},{128,256},{160,288},{192,320},{... | collective-permute-start | bytes 1179656 | tf_op jit(solution)/shard_map/ppermute | solution.py:259
  162.6 27.1 %collective-permute-start.23 = (bf16[2,128,768]{2,1,0:T(8,128)(2,1)S(1)}, bf16[2,128,768]{2,1,0:T(8,128)(2,1)S(1)}, u32[]{:S(2)}, u32[]{:S(2)}) collective-permute-start(bf16[2,128,768]{2,1,0:T(8,128)(2,1)S(1)} %get-tuple-element.45), channel_id=1, source_target_pairs={{0,256},{32,288},{64,320},{96,352},{128,384},{160,416},{192,448},{... | collective-permute-start | bytes 1179656 | tf_op jit(solution)/shard_map/ppermute | solution.py:259
  165.3 28.8 %collective-permute-start.24 = (bf16[2,128,768]{2,1,0:T(8,128)(2,1)S(1)}, bf16[2,128,768]{2,1,0:T(8,128)(2,1)S(1)}, u32[]{:S(2)}, u32[]{:S(2)}) collective-permute-start(bf16[2,128,768]{2,1,0:T(8,128)(2,1)S(1)} %get-tuple-element.46), channel_id=1, source_target_pairs={{0,384},{32,416},{64,448},{96,480},{128,0},{160,32},{192,64},{224,... | collective-permute-start | bytes 1179656 | tf_op jit(solution)/shard_map/ppermute | solution.py:259
  172.8 26.4 %collective-permute-start.26 = (bf16[2,128,768]{2,1,0:T(8,128)(2,1)S(1)}, bf16[2,128,768]{2,1,0:T(8,128)(2,1)S(1)}, u32[]{:S(2)}, u32[]{:S(2)}) collective-permute-start(bf16[2,128,768]{2,1,0:T(8,128)(2,1)S(1)} %get-tuple-element.48), channel_id=1, source_target_pairs={{0,128},{32,160},{64,192},{96,224},{128,256},{160,288},{192,320},{... | collective-permute-start | bytes 1179656 | tf_op jit(solution)/shard_map/ppermute | solution.py:259
  174.7 31.8 %collective-permute-start.27 = (bf16[2,128,768]{2,1,0:T(8,128)(2,1)S(1)}, bf16[2,128,768]{2,1,0:T(8,128)(2,1)S(1)}, u32[]{:S(2)}, u32[]{:S(2)}) collective-permute-start(bf16[2,128,768]{2,1,0:T(8,128)(2,1)S(1)} %get-tuple-element.49), channel_id=1, source_target_pairs={{0,256},{32,288},{64,320},{96,352},{128,384},{160,416},{192,448},{... | collective-permute-start | bytes 1179656 | tf_op jit(solution)/shard_map/ppermute | solution.py:259
  182.3 25.4 %collective-permute-start.28 = (bf16[2,128,768]{2,1,0:T(8,128)(2,1)S(1)}, bf16[2,128,768]{2,1,0:T(8,128)(2,1)S(1)}, u32[]{:S(2)}, u32[]{:S(2)}) collective-permute-start(bf16[2,128,768]{2,1,0:T(8,128)(2,1)S(1)} %get-tuple-element.50), channel_id=1, source_target_pairs={{0,384},{32,416},{64,448},{96,480},{128,0},{160,32},{192,64},{224,... | collective-permute-start | bytes 1179656 | tf_op jit(solution)/shard_map/ppermute | solution.py:259
  189.7 22.8 %collective-permute-start.21 = (bf16[128,768]{1,0:T(8,128)(2,1)S(1)}, bf16[128,768]{1,0:T(8,128)(2,1)S(1)}, u32[]{:S(2)}, u32[]{:S(2)}) collective-permute-start(bf16[128,768]{1,0:T(8,128)(2,1)S(1)} %fusion.6), channel_id=1, source_target_pairs={{0,64},{32,96},{64,0},{96,32},{128,192},{160,224},{192,128},{224,1... | collective-permute-start | bytes 589832 | tf_op jit(solution)/shard_map/ppermute | solution.py:259
  194.4 18.9 %collective-permute-start.25 = (bf16[128,768]{1,0:T(8,128)(2,1)S(1)}, bf16[128,768]{1,0:T(8,128)(2,1)S(1)}, u32[]{:S(2)}, u32[]{:S(2)}) collective-permute-start(bf16[128,768]{1,0:T(8,128)(2,1)S(1)} %fusion.7), channel_id=1, source_target_pairs={{0,64},{32,96},{64,0},{96,32},{128,192},{160,224},{192,128},{224,1... | collective-permute-start | bytes 589832 | tf_op jit(solution)/shard_map/ppermute | solution.py:259
  207.9 25.6 %copy-start.3 = (s32[128,1]{0,1:T(1,128)S(1)}, s32[128,1]{0,1:T(1,128)}, u32[]{:S(2)}) copy-start(s32[128,1]{0,1:T(1,128)} %param.9) | copy-start | bytes 1540
  208.0 8.5 %collective-permute-start.29 = (bf16[128,768]{1,0:T(8,128)(2,1)S(1)}, bf16[128,768]{1,0:T(8,128)(2,1)S(1)}, u32[]{:S(2)}, u32[]{:S(2)}) collective-permute-start(bf16[128,768]{1,0:T(8,128)(2,1)S(1)} %fusion.8), channel_id=1, source_target_pairs={{0,64},{32,96},{64,0},{96,32},{128,192},{160,224},{192,128},{224,1... | collective-permute-start | bytes 589832 | tf_op jit(solution)/shard_map/ppermute | solution.py:259

commit v7 on v6

--- a/solution.py
+++ b/solution.py
@@ -96,13 +96,14 @@
 
 
 def expert_kernel(order_ref, *refs):
-    pairs = order_ref.shape[0] - 1
+    pairs = (order_ref.shape[0] - 1) // 2
     rows, shards_in = refs[0], refs[1 : 1 + 2 * pairs]
     send_out, hid, dpre, dlin, shards, send, in_sems, out_sems = refs[1 + 2 * pairs :]
     block, units = shards.shape[2:]
     width = rows.shape[1] // 2
-    core = order_ref[pairs]
-    halves = [pl.ds(0, width), pl.ds(width, width)]
+    core = order_ref[2 * pairs]
+    parts = out_sems.shape[0]
+    cuts = [pl.ds(n * 2 * width // parts, 2 * width // parts) for n in range(parts)]
 
     loads = [
         pltpu.make_async_copy(shards_in[n], shards.at[n], in_sems.at[n]) for n in range(2 * pairs)
@@ -110,8 +111,8 @@
     for load in loads:
         load.start()
     stores = [
-        pltpu.make_async_copy(send.at[:, half], send_out.at[:, half], out_sems.at[n])
-        for n, half in enumerate(halves)
+        pltpu.make_async_copy(send.at[:, cut], send_out.at[:, cut], out_sems.at[n])
+        for n, cut in enumerate(cuts)
     ]
 
     def spots(p, first):
@@ -138,16 +139,19 @@
     hid[...] = (active * lin).astype(BF)
     dpre[...] = (dhid * lin * sig * (1.0 + pre * (1.0 - sig))).astype(BF)
     dlin[...] = (dhid * active).astype(BF)
-    for h in range(2):
-        for p in range(pairs):
-            if h == 0:
-                value = mm(hid[...], right(p, 2, every), NT)
-            else:
-                value = mm(dpre[...], right(p, 0, every), NT) + mm(dlin[...], right(p, 1, every), NT)
-            value = value.astype(BF)
-            for n, s in enumerate(spots(p, h * width)):
-                send[:, s] = value[:, n * block : (n + 1) * block]
-        stores[h].start()
+    def chip(c, m):
+        first = order_ref[pairs + c] * 2
+        return jnp.concatenate([shards[first + core, m], shards[first + 1 - core, m]], axis=0)
+
+    for n in range(2 * pairs):
+        c = n % pairs
+        if n < pairs:
+            value = mm(hid[...], chip(c, 2), NT)
+        else:
+            value = mm(dpre[...], chip(c, 0), NT) + mm(dlin[...], chip(c, 1), NT)
+        send[:, n * 2 * block : (n + 1) * 2 * block] = value.astype(BF)
+        if (n + 1) * parts % (2 * pairs) == 0:
+            stores[(n + 1) * parts // (2 * pairs) - 1].start()
     for copy in stores:
         copy.wait()
 
@@ -168,7 +172,7 @@
             VM((count, 3, block, units), BF),
             VM((slots, both), BF),
             pltpu.SemaphoreType.DMA((count,)),
-            pltpu.SemaphoreType.DMA((2,)),
+            pltpu.SemaphoreType.DMA((8,)),
         ],
         compiler_params=params(32),
         cost_estimate=pl.CostEstimate(
@@ -268,8 +272,10 @@
         for n in range(4):
             shard = permute(start, lambda i: (i + 4 * n) % groups) if n else start
             shards += [shard, permute(shard, lambda i: i ^ 1)]
-    source = ((x - k) & 3) * 2 + (far ^ (k >> 2))
-    source = jnp.concatenate([source, core[None]])
+    j = jnp.arange(17, dtype=jnp.int32)
+    chip = ((x - j) & 3) * 2 + (far ^ ((j >> 2) & 1))
+    pair = (((j & 1) ^ far) << 2) | ((x - ((j - 8) >> 1)) & 3)
+    source = jnp.where(j < 8, chip, jnp.where(j < 16, pair, core))
 
     def exchange(rows):
         cut = rows.reshape(experts, capacity, 2 * width)

time: 236 us -> 236 us (level)
  no operation moved by 1% of the time
where the time goes in v7:
time: 236 us; the launch traced here: 235 us
  starting transfers between devices  129 us (55%)
  waiting for transfers between devices  82 us (35%)
  Pallas kernels  17.8 us (8%)
  other arithmetic  2.92 us (1%)
    ppermute x30, starting transfers between devices, permute(): return lax.ppermute(a, 'dp', [(i, to(i)) for i in range(groups)])  109 us
    all_to_all x2, waiting for transfers between devices, exchange(): got = lax.all_to_all(cut, 'expert', split_axis=0, concat_axis=0, tiled=True)  42.3 us
    ppermute x30, waiting for transfers between devices, permute(): return lax.ppermute(a, 'dp', [(i, to(i)) for i in range(groups)])  39.7 us
    all_to_all x2, starting transfers between devices, exchange(): got = lax.all_to_all(cut, 'expert', split_axis=0, concat_axis=0, tiled=True)  19.8 us
    pallas_call x1, Pallas kernels, experts_call(): pl.pallas_call(expert_kernel, in_specs=[pl.BlockSpec(memory_space=pltpu.S...  9.54 us
  transfers between devices with their start and end apart: 32, of which 15 were waited for; matrix products, arithmetic and copies ran while one was open for 1% of the time, Pallas kernels for 2%

profile of v7, /device:TPU:33, one launch (start us, length us, event | category | flops | bytes accessed | tf_op | source)
XLA Modules:
  0.0 234.6 jit_solution(15657896159002197211)
XLA Ops:
  0.6 2.9 %shard_map.110 = (bf16[256,4096]{1,0:T(8,128)(2,1)}, bf16[256,128]{1,0:T(8,128)(2,1)S(1)}) custom-call(s32[1,128]{1,0:T(1,128)} %bitcast.44, s32[1,128]{1,0:T(1,128)} %bitcast.40, bf16[128,2048]{1,0:T(8,128)(2,1)} %refs_2_.1, bf16[128,2048]{1,0:T(8,128)(2,1)} %refs_3_.1), custom_call_target="tpu_custom_call" | custom-call | flops 268435456 | bytes 3145728 | tf_op jit(solution)/shard_map/pallas_call | solution.py:79
  3.6 0.0 copy-start.4
  3.6 0.0 copy-start.5
  3.6 0.0 copy-start.6
  3.6 16.0 %all-to-all-start = ((bf16[32,8,4096]{2,1,0:T(8,128)(2,1)}), bf16[32,8,4096]{2,1,0:T(8,128)(2,1)S(1)}, u32[]{:S(2)}, u32[]{:S(2)}) async-start(bf16[32,8,4096]{2,1,0:T(8,128)(2,1)} %bitcast.43), calls=%async_computation | async-start | bytes 4194304 | tf_op jit(solution)/shard_map/all_to_all | solution.py:282
  19.7 4.5 %collective-permute-start.7 = (bf16[3,128,768]{2,1,0:T(8,128)(2,1)S(1)}, bf16[3,128,768]{2,1,0:T(8,128)(2,1)S(1)}, u32[]{:S(2)}, u32[]{:S(2)}) collective-permute-start(bf16[3,128,768]{2,1,0:T(8,128)(2,1)S(1)} %constant_dynamic-update-slice_fusion.refs_1_), channel_id=1, source_target_pairs={{0,64},{32,96},{64,0},{96,32},{128,192},{160,224},{192,128},{224,1... | collective-permute-start | bytes 1769480 | tf_op jit(solution)/shard_map/ppermute | solution.py:263
  24.2 4.4 %collective-permute-start.5 = (bf16[3,128,768]{2,1,0:T(8,128)(2,1)S(1)}, bf16[3,128,768]{2,1,0:T(8,128)(2,1)S(1)}, u32[]{:S(2)}, u32[]{:S(2)}) collective-permute-start(bf16[3,128,768]{2,1,0:T(8,128)(2,1)S(1)} %constant_dynamic-update-slice_fusion.refs_1_), channel_id=1, source_target_pairs={{0,384},{32,416},{64,448},{96,480},{128,0},{160,32},{192,64},{224,... | collective-permute-start | bytes 1769480 | tf_op jit(solution)/shard_map/ppermute | solution.py:263
  28.6 2.4 %collective-permute-start.3 = (bf16[3,128,768]{2,1,0:T(8,128)(2,1)S(1)}, bf16[3,128,768]{2,1,0:T(8,128)(2,1)S(1)}, u32[]{:S(2)}, u32[]{:S(2)}) collective-permute-start(bf16[3,128,768]{2,1,0:T(8,128)(2,1)S(1)} %constant_dynamic-update-slice_fusion.refs_1_), channel_id=1, source_target_pairs={{0,256},{32,288},{64,320},{96,352},{128,384},{160,416},{192,448},{... | collective-permute-start | bytes 1769480 | tf_op jit(solution)/shard_map/ppermute | solution.py:263
  31.0 2.5 %collective-permute-start.1 = (bf16[3,128,768]{2,1,0:T(8,128)(2,1)S(1)}, bf16[3,128,768]{2,1,0:T(8,128)(2,1)S(1)}, u32[]{:S(2)}, u32[]{:S(2)}) collective-permute-start(bf16[3,128,768]{2,1,0:T(8,128)(2,1)S(1)} %constant_dynamic-update-slice_fusion.refs_1_), channel_id=1, source_target_pairs={{0,128},{32,160},{64,192},{96,224},{128,256},{160,288},{192,320},{... | collective-permute-start | bytes 1769480 | tf_op jit(solution)/shard_map/ppermute | solution.py:263
  33.6 4.3 %collective-permute-start = (bf16[3,128,768]{2,1,0:T(8,128)(2,1)S(1)}, bf16[3,128,768]{2,1,0:T(8,128)(2,1)S(1)}, u32[]{:S(2)}, u32[]{:S(2)}) collective-permute-start(bf16[3,128,768]{2,1,0:T(8,128)(2,1)S(1)} %constant_dynamic-update-slice_fusion.refs_1_), channel_id=1, source_target_pairs={{0,32},{32,0},{64,96},{96,64},{128,160},{160,128},{192,224},{224,1... | collective-permute-start | bytes 1769480 | tf_op jit(solution)/shard_map/ppermute | solution.py:263
  37.8 1.6 collective-permute-done.7.refs_9_
  39.4 4.4 %collective-permute-start.13 = (bf16[3,128,768]{2,1,0:T(8,128)(2,1)S(1)}, bf16[3,128,768]{2,1,0:T(8,128)(2,1)}, u32[]{:S(2)}, u32[]{:S(2)}) collective-permute-start(bf16[3,128,768]{2,1,0:T(8,128)(2,1)S(1)} %collective-permute-done.7.refs_9_), channel_id=1, source_target_pairs={{0,384},{32,416},{64,448},{96,480},{128,0},{160,32},{192,64},{224,... | collective-permute-start | bytes 1769480 | tf_op jit(solution)/shard_map/ppermute | solution.py:263
  43.8 0.0 collective-permute-done.5.refs_7_
  43.8 2.4 %collective-permute-start.11 = (bf16[3,128,768]{2,1,0:T(8,128)(2,1)S(1)}, bf16[3,128,768]{2,1,0:T(8,128)(2,1)}, u32[]{:S(2)}, u32[]{:S(2)}) collective-permute-start(bf16[3,128,768]{2,1,0:T(8,128)(2,1)S(1)} %collective-permute-done.7.refs_9_), channel_id=1, source_target_pairs={{0,256},{32,288},{64,320},{96,352},{128,384},{160,416},{192,448},{... | collective-permute-start | bytes 1769480 | tf_op jit(solution)/shard_map/ppermute | solution.py:263
  46.3 9.8 %collective-permute-start.9 = (bf16[3,128,768]{2,1,0:T(8,128)(2,1)S(1)}, bf16[3,128,768]{2,1,0:T(8,128)(2,1)}, u32[]{:S(2)}, u32[]{:S(2)}) collective-permute-start(bf16[3,128,768]{2,1,0:T(8,128)(2,1)S(1)} %collective-permute-done.7.refs_9_), channel_id=1, source_target_pairs={{0,128},{32,160},{64,192},{96,224},{128,256},{160,288},{192,320},{... | collective-permute-start | bytes 1769480 | tf_op jit(solution)/shard_map/ppermute | solution.py:263
  56.1 5.9 %collective-permute-done.1.refs_3_ = bf16[3,128,768]{2,1,0:T(8,128)(2,1)S(1)} collective-permute-done((bf16[3,128,768]{2,1,0:T(8,128)(2,1)S(1)}, bf16[3,128,768]{2,1,0:T(8,128)(2,1)S(1)}, u32[]{:S(2)}, u32[]{:S(2)}) %collective-permute-start.1) | collective-permute-done | bytes 589856 | tf_op jit(solution)/shard_map/ppermute | solution.py:263
  62.1 4.1 %collective-permute-start.8 = (bf16[3,128,768]{2,1,0:T(8,128)(2,1)S(1)}, bf16[3,128,768]{2,1,0:T(8,128)(2,1)S(1)}, u32[]{:S(2)}, u32[]{:S(2)}) collective-permute-start(bf16[3,128,768]{2,1,0:T(8,128)(2,1)S(1)} %collective-permute-done.7.refs_9_), channel_id=1, source_target_pairs={{0,32},{32,0},{64,96},{96,64},{128,160},{160,128},{192,224},{224,1... | collective-permute-start | bytes 1769480 | tf_op jit(solution)/shard_map/ppermute | solution.py:263
  66.3 1.9 collective-permute-start.6
  68.2 13.8 %collective-permute-start.4 = (bf16[3,128,768]{2,1,0:T(8,128)(2,1)S(1)}, bf16[3,128,768]{2,1,0:T(8,128)(2,1)}, u32[]{:S(2)}, u32[]{:S(2)}) collective-permute-start(bf16[3,128,768]{2,1,0:T(8,128)(2,1)S(1)} %collective-permute-done.3.refs_5_), channel_id=1, source_target_pairs={{0,32},{32,0},{64,96},{96,64},{128,160},{160,128},{192,224},{224,1... | collective-permute-start | bytes 1769480 | tf_op jit(solution)/shard_map/ppermute | solution.py:263
  82.0 1.9 collective-permute-start.2
  83.9 1.2 collective-permute-done.9.refs_11_
  85.2 2.5 %collective-permute-start.14 = (bf16[3,128,768]{2,1,0:T(8,128)(2,1)}, bf16[3,128,768]{2,1,0:T(8,128)(2,1)}, u32[]{:S(2)}, u32[]{:S(2)}) collective-permute-start(bf16[3,128,768]{2,1,0:T(8,128)(2,1)} %collective-permute-done.13.refs_15_), channel_id=1, source_target_pairs={{0,32},{32,0},{64,96},{96,64},{128,160},{160,128},{192,224},{224,1... | collective-permute-start | bytes 1769480 | tf_op jit(solution)/shard_map/ppermute | solution.py:263
  87.7 1.9 collective-permute-start.12
  89.7 2.4 %collective-permute-start.10 = (bf16[3,128,768]{2,1,0:T(8,128)(2,1)}, bf16[3,128,768]{2,1,0:T(8,128)(2,1)}, u32[]{:S(2)}, u32[]{:S(2)}) collective-permute-start(bf16[3,128,768]{2,1,0:T(8,128)(2,1)} %collective-permute-done.9.refs_11_), channel_id=1, source_target_pairs={{0,32},{32,0},{64,96},{96,64},{128,160},{160,128},{192,224},{224,1... | collective-permute-start | bytes 1769480 | tf_op jit(solution)/shard_map/ppermute | solution.py:263
  92.2 1.9 collective-permute-done.10.refs_12_
  94.0 26.1 %all-to-all-done = bf16[32,8,4096]{2,1,0:T(8,128)(2,1)S(1)} async-done(((bf16[32,8,4096]{2,1,0:T(8,128)(2,1)}), bf16[32,8,4096]{2,1,0:T(8,128)(2,1)S(1)}, u32[]{:S(2)}, u32[]{:S(2)}) %all-to-all-start) | async-done | bytes 2097184 | tf_op jit(solution)/shard_map/all_to_all | solution.py:282
  120.1 9.5 %shard_map.111 = (bf16[256,4096]{1,0:T(8,128)(2,1)}, bf16[256,768]{1,0:T(8,128)(2,1)S(1)}, bf16[256,768]{1,0:T(8,128)(2,1)S(1)}, bf16[256,768]{1,0:T(8,128)(2,1)S(1)}) custom-call(s32[17]{0:T(128)S(1)} %compare_select_fusion.1.order_ref, bf16[256,4096]{1,0:T(8,128)(2,1)S(1)} %bitcast.37, bf16[3,128,768]{2,1,0:T(8,128)(2,1)} %copy-done.7, ...), custom_call_target="tpu_custom_call" | custom-call | flops 4831838208 | bytes 13631488 | tf_op jit(solution)/shard_map/pallas_call | solution.py:166
  129.7 3.8 %all-to-all-start.1 = ((bf16[32,8,4096]{2,1,0:T(8,128)(2,1)}), bf16[32,8,4096]{2,1,0:T(8,128)(2,1)S(1)}, u32[]{:S(2)}, u32[]{:S(2)}) async-start(bf16[32,8,4096]{2,1,0:T(8,128)(2,1)} %bitcast.42), calls=%async_computation.1 | async-start | bytes 4194304 | tf_op jit(solution)/shard_map/all_to_all | solution.py:282
  133.5 1.6 copy-done.1
  135.1 2.0 shard_map.113
  137.1 2.7 %collective-permute-start.15 = (bf16[8,128,768]{2,1,0:T(8,128)(2,1)S(1)}, bf16[8,128,768]{2,1,0:T(8,128)(2,1)S(1)}, u32[]{:S(2)}, u32[]{:S(2)}) collective-permute-start(bf16[8,128,768]{2,1,0:T(8,128)(2,1)S(1)} %get-tuple-element.36), channel_id=1, source_target_pairs={{0,32},{32,0},{64,96},{96,64},{128,160},{160,128},{192,224},{224,1... | collective-permute-start | bytes 4718600 | tf_op jit(solution)/shard_map/ppermute | solution.py:263
  139.8 1.9 collective-permute-start.16
  141.7 2.6 %collective-permute-start.17 = (bf16[8,128,768]{2,1,0:T(8,128)(2,1)S(1)}, bf16[8,128,768]{2,1,0:T(8,128)(2,1)S(1)}, u32[]{:S(2)}, u32[]{:S(2)}) collective-permute-start(bf16[8,128,768]{2,1,0:T(8,128)(2,1)S(1)} %get-tuple-element.38), channel_id=1, source_target_pairs={{0,32},{32,0},{64,96},{96,64},{128,160},{160,128},{192,224},{224,1... | collective-permute-start | bytes 4718600 | tf_op jit(solution)/shard_map/ppermute | solution.py:263
  144.3 0.8 collective-permute-done.16.refs_6_
  145.1 2.2 collective-permute-done.17.refs_7_
  147.3 2.1 shard_map.114
  149.4 3.1 %collective-permute-start.18 = (bf16[2,128,768]{2,1,0:T(8,128)(2,1)S(1)}, bf16[2,128,768]{2,1,0:T(8,128)(2,1)S(1)}, u32[]{:S(2)}, u32[]{:S(2)}) collective-permute-start(bf16[2,128,768]{2,1,0:T(8,128)(2,1)S(1)} %get-tuple-element.40), channel_id=1, source_target_pairs={{0,128},{32,160},{64,192},{96,224},{128,256},{160,288},{192,320},{... | collective-permute-start | bytes 1179656 | tf_op jit(solution)/shard_map/ppermute | solution.py:263
  152.5 4.4 %collective-permute-start.19 = (bf16[2,128,768]{2,1,0:T(8,128)(2,1)S(1)}, bf16[2,128,768]{2,1,0:T(8,128)(2,1)S(1)}, u32[]{:S(2)}, u32[]{:S(2)}) collective-permute-start(bf16[2,128,768]{2,1,0:T(8,128)(2,1)S(1)} %get-tuple-element.41), channel_id=1, source_target_pairs={{0,256},{32,288},{64,320},{96,352},{128,384},{160,416},{192,448},{... | collective-permute-start | bytes 1179656 | tf_op jit(solution)/shard_map/ppermute | solution.py:263
  156.9 3.1 %collective-permute-start.20 = (bf16[2,128,768]{2,1,0:T(8,128)(2,1)S(1)}, bf16[2,128,768]{2,1,0:T(8,128)(2,1)S(1)}, u32[]{:S(2)}, u32[]{:S(2)}) collective-permute-start(bf16[2,128,768]{2,1,0:T(8,128)(2,1)S(1)} %get-tuple-element.42), channel_id=1, source_target_pairs={{0,384},{32,416},{64,448},{96,480},{128,0},{160,32},{192,64},{224,... | collective-permute-start | bytes 1179656 | tf_op jit(solution)/shard_map/ppermute | solution.py:263
  160.0 2.2 collective-permute-start.22
  162.2 2.8 %collective-permute-start.23 = (bf16[2,128,768]{2,1,0:T(8,128)(2,1)S(1)}, bf16[2,128,768]{2,1,0:T(8,128)(2,1)S(1)}, u32[]{:S(2)}, u32[]{:S(2)}) collective-permute-start(bf16[2,128,768]{2,1,0:T(8,128)(2,1)S(1)} %get-tuple-element.45), channel_id=1, source_target_pairs={{0,256},{32,288},{64,320},{96,352},{128,384},{160,416},{192,448},{... | collective-permute-start | bytes 1179656 | tf_op jit(solution)/shard_map/ppermute | solution.py:263
  165.0 3.4 %collective-permute-start.24 = (bf16[2,128,768]{2,1,0:T(8,128)(2,1)S(1)}, bf16[2,128,768]{2,1,0:T(8,128)(2,1)S(1)}, u32[]{:S(2)}, u32[]{:S(2)}) collective-permute-start(bf16[2,128,768]{2,1,0:T(8,128)(2,1)S(1)} %get-tuple-element.46), channel_id=1, source_target_pairs={{0,384},{32,416},{64,448},{96,480},{128,0},{160,32},{192,64},{224,... | collective-permute-start | bytes 1179656 | tf_op jit(solution)/shard_map/ppermute | solution.py:263
  168.4 4.0 %collective-permute-done.19 = bf16[2,128,768]{2,1,0:T(8,128)(2,1)S(1)} collective-permute-done((bf16[2,128,768]{2,1,0:T(8,128)(2,1)S(1)}, bf16[2,128,768]{2,1,0:T(8,128)(2,1)S(1)}, u32[]{:S(2)}, u32[]{:S(2)}) %collective-permute-start.19) | collective-permute-done | bytes 393248 | tf_op jit(solution)/shard_map/ppermute | solution.py:263
  172.4 1.9 collective-permute-start.26
  174.3 4.1 %collective-permute-start.27 = (bf16[2,128,768]{2,1,0:T(8,128)(2,1)S(1)}, bf16[2,128,768]{2,1,0:T(8,128)(2,1)S(1)}, u32[]{:S(2)}, u32[]{:S(2)}) collective-permute-start(bf16[2,128,768]{2,1,0:T(8,128)(2,1)S(1)} %get-tuple-element.49), channel_id=1, source_target_pairs={{0,256},{32,288},{64,320},{96,352},{128,384},{160,416},{192,448},{... | collective-permute-start | bytes 1179656 | tf_op jit(solution)/shard_map/ppermute | solution.py:263
  178.5 0.2 convert_add_fusion.2
  178.7 3.2 %collective-permute-done.22 = bf16[2,128,768]{2,1,0:T(8,128)(2,1)S(1)} collective-permute-done((bf16[2,128,768]{2,1,0:T(8,128)(2,1)S(1)}, bf16[2,128,768]{2,1,0:T(8,128)(2,1)S(1)}, u32[]{:S(2)}, u32[]{:S(2)}) %collective-permute-start.22) | collective-permute-done | bytes 393248 | tf_op jit(solution)/shard_map/ppermute | solution.py:263
  181.9 2.0 collective-permute-start.28
  183.9 5.4 %collective-permute-done.23 = bf16[2,128,768]{2,1,0:T(8,128)(2,1)S(1)} collective-permute-done((bf16[2,128,768]{2,1,0:T(8,128)(2,1)S(1)}, bf16[2,128,768]{2,1,0:T(8,128)(2,1)S(1)}, u32[]{:S(2)}, u32[]{:S(2)}) %collective-permute-start.23) | collective-permute-done | bytes 393248 | tf_op jit(solution)/shard_map/ppermute | solution.py:263
  189.3 4.5 %collective-permute-start.21 = (bf16[128,768]{1,0:T(8,128)(2,1)S(1)}, bf16[128,768]{1,0:T(8,128)(2,1)S(1)}, u32[]{:S(2)}, u32[]{:S(2)}) collective-permute-start(bf16[128,768]{1,0:T(8,128)(2,1)S(1)} %fusion.6), channel_id=1, source_target_pairs={{0,64},{32,96},{64,0},{96,32},{128,192},{160,224},{192,128},{224,1... | collective-permute-start | bytes 589832 | tf_op jit(solution)/shard_map/ppermute | solution.py:263
  193.8 0.2 convert_add_fusion.1
  194.0 2.3 collective-permute-start.25
  196.3 2.4 %collective-permute-done.26 = bf16[2,128,768]{2,1,0:T(8,128)(2,1)S(1)} collective-permute-done((bf16[2,128,768]{2,1,0:T(8,128)(2,1)S(1)}, bf16[2,128,768]{2,1,0:T(8,128)(2,1)S(1)}, u32[]{:S(2)}, u32[]{:S(2)}) %collective-permute-start.26) | collective-permute-done | bytes 393248 | tf_op jit(solution)/shard_map/ppermute | solution.py:263
  198.7 7.4 %collective-permute-done.27 = bf16[2,128,768]{2,1,0:T(8,128)(2,1)S(1)} collective-permute-done((bf16[2,128,768]{2,1,0:T(8,128)(2,1)S(1)}, bf16[2,128,768]{2,1,0:T(8,128)(2,1)S(1)}, u32[]{:S(2)}, u32[]{:S(2)}) %collective-permute-start.27) | collective-permute-done | bytes 393248 | tf_op jit(solution)/shard_map/ppermute | solution.py:263
  206.1 1.2 collective-permute-done.28
  207.4 0.2 convert_add_fusion
  207.6 0.0 copy-start.3
  207.6 4.5 %collective-permute-start.29 = (bf16[128,768]{1,0:T(8,128)(2,1)S(1)}, bf16[128,768]{1,0:T(8,128)(2,1)S(1)}, u32[]{:S(2)}, u32[]{:S(2)}) collective-permute-start(bf16[128,768]{1,0:T(8,128)(2,1)S(1)} %fusion.8), channel_id=1, source_target_pairs={{0,64},{32,96},{64,0},{96,32},{128,192},{160,224},{192,128},{224,1... | collective-permute-start | bytes 589832 | tf_op jit(solution)/shard_map/ppermute | solution.py:263
  212.2 0.8 fusion.5
  212.9 0.8 fusion.3
  213.7 2.4 %collective-permute-done.29 = bf16[128,768]{1,0:T(8,128)(2,1)S(1)} collective-permute-done((bf16[128,768]{1,0:T(8,128)(2,1)S(1)}, bf16[128,768]{1,0:T(8,128)(2,1)S(1)}, u32[]{:S(2)}, u32[]{:S(2)}) %collective-permute-start.29) | collective-permute-done | bytes 196640 | tf_op jit(solution)/shard_map/ppermute | solution.py:263
  216.1 0.8 fusion.1
  216.9 16.2 %all-to-all-done.1 = bf16[32,8,4096]{2,1,0:T(8,128)(2,1)S(1)} async-done(((bf16[32,8,4096]{2,1,0:T(8,128)(2,1)}), bf16[32,8,4096]{2,1,0:T(8,128)(2,1)S(1)}, u32[]{:S(2)}, u32[]{:S(2)}) %all-to-all-start.1) | async-done | bytes 2097184 | tf_op jit(solution)/shard_map/all_to_all | solution.py:282
  233.1 1.3 shard_map.112
  (50 shorter events, 0.2 us)
Async XLA Ops:
  3.6 16.0 %copy-start.4 = (bf16[1,128,768]{2,1,0:T(8,128)(2,1)S(1)}, bf16[1,128,768]{2,1,0:T(8,128)(2,1)}, u32[]{:S(2)}) copy-start(bf16[1,128,768]{2,1,0:T(8,128)(2,1)} %param.11) | copy-start | bytes 589828
  3.6 16.0 %copy-start.5 = (bf16[1,128,768]{2,1,0:T(8,128)(2,1)S(1)}, bf16[1,128,768]{2,1,0:T(8,128)(2,1)}, u32[]{:S(2)}) copy-start(bf16[1,128,768]{2,1,0:T(8,128)(2,1)} %param.12) | copy-start | bytes 589828
  3.6 16.0 %copy-start.6 = (bf16[1,128,768]{2,1,0:T(8,128)(2,1)S(1)}, bf16[1,128,768]{2,1,0:T(8,128)(2,1)}, u32[]{:S(2)}) copy-start(bf16[1,128,768]{2,1,0:T(8,128)(2,1)} %param.13) | copy-start | bytes 589828
  3.6 116.5 %all-to-all-start = ((bf16[32,8,4096]{2,1,0:T(8,128)(2,1)}), bf16[32,8,4096]{2,1,0:T(8,128)(2,1)S(1)}, u32[]{:S(2)}, u32[]{:S(2)}) async-start(bf16[32,8,4096]{2,1,0:T(8,128)(2,1)} %bitcast.43), calls=%async_computation | async-start | bytes 4194304 | tf_op jit(solution)/shard_map/all_to_all | solution.py:282
  19.7 13.9 %copy-start.7 = (bf16[3,128,768]{2,1,0:T(8,128)(2,1)}, bf16[3,128,768]{2,1,0:T(8,128)(2,1)S(1)}, u32[]{:S(2)}) copy-start(bf16[3,128,768]{2,1,0:T(8,128)(2,1)S(1)} %constant_dynamic-update-slice_fusion.refs_1_) | copy-start | bytes 1769476
  19.7 19.7 %collective-permute-start.7 = (bf16[3,128,768]{2,1,0:T(8,128)(2,1)S(1)}, bf16[3,128,768]{2,1,0:T(8,128)(2,1)S(1)}, u32[]{:S(2)}, u32[]{:S(2)}) collective-permute-start(bf16[3,128,768]{2,1,0:T(8,128)(2,1)S(1)} %constant_dynamic-update-slice_fusion.refs_1_), channel_id=1, source_target_pairs={{0,64},{32,96},{64,0},{96,32},{128,192},{160,224},{192,128},{224,1... | collective-permute-start | bytes 1769480 | tf_op jit(solution)/shard_map/ppermute | solution.py:263
  24.2 19.6 %collective-permute-start.5 = (bf16[3,128,768]{2,1,0:T(8,128)(2,1)S(1)}, bf16[3,128,768]{2,1,0:T(8,128)(2,1)S(1)}, u32[]{:S(2)}, u32[]{:S(2)}) collective-permute-start(bf16[3,128,768]{2,1,0:T(8,128)(2,1)S(1)} %constant_dynamic-update-slice_fusion.refs_1_), channel_id=1, source_target_pairs={{0,384},{32,416},{64,448},{96,480},{128,0},{160,32},{192,64},{224,... | collective-permute-start | bytes 1769480 | tf_op jit(solution)/shard_map/ppermute | solution.py:263
  28.6 17.7 %collective-permute-start.3 = (bf16[3,128,768]{2,1,0:T(8,128)(2,1)S(1)}, bf16[3,128,768]{2,1,0:T(8,128)(2,1)S(1)}, u32[]{:S(2)}, u32[]{:S(2)}) collective-permute-start(bf16[3,128,768]{2,1,0:T(8,128)(2,1)S(1)} %constant_dynamic-update-slice_fusion.refs_1_), channel_id=1, source_target_pairs={{0,256},{32,288},{64,320},{96,352},{128,384},{160,416},{192,448},{... | collective-permute-start | bytes 1769480 | tf_op jit(solution)/shard_map/ppermute | solution.py:263
  31.0 31.0 %collective-permute-start.1 = (bf16[3,128,768]{2,1,0:T(8,128)(2,1)S(1)}, bf16[3,128,768]{2,1,0:T(8,128)(2,1)S(1)}, u32[]{:S(2)}, u32[]{:S(2)}) collective-permute-start(bf16[3,128,768]{2,1,0:T(8,128)(2,1)S(1)} %constant_dynamic-update-slice_fusion.refs_1_), channel_id=1, source_target_pairs={{0,128},{32,160},{64,192},{96,224},{128,256},{160,288},{192,320},{... | collective-permute-start | bytes 1769480 | tf_op jit(solution)/shard_map/ppermute | solution.py:263
  33.6 32.7 %collective-permute-start = (bf16[3,128,768]{2,1,0:T(8,128)(2,1)S(1)}, bf16[3,128,768]{2,1,0:T(8,128)(2,1)S(1)}, u32[]{:S(2)}, u32[]{:S(2)}) collective-permute-start(bf16[3,128,768]{2,1,0:T(8,128)(2,1)S(1)} %constant_dynamic-update-slice_fusion.refs_1_), channel_id=1, source_target_pairs={{0,32},{32,0},{64,96},{96,64},{128,160},{160,128},{192,224},{224,1... | collective-permute-start | bytes 1769480 | tf_op jit(solution)/shard_map/ppermute | solution.py:263
  39.4 26.8 %copy-start.8 = (bf16[3,128,768]{2,1,0:T(8,128)(2,1)}, bf16[3,128,768]{2,1,0:T(8,128)(2,1)S(1)}, u32[]{:S(2)}) copy-start(bf16[3,128,768]{2,1,0:T(8,128)(2,1)S(1)} %collective-permute-done.7.refs_9_) | copy-start | bytes 1769476
  39.4 28.8 %collective-permute-start.13 = (bf16[3,128,768]{2,1,0:T(8,128)(2,1)S(1)}, bf16[3,128,768]{2,1,0:T(8,128)(2,1)}, u32[]{:S(2)}, u32[]{:S(2)}) collective-permute-start(bf16[3,128,768]{2,1,0:T(8,128)(2,1)S(1)} %collective-permute-done.7.refs_9_), channel_id=1, source_target_pairs={{0,384},{32,416},{64,448},{96,480},{128,0},{160,32},{192,64},{224,... | collective-permute-start | bytes 1769480 | tf_op jit(solution)/shard_map/ppermute | solution.py:263
  43.8 43.9 %copy-start.9 = (bf16[3,128,768]{2,1,0:T(8,128)(2,1)}, bf16[3,128,768]{2,1,0:T(8,128)(2,1)S(1)}, u32[]{:S(2)}) copy-start(bf16[3,128,768]{2,1,0:T(8,128)(2,1)S(1)} %collective-permute-done.5.refs_7_) | copy-start | bytes 1769476
  43.8 38.2 %collective-permute-start.11 = (bf16[3,128,768]{2,1,0:T(8,128)(2,1)S(1)}, bf16[3,128,768]{2,1,0:T(8,128)(2,1)}, u32[]{:S(2)}, u32[]{:S(2)}) collective-permute-start(bf16[3,128,768]{2,1,0:T(8,128)(2,1)S(1)} %collective-permute-done.7.refs_9_), channel_id=1, source_target_pairs={{0,256},{32,288},{64,320},{96,352},{128,384},{160,416},{192,448},{... | collective-permute-start | bytes 1769480 | tf_op jit(solution)/shard_map/ppermute | solution.py:263
  46.3 73.8 %copy-start.10 = (bf16[3,128,768]{2,1,0:T(8,128)(2,1)}, bf16[3,128,768]{2,1,0:T(8,128)(2,1)S(1)}, u32[]{:S(2)}) copy-start(bf16[3,128,768]{2,1,0:T(8,128)(2,1)S(1)} %collective-permute-done.3.refs_5_) | copy-start | bytes 1769476
  46.3 38.9 %collective-permute-start.9 = (bf16[3,128,768]{2,1,0:T(8,128)(2,1)S(1)}, bf16[3,128,768]{2,1,0:T(8,128)(2,1)}, u32[]{:S(2)}, u32[]{:S(2)}) collective-permute-start(bf16[3,128,768]{2,1,0:T(8,128)(2,1)S(1)} %collective-permute-done.7.refs_9_), channel_id=1, source_target_pairs={{0,128},{32,160},{64,192},{96,224},{128,256},{160,288},{192,320},{... | collective-permute-start | bytes 1769480 | tf_op jit(solution)/shard_map/ppermute | solution.py:263
  62.1 58.0 %copy-start.11 = (bf16[3,128,768]{2,1,0:T(8,128)(2,1)}, bf16[3,128,768]{2,1,0:T(8,128)(2,1)S(1)}, u32[]{:S(2)}) copy-start(bf16[3,128,768]{2,1,0:T(8,128)(2,1)S(1)} %collective-permute-done.1.refs_3_) | copy-start | bytes 1769476
  62.1 25.6 %collective-permute-start.8 = (bf16[3,128,768]{2,1,0:T(8,128)(2,1)S(1)}, bf16[3,128,768]{2,1,0:T(8,128)(2,1)S(1)}, u32[]{:S(2)}, u32[]{:S(2)}) collective-permute-start(bf16[3,128,768]{2,1,0:T(8,128)(2,1)S(1)} %collective-permute-done.7.refs_9_), channel_id=1, source_target_pairs={{0,32},{32,0},{64,96},{96,64},{128,160},{160,128},{192,224},{224,1... | collective-permute-start | bytes 1769480 | tf_op jit(solution)/shard_map/ppermute | solution.py:263
  66.3 23.4 %copy-start.12 = (bf16[3,128,768]{2,1,0:T(8,128)(2,1)}, bf16[3,128,768]{2,1,0:T(8,128)(2,1)S(1)}, u32[]{:S(2)}) copy-start(bf16[3,128,768]{2,1,0:T(8,128)(2,1)S(1)} %collective-permute-done.refs_2_) | copy-start | bytes 1769476
  66.3 23.4 %collective-permute-start.6 = (bf16[3,128,768]{2,1,0:T(8,128)(2,1)S(1)}, bf16[3,128,768]{2,1,0:T(8,128)(2,1)S(1)}, u32[]{:S(2)}, u32[]{:S(2)}) collective-permute-start(bf16[3,128,768]{2,1,0:T(8,128)(2,1)S(1)} %collective-permute-done.5.refs_7_), channel_id=1, source_target_pairs={{0,32},{32,0},{64,96},{96,64},{128,160},{160,128},{192,224},{224,1... | collective-permute-start | bytes 1769480 | tf_op jit(solution)/shard_map/ppermute | solution.py:263
  68.2 23.9 %collective-permute-start.4 = (bf16[3,128,768]{2,1,0:T(8,128)(2,1)S(1)}, bf16[3,128,768]{2,1,0:T(8,128)(2,1)}, u32[]{:S(2)}, u32[]{:S(2)}) collective-permute-start(bf16[3,128,768]{2,1,0:T(8,128)(2,1)S(1)} %collective-permute-done.3.refs_5_), channel_id=1, source_target_pairs={{0,32},{32,0},{64,96},{96,64},{128,160},{160,128},{192,224},{224,1... | collective-permute-start | bytes 1769480 | tf_op jit(solution)/shard_map/ppermute | solution.py:263
  82.0 10.1 %collective-permute-start.2 = (bf16[3,128,768]{2,1,0:T(8,128)(2,1)S(1)}, bf16[3,128,768]{2,1,0:T(8,128)(2,1)}, u32[]{:S(2)}, u32[]{:S(2)}) collective-permute-start(bf16[3,128,768]{2,1,0:T(8,128)(2,1)S(1)} %collective-permute-done.1.refs_3_), channel_id=1, source_target_pairs={{0,32},{32,0},{64,96},{96,64},{128,160},{160,128},{192,224},{224,1... | collective-permute-start | bytes 1769480 | tf_op jit(solution)/shard_map/ppermute | solution.py:263
  85.2 7.0 %collective-permute-start.14 = (bf16[3,128,768]{2,1,0:T(8,128)(2,1)}, bf16[3,128,768]{2,1,0:T(8,128)(2,1)}, u32[]{:S(2)}, u32[]{:S(2)}) collective-permute-start(bf16[3,128,768]{2,1,0:T(8,128)(2,1)} %collective-permute-done.13.refs_15_), channel_id=1, source_target_pairs={{0,32},{32,0},{64,96},{96,64},{128,160},{160,128},{192,224},{224,1... | collective-permute-start | bytes 1769480 | tf_op jit(solution)/shard_map/ppermute | solution.py:263
  87.7 4.4 %copy-start.13 = (bf16[3,128,768]{2,1,0:T(8,128)(2,1)}, bf16[3,128,768]{2,1,0:T(8,128)(2,1)S(1)}, u32[]{:S(2)}) copy-start(bf16[3,128,768]{2,1,0:T(8,128)(2,1)S(1)} %collective-permute-done.8.refs_10_) | copy-start | bytes 1769476
  87.7 4.5 %collective-permute-start.12 = (bf16[3,128,768]{2,1,0:T(8,128)(2,1)}, bf16[3,128,768]{2,1,0:T(8,128)(2,1)}, u32[]{:S(2)}, u32[]{:S(2)}) collective-permute-start(bf16[3,128,768]{2,1,0:T(8,128)(2,1)} %collective-permute-done.11.refs_13_), channel_id=1, source_target_pairs={{0,32},{32,0},{64,96},{96,64},{128,160},{160,128},{192,224},{224,1... | collective-permute-start | bytes 1769480 | tf_op jit(solution)/shard_map/ppermute | solution.py:263
  89.7 2.4 %copy-start.14 = (bf16[3,128,768]{2,1,0:T(8,128)(2,1)}, bf16[3,128,768]{2,1,0:T(8,128)(2,1)S(1)}, u32[]{:S(2)}) copy-start(bf16[3,128,768]{2,1,0:T(8,128)(2,1)S(1)} %collective-permute-done.6.refs_8_) | copy-start | bytes 1769476
  89.7 4.4 %collective-permute-start.10 = (bf16[3,128,768]{2,1,0:T(8,128)(2,1)}, bf16[3,128,768]{2,1,0:T(8,128)(2,1)}, u32[]{:S(2)}, u32[]{:S(2)}) collective-permute-start(bf16[3,128,768]{2,1,0:T(8,128)(2,1)} %collective-permute-done.9.refs_11_), channel_id=1, source_target_pairs={{0,32},{32,0},{64,96},{96,64},{128,160},{160,128},{192,224},{224,1... | collective-permute-start | bytes 1769480 | tf_op jit(solution)/shard_map/ppermute | solution.py:263
  120.1 9.6 %copy-start = (bf16[32,8,4096]{2,1,0:T(8,128)(2,1)}, bf16[32,8,4096]{2,1,0:T(8,128)(2,1)S(1)}, u32[]{:S(2)}) copy-start(bf16[32,8,4096]{2,1,0:T(8,128)(2,1)S(1)} %all-to-all-done) | copy-start | bytes 6291460
  129.7 103.4 %all-to-all-start.1 = ((bf16[32,8,4096]{2,1,0:T(8,128)(2,1)}), bf16[32,8,4096]{2,1,0:T(8,128)(2,1)S(1)}, u32[]{:S(2)}, u32[]{:S(2)}) async-start(bf16[32,8,4096]{2,1,0:T(8,128)(2,1)} %bitcast.42), calls=%async_computation.1 | async-start | bytes 4194304 | tf_op jit(solution)/shard_map/all_to_all | solution.py:282
  133.5 1.6 copy-start.1
  135.1 12.2 %copy-start.2 = (bf16[32,8,4096]{2,1,0:T(8,128)(2,1)S(1)}, bf16[32,8,4096]{2,1,0:T(8,128)(2,1)}, u32[]{:S(2)}) copy-start(bf16[32,8,4096]{2,1,0:T(8,128)(2,1)} %copy-done) | copy-start | bytes 6291460
  137.1 7.2 %collective-permute-start.15 = (bf16[8,128,768]{2,1,0:T(8,128)(2,1)S(1)}, bf16[8,128,768]{2,1,0:T(8,128)(2,1)S(1)}, u32[]{:S(2)}, u32[]{:S(2)}) collective-permute-start(bf16[8,128,768]{2,1,0:T(8,128)(2,1)S(1)} %get-tuple-element.36), channel_id=1, source_target_pairs={{0,32},{32,0},{64,96},{96,64},{128,160},{160,128},{192,224},{224,1... | collective-permute-start | bytes 4718600 | tf_op jit(solution)/shard_map/ppermute | solution.py:263
  139.8 5.3 %collective-permute-start.16 = (bf16[8,128,768]{2,1,0:T(8,128)(2,1)S(1)}, bf16[8,128,768]{2,1,0:T(8,128)(2,1)S(1)}, u32[]{:S(2)}, u32[]{:S(2)}) collective-permute-start(bf16[8,128,768]{2,1,0:T(8,128)(2,1)S(1)} %get-tuple-element.37), channel_id=1, source_target_pairs={{0,32},{32,0},{64,96},{96,64},{128,160},{160,128},{192,224},{224,1... | collective-permute-start | bytes 4718600 | tf_op jit(solution)/shard_map/ppermute | solution.py:263
  141.7 5.6 %collective-permute-start.17 = (bf16[8,128,768]{2,1,0:T(8,128)(2,1)S(1)}, bf16[8,128,768]{2,1,0:T(8,128)(2,1)S(1)}, u32[]{:S(2)}, u32[]{:S(2)}) collective-permute-start(bf16[8,128,768]{2,1,0:T(8,128)(2,1)S(1)} %get-tuple-element.38), channel_id=1, source_target_pairs={{0,32},{32,0},{64,96},{96,64},{128,160},{160,128},{192,224},{224,1... | collective-permute-start | bytes 4718600 | tf_op jit(solution)/shard_map/ppermute | solution.py:263
  149.4 15.6 %collective-permute-start.18 = (bf16[2,128,768]{2,1,0:T(8,128)(2,1)S(1)}, bf16[2,128,768]{2,1,0:T(8,128)(2,1)S(1)}, u32[]{:S(2)}, u32[]{:S(2)}) collective-permute-start(bf16[2,128,768]{2,1,0:T(8,128)(2,1)S(1)} %get-tuple-element.40), channel_id=1, source_target_pairs={{0,128},{32,160},{64,192},{96,224},{128,256},{160,288},{192,320},{... | collective-permute-start | bytes 1179656 | tf_op jit(solution)/shard_map/ppermute | solution.py:263
  152.5 19.9 %collective-permute-start.19 = (bf16[2,128,768]{2,1,0:T(8,128)(2,1)S(1)}, bf16[2,128,768]{2,1,0:T(8,128)(2,1)S(1)}, u32[]{:S(2)}, u32[]{:S(2)}) collective-permute-start(bf16[2,128,768]{2,1,0:T(8,128)(2,1)S(1)} %get-tuple-element.41), channel_id=1, source_target_pairs={{0,256},{32,288},{64,320},{96,352},{128,384},{160,416},{192,448},{... | collective-permute-start | bytes 1179656 | tf_op jit(solution)/shard_map/ppermute | solution.py:263
  156.9 17.4 %collective-permute-start.20 = (bf16[2,128,768]{2,1,0:T(8,128)(2,1)S(1)}, bf16[2,128,768]{2,1,0:T(8,128)(2,1)S(1)}, u32[]{:S(2)}, u32[]{:S(2)}) collective-permute-start(bf16[2,128,768]{2,1,0:T(8,128)(2,1)S(1)} %get-tuple-element.42), channel_id=1, source_target_pairs={{0,384},{32,416},{64,448},{96,480},{128,0},{160,32},{192,64},{224,... | collective-permute-start | bytes 1179656 | tf_op jit(solution)/shard_map/ppermute | solution.py:263
  160.0 22.0 %collective-permute-start.22 = (bf16[2,128,768]{2,1,0:T(8,128)(2,1)S(1)}, bf16[2,128,768]{2,1,0:T(8,128)(2,1)S(1)}, u32[]{:S(2)}, u32[]{:S(2)}) collective-permute-start(bf16[2,128,768]{2,1,0:T(8,128)(2,1)S(1)} %get-tuple-element.44), channel_id=1, source_target_pairs={{0,128},{32,160},{64,192},{96,224},{128,256},{160,288},{192,320},{... | collective-permute-start | bytes 1179656 | tf_op jit(solution)/shard_map/ppermute | solution.py:263
  162.2 27.1 %collective-permute-start.23 = (bf16[2,128,768]{2,1,0:T(8,128)(2,1)S(1)}, bf16[2,128,768]{2,1,0:T(8,128)(2,1)S(1)}, u32[]{:S(2)}, u32[]{:S(2)}) collective-permute-start(bf16[2,128,768]{2,1,0:T(8,128)(2,1)S(1)} %get-tuple-element.45), channel_id=1, source_target_pairs={{0,256},{32,288},{64,320},{96,352},{128,384},{160,416},{192,448},{... | collective-permute-start | bytes 1179656 | tf_op jit(solution)/shard_map/ppermute | solution.py:263
  165.0 28.8 %collective-permute-start.24 = (bf16[2,128,768]{2,1,0:T(8,128)(2,1)S(1)}, bf16[2,128,768]{2,1,0:T(8,128)(2,1)S(1)}, u32[]{:S(2)}, u32[]{:S(2)}) collective-permute-start(bf16[2,128,768]{2,1,0:T(8,128)(2,1)S(1)} %get-tuple-element.46), channel_id=1, source_target_pairs={{0,384},{32,416},{64,448},{96,480},{128,0},{160,32},{192,64},{224,... | collective-permute-start | bytes 1179656 | tf_op jit(solution)/shard_map/ppermute | solution.py:263
  172.4 26.3 %collective-permute-start.26 = (bf16[2,128,768]{2,1,0:T(8,128)(2,1)S(1)}, bf16[2,128,768]{2,1,0:T(8,128)(2,1)S(1)}, u32[]{:S(2)}, u32[]{:S(2)}) collective-permute-start(bf16[2,128,768]{2,1,0:T(8,128)(2,1)S(1)} %get-tuple-element.48), channel_id=1, source_target_pairs={{0,128},{32,160},{64,192},{96,224},{128,256},{160,288},{192,320},{... | collective-permute-start | bytes 1179656 | tf_op jit(solution)/shard_map/ppermute | solution.py:263
  174.3 31.8 %collective-permute-start.27 = (bf16[2,128,768]{2,1,0:T(8,128)(2,1)S(1)}, bf16[2,128,768]{2,1,0:T(8,128)(2,1)S(1)}, u32[]{:S(2)}, u32[]{:S(2)}) collective-permute-start(bf16[2,128,768]{2,1,0:T(8,128)(2,1)S(1)} %get-tuple-element.49), channel_id=1, source_target_pairs={{0,256},{32,288},{64,320},{96,352},{128,384},{160,416},{192,448},{... | collective-permute-start | bytes 1179656 | tf_op jit(solution)/shard_map/ppermute | solution.py:263
  181.9 25.4 %collective-permute-start.28 = (bf16[2,128,768]{2,1,0:T(8,128)(2,1)S(1)}, bf16[2,128,768]{2,1,0:T(8,128)(2,1)S(1)}, u32[]{:S(2)}, u32[]{:S(2)}) collective-permute-start(bf16[2,128,768]{2,1,0:T(8,128)(2,1)S(1)} %get-tuple-element.50), channel_id=1, source_target_pairs={{0,384},{32,416},{64,448},{96,480},{128,0},{160,32},{192,64},{224,... | collective-permute-start | bytes 1179656 | tf_op jit(solution)/shard_map/ppermute | solution.py:263
  189.3 22.9 %collective-permute-start.21 = (bf16[128,768]{1,0:T(8,128)(2,1)S(1)}, bf16[128,768]{1,0:T(8,128)(2,1)S(1)}, u32[]{:S(2)}, u32[]{:S(2)}) collective-permute-start(bf16[128,768]{1,0:T(8,128)(2,1)S(1)} %fusion.6), channel_id=1, source_target_pairs={{0,64},{32,96},{64,0},{96,32},{128,192},{160,224},{192,128},{224,1... | collective-permute-start | bytes 589832 | tf_op jit(solution)/shard_map/ppermute | solution.py:263
  194.0 18.9 %collective-permute-start.25 = (bf16[128,768]{1,0:T(8,128)(2,1)S(1)}, bf16[128,768]{1,0:T(8,128)(2,1)S(1)}, u32[]{:S(2)}, u32[]{:S(2)}) collective-permute-start(bf16[128,768]{1,0:T(8,128)(2,1)S(1)} %fusion.7), channel_id=1, source_target_pairs={{0,64},{32,96},{64,0},{96,32},{128,192},{160,224},{192,128},{224,1... | collective-permute-start | bytes 589832 | tf_op jit(solution)/shard_map/ppermute | solution.py:263
  207.6 25.5 %copy-start.3 = (s32[128,1]{0,1:T(1,128)S(1)}, s32[128,1]{0,1:T(1,128)}, u32[]{:S(2)}) copy-start(s32[128,1]{0,1:T(1,128)} %param.9) | copy-start | bytes 1540
  207.6 8.5 %collective-permute-start.29 = (bf16[128,768]{1,0:T(8,128)(2,1)S(1)}, bf16[128,768]{1,0:T(8,128)(2,1)S(1)}, u32[]{:S(2)}, u32[]{:S(2)}) collective-permute-start(bf16[128,768]{1,0:T(8,128)(2,1)S(1)} %fusion.8), channel_id=1, source_target_pairs={{0,64},{32,96},{64,0},{96,32},{128,192},{160,224},{192,128},{224,1... | collective-permute-start | bytes 589832 | tf_op jit(solution)/shard_map/ppermute | solution.py:263

commit v8 on v7

--- a/solution.py
+++ b/solution.py
@@ -108,7 +108,8 @@
     loads = [
         pltpu.make_async_copy(shards_in[n], shards.at[n], in_sems.at[n]) for n in range(2 * pairs)
     ]
-    for load in loads:
+    ahead = 2 * 4
+    for load in loads[:ahead]:
         load.start()
     stores = [
         pltpu.make_async_copy(send.at[:, cut], send_out.at[:, cut], out_sems.at[n])
@@ -130,6 +131,8 @@
     for p in range(pairs):
         loads[2 * p].wait()
         loads[2 * p + 1].wait()
+        for load in loads[2 * p + ahead : 2 * p + 2 + ahead]:
+            load.start()
         x = left(p, 0)
         pre = pre + mm(x, right(p, 0, every), NN)
         lin = lin + mm(x, right(p, 1, every), NN)
@@ -203,15 +206,25 @@
 
 def finish_kernel(pick_ref, unit_ref, got_ref, mixed_out, back_out, mixed, back, sems):
     width = mixed.shape[1]
+    parts = sems.shape[1]
+    step = width // parts
+    cuts = [pl.ds(n * step, step) for n in range(parts)]
+    stores = []
+
+    def store(m, n, source, target):
+        stores.append(pltpu.make_async_copy(source.at[:, cuts[n]], target.at[:, cuts[n]], sems.at[m, n]))
+        stores[-1].start()
+
+    for n, cut in enumerate(cuts):
+        other = pl.ds(width + n * step, step)
+        back[:, cut] = mm(pick_ref[...], got_ref[:, other], TN).astype(BF)
+        store(1, n, back, back_out)
     scale = column(unit_ref[...].astype(F32) / 256.0)
-    mixed[...] = (scale * mm(pick_ref[...], got_ref[:, :width], TN)).astype(BF)
-    first = pltpu.make_async_copy(mixed, mixed_out, sems.at[0])
-    first.start()
-    back[...] = mm(pick_ref[...], got_ref[:, width:], TN).astype(BF)
-    second = pltpu.make_async_copy(back, back_out, sems.at[1])
-    second.start()
-    first.wait()
-    second.wait()
+    for n, cut in enumerate(cuts):
+        mixed[:, cut] = (scale * mm(pick_ref[...], got_ref[:, cut], TN)).astype(BF)
+        store(0, n, mixed, mixed_out)
+    for copy in stores:
+        copy.wait()
 
 
 def finish_call(pick, units, got):
@@ -223,7 +236,7 @@
         in_specs=[near] * 3,
         out_specs=[far] * 2,
         out_shape=[pltpu.HBM((tok, width), BF)] * 2,
-        scratch_shapes=[*[VM((tok, width), BF)] * 2, pltpu.SemaphoreType.DMA((2,))],
+        scratch_shapes=[*[VM((tok, width), BF)] * 2, pltpu.SemaphoreType.DMA((2, 2))],
         compiler_params=params(24),
         cost_estimate=pl.CostEstimate(
             flops=4 * tok * slots * width, bytes_accessed=12 * tok * width, transcendentals=0

time: 236 us -> 236 us (level)
  no operation moved by 1% of the time
where the time goes in v8:
time: 236 us; the launch traced here: 235 us
  starting transfers between devices  129 us (55%)
  waiting for transfers between devices  82 us (35%)
  Pallas kernels  17.8 us (8%)
  other arithmetic  2.92 us (1%)
    ppermute x30, starting transfers between devices, permute(): return lax.ppermute(a, 'dp', [(i, to(i)) for i in range(groups)])  109 us
    all_to_all x2, waiting for transfers between devices, exchange(): got = lax.all_to_all(cut, 'expert', split_axis=0, concat_axis=0, tiled=True)  42.3 us
    ppermute x30, waiting for transfers between devices, permute(): return lax.ppermute(a, 'dp', [(i, to(i)) for i in range(groups)])  39.7 us
    all_to_all x2, starting transfers between devices, exchange(): got = lax.all_to_all(cut, 'expert', split_axis=0, concat_axis=0, tiled=True)  19.8 us
    pallas_call x1, Pallas kernels, experts_call(): pl.pallas_call(expert_kernel, in_specs=[pl.BlockSpec(memory_space=pltpu.S...  9.55 us
  transfers between devices with their start and end apart: 32, of which 15 were waited for; matrix products, arithmetic and copies ran while one was open for 1% of the time, Pallas kernels for 2%

profile of v8, /device:TPU:33, one launch (start us, length us, event | category | flops | bytes accessed | tf_op | source)
XLA Modules:
  0.0 234.6 jit_solution(13140198958315540611)
XLA Ops:
  0.6 2.9 %shard_map.110 = (bf16[256,4096]{1,0:T(8,128)(2,1)}, bf16[256,128]{1,0:T(8,128)(2,1)S(1)}) custom-call(s32[1,128]{1,0:T(1,128)} %bitcast.44, s32[1,128]{1,0:T(1,128)} %bitcast.40, bf16[128,2048]{1,0:T(8,128)(2,1)} %refs_2_.1, bf16[128,2048]{1,0:T(8,128)(2,1)} %refs_3_.1), custom_call_target="tpu_custom_call" | custom-call | flops 268435456 | bytes 3145728 | tf_op jit(solution)/shard_map/pallas_call | solution.py:79
  3.6 0.0 copy-start.4
  3.6 0.0 copy-start.5
  3.6 0.0 copy-start.6
  3.6 16.0 %all-to-all-start = ((bf16[32,8,4096]{2,1,0:T(8,128)(2,1)}), bf16[32,8,4096]{2,1,0:T(8,128)(2,1)S(1)}, u32[]{:S(2)}, u32[]{:S(2)}) async-start(bf16[32,8,4096]{2,1,0:T(8,128)(2,1)} %bitcast.43), calls=%async_computation | async-start | bytes 4194304 | tf_op jit(solution)/shard_map/all_to_all | solution.py:295
  19.7 4.5 %collective-permute-start.7 = (bf16[3,128,768]{2,1,0:T(8,128)(2,1)S(1)}, bf16[3,128,768]{2,1,0:T(8,128)(2,1)S(1)}, u32[]{:S(2)}, u32[]{:S(2)}) collective-permute-start(bf16[3,128,768]{2,1,0:T(8,128)(2,1)S(1)} %constant_dynamic-update-slice_fusion.refs_1_), channel_id=1, source_target_pairs={{0,64},{32,96},{64,0},{96,32},{128,192},{160,224},{192,128},{224,1... | collective-permute-start | bytes 1769480 | tf_op jit(solution)/shard_map/ppermute | solution.py:276
  24.2 4.4 %collective-permute-start.5 = (bf16[3,128,768]{2,1,0:T(8,128)(2,1)S(1)}, bf16[3,128,768]{2,1,0:T(8,128)(2,1)S(1)}, u32[]{:S(2)}, u32[]{:S(2)}) collective-permute-start(bf16[3,128,768]{2,1,0:T(8,128)(2,1)S(1)} %constant_dynamic-update-slice_fusion.refs_1_), channel_id=1, source_target_pairs={{0,384},{32,416},{64,448},{96,480},{128,0},{160,32},{192,64},{224,... | collective-permute-start | bytes 1769480 | tf_op jit(solution)/shard_map/ppermute | solution.py:276
  28.6 2.4 %collective-permute-start.3 = (bf16[3,128,768]{2,1,0:T(8,128)(2,1)S(1)}, bf16[3,128,768]{2,1,0:T(8,128)(2,1)S(1)}, u32[]{:S(2)}, u32[]{:S(2)}) collective-permute-start(bf16[3,128,768]{2,1,0:T(8,128)(2,1)S(1)} %constant_dynamic-update-slice_fusion.refs_1_), channel_id=1, source_target_pairs={{0,256},{32,288},{64,320},{96,352},{128,384},{160,416},{192,448},{... | collective-permute-start | bytes 1769480 | tf_op jit(solution)/shard_map/ppermute | solution.py:276
  31.0 2.5 %collective-permute-start.1 = (bf16[3,128,768]{2,1,0:T(8,128)(2,1)S(1)}, bf16[3,128,768]{2,1,0:T(8,128)(2,1)S(1)}, u32[]{:S(2)}, u32[]{:S(2)}) collective-permute-start(bf16[3,128,768]{2,1,0:T(8,128)(2,1)S(1)} %constant_dynamic-update-slice_fusion.refs_1_), channel_id=1, source_target_pairs={{0,128},{32,160},{64,192},{96,224},{128,256},{160,288},{192,320},{... | collective-permute-start | bytes 1769480 | tf_op jit(solution)/shard_map/ppermute | solution.py:276
  33.6 4.3 %collective-permute-start = (bf16[3,128,768]{2,1,0:T(8,128)(2,1)S(1)}, bf16[3,128,768]{2,1,0:T(8,128)(2,1)S(1)}, u32[]{:S(2)}, u32[]{:S(2)}) collective-permute-start(bf16[3,128,768]{2,1,0:T(8,128)(2,1)S(1)} %constant_dynamic-update-slice_fusion.refs_1_), channel_id=1, source_target_pairs={{0,32},{32,0},{64,96},{96,64},{128,160},{160,128},{192,224},{224,1... | collective-permute-start | bytes 1769480 | tf_op jit(solution)/shard_map/ppermute | solution.py:276
  37.8 1.6 collective-permute-done.7.refs_9_
  39.4 4.4 %collective-permute-start.13 = (bf16[3,128,768]{2,1,0:T(8,128)(2,1)S(1)}, bf16[3,128,768]{2,1,0:T(8,128)(2,1)}, u32[]{:S(2)}, u32[]{:S(2)}) collective-permute-start(bf16[3,128,768]{2,1,0:T(8,128)(2,1)S(1)} %collective-permute-done.7.refs_9_), channel_id=1, source_target_pairs={{0,384},{32,416},{64,448},{96,480},{128,0},{160,32},{192,64},{224,... | collective-permute-start | bytes 1769480 | tf_op jit(solution)/shard_map/ppermute | solution.py:276
  43.8 0.0 collective-permute-done.5.refs_7_
  43.8 2.4 %collective-permute-start.11 = (bf16[3,128,768]{2,1,0:T(8,128)(2,1)S(1)}, bf16[3,128,768]{2,1,0:T(8,128)(2,1)}, u32[]{:S(2)}, u32[]{:S(2)}) collective-permute-start(bf16[3,128,768]{2,1,0:T(8,128)(2,1)S(1)} %collective-permute-done.7.refs_9_), channel_id=1, source_target_pairs={{0,256},{32,288},{64,320},{96,352},{128,384},{160,416},{192,448},{... | collective-permute-start | bytes 1769480 | tf_op jit(solution)/shard_map/ppermute | solution.py:276
  46.3 9.8 %collective-permute-start.9 = (bf16[3,128,768]{2,1,0:T(8,128)(2,1)S(1)}, bf16[3,128,768]{2,1,0:T(8,128)(2,1)}, u32[]{:S(2)}, u32[]{:S(2)}) collective-permute-start(bf16[3,128,768]{2,1,0:T(8,128)(2,1)S(1)} %collective-permute-done.7.refs_9_), channel_id=1, source_target_pairs={{0,128},{32,160},{64,192},{96,224},{128,256},{160,288},{192,320},{... | collective-permute-start | bytes 1769480 | tf_op jit(solution)/shard_map/ppermute | solution.py:276
  56.1 5.9 %collective-permute-done.1.refs_3_ = bf16[3,128,768]{2,1,0:T(8,128)(2,1)S(1)} collective-permute-done((bf16[3,128,768]{2,1,0:T(8,128)(2,1)S(1)}, bf16[3,128,768]{2,1,0:T(8,128)(2,1)S(1)}, u32[]{:S(2)}, u32[]{:S(2)}) %collective-permute-start.1) | collective-permute-done | bytes 589856 | tf_op jit(solution)/shard_map/ppermute | solution.py:276
  62.1 4.1 %collective-permute-start.8 = (bf16[3,128,768]{2,1,0:T(8,128)(2,1)S(1)}, bf16[3,128,768]{2,1,0:T(8,128)(2,1)S(1)}, u32[]{:S(2)}, u32[]{:S(2)}) collective-permute-start(bf16[3,128,768]{2,1,0:T(8,128)(2,1)S(1)} %collective-permute-done.7.refs_9_), channel_id=1, source_target_pairs={{0,32},{32,0},{64,96},{96,64},{128,160},{160,128},{192,224},{224,1... | collective-permute-start | bytes 1769480 | tf_op jit(solution)/shard_map/ppermute | solution.py:276
  66.3 1.9 collective-permute-start.6
  68.2 13.8 %collective-permute-start.4 = (bf16[3,128,768]{2,1,0:T(8,128)(2,1)S(1)}, bf16[3,128,768]{2,1,0:T(8,128)(2,1)}, u32[]{:S(2)}, u32[]{:S(2)}) collective-permute-start(bf16[3,128,768]{2,1,0:T(8,128)(2,1)S(1)} %collective-permute-done.3.refs_5_), channel_id=1, source_target_pairs={{0,32},{32,0},{64,96},{96,64},{128,160},{160,128},{192,224},{224,1... | collective-permute-start | bytes 1769480 | tf_op jit(solution)/shard_map/ppermute | solution.py:276
  82.0 1.9 collective-permute-start.2
  83.9 1.2 collective-permute-done.9.refs_11_
  85.2 2.5 %collective-permute-start.14 = (bf16[3,128,768]{2,1,0:T(8,128)(2,1)}, bf16[3,128,768]{2,1,0:T(8,128)(2,1)}, u32[]{:S(2)}, u32[]{:S(2)}) collective-permute-start(bf16[3,128,768]{2,1,0:T(8,128)(2,1)} %collective-permute-done.13.refs_15_), channel_id=1, source_target_pairs={{0,32},{32,0},{64,96},{96,64},{128,160},{160,128},{192,224},{224,1... | collective-permute-start | bytes 1769480 | tf_op jit(solution)/shard_map/ppermute | solution.py:276
  87.7 1.9 collective-permute-start.12
  89.7 2.4 %collective-permute-start.10 = (bf16[3,128,768]{2,1,0:T(8,128)(2,1)}, bf16[3,128,768]{2,1,0:T(8,128)(2,1)}, u32[]{:S(2)}, u32[]{:S(2)}) collective-permute-start(bf16[3,128,768]{2,1,0:T(8,128)(2,1)} %collective-permute-done.9.refs_11_), channel_id=1, source_target_pairs={{0,32},{32,0},{64,96},{96,64},{128,160},{160,128},{192,224},{224,1... | collective-permute-start | bytes 1769480 | tf_op jit(solution)/shard_map/ppermute | solution.py:276
  92.2 1.9 collective-permute-done.10.refs_12_
  94.0 26.1 %all-to-all-done = bf16[32,8,4096]{2,1,0:T(8,128)(2,1)S(1)} async-done(((bf16[32,8,4096]{2,1,0:T(8,128)(2,1)}), bf16[32,8,4096]{2,1,0:T(8,128)(2,1)S(1)}, u32[]{:S(2)}, u32[]{:S(2)}) %all-to-all-start) | async-done | bytes 2097184 | tf_op jit(solution)/shard_map/all_to_all | solution.py:295
  120.1 9.6 %shard_map.111 = (bf16[256,4096]{1,0:T(8,128)(2,1)}, bf16[256,768]{1,0:T(8,128)(2,1)S(1)}, bf16[256,768]{1,0:T(8,128)(2,1)S(1)}, bf16[256,768]{1,0:T(8,128)(2,1)S(1)}) custom-call(s32[17]{0:T(128)S(1)} %compare_select_fusion.1.order_ref, bf16[256,4096]{1,0:T(8,128)(2,1)S(1)} %bitcast.37, bf16[3,128,768]{2,1,0:T(8,128)(2,1)} %copy-done.7, ...), custom_call_target="tpu_custom_call" | custom-call | flops 4831838208 | bytes 13631488 | tf_op jit(solution)/shard_map/pallas_call | solution.py:169
  129.7 3.8 %all-to-all-start.1 = ((bf16[32,8,4096]{2,1,0:T(8,128)(2,1)}), bf16[32,8,4096]{2,1,0:T(8,128)(2,1)S(1)}, u32[]{:S(2)}, u32[]{:S(2)}) async-start(bf16[32,8,4096]{2,1,0:T(8,128)(2,1)} %bitcast.42), calls=%async_computation.1 | async-start | bytes 4194304 | tf_op jit(solution)/shard_map/all_to_all | solution.py:295
  133.5 1.6 copy-done.1
  135.1 2.0 shard_map.113
  137.1 2.7 %collective-permute-start.15 = (bf16[8,128,768]{2,1,0:T(8,128)(2,1)S(1)}, bf16[8,128,768]{2,1,0:T(8,128)(2,1)S(1)}, u32[]{:S(2)}, u32[]{:S(2)}) collective-permute-start(bf16[8,128,768]{2,1,0:T(8,128)(2,1)S(1)} %get-tuple-element.36), channel_id=1, source_target_pairs={{0,32},{32,0},{64,96},{96,64},{128,160},{160,128},{192,224},{224,1... | collective-permute-start | bytes 4718600 | tf_op jit(solution)/shard_map/ppermute | solution.py:276
  139.8 1.9 collective-permute-start.16
  141.7 2.6 %collective-permute-start.17 = (bf16[8,128,768]{2,1,0:T(8,128)(2,1)S(1)}, bf16[8,128,768]{2,1,0:T(8,128)(2,1)S(1)}, u32[]{:S(2)}, u32[]{:S(2)}) collective-permute-start(bf16[8,128,768]{2,1,0:T(8,128)(2,1)S(1)} %get-tuple-element.38), channel_id=1, source_target_pairs={{0,32},{32,0},{64,96},{96,64},{128,160},{160,128},{192,224},{224,1... | collective-permute-start | bytes 4718600 | tf_op jit(solution)/shard_map/ppermute | solution.py:276
  144.3 0.8 collective-permute-done.16.refs_6_
  145.1 2.2 collective-permute-done.17.refs_7_
  147.3 2.1 shard_map.114
  149.4 3.1 %collective-permute-start.18 = (bf16[2,128,768]{2,1,0:T(8,128)(2,1)S(1)}, bf16[2,128,768]{2,1,0:T(8,128)(2,1)S(1)}, u32[]{:S(2)}, u32[]{:S(2)}) collective-permute-start(bf16[2,128,768]{2,1,0:T(8,128)(2,1)S(1)} %get-tuple-element.40), channel_id=1, source_target_pairs={{0,128},{32,160},{64,192},{96,224},{128,256},{160,288},{192,320},{... | collective-permute-start | bytes 1179656 | tf_op jit(solution)/shard_map/ppermute | solution.py:276
  152.5 4.4 %collective-permute-start.19 = (bf16[2,128,768]{2,1,0:T(8,128)(2,1)S(1)}, bf16[2,128,768]{2,1,0:T(8,128)(2,1)S(1)}, u32[]{:S(2)}, u32[]{:S(2)}) collective-permute-start(bf16[2,128,768]{2,1,0:T(8,128)(2,1)S(1)} %get-tuple-element.41), channel_id=1, source_target_pairs={{0,256},{32,288},{64,320},{96,352},{128,384},{160,416},{192,448},{... | collective-permute-start | bytes 1179656 | tf_op jit(solution)/shard_map/ppermute | solution.py:276
  156.9 3.1 %collective-permute-start.20 = (bf16[2,128,768]{2,1,0:T(8,128)(2,1)S(1)}, bf16[2,128,768]{2,1,0:T(8,128)(2,1)S(1)}, u32[]{:S(2)}, u32[]{:S(2)}) collective-permute-start(bf16[2,128,768]{2,1,0:T(8,128)(2,1)S(1)} %get-tuple-element.42), channel_id=1, source_target_pairs={{0,384},{32,416},{64,448},{96,480},{128,0},{160,32},{192,64},{224,... | collective-permute-start | bytes 1179656 | tf_op jit(solution)/shard_map/ppermute | solution.py:276
  160.0 2.2 collective-permute-start.22
  162.2 2.8 %collective-permute-start.23 = (bf16[2,128,768]{2,1,0:T(8,128)(2,1)S(1)}, bf16[2,128,768]{2,1,0:T(8,128)(2,1)S(1)}, u32[]{:S(2)}, u32[]{:S(2)}) collective-permute-start(bf16[2,128,768]{2,1,0:T(8,128)(2,1)S(1)} %get-tuple-element.45), channel_id=1, source_target_pairs={{0,256},{32,288},{64,320},{96,352},{128,384},{160,416},{192,448},{... | collective-permute-start | bytes 1179656 | tf_op jit(solution)/shard_map/ppermute | solution.py:276
  165.0 3.4 %collective-permute-start.24 = (bf16[2,128,768]{2,1,0:T(8,128)(2,1)S(1)}, bf16[2,128,768]{2,1,0:T(8,128)(2,1)S(1)}, u32[]{:S(2)}, u32[]{:S(2)}) collective-permute-start(bf16[2,128,768]{2,1,0:T(8,128)(2,1)S(1)} %get-tuple-element.46), channel_id=1, source_target_pairs={{0,384},{32,416},{64,448},{96,480},{128,0},{160,32},{192,64},{224,... | collective-permute-start | bytes 1179656 | tf_op jit(solution)/shard_map/ppermute | solution.py:276
  168.4 3.9 %collective-permute-done.19 = bf16[2,128,768]{2,1,0:T(8,128)(2,1)S(1)} collective-permute-done((bf16[2,128,768]{2,1,0:T(8,128)(2,1)S(1)}, bf16[2,128,768]{2,1,0:T(8,128)(2,1)S(1)}, u32[]{:S(2)}, u32[]{:S(2)}) %collective-permute-start.19) | collective-permute-done | bytes 393248 | tf_op jit(solution)/shard_map/ppermute | solution.py:276
  172.4 1.9 collective-permute-start.26
  174.3 4.2 %collective-permute-start.27 = (bf16[2,128,768]{2,1,0:T(8,128)(2,1)S(1)}, bf16[2,128,768]{2,1,0:T(8,128)(2,1)S(1)}, u32[]{:S(2)}, u32[]{:S(2)}) collective-permute-start(bf16[2,128,768]{2,1,0:T(8,128)(2,1)S(1)} %get-tuple-element.49), channel_id=1, source_target_pairs={{0,256},{32,288},{64,320},{96,352},{128,384},{160,416},{192,448},{... | collective-permute-start | bytes 1179656 | tf_op jit(solution)/shard_map/ppermute | solution.py:276
  178.5 0.2 convert_add_fusion.2
  178.7 3.3 %collective-permute-done.22 = bf16[2,128,768]{2,1,0:T(8,128)(2,1)S(1)} collective-permute-done((bf16[2,128,768]{2,1,0:T(8,128)(2,1)S(1)}, bf16[2,128,768]{2,1,0:T(8,128)(2,1)S(1)}, u32[]{:S(2)}, u32[]{:S(2)}) %collective-permute-start.22) | collective-permute-done | bytes 393248 | tf_op jit(solution)/shard_map/ppermute | solution.py:276
  181.9 2.0 collective-permute-start.28
  183.9 5.4 %collective-permute-done.23 = bf16[2,128,768]{2,1,0:T(8,128)(2,1)S(1)} collective-permute-done((bf16[2,128,768]{2,1,0:T(8,128)(2,1)S(1)}, bf16[2,128,768]{2,1,0:T(8,128)(2,1)S(1)}, u32[]{:S(2)}, u32[]{:S(2)}) %collective-permute-start.23) | collective-permute-done | bytes 393248 | tf_op jit(solution)/shard_map/ppermute | solution.py:276
  189.3 4.5 %collective-permute-start.21 = (bf16[128,768]{1,0:T(8,128)(2,1)S(1)}, bf16[128,768]{1,0:T(8,128)(2,1)S(1)}, u32[]{:S(2)}, u32[]{:S(2)}) collective-permute-start(bf16[128,768]{1,0:T(8,128)(2,1)S(1)} %fusion.6), channel_id=1, source_target_pairs={{0,64},{32,96},{64,0},{96,32},{128,192},{160,224},{192,128},{224,1... | collective-permute-start | bytes 589832 | tf_op jit(solution)/shard_map/ppermute | solution.py:276
  193.8 0.2 convert_add_fusion.1
  194.0 2.3 collective-permute-start.25
  196.3 2.5 %collective-permute-done.26 = bf16[2,128,768]{2,1,0:T(8,128)(2,1)S(1)} collective-permute-done((bf16[2,128,768]{2,1,0:T(8,128)(2,1)S(1)}, bf16[2,128,768]{2,1,0:T(8,128)(2,1)S(1)}, u32[]{:S(2)}, u32[]{:S(2)}) %collective-permute-start.26) | collective-permute-done | bytes 393248 | tf_op jit(solution)/shard_map/ppermute | solution.py:276
  198.8 7.4 %collective-permute-done.27 = bf16[2,128,768]{2,1,0:T(8,128)(2,1)S(1)} collective-permute-done((bf16[2,128,768]{2,1,0:T(8,128)(2,1)S(1)}, bf16[2,128,768]{2,1,0:T(8,128)(2,1)S(1)}, u32[]{:S(2)}, u32[]{:S(2)}) %collective-permute-start.27) | collective-permute-done | bytes 393248 | tf_op jit(solution)/shard_map/ppermute | solution.py:276
  206.1 1.3 collective-permute-done.28
  207.4 0.2 convert_add_fusion
  207.6 0.0 copy-start.3
  207.6 4.5 %collective-permute-start.29 = (bf16[128,768]{1,0:T(8,128)(2,1)S(1)}, bf16[128,768]{1,0:T(8,128)(2,1)S(1)}, u32[]{:S(2)}, u32[]{:S(2)}) collective-permute-start(bf16[128,768]{1,0:T(8,128)(2,1)S(1)} %fusion.8), channel_id=1, source_target_pairs={{0,64},{32,96},{64,0},{96,32},{128,192},{160,224},{192,128},{224,1... | collective-permute-start | bytes 589832 | tf_op jit(solution)/shard_map/ppermute | solution.py:276
  212.2 0.8 fusion.5
  213.0 0.8 fusion.3
  213.7 2.4 %collective-permute-done.29 = bf16[128,768]{1,0:T(8,128)(2,1)S(1)} collective-permute-done((bf16[128,768]{1,0:T(8,128)(2,1)S(1)}, bf16[128,768]{1,0:T(8,128)(2,1)S(1)}, u32[]{:S(2)}, u32[]{:S(2)}) %collective-permute-start.29) | collective-permute-done | bytes 196640 | tf_op jit(solution)/shard_map/ppermute | solution.py:276
  216.1 0.8 fusion.1
  216.9 16.2 %all-to-all-done.1 = bf16[32,8,4096]{2,1,0:T(8,128)(2,1)S(1)} async-done(((bf16[32,8,4096]{2,1,0:T(8,128)(2,1)}), bf16[32,8,4096]{2,1,0:T(8,128)(2,1)S(1)}, u32[]{:S(2)}, u32[]{:S(2)}) %all-to-all-start.1) | async-done | bytes 2097184 | tf_op jit(solution)/shard_map/all_to_all | solution.py:295
  233.1 1.3 shard_map.112
  (50 shorter events, 0.2 us)
Async XLA Ops:
  3.6 16.0 %copy-start.4 = (bf16[1,128,768]{2,1,0:T(8,128)(2,1)S(1)}, bf16[1,128,768]{2,1,0:T(8,128)(2,1)}, u32[]{:S(2)}) copy-start(bf16[1,128,768]{2,1,0:T(8,128)(2,1)} %param.11) | copy-start | bytes 589828
  3.6 16.0 %copy-start.5 = (bf16[1,128,768]{2,1,0:T(8,128)(2,1)S(1)}, bf16[1,128,768]{2,1,0:T(8,128)(2,1)}, u32[]{:S(2)}) copy-start(bf16[1,128,768]{2,1,0:T(8,128)(2,1)} %param.12) | copy-start | bytes 589828
  3.6 16.0 %copy-start.6 = (bf16[1,128,768]{2,1,0:T(8,128)(2,1)S(1)}, bf16[1,128,768]{2,1,0:T(8,128)(2,1)}, u32[]{:S(2)}) copy-start(bf16[1,128,768]{2,1,0:T(8,128)(2,1)} %param.13) | copy-start | bytes 589828
  3.6 116.5 %all-to-all-start = ((bf16[32,8,4096]{2,1,0:T(8,128)(2,1)}), bf16[32,8,4096]{2,1,0:T(8,128)(2,1)S(1)}, u32[]{:S(2)}, u32[]{:S(2)}) async-start(bf16[32,8,4096]{2,1,0:T(8,128)(2,1)} %bitcast.43), calls=%async_computation | async-start | bytes 4194304 | tf_op jit(solution)/shard_map/all_to_all | solution.py:295
  19.7 13.9 %copy-start.7 = (bf16[3,128,768]{2,1,0:T(8,128)(2,1)}, bf16[3,128,768]{2,1,0:T(8,128)(2,1)S(1)}, u32[]{:S(2)}) copy-start(bf16[3,128,768]{2,1,0:T(8,128)(2,1)S(1)} %constant_dynamic-update-slice_fusion.refs_1_) | copy-start | bytes 1769476
  19.7 19.7 %collective-permute-start.7 = (bf16[3,128,768]{2,1,0:T(8,128)(2,1)S(1)}, bf16[3,128,768]{2,1,0:T(8,128)(2,1)S(1)}, u32[]{:S(2)}, u32[]{:S(2)}) collective-permute-start(bf16[3,128,768]{2,1,0:T(8,128)(2,1)S(1)} %constant_dynamic-update-slice_fusion.refs_1_), channel_id=1, source_target_pairs={{0,64},{32,96},{64,0},{96,32},{128,192},{160,224},{192,128},{224,1... | collective-permute-start | bytes 1769480 | tf_op jit(solution)/shard_map/ppermute | solution.py:276
  24.2 19.6 %collective-permute-start.5 = (bf16[3,128,768]{2,1,0:T(8,128)(2,1)S(1)}, bf16[3,128,768]{2,1,0:T(8,128)(2,1)S(1)}, u32[]{:S(2)}, u32[]{:S(2)}) collective-permute-start(bf16[3,128,768]{2,1,0:T(8,128)(2,1)S(1)} %constant_dynamic-update-slice_fusion.refs_1_), channel_id=1, source_target_pairs={{0,384},{32,416},{64,448},{96,480},{128,0},{160,32},{192,64},{224,... | collective-permute-start | bytes 1769480 | tf_op jit(solution)/shard_map/ppermute | solution.py:276
  28.6 17.7 %collective-permute-start.3 = (bf16[3,128,768]{2,1,0:T(8,128)(2,1)S(1)}, bf16[3,128,768]{2,1,0:T(8,128)(2,1)S(1)}, u32[]{:S(2)}, u32[]{:S(2)}) collective-permute-start(bf16[3,128,768]{2,1,0:T(8,128)(2,1)S(1)} %constant_dynamic-update-slice_fusion.refs_1_), channel_id=1, source_target_pairs={{0,256},{32,288},{64,320},{96,352},{128,384},{160,416},{192,448},{... | collective-permute-start | bytes 1769480 | tf_op jit(solution)/shard_map/ppermute | solution.py:276
  31.0 31.0 %collective-permute-start.1 = (bf16[3,128,768]{2,1,0:T(8,128)(2,1)S(1)}, bf16[3,128,768]{2,1,0:T(8,128)(2,1)S(1)}, u32[]{:S(2)}, u32[]{:S(2)}) collective-permute-start(bf16[3,128,768]{2,1,0:T(8,128)(2,1)S(1)} %constant_dynamic-update-slice_fusion.refs_1_), channel_id=1, source_target_pairs={{0,128},{32,160},{64,192},{96,224},{128,256},{160,288},{192,320},{... | collective-permute-start | bytes 1769480 | tf_op jit(solution)/shard_map/ppermute | solution.py:276
  33.6 32.7 %collective-permute-start = (bf16[3,128,768]{2,1,0:T(8,128)(2,1)S(1)}, bf16[3,128,768]{2,1,0:T(8,128)(2,1)S(1)}, u32[]{:S(2)}, u32[]{:S(2)}) collective-permute-start(bf16[3,128,768]{2,1,0:T(8,128)(2,1)S(1)} %constant_dynamic-update-slice_fusion.refs_1_), channel_id=1, source_target_pairs={{0,32},{32,0},{64,96},{96,64},{128,160},{160,128},{192,224},{224,1... | collective-permute-start | bytes 1769480 | tf_op jit(solution)/shard_map/ppermute | solution.py:276
  39.4 26.8 %copy-start.8 = (bf16[3,128,768]{2,1,0:T(8,128)(2,1)}, bf16[3,128,768]{2,1,0:T(8,128)(2,1)S(1)}, u32[]{:S(2)}) copy-start(bf16[3,128,768]{2,1,0:T(8,128)(2,1)S(1)} %collective-permute-done.7.refs_9_) | copy-start | bytes 1769476
  39.4 28.8 %collective-permute-start.13 = (bf16[3,128,768]{2,1,0:T(8,128)(2,1)S(1)}, bf16[3,128,768]{2,1,0:T(8,128)(2,1)}, u32[]{:S(2)}, u32[]{:S(2)}) collective-permute-start(bf16[3,128,768]{2,1,0:T(8,128)(2,1)S(1)} %collective-permute-done.7.refs_9_), channel_id=1, source_target_pairs={{0,384},{32,416},{64,448},{96,480},{128,0},{160,32},{192,64},{224,... | collective-permute-start | bytes 1769480 | tf_op jit(solution)/shard_map/ppermute | solution.py:276
  43.8 43.9 %copy-start.9 = (bf16[3,128,768]{2,1,0:T(8,128)(2,1)}, bf16[3,128,768]{2,1,0:T(8,128)(2,1)S(1)}, u32[]{:S(2)}) copy-start(bf16[3,128,768]{2,1,0:T(8,128)(2,1)S(1)} %collective-permute-done.5.refs_7_) | copy-start | bytes 1769476
  43.8 38.2 %collective-permute-start.11 = (bf16[3,128,768]{2,1,0:T(8,128)(2,1)S(1)}, bf16[3,128,768]{2,1,0:T(8,128)(2,1)}, u32[]{:S(2)}, u32[]{:S(2)}) collective-permute-start(bf16[3,128,768]{2,1,0:T(8,128)(2,1)S(1)} %collective-permute-done.7.refs_9_), channel_id=1, source_target_pairs={{0,256},{32,288},{64,320},{96,352},{128,384},{160,416},{192,448},{... | collective-permute-start | bytes 1769480 | tf_op jit(solution)/shard_map/ppermute | solution.py:276
  46.3 73.8 %copy-start.10 = (bf16[3,128,768]{2,1,0:T(8,128)(2,1)}, bf16[3,128,768]{2,1,0:T(8,128)(2,1)S(1)}, u32[]{:S(2)}) copy-start(bf16[3,128,768]{2,1,0:T(8,128)(2,1)S(1)} %collective-permute-done.3.refs_5_) | copy-start | bytes 1769476
  46.3 38.9 %collective-permute-start.9 = (bf16[3,128,768]{2,1,0:T(8,128)(2,1)S(1)}, bf16[3,128,768]{2,1,0:T(8,128)(2,1)}, u32[]{:S(2)}, u32[]{:S(2)}) collective-permute-start(bf16[3,128,768]{2,1,0:T(8,128)(2,1)S(1)} %collective-permute-done.7.refs_9_), channel_id=1, source_target_pairs={{0,128},{32,160},{64,192},{96,224},{128,256},{160,288},{192,320},{... | collective-permute-start | bytes 1769480 | tf_op jit(solution)/shard_map/ppermute | solution.py:276
  62.1 58.0 %copy-start.11 = (bf16[3,128,768]{2,1,0:T(8,128)(2,1)}, bf16[3,128,768]{2,1,0:T(8,128)(2,1)S(1)}, u32[]{:S(2)}) copy-start(bf16[3,128,768]{2,1,0:T(8,128)(2,1)S(1)} %collective-permute-done.1.refs_3_) | copy-start | bytes 1769476
  62.1 25.6 %collective-permute-start.8 = (bf16[3,128,768]{2,1,0:T(8,128)(2,1)S(1)}, bf16[3,128,768]{2,1,0:T(8,128)(2,1)S(1)}, u32[]{:S(2)}, u32[]{:S(2)}) collective-permute-start(bf16[3,128,768]{2,1,0:T(8,128)(2,1)S(1)} %collective-permute-done.7.refs_9_), channel_id=1, source_target_pairs={{0,32},{32,0},{64,96},{96,64},{128,160},{160,128},{192,224},{224,1... | collective-permute-start | bytes 1769480 | tf_op jit(solution)/shard_map/ppermute | solution.py:276
  66.3 23.4 %copy-start.12 = (bf16[3,128,768]{2,1,0:T(8,128)(2,1)}, bf16[3,128,768]{2,1,0:T(8,128)(2,1)S(1)}, u32[]{:S(2)}) copy-start(bf16[3,128,768]{2,1,0:T(8,128)(2,1)S(1)} %collective-permute-done.refs_2_) | copy-start | bytes 1769476
  66.3 23.4 %collective-permute-start.6 = (bf16[3,128,768]{2,1,0:T(8,128)(2,1)S(1)}, bf16[3,128,768]{2,1,0:T(8,128)(2,1)S(1)}, u32[]{:S(2)}, u32[]{:S(2)}) collective-permute-start(bf16[3,128,768]{2,1,0:T(8,128)(2,1)S(1)} %collective-permute-done.5.refs_7_), channel_id=1, source_target_pairs={{0,32},{32,0},{64,96},{96,64},{128,160},{160,128},{192,224},{224,1... | collective-permute-start | bytes 1769480 | tf_op jit(solution)/shard_map/ppermute | solution.py:276
  68.2 23.9 %collective-permute-start.4 = (bf16[3,128,768]{2,1,0:T(8,128)(2,1)S(1)}, bf16[3,128,768]{2,1,0:T(8,128)(2,1)}, u32[]{:S(2)}, u32[]{:S(2)}) collective-permute-start(bf16[3,128,768]{2,1,0:T(8,128)(2,1)S(1)} %collective-permute-done.3.refs_5_), channel_id=1, source_target_pairs={{0,32},{32,0},{64,96},{96,64},{128,160},{160,128},{192,224},{224,1... | collective-permute-start | bytes 1769480 | tf_op jit(solution)/shard_map/ppermute | solution.py:276
  82.0 10.1 %collective-permute-start.2 = (bf16[3,128,768]{2,1,0:T(8,128)(2,1)S(1)}, bf16[3,128,768]{2,1,0:T(8,128)(2,1)}, u32[]{:S(2)}, u32[]{:S(2)}) collective-permute-start(bf16[3,128,768]{2,1,0:T(8,128)(2,1)S(1)} %collective-permute-done.1.refs_3_), channel_id=1, source_target_pairs={{0,32},{32,0},{64,96},{96,64},{128,160},{160,128},{192,224},{224,1... | collective-permute-start | bytes 1769480 | tf_op jit(solution)/shard_map/ppermute | solution.py:276
  85.2 7.0 %collective-permute-start.14 = (bf16[3,128,768]{2,1,0:T(8,128)(2,1)}, bf16[3,128,768]{2,1,0:T(8,128)(2,1)}, u32[]{:S(2)}, u32[]{:S(2)}) collective-permute-start(bf16[3,128,768]{2,1,0:T(8,128)(2,1)} %collective-permute-done.13.refs_15_), channel_id=1, source_target_pairs={{0,32},{32,0},{64,96},{96,64},{128,160},{160,128},{192,224},{224,1... | collective-permute-start | bytes 1769480 | tf_op jit(solution)/shard_map/ppermute | solution.py:276
  87.7 4.4 %copy-start.13 = (bf16[3,128,768]{2,1,0:T(8,128)(2,1)}, bf16[3,128,768]{2,1,0:T(8,128)(2,1)S(1)}, u32[]{:S(2)}) copy-start(bf16[3,128,768]{2,1,0:T(8,128)(2,1)S(1)} %collective-permute-done.8.refs_10_) | copy-start | bytes 1769476
  87.7 4.5 %collective-permute-start.12 = (bf16[3,128,768]{2,1,0:T(8,128)(2,1)}, bf16[3,128,768]{2,1,0:T(8,128)(2,1)}, u32[]{:S(2)}, u32[]{:S(2)}) collective-permute-start(bf16[3,128,768]{2,1,0:T(8,128)(2,1)} %collective-permute-done.11.refs_13_), channel_id=1, source_target_pairs={{0,32},{32,0},{64,96},{96,64},{128,160},{160,128},{192,224},{224,1... | collective-permute-start | bytes 1769480 | tf_op jit(solution)/shard_map/ppermute | solution.py:276
  89.7 2.4 %copy-start.14 = (bf16[3,128,768]{2,1,0:T(8,128)(2,1)}, bf16[3,128,768]{2,1,0:T(8,128)(2,1)S(1)}, u32[]{:S(2)}) copy-start(bf16[3,128,768]{2,1,0:T(8,128)(2,1)S(1)} %collective-permute-done.6.refs_8_) | copy-start | bytes 1769476
  89.7 4.4 %collective-permute-start.10 = (bf16[3,128,768]{2,1,0:T(8,128)(2,1)}, bf16[3,128,768]{2,1,0:T(8,128)(2,1)}, u32[]{:S(2)}, u32[]{:S(2)}) collective-permute-start(bf16[3,128,768]{2,1,0:T(8,128)(2,1)} %collective-permute-done.9.refs_11_), channel_id=1, source_target_pairs={{0,32},{32,0},{64,96},{96,64},{128,160},{160,128},{192,224},{224,1... | collective-permute-start | bytes 1769480 | tf_op jit(solution)/shard_map/ppermute | solution.py:276
  120.1 9.6 %copy-start = (bf16[32,8,4096]{2,1,0:T(8,128)(2,1)}, bf16[32,8,4096]{2,1,0:T(8,128)(2,1)S(1)}, u32[]{:S(2)}) copy-start(bf16[32,8,4096]{2,1,0:T(8,128)(2,1)S(1)} %all-to-all-done) | copy-start | bytes 6291460
  129.7 103.4 %all-to-all-start.1 = ((bf16[32,8,4096]{2,1,0:T(8,128)(2,1)}), bf16[32,8,4096]{2,1,0:T(8,128)(2,1)S(1)}, u32[]{:S(2)}, u32[]{:S(2)}) async-start(bf16[32,8,4096]{2,1,0:T(8,128)(2,1)} %bitcast.42), calls=%async_computation.1 | async-start | bytes 4194304 | tf_op jit(solution)/shard_map/all_to_all | solution.py:295
  133.5 1.6 copy-start.1
  135.1 12.2 %copy-start.2 = (bf16[32,8,4096]{2,1,0:T(8,128)(2,1)S(1)}, bf16[32,8,4096]{2,1,0:T(8,128)(2,1)}, u32[]{:S(2)}) copy-start(bf16[32,8,4096]{2,1,0:T(8,128)(2,1)} %copy-done) | copy-start | bytes 6291460
  137.1 7.2 %collective-permute-start.15 = (bf16[8,128,768]{2,1,0:T(8,128)(2,1)S(1)}, bf16[8,128,768]{2,1,0:T(8,128)(2,1)S(1)}, u32[]{:S(2)}, u32[]{:S(2)}) collective-permute-start(bf16[8,128,768]{2,1,0:T(8,128)(2,1)S(1)} %get-tuple-element.36), channel_id=1, source_target_pairs={{0,32},{32,0},{64,96},{96,64},{128,160},{160,128},{192,224},{224,1... | collective-permute-start | bytes 4718600 | tf_op jit(solution)/shard_map/ppermute | solution.py:276
  139.8 5.3 %collective-permute-start.16 = (bf16[8,128,768]{2,1,0:T(8,128)(2,1)S(1)}, bf16[8,128,768]{2,1,0:T(8,128)(2,1)S(1)}, u32[]{:S(2)}, u32[]{:S(2)}) collective-permute-start(bf16[8,128,768]{2,1,0:T(8,128)(2,1)S(1)} %get-tuple-element.37), channel_id=1, source_target_pairs={{0,32},{32,0},{64,96},{96,64},{128,160},{160,128},{192,224},{224,1... | collective-permute-start | bytes 4718600 | tf_op jit(solution)/shard_map/ppermute | solution.py:276
  141.7 5.6 %collective-permute-start.17 = (bf16[8,128,768]{2,1,0:T(8,128)(2,1)S(1)}, bf16[8,128,768]{2,1,0:T(8,128)(2,1)S(1)}, u32[]{:S(2)}, u32[]{:S(2)}) collective-permute-start(bf16[8,128,768]{2,1,0:T(8,128)(2,1)S(1)} %get-tuple-element.38), channel_id=1, source_target_pairs={{0,32},{32,0},{64,96},{96,64},{128,160},{160,128},{192,224},{224,1... | collective-permute-start | bytes 4718600 | tf_op jit(solution)/shard_map/ppermute | solution.py:276
  149.4 15.6 %collective-permute-start.18 = (bf16[2,128,768]{2,1,0:T(8,128)(2,1)S(1)}, bf16[2,128,768]{2,1,0:T(8,128)(2,1)S(1)}, u32[]{:S(2)}, u32[]{:S(2)}) collective-permute-start(bf16[2,128,768]{2,1,0:T(8,128)(2,1)S(1)} %get-tuple-element.40), channel_id=1, source_target_pairs={{0,128},{32,160},{64,192},{96,224},{128,256},{160,288},{192,320},{... | collective-permute-start | bytes 1179656 | tf_op jit(solution)/shard_map/ppermute | solution.py:276
  152.5 19.9 %collective-permute-start.19 = (bf16[2,128,768]{2,1,0:T(8,128)(2,1)S(1)}, bf16[2,128,768]{2,1,0:T(8,128)(2,1)S(1)}, u32[]{:S(2)}, u32[]{:S(2)}) collective-permute-start(bf16[2,128,768]{2,1,0:T(8,128)(2,1)S(1)} %get-tuple-element.41), channel_id=1, source_target_pairs={{0,256},{32,288},{64,320},{96,352},{128,384},{160,416},{192,448},{... | collective-permute-start | bytes 1179656 | tf_op jit(solution)/shard_map/ppermute | solution.py:276
  156.9 17.4 %collective-permute-start.20 = (bf16[2,128,768]{2,1,0:T(8,128)(2,1)S(1)}, bf16[2,128,768]{2,1,0:T(8,128)(2,1)S(1)}, u32[]{:S(2)}, u32[]{:S(2)}) collective-permute-start(bf16[2,128,768]{2,1,0:T(8,128)(2,1)S(1)} %get-tuple-element.42), channel_id=1, source_target_pairs={{0,384},{32,416},{64,448},{96,480},{128,0},{160,32},{192,64},{224,... | collective-permute-start | bytes 1179656 | tf_op jit(solution)/shard_map/ppermute | solution.py:276
  160.0 22.0 %collective-permute-start.22 = (bf16[2,128,768]{2,1,0:T(8,128)(2,1)S(1)}, bf16[2,128,768]{2,1,0:T(8,128)(2,1)S(1)}, u32[]{:S(2)}, u32[]{:S(2)}) collective-permute-start(bf16[2,128,768]{2,1,0:T(8,128)(2,1)S(1)} %get-tuple-element.44), channel_id=1, source_target_pairs={{0,128},{32,160},{64,192},{96,224},{128,256},{160,288},{192,320},{... | collective-permute-start | bytes 1179656 | tf_op jit(solution)/shard_map/ppermute | solution.py:276
  162.2 27.1 %collective-permute-start.23 = (bf16[2,128,768]{2,1,0:T(8,128)(2,1)S(1)}, bf16[2,128,768]{2,1,0:T(8,128)(2,1)S(1)}, u32[]{:S(2)}, u32[]{:S(2)}) collective-permute-start(bf16[2,128,768]{2,1,0:T(8,128)(2,1)S(1)} %get-tuple-element.45), channel_id=1, source_target_pairs={{0,256},{32,288},{64,320},{96,352},{128,384},{160,416},{192,448},{... | collective-permute-start | bytes 1179656 | tf_op jit(solution)/shard_map/ppermute | solution.py:276
  165.0 28.8 %collective-permute-start.24 = (bf16[2,128,768]{2,1,0:T(8,128)(2,1)S(1)}, bf16[2,128,768]{2,1,0:T(8,128)(2,1)S(1)}, u32[]{:S(2)}, u32[]{:S(2)}) collective-permute-start(bf16[2,128,768]{2,1,0:T(8,128)(2,1)S(1)} %get-tuple-element.46), channel_id=1, source_target_pairs={{0,384},{32,416},{64,448},{96,480},{128,0},{160,32},{192,64},{224,... | collective-permute-start | bytes 1179656 | tf_op jit(solution)/shard_map/ppermute | solution.py:276
  172.4 26.4 %collective-permute-start.26 = (bf16[2,128,768]{2,1,0:T(8,128)(2,1)S(1)}, bf16[2,128,768]{2,1,0:T(8,128)(2,1)S(1)}, u32[]{:S(2)}, u32[]{:S(2)}) collective-permute-start(bf16[2,128,768]{2,1,0:T(8,128)(2,1)S(1)} %get-tuple-element.48), channel_id=1, source_target_pairs={{0,128},{32,160},{64,192},{96,224},{128,256},{160,288},{192,320},{... | collective-permute-start | bytes 1179656 | tf_op jit(solution)/shard_map/ppermute | solution.py:276
  174.3 31.8 %collective-permute-start.27 = (bf16[2,128,768]{2,1,0:T(8,128)(2,1)S(1)}, bf16[2,128,768]{2,1,0:T(8,128)(2,1)S(1)}, u32[]{:S(2)}, u32[]{:S(2)}) collective-permute-start(bf16[2,128,768]{2,1,0:T(8,128)(2,1)S(1)} %get-tuple-element.49), channel_id=1, source_target_pairs={{0,256},{32,288},{64,320},{96,352},{128,384},{160,416},{192,448},{... | collective-permute-start | bytes 1179656 | tf_op jit(solution)/shard_map/ppermute | solution.py:276
  181.9 25.4 %collective-permute-start.28 = (bf16[2,128,768]{2,1,0:T(8,128)(2,1)S(1)}, bf16[2,128,768]{2,1,0:T(8,128)(2,1)S(1)}, u32[]{:S(2)}, u32[]{:S(2)}) collective-permute-start(bf16[2,128,768]{2,1,0:T(8,128)(2,1)S(1)} %get-tuple-element.50), channel_id=1, source_target_pairs={{0,384},{32,416},{64,448},{96,480},{128,0},{160,32},{192,64},{224,... | collective-permute-start | bytes 1179656 | tf_op jit(solution)/shard_map/ppermute | solution.py:276
  189.3 22.9 %collective-permute-start.21 = (bf16[128,768]{1,0:T(8,128)(2,1)S(1)}, bf16[128,768]{1,0:T(8,128)(2,1)S(1)}, u32[]{:S(2)}, u32[]{:S(2)}) collective-permute-start(bf16[128,768]{1,0:T(8,128)(2,1)S(1)} %fusion.6), channel_id=1, source_target_pairs={{0,64},{32,96},{64,0},{96,32},{128,192},{160,224},{192,128},{224,1... | collective-permute-start | bytes 589832 | tf_op jit(solution)/shard_map/ppermute | solution.py:276
  194.0 18.9 %collective-permute-start.25 = (bf16[128,768]{1,0:T(8,128)(2,1)S(1)}, bf16[128,768]{1,0:T(8,128)(2,1)S(1)}, u32[]{:S(2)}, u32[]{:S(2)}) collective-permute-start(bf16[128,768]{1,0:T(8,128)(2,1)S(1)} %fusion.7), channel_id=1, source_target_pairs={{0,64},{32,96},{64,0},{96,32},{128,192},{160,224},{192,128},{224,1... | collective-permute-start | bytes 589832 | tf_op jit(solution)/shard_map/ppermute | solution.py:276
  207.6 25.5 %copy-start.3 = (s32[128,1]{0,1:T(1,128)S(1)}, s32[128,1]{0,1:T(1,128)}, u32[]{:S(2)}) copy-start(s32[128,1]{0,1:T(1,128)} %param.9) | copy-start | bytes 1540
  207.6 8.5 %collective-permute-start.29 = (bf16[128,768]{1,0:T(8,128)(2,1)S(1)}, bf16[128,768]{1,0:T(8,128)(2,1)S(1)}, u32[]{:S(2)}, u32[]{:S(2)}) collective-permute-start(bf16[128,768]{1,0:T(8,128)(2,1)S(1)} %fusion.8), channel_id=1, source_target_pairs={{0,64},{32,96},{64,0},{96,32},{128,192},{160,224},{192,128},{224,1... | collective-permute-start | bytes 589832 | tf_op jit(solution)/shard_map/ppermute | solution.py:276
